TPU v7x, 512 devices: a whole 4x8x8 slice. The times are simulated.
512 devices in a mesh: group: 16 (over z, core), dom: 32 (over y, x).
Axes of the slice: x: 4, y: 8, z: 8, core: 2. Of those that a mesh axis runs over, the one named last changes fastest.
Arguments:
- queries: bfloat16 [131072, 512], P(('group', 'dom')), may hold values from -8 to 8
- keys: bfloat16 [131072, 512], P(('group', 'dom')), may hold values from -8 to 8
- values: bfloat16 [131072, 512], P(('group', 'dom')), may hold values from -6 to 6
- cotangent: bfloat16 [131072, 512], P(('group', 'dom')), may hold values from -6 to 6
- local_list: int32 [1024, 3], P('group'), may hold values from 0 to 63, as said below
- far_list: int32 [32, 32, 3], P('dom'), may hold values from 0 to 31, as said below
Outputs:
- attended: bfloat16 [131072, 512], P(('group', 'dom'))
- grad_queries: bfloat16 [131072, 512], P(('group', 'dom'))
- grad_keys: bfloat16 [131072, 512], P(('group', 'dom'))
- grad_values: bfloat16 [131072, 512], P(('group', 'dom'))
Inputs may be any that keep to these rules, and one draw needn't show every extreme that they name: `local_list`: an entry names a block of the query block's own cluster held by the same device or by a device at most 2 places away along dom. Over the 2 query blocks of one device, the entries name exactly one block of each other device within that reach; devices with fewer than 2 neighbours on a side list their own blocks in those places. Row g * 2 + s of far_list[d] belongs to query block (g, d, s); an entry v names slot v % 2 of the device at position d of cluster v // 2, never cluster g. Over the 2 query blocks of one device, at most one distinct block of each other cluster is named.
All inputs are finite; a program needn't handle non-finite values.
Results may differ from a plain program's by a relative error of at most 0.012.
The roundings to bfloat16 on the way count: a program that leaves them out, or rounds other values in their place, can miss the bound.
Values may be sent and summed in bfloat16 or wider, within the bound.
No kernel may reach another device: no remote copies, remote signals or barrier semaphores. Data moves between devices by JAX's collectives and lax.ppermute only.
A program may use at most 128 MiB of HBM per device.

v0:
```python
import math

import jax
import jax.numpy as jnp
from jax import lax
from jax.sharding import PartitionSpec as P

D = 512
H = 8
BS = 128
NB = 2
LOC = 3
EXP = 3
W = 2


def shifted(array, axis, by):
    size = lax.axis_size(axis)
    pairs = [(i, i + by) for i in range(size) if 0 <= i + by < size]
    return lax.ppermute(array, axis, pairs)


def attend_block(query_blk, grad_blk, key_set, value_set):
    head_size = D // H
    score_scale = 1.0 / math.sqrt(head_size)
    query_heads = query_blk.reshape(BS, H, head_size)
    grad_heads = grad_blk.reshape(BS, H, head_size)
    key_heads = key_set.reshape(-1, H, head_size)
    value_heads = value_set.reshape(-1, H, head_size)
    scores = (
        jnp.einsum("ihe,nhe->hin", query_heads, key_heads, preferred_element_type=jnp.float32)
        * score_scale
    )
    highest = jnp.max(scores, axis=-1, keepdims=True)
    raised = jnp.exp(scores - highest)
    attention = raised / jnp.sum(raised, axis=-1, keepdims=True)
    attention_low = attention.astype(jnp.bfloat16)
    mixture = jnp.einsum(
        "hin,nhe->ihe", attention_low, value_heads, preferred_element_type=jnp.float32
    )
    carried = jnp.sum(grad_heads.astype(jnp.float32) * mixture, axis=-1)
    grad_attention = jnp.einsum(
        "ihe,nhe->hin", grad_heads, value_heads, preferred_element_type=jnp.float32
    )
    grad_scores = (attention * (grad_attention - carried.T[:, :, None]) * score_scale).astype(
        jnp.bfloat16
    )
    grad_query = jnp.einsum(
        "hin,nhe->ihe", grad_scores, key_heads, preferred_element_type=jnp.float32
    )
    grad_key = jnp.einsum(
        "hin,ihe->nhe", grad_scores, query_heads, preferred_element_type=jnp.float32
    )
    grad_value = jnp.einsum(
        "hin,ihe->nhe", attention_low, grad_heads, preferred_element_type=jnp.float32
    )
    return (
        mixture.reshape(BS, D).astype(jnp.bfloat16),
        grad_query.reshape(BS, D).astype(jnp.bfloat16),
        grad_key.reshape(-1, BS, D),
        grad_value.reshape(-1, BS, D),
    )


def on_device(queries, keys, values, cotangent, local_list, far_list):
    group_count = lax.axis_size("group")
    dom_index = lax.axis_index("dom")
    group_index = lax.axis_index("group")
    query_blocks = queries.reshape(NB, BS, D)
    grad_blocks = cotangent.reshape(NB, BS, D)
    paired = jnp.stack([keys.reshape(NB, BS, D), values.reshape(NB, BS, D)])
    own_rows = lax.dynamic_slice_in_dim(local_list, dom_index * NB, NB, 0)
    far_rows = far_list[0]
    own_far = lax.dynamic_slice_in_dim(far_rows, group_index * NB, NB, 0)
    offsets = [distance for distance in range(-W, W + 1) if distance != 0]
    slot_range = jnp.arange(NB, dtype=jnp.int32)
    window_pieces = []
    for distance in range(-W, W + 1):
        if distance == 0:
            window_pieces.append(paired)
        else:
            window_pieces.append(shifted(paired, "dom", -distance))
    local_set = jnp.concatenate(window_pieces, axis=1)
    local_index = own_rows - (dom_index - W) * NB
    self_index = W * NB + slot_range
    asked = far_rows.reshape(group_count, NB * EXP)
    far_hit = asked // NB == group_index
    far_given = jnp.max(jnp.where(far_hit, asked % NB, 0), axis=1)
    far_out = jnp.take(paired, far_given, axis=1)
    far_set = lax.all_to_all(far_out, "group", split_axis=1, concat_axis=1, tiled=True)
    near_listed = jnp.concatenate([self_index[:, None], local_index], axis=1)
    far_listed = own_far // NB

    def visit_block(totals, inputs):
        near_keys, near_values, far_keys, far_values = totals
        query_blk, grad_blk, near_pick, far_pick = inputs
        near_sel = jnp.take(local_set, near_pick, axis=1)
        far_sel = jnp.take(far_set, far_pick, axis=1)
        picked = jnp.concatenate([near_sel, far_sel], axis=1)
        mixture, grad_query, grad_key, grad_value = attend_block(
            query_blk, grad_blk, picked[0].reshape(-1, D), picked[1].reshape(-1, D)
        )
        near_keys = near_keys.at[near_pick].add(grad_key[: 1 + LOC])
        near_values = near_values.at[near_pick].add(grad_value[: 1 + LOC])
        far_keys = far_keys.at[far_pick].add(grad_key[1 + LOC :])
        far_values = far_values.at[far_pick].add(grad_value[1 + LOC :])
        return ((near_keys, near_values, far_keys, far_values), (mixture, grad_query))

    near_empty = jnp.zeros((local_set.shape[1], BS, D), jnp.float32)
    far_empty = jnp.zeros((far_set.shape[1], BS, D), jnp.float32)
    totals, stacked = lax.scan(
        visit_block,
        (near_empty, near_empty, far_empty, far_empty),
        (query_blocks, grad_blocks, near_listed, far_listed),
    )
    near_keys, near_values, far_keys, far_values = totals
    mixture, grad_query = stacked
    local_parts = jnp.stack([near_keys, near_values]).astype(jnp.bfloat16)
    far_parts = jnp.stack([far_keys, far_values]).astype(jnp.bfloat16)
    owned_total = local_parts[:, W * NB : (W + 1) * NB].astype(jnp.float32)
    for offset in offsets:
        start_row = (W + offset) * NB
        returned = shifted(local_parts[:, start_row : start_row + NB], "dom", offset)
        owned_total = owned_total + returned.astype(jnp.float32)
    far_back = lax.all_to_all(far_parts, "group", split_axis=1, concat_axis=1, tiled=True)
    owned_total = owned_total.at[:, far_given].add(far_back.astype(jnp.float32))
    attended = mixture.reshape(NB * BS, D)
    grad_queries = grad_query.reshape(NB * BS, D)
    grad_keys = owned_total[0].reshape(NB * BS, D).astype(jnp.bfloat16)
    grad_values = owned_total[1].reshape(NB * BS, D).astype(jnp.bfloat16)
    return (attended, grad_queries, grad_keys, grad_values)


def solution(mesh):
    in_specs = (
        P(("group", "dom"), None),
        P(("group", "dom"), None),
        P(("group", "dom"), None),
        P(("group", "dom"), None),
        P("group", None),
        P("dom", None, None),
    )
    out_specs = (
        P(("group", "dom"), None),
        P(("group", "dom"), None),
        P(("group", "dom"), None),
        P(("group", "dom"), None),
    )
    return jax.shard_map(
        on_device, mesh=mesh, in_specs=in_specs, out_specs=out_specs, check_vma=False
    )
```

profile of v0, /device:TPU:57, one launch (start us, length us, event | category | flops | bytes accessed | tf_op | source)
XLA Modules:
  0.0 356.2 jit_solution(4932936862901591267)
XLA Ops:
  3.2 2.8 gather_fusion.2
  5.9 4.6 %select_bitcast_fusion.2 = bf16[2,16,128,512]{3,2,0,1:T(8,128)(2,1)} fusion(bf16[16,2,128,512]{3,2,1,0:T(8,128)(2,1)} %gather_fusion.2, pred[16]{0:T(512)(128)(4,1)S(1)} %compare_and_fusion.2), kind=kLoop, calls=%fused_computation.47 | loop fusion | flops 2097152 | bytes 8388624 | tf_op jit(solution)/shard_map/jit(_take)/select_n | solution.py:89
  10.6 11.1 %all-to-all-start = ((bf16[2,16,128,512]{3,2,0,1:T(8,128)(2,1)}), bf16[2,16,128,512]{3,2,0,1:T(8,128)(2,1)}, u32[]{:S(2)}, u32[]{:S(2)}) async-start(bf16[2,16,128,512]{3,2,0,1:T(8,128)(2,1)} %select_bitcast_fusion.2), calls=%async_computation | async-start | bytes 8388608 | tf_op jit(solution)/shard_map/all_to_all | solution.py:90
  21.7 5.4 %collective-permute-start.3 = (bf16[2,2,128,512]{3,2,1,0:T(8,128)(2,1)S(1)}, bf16[2,2,128,512]{3,2,1,0:T(8,128)(2,1)S(1)}, u32[]{:S(2)}, u32[]{:S(2)}) collective-permute-start(bf16[2,2,128,512]{3,2,1,0:T(8,128)(2,1)S(1)} %pad_maximum_fusion.3), channel_id=1, source_target_pairs={{2,0},{3,1},{4,2},{5,3},{6,4},{7,5},{8,6},{9,7},{10,8},{11,9},{12,... | collective-permute-start | bytes 1572872 | tf_op jit(solution)/shard_map/ppermute | solution.py:20
  27.1 2.8 collective-permute-start.2
  29.9 2.5 collective-permute-start.1
  32.4 2.6 collective-permute-start
  35.5 22.8 %collective-permute-done = bf16[2,2,128,512]{3,2,1,0:T(8,128)(2,1)S(1)} collective-permute-done((bf16[2,2,128,512]{3,2,1,0:T(8,128)(2,1)S(1)}, bf16[2,2,128,512]{3,2,1,0:T(8,128)(2,1)S(1)}, u32[]{:S(2)}, u32[]{:S(2)}) %collective-permute-start) | collective-permute-done | bytes 524320 | tf_op jit(solution)/shard_map/ppermute | solution.py:20
  62.5 52.8 %all-to-all-done = bf16[2,16,128,512]{3,2,0,1:T(8,128)(2,1)} async-done(((bf16[2,16,128,512]{3,2,0,1:T(8,128)(2,1)}), bf16[2,16,128,512]{3,2,0,1:T(8,128)(2,1)}, u32[]{:S(2)}, u32[]{:S(2)}) %all-to-all-start) | async-done | bytes 4194336 | tf_op jit(solution)/shard_map/all_to_all | solution.py:90
  115.3 4.6 %copy.43 = bf16[2,16,128,512]{3,2,1,0:T(8,128)(2,1)} copy(bf16[2,16,128,512]{3,2,0,1:T(8,128)(2,1)} %all-to-all-done) | data formatting | bytes 8388608 | tf_op jit(solution)/shard_map/while | solution.py:111
  119.9 1.8 broadcast_in_dim.50.clone
  121.7 1.8 broadcast_in_dim.50
  123.5 2.5 broadcast_in_dim.51.clone
  126.0 2.5 broadcast_in_dim.51
  128.5 103.5 %while.20 = (s32[]{:T(128)}, f32[10,128,512]{2,1,0:T(8,128)}, f32[10,128,512]{2,1,0:T(8,128)}, f32[16,128,512]{2,1,0:T(8,128)}, f32[16,128,512]{2,1,0:T(8,128)},...) while((s32[]{:T(128)}, f32[10,128,512]{2,1,0:T(8,128)}, ...), condition=%wide.region_10.11_spmd, body=%wide.region_2.10_spmd.sunk | while | flops 716900288 | bytes 125727336 | solution.py:111
  130.7 2.8 gather_fusion.1
  133.5 1.1 select_bitcast_fusion.6
  134.5 2.4 gather_fusion
  139.0 2.0 squeeze.24
  142.8 3.0 fusion.68
  145.8 2.5 fusion.69
  149.6 2.3 copy-done.4
  153.6 1.7 convolution_bitcast_fusion.5
  156.6 1.3 reshape.254
  157.9 2.6 copy.68
  160.5 1.4 reshape.256
  161.9 2.4 copy.70
  164.8 1.4 copy.69
  166.5 1.2 copy.71
  167.7 3.5 scatter_fusion.1
  171.3 3.2 scatter_fusion
  174.5 2.9 scatter_fusion.3
  177.4 3.0 scatter_fusion.2
  182.5 2.8 gather_fusion.1
  185.3 1.1 select_bitcast_fusion.6
  186.4 2.4 gather_fusion
  190.9 2.0 squeeze.24
  194.7 3.0 fusion.68
  197.7 2.5 fusion.69
  201.4 2.3 copy-done.4
  205.5 1.7 convolution_bitcast_fusion.5
  208.5 1.3 reshape.254
  209.8 2.6 copy.68
  212.4 1.4 reshape.256
  213.8 2.4 copy.70
  216.7 1.4 copy.69
  218.4 1.2 copy.71
  219.6 3.4 scatter_fusion.1
  223.1 3.0 scatter_fusion
  226.1 2.9 scatter_fusion.3
  229.1 2.9 scatter_fusion.2
  232.0 4.1 %convert_bitcast_fusion.1 = (bf16[1,16,128,512]{3,2,0,1:T(8,128)(2,1)S(1)}, bf16[1,16,128,512]{3,2,0,1:T(8,128)(2,1)S(1)}) fusion(f32[16,128,512]{2,1,0:T(8,128)} %get-tuple-element.81, f32[16,128,512]{2,1,0:T(8,128)} %get-tuple-element.80), kind=kLoop, calls=%fused_computation.56 | loop fusion | flops 2097152 | bytes 12582912 | tf_op jit(solution)/shard_map/stack | solution.py:119
  236.1 2.3 pad_maximum_fusion.1
  238.4 5.8 %all-to-all-start.1 = ((bf16[2,16,128,512]{3,2,0,1:T(8,128)(2,1)}), bf16[2,16,128,512]{3,2,0,1:T(8,128)(2,1)}, u32[]{:S(2)}, u32[]{:S(2)}) async-start(bf16[2,16,128,512]{3,2,0,1:T(8,128)(2,1)} %pad_maximum_fusion.1), calls=%async_computation.1 | async-start | bytes 8388608 | tf_op jit(solution)/shard_map/all_to_all | solution.py:125
  244.2 2.1 convert_bitcast_fusion.3
  246.5 5.4 %collective-permute-start.4 = (bf16[2,2,128,512]{3,2,1,0:T(8,128)(2,1)S(1)}, bf16[2,2,128,512]{3,2,1,0:T(8,128)(2,1)S(1)}, u32[]{:S(2)}, u32[]{:S(2)}) collective-permute-start(bf16[2,2,128,512]{3,2,1,0:T(8,128)(2,1)S(1)} %get-tuple-element.142), channel_id=1, source_target_pairs={{2,0},{3,1},{4,2},{5,3},{6,4},{7,5},{8,6},{9,7},{10,8},{11,9},{12,... | collective-permute-start | bytes 1572872 | tf_op jit(solution)/shard_map/ppermute | solution.py:20
  251.9 2.8 collective-permute-start.5
  254.8 3.0 collective-permute-start.7
  257.8 1.9 collective-permute-start.6
  259.7 16.5 %collective-permute-done.4 = bf16[2,2,128,512]{3,2,1,0:T(8,128)(2,1)S(1)} collective-permute-done((bf16[2,2,128,512]{3,2,1,0:T(8,128)(2,1)S(1)}, bf16[2,2,128,512]{3,2,1,0:T(8,128)(2,1)S(1)}, u32[]{:S(2)}, u32[]{:S(2)}) %collective-permute-start.4) | collective-permute-done | bytes 524320 | tf_op jit(solution)/shard_map/ppermute | solution.py:20
  276.2 9.0 %collective-permute-done.6 = bf16[2,2,128,512]{3,2,1,0:T(8,128)(2,1)S(1)} collective-permute-done((bf16[2,2,128,512]{3,2,1,0:T(8,128)(2,1)S(1)}, bf16[2,2,128,512]{3,2,1,0:T(8,128)(2,1)S(1)}, u32[]{:S(2)}, u32[]{:S(2)}) %collective-permute-start.6) | collective-permute-done | bytes 524320 | tf_op jit(solution)/shard_map/ppermute | solution.py:20
  285.6 52.2 %all-to-all-done.1 = bf16[2,16,128,512]{3,2,0,1:T(8,128)(2,1)} async-done(((bf16[2,16,128,512]{3,2,0,1:T(8,128)(2,1)}), bf16[2,16,128,512]{3,2,0,1:T(8,128)(2,1)}, u32[]{:S(2)}, u32[]{:S(2)}) %all-to-all-start.1) | async-done | bytes 4194336 | tf_op jit(solution)/shard_map/all_to_all | solution.py:125
  337.8 6.5 %convert_bitcast_fusion = f32[16,2,128,512]{3,2,1,0:T(8,128)} fusion(bf16[2,16,128,512]{3,2,0,1:T(8,128)(2,1)} %all-to-all-done.1), kind=kLoop, calls=%fused_computation.45 | loop fusion | flops 2097152 | bytes 12582912 | tf_op jit(solution)/shard_map/convert_element_type | solution.py:126
  344.4 10.9 %scatter_fusion.4 = f32[2,2,128,512]{3,2,1,0:T(8,128)S(1)} fusion(f32[2,2,128,512]{3,2,1,0:T(8,128)S(1)} %convert_add_fusion, s32[16]{0:T(128)S(1)} %copy-done.14, f32[16,2,128,512]{3,2,1,0:T(8,128)} %convert_bitcast_fusion), kind=kCustom, calls=%fused_computation.7 | custom fusion | flops 2097152 | bytes 25165888 | tf_op jit(solution)/shard_map/scatter-add | solution.py:126
  (135 shorter events, 30.8 us)
Async XLA Ops:
  0.6 34.6 %copy-start = (s32[64,3]{0,1:T(4,128)S(1)}, s32[64,3]{0,1:T(4,128)}, u32[]{:S(2)}) copy-start(s32[64,3]{0,1:T(4,128)} %param.12) | copy-start | bytes 2308
  1.6 0.5 copy-start.13
  10.6 24.4 %copy-start.12 = (s32[1,32,3]{1,0,2:T(1,128)S(1)}, s32[1,32,3]{1,0,2:T(1,128)}, u32[]{:S(2)}) copy-start(s32[1,32,3]{1,0,2:T(1,128)} %param.13) | copy-start | bytes 1156
  10.6 49.4 %copy-start.10 = (bf16[256,512]{1,0:T(8,128)(2,1)S(1)}, bf16[256,512]{1,0:T(8,128)(2,1)}, u32[]{:S(2)}) copy-start(bf16[256,512]{1,0:T(8,128)(2,1)} %param.10) | copy-start | bytes 786436
  10.6 49.4 %copy-start.11 = (bf16[256,512]{1,0:T(8,128)(2,1)S(1)}, bf16[256,512]{1,0:T(8,128)(2,1)}, u32[]{:S(2)}) copy-start(bf16[256,512]{1,0:T(8,128)(2,1)} %param.9) | copy-start | bytes 786436
  10.6 104.7 %all-to-all-start = ((bf16[2,16,128,512]{3,2,0,1:T(8,128)(2,1)}), bf16[2,16,128,512]{3,2,0,1:T(8,128)(2,1)}, u32[]{:S(2)}, u32[]{:S(2)}) async-start(bf16[2,16,128,512]{3,2,0,1:T(8,128)(2,1)} %select_bitcast_fusion.2), calls=%async_computation | async-start | bytes 8388608 | tf_op jit(solution)/shard_map/all_to_all | solution.py:90
  21.7 39.9 %collective-permute-start.3 = (bf16[2,2,128,512]{3,2,1,0:T(8,128)(2,1)S(1)}, bf16[2,2,128,512]{3,2,1,0:T(8,128)(2,1)S(1)}, u32[]{:S(2)}, u32[]{:S(2)}) collective-permute-start(bf16[2,2,128,512]{3,2,1,0:T(8,128)(2,1)S(1)} %pad_maximum_fusion.3), channel_id=1, source_target_pairs={{2,0},{3,1},{4,2},{5,3},{6,4},{7,5},{8,6},{9,7},{10,8},{11,9},{12,... | collective-permute-start | bytes 1572872 | tf_op jit(solution)/shard_map/ppermute | solution.py:20
  27.1 33.6 %collective-permute-start.2 = (bf16[2,2,128,512]{3,2,1,0:T(8,128)(2,1)S(1)}, bf16[2,2,128,512]{3,2,1,0:T(8,128)(2,1)S(1)}, u32[]{:S(2)}, u32[]{:S(2)}) collective-permute-start(bf16[2,2,128,512]{3,2,1,0:T(8,128)(2,1)S(1)} %pad_maximum_fusion.3), channel_id=1, source_target_pairs={{1,0},{2,1},{3,2},{4,3},{5,4},{6,5},{7,6},{8,7},{9,8},{10,9},{11,1... | collective-permute-start | bytes 1572872 | tf_op jit(solution)/shard_map/ppermute | solution.py:20
  29.9 29.2 %collective-permute-start.1 = (bf16[2,2,128,512]{3,2,1,0:T(8,128)(2,1)S(1)}, bf16[2,2,128,512]{3,2,1,0:T(8,128)(2,1)S(1)}, u32[]{:S(2)}, u32[]{:S(2)}) collective-permute-start(bf16[2,2,128,512]{3,2,1,0:T(8,128)(2,1)S(1)} %pad_maximum_fusion.3), channel_id=1, source_target_pairs={{0,1},{1,2},{2,3},{3,4},{4,5},{5,6},{6,7},{7,8},{8,9},{9,10},{10,1... | collective-permute-start | bytes 1572872 | tf_op jit(solution)/shard_map/ppermute | solution.py:20
  32.4 25.8 %collective-permute-start = (bf16[2,2,128,512]{3,2,1,0:T(8,128)(2,1)S(1)}, bf16[2,2,128,512]{3,2,1,0:T(8,128)(2,1)S(1)}, u32[]{:S(2)}, u32[]{:S(2)}) collective-permute-start(bf16[2,2,128,512]{3,2,1,0:T(8,128)(2,1)S(1)} %pad_maximum_fusion.3), channel_id=1, source_target_pairs={{0,2},{1,3},{2,4},{3,5},{4,6},{5,7},{6,8},{7,9},{8,10},{9,11},{10,... | collective-permute-start | bytes 1572872 | tf_op jit(solution)/shard_map/ppermute | solution.py:20
  136.9 1.1 copy-start.8
  145.8 2.5 copy-start.5
  149.1 2.7 copy-start.4
  149.5 14.7 %copy-start.2 = (f32[896,8,64]{0,2,1:T(8,128)}, f32[896,8,64]{0,2,1:T(8,128)S(1)}, u32[]{:S(2)}) copy-start(f32[896,8,64]{0,2,1:T(8,128)S(1)} %convolution_bitcast_fusion.6) | copy-start | bytes 5505028 | tf_op jit(solution)/shard_map/while
  155.3 1.3 slice-start.2
  157.9 2.6 slice-start.1
  164.4 1.8 slice-start
  166.5 4.8 %copy-start.3 = (f32[4,128,512]{2,1,0:T(8,128)S(1)}, f32[4,128,512]{2,1,0:T(8,128)}, u32[]{:S(2)}) copy-start(f32[4,128,512]{2,1,0:T(8,128)} %copy.68) | copy-start | bytes 3145732 | tf_op jit(solution)/shard_map/while
  167.7 6.7 %copy-start.7 = (f32[3,128,512]{2,1,0:T(8,128)S(1)}, f32[3,128,512]{2,1,0:T(8,128)}, u32[]{:S(2)}) copy-start(f32[3,128,512]{2,1,0:T(8,128)} %copy.71) | copy-start | bytes 2359300 | tf_op jit(solution)/shard_map/while
  171.3 6.1 %copy-start.6 = (f32[3,128,512]{2,1,0:T(8,128)S(1)}, f32[3,128,512]{2,1,0:T(8,128)}, u32[]{:S(2)}) copy-start(f32[3,128,512]{2,1,0:T(8,128)} %copy.70) | copy-start | bytes 2359300 | tf_op jit(solution)/shard_map/while
  188.8 1.1 copy-start.8
  197.7 2.5 copy-start.5
  201.0 2.7 copy-start.4
  201.4 14.7 %copy-start.2 = (f32[896,8,64]{0,2,1:T(8,128)}, f32[896,8,64]{0,2,1:T(8,128)S(1)}, u32[]{:S(2)}) copy-start(f32[896,8,64]{0,2,1:T(8,128)S(1)} %convolution_bitcast_fusion.6) | copy-start | bytes 5505028 | tf_op jit(solution)/shard_map/while
  207.2 1.3 slice-start.2
  209.8 2.6 slice-start.1
  216.3 1.8 slice-start
  218.4 4.7 %copy-start.3 = (f32[4,128,512]{2,1,0:T(8,128)S(1)}, f32[4,128,512]{2,1,0:T(8,128)}, u32[]{:S(2)}) copy-start(f32[4,128,512]{2,1,0:T(8,128)} %copy.68) | copy-start | bytes 3145732 | tf_op jit(solution)/shard_map/while
  219.6 6.5 %copy-start.7 = (f32[3,128,512]{2,1,0:T(8,128)S(1)}, f32[3,128,512]{2,1,0:T(8,128)}, u32[]{:S(2)}) copy-start(f32[3,128,512]{2,1,0:T(8,128)} %copy.71) | copy-start | bytes 2359300 | tf_op jit(solution)/shard_map/while
  223.1 6.0 %copy-start.6 = (f32[3,128,512]{2,1,0:T(8,128)S(1)}, f32[3,128,512]{2,1,0:T(8,128)}, u32[]{:S(2)}) copy-start(f32[3,128,512]{2,1,0:T(8,128)} %copy.70) | copy-start | bytes 2359300 | tf_op jit(solution)/shard_map/while
  238.4 5.8 %copy-start.9 = (f32[10,128,512]{2,1,0:T(8,128)S(1)}, f32[10,128,512]{2,1,0:T(8,128)}, u32[]{:S(2)}) copy-start(f32[10,128,512]{2,1,0:T(8,128)} %get-tuple-element.79) | copy-start | bytes 7864324
  238.4 99.4 %all-to-all-start.1 = ((bf16[2,16,128,512]{3,2,0,1:T(8,128)(2,1)}), bf16[2,16,128,512]{3,2,0,1:T(8,128)(2,1)}, u32[]{:S(2)}, u32[]{:S(2)}) async-start(bf16[2,16,128,512]{3,2,0,1:T(8,128)(2,1)} %pad_maximum_fusion.1), calls=%async_computation.1 | async-start | bytes 8388608 | tf_op jit(solution)/shard_map/all_to_all | solution.py:125
  246.5 29.7 %collective-permute-start.4 = (bf16[2,2,128,512]{3,2,1,0:T(8,128)(2,1)S(1)}, bf16[2,2,128,512]{3,2,1,0:T(8,128)(2,1)S(1)}, u32[]{:S(2)}, u32[]{:S(2)}) collective-permute-start(bf16[2,2,128,512]{3,2,1,0:T(8,128)(2,1)S(1)} %get-tuple-element.142), channel_id=1, source_target_pairs={{2,0},{3,1},{4,2},{5,3},{6,4},{7,5},{8,6},{9,7},{10,8},{11,9},{12,... | collective-permute-start | bytes 1572872 | tf_op jit(solution)/shard_map/ppermute | solution.py:20
  251.9 24.3 %collective-permute-start.5 = (bf16[2,2,128,512]{3,2,1,0:T(8,128)(2,1)S(1)}, bf16[2,2,128,512]{3,2,1,0:T(8,128)(2,1)S(1)}, u32[]{:S(2)}, u32[]{:S(2)}) collective-permute-start(bf16[2,2,128,512]{3,2,1,0:T(8,128)(2,1)S(1)} %get-tuple-element.143), channel_id=1, source_target_pairs={{1,0},{2,1},{3,2},{4,3},{5,4},{6,5},{7,6},{8,7},{9,8},{10,9},{11,1... | collective-permute-start | bytes 1572872 | tf_op jit(solution)/shard_map/ppermute | solution.py:20
  254.8 21.5 %collective-permute-start.7 = (bf16[2,2,128,512]{3,2,1,0:T(8,128)(2,1)S(1)}, bf16[2,2,128,512]{3,2,1,0:T(8,128)(2,1)S(1)}, u32[]{:S(2)}, u32[]{:S(2)}) collective-permute-start(bf16[2,2,128,512]{3,2,1,0:T(8,128)(2,1)S(1)} %get-tuple-element.144), channel_id=1, source_target_pairs={{0,2},{1,3},{2,4},{3,5},{4,6},{5,7},{6,8},{7,9},{8,10},{9,11},{10,... | collective-permute-start | bytes 1572872 | tf_op jit(solution)/shard_map/ppermute | solution.py:20
  257.8 27.5 %collective-permute-start.6 = (bf16[2,2,128,512]{3,2,1,0:T(8,128)(2,1)S(1)}, bf16[2,2,128,512]{3,2,1,0:T(8,128)(2,1)S(1)}, u32[]{:S(2)}, u32[]{:S(2)}) collective-permute-start(bf16[2,2,128,512]{3,2,1,0:T(8,128)(2,1)S(1)} %get-tuple-element.145), channel_id=1, source_target_pairs={{0,1},{1,2},{2,3},{3,4},{4,5},{5,6},{6,7},{7,8},{8,9},{9,10},{10,1... | collective-permute-start | bytes 1572872 | tf_op jit(solution)/shard_map/ppermute | solution.py:20
  285.6 58.8 %copy-start.14 = (s32[16]{0:T(128)S(1)}, s32[16]{0:T(128)}, u32[]{:S(2)}) copy-start(s32[16]{0:T(128)} %copy-done.13) | copy-start | bytes 196
  344.4 11.8 %copy-start.1 = (s32[64,3]{0,1:T(4,128)S(1)}, s32[64,3]{0,1:T(4,128)}, u32[]{:S(2)}) copy-start(s32[64,3]{0,1:T(4,128)} %param.12) | copy-start | bytes 2308
where the time goes:
time: 358 us; the launch traced here: 356 us
  waiting for transfers between devices  153 us (43%)
  local copies, waits for them, and re-layouts  75.9 us (21%)
  other arithmetic  66.8 us (19%)
  starting transfers between devices  43.3 us (12%)
  matrix products  15.4 us (4%)
    all_to_all x1, waiting for transfers between devices, on_device(): lax.all_to_all(far_out, 'group', split_axis=1, concat_axis=1, tiled=True)  52.8 us
    all_to_all x1, waiting for transfers between devices, on_device(): lax.all_to_all(far_parts, 'group', split_axis=1, concat_axis=1, tiled=True)  52.2 us
    ppermute x8, waiting for transfers between devices, shifted(): return lax.ppermute(array, axis, pairs)  48.3 us
    ppermute x8, starting transfers between devices, shifted(): return lax.ppermute(array, axis, pairs)  26.4 us
    all_to_all x1, starting transfers between devices, on_device(): lax.all_to_all(far_out, 'group', split_axis=1, concat_axis=1, tiled=True)  11.1 us
    scatter-add x1, other arithmetic, on_device(): owned_total = owned_total.at[:, far_given].add(far_back.astype(jnp.float32))  10.9 us
    slice x8, local copies, waits for them, and re-layouts, visit_block(): near_keys = near_keys.at[near_pick].add(grad_key[:1 + LOC])  8.48 us
    slice x8, local copies, waits for them, and re-layouts, visit_block(): far_keys = far_keys.at[far_pick].add(grad_key[1 + LOC:])  7.5 us
  transfers between devices with their start and end apart: 10, of which 5 were waited for; matrix products, arithmetic and copies ran while one was open for 2% of the time, Pallas kernels for 0%

commit v1 on v0

v1 whole, which is shorter than its diff:
```python
import functools
import math

import jax
import jax.numpy as jnp
from jax import lax
from jax.experimental import pallas as pl
from jax.experimental.pallas import tpu as pltpu
from jax.sharding import PartitionSpec as P

D = 512
BS = 128
NB = 2
LOC = 3
EXP = 3
W = 2
KB = 1 + LOC + EXP
ENTRIES = NB * KB
ROWS = KB * BS
FAR = NB * EXP
NEAR = NB + 2 * W
PAIRS = D // 128
BF = jnp.bfloat16
F32 = jnp.float32
OFFSETS = (-2, -1, 1, 2)

ANY = pl.BlockSpec(memory_space=pl.ANY)
VMEM = pl.BlockSpec(memory_space=pltpu.VMEM)
SMEM = pl.BlockSpec(memory_space=pltpu.SMEM)

SIBLING, FLOW_A, FLOW_B, PICKED = 0, 0, 4, 8


def ring_step(array):
    size = lax.axis_size("group")
    return lax.ppermute(array, "group", [(g, (g + (2 if g % 2 == 0 else -2)) % size) for g in range(size)])


def swap_cores(array):
    size = lax.axis_size("group")
    return lax.ppermute(array, "group", [(g, g ^ 1) for g in range(size)])


def shifted(array, by):
    size = lax.axis_size("dom")
    return lax.ppermute(array, "dom", [(i, i + by) for i in range(size) if 0 <= i + by < size])


def place_of(cluster, chip, core, chips):
    other_chip, other_core = cluster // 2, cluster % 2
    distance = jnp.where(core == 0, chip - other_chip, other_chip - chip) % chips
    same = other_core == core
    half = chips // 2
    here = jnp.where(same, FLOW_A + distance, FLOW_B + distance)
    held = jnp.where(same, distance <= half, distance < half)
    return jnp.where(distance == 0, SIBLING, jnp.where(held, here, PICKED))


def first_of(values):
    order = jnp.arange(values.shape[0], dtype=jnp.int32)
    same = values[:, None] == values[None, :]
    return jnp.min(jnp.where(same, order[None, :], values.shape[0]), axis=1)


def slot_in(values, wanted):
    order = jnp.arange(values.shape[0], dtype=jnp.int32)
    hit = values[None, :] == wanted[:, None]
    found = jnp.min(jnp.where(hit, order[None, :], values.shape[0]), axis=1)
    return jnp.where(found == values.shape[0], -1, found).astype(jnp.int32)


def pick_kernel(table, *refs):
    places, out, sem = refs[:8], refs[8], refs[9]
    copies = []
    for t in range(FAR):
        for code, place in enumerate(places):

            @pl.when(table[0, t] == code)
            def _():
                rows = pl.ds(pl.multiple_of(table[1, t] * BS, BS), BS)
                pltpu.make_async_copy(place.at[:, rows, :], out.at[t], sem.at[t]).start()

    for t in range(FAR):

        @pl.when(table[0, t] < 8)
        def _():
            pltpu.make_async_copy(places[0].at[:, pl.ds(0, BS), :], out.at[t], sem.at[t]).wait()


def pick(table, places):
    return pl.pallas_call(
        pick_kernel,
        out_shape=jax.ShapeDtypeStruct((FAR, 2, BS, D), BF),
        in_specs=[SMEM] + [ANY] * 8,
        out_specs=ANY,
        scratch_shapes=[pltpu.SemaphoreType.DMA((FAR,))],
        cost_estimate=pl.CostEstimate(flops=0, bytes_accessed=6 * 2**20, transcendentals=0),
    )(table, *places)


def attend_pair(step, table, q_ref, g_ref, listed, att_ref, gq_ref, totals):
    low = lax.broadcasted_iota(jnp.int32, (BS, 128), 1) < 64
    last = (((1,), (1,)), ((), ()))
    first = (((0,), (0,)), ((), ()))
    s = step // PAIRS
    p = step % PAIRS
    cols = pl.ds(pl.multiple_of(p * 128, 128), 128)
    query = q_ref[s, :, cols]
    grad = g_ref[s, :, cols]
    zero = jnp.zeros_like(query)
    query2 = jnp.concatenate([jnp.where(low, query, zero), jnp.where(low, zero, query)], axis=0)
    grad2 = jnp.concatenate([jnp.where(low, grad, zero), jnp.where(low, zero, grad)], axis=0)
    keys = listed[s, 0, :, cols]
    values = listed[s, 1, :, cols]

    def own_heads(both):
        return jnp.concatenate([both[:64, :128], both[64:, 128:]], axis=0)

    scores = lax.dot_general(keys, query2, last, preferred_element_type=F32)
    highest = jnp.max(scores, axis=0, keepdims=True)
    raised = jnp.exp2((scores - highest) * (0.125 * math.log2(math.e)))
    weights = raised * (1.0 / jnp.sum(raised, axis=0, keepdims=True))
    weights_low = weights.astype(BF)
    mixture = own_heads(lax.dot_general(values, weights_low, first, preferred_element_type=F32))
    att_ref[s, :, cols] = mixture.T.astype(BF)
    product = mixture * grad.astype(F32).T
    carried = jnp.concatenate(
        [jnp.sum(product[:64], axis=0, keepdims=True), jnp.sum(product[64:], axis=0, keepdims=True)], axis=1
    )
    grad_weights = lax.dot_general(values, grad2, last, preferred_element_type=F32)
    grad_scores = ((weights * (grad_weights - carried)) * 0.125).astype(BF)
    grad_query = own_heads(lax.dot_general(keys, grad_scores, first, preferred_element_type=F32))
    gq_ref[s, :, cols] = grad_query.T.astype(BF)
    grad_key = jnp.dot(grad_scores, query2, preferred_element_type=F32)
    grad_value = jnp.dot(weights_low, grad2, preferred_element_type=F32)
    for j in range(KB):
        slot = table[2, s * KB + j]
        leads = table[3, s * KB + j]
        rows = slice(j * BS, (j + 1) * BS)

        @pl.when(leads == 1)
        def _():
            totals[slot, 0, :, cols] = grad_key[rows]
            totals[slot, 1, :, cols] = grad_value[rows]

        @pl.when(leads == 0)
        def _():
            totals[slot, 0, :, cols] += grad_key[rows]
            totals[slot, 1, :, cols] += grad_value[rows]


def attend_kernel(table, q_ref, g_ref, *refs):
    own, near, places, picked = refs[0], refs[1:5], refs[5:13], refs[13]
    att_ref, gq_ref, near_out, far_out, listed, totals, sem = refs[14:]

    def bring(source, s, j):
        pltpu.make_async_copy(source, listed.at[s, :, pl.ds(j * BS, BS), :], sem.at[s]).start()

    for s in range(NB):
        bring(own.at[:, pl.ds(s * BS, BS), :], s, 0)
        for j in range(1, KB):
            code, place = table[0, s * KB + j], table[1, s * KB + j]
            rows = pl.ds(pl.multiple_of(place * BS, BS), BS)
            if j <= LOC:

                @pl.when(code == 0)
                def _():
                    bring(own.at[:, rows, :], s, j)

                for t in range(2 * W):

                    @pl.when(code == 1 + t)
                    def _():
                        bring(near[t], s, j)

            else:
                for t in range(8):

                    @pl.when(code == t)
                    def _():
                        bring(places[t].at[:, rows, :], s, j)

                @pl.when(code == 8)
                def _():
                    bring(picked.at[s * EXP + j - 1 - LOC], s, j)

    for s in range(NB):
        pltpu.make_async_copy(listed.at[s], listed.at[s], sem.at[s]).wait()

    def body(step, carry):
        attend_pair(step, table, q_ref, g_ref, listed, att_ref, gq_ref, totals)
        return carry

    lax.fori_loop(0, NB * PAIRS, body, 0)
    near_out[...] = totals[:NEAR].astype(BF)
    far_out[...] = totals[NEAR:].astype(BF)


def attend(table, queries, cotangent, own, near, places, picked):
    return pl.pallas_call(
        attend_kernel,
        out_shape=(
            jax.ShapeDtypeStruct((NB, BS, D), BF),
            jax.ShapeDtypeStruct((NB, BS, D), BF),
            jax.ShapeDtypeStruct((NEAR, 2, BS, D), BF),
            jax.ShapeDtypeStruct((FAR, 2, BS, D), BF),
        ),
        in_specs=[SMEM, VMEM, VMEM] + [ANY] * 14,
        out_specs=(VMEM, VMEM, VMEM, VMEM),
        scratch_shapes=[
            pltpu.VMEM((NB, 2, ROWS, D), BF),
            pltpu.VMEM((NEAR + FAR, 2, BS, D), F32),
            pltpu.SemaphoreType.DMA((NB,)),
        ],
        compiler_params=pltpu.CompilerParams(vmem_limit_bytes=40 * 2**20),
        cost_estimate=pl.CostEstimate(
            flops=12 * NB * BS * ROWS * D, bytes_accessed=12 * 2**20, transcendentals=NB * 8 * BS * ROWS
        ),
    )(table, queries, cotangent, own, *near, *places, picked)


def spread_kernel(count, table, mine, theirs, *outs):
    for n in range(count):
        out = outs[n]
        for s in range(NB):
            a, b = table[0, n * NB + s], table[1, n * NB + s]

            @pl.when((a < 0) & (b < 0))
            def _():
                out[s] = jnp.zeros((2, BS, D), BF)

            @pl.when((a >= 0) & (b < 0))
            def _():
                out[s] = mine[a]

            @pl.when((a < 0) & (b >= 0))
            def _():
                out[s] = theirs[b]

            @pl.when((a >= 0) & (b >= 0))
            def _():
                out[s] = (mine[a].astype(F32) + theirs[b].astype(F32)).astype(BF)


def spread(table, mine, theirs):
    count = table.shape[1] // NB
    return pl.pallas_call(
        functools.partial(spread_kernel, count),
        out_shape=tuple(jax.ShapeDtypeStruct((NB, 2, BS, D), BF) for _ in range(count)),
        in_specs=[SMEM, VMEM, VMEM],
        out_specs=(VMEM,) * count,
        compiler_params=pltpu.CompilerParams(vmem_limit_bytes=24 * 2**20),
        cost_estimate=pl.CostEstimate(flops=0, bytes_accessed=(3 + count) * 2**19, transcendentals=0),
    )(table, mine, theirs)


def close_kernel(table, near, theirs, from_a, from_b, *refs):
    returned, (gk_ref, gv_ref) = refs[:4], refs[4:]
    for s in range(NB):
        for half, out in enumerate((gk_ref, gv_ref)):
            total = near[s, half].astype(F32)
            for t in range(2 * W):
                total = total + jnp.where(table[t] == s, returned[t][half].astype(F32), 0.0)
            total = total + from_a[s, half].astype(F32) + from_b[s, half].astype(F32)
            b = table[4 + s]
            direct = theirs[jnp.maximum(b, 0), half].astype(F32)
            total = total + jnp.where(b >= 0, direct, 0.0)
            out[pl.ds(s * BS, BS), :] = total.astype(BF)


def close(table, near, theirs, from_a, from_b, returned):
    return pl.pallas_call(
        close_kernel,
        out_shape=(jax.ShapeDtypeStruct((NB * BS, D), BF),) * 2,
        in_specs=[SMEM] + [VMEM] * 8,
        out_specs=(VMEM, VMEM),
        compiler_params=pltpu.CompilerParams(vmem_limit_bytes=24 * 2**20),
        cost_estimate=pl.CostEstimate(flops=2**22, bytes_accessed=6 * 2**20, transcendentals=0),
    )(table, near, theirs, from_a, from_b, *returned)


def on_device(queries, keys, values, cotangent, local_list, far_list):
    groups = lax.axis_size("group")
    doms = lax.axis_size("dom")
    chips = groups // 2
    dom = lax.axis_index("dom").astype(jnp.int32)
    group = lax.axis_index("group").astype(jnp.int32)
    chip, core = group // 2, group % 2
    i32 = jnp.int32

    own = jnp.stack([keys, values])
    flow_a = [ring_step(own)]
    sibling = swap_cores(own)
    flow_b = [ring_step(sibling)]
    for _ in range(2):
        flow_a.append(ring_step(flow_a[-1]))
        flow_b.append(ring_step(flow_b[-1]))
    flow_a.append(ring_step(flow_a[-1]))

    padded = jnp.pad(local_list, ((W * NB, W * NB), (0, 0)), constant_values=-1)
    around = lax.dynamic_slice_in_dim(padded, dom * NB, (2 * W + 1) * NB, 0).reshape(2 * W + 1, NB * LOC)
    given = jnp.max(jnp.where(around // NB == dom, around % NB, 0), axis=1).astype(i32)
    blocks = own.reshape(2, NB, BS, D)
    near = []
    for offset in OFFSETS:
        piece = lax.dynamic_index_in_dim(blocks, given[W + offset], 1, keepdims=False)
        near.append(shifted(piece, offset))
    local = around[W].reshape(NB, LOC)
    holder = local // NB - dom
    near_code = jnp.where(holder == 0, 0, jnp.where(holder > 0, 3 - holder, 2 - holder))
    near_key = jnp.where(holder == 0, local % NB, NB - 1 + near_code)

    far_rows = far_list[0].reshape(groups, FAR)
    mine = lax.dynamic_index_in_dim(far_rows, group, 0, keepdims=False)
    theirs = lax.dynamic_index_in_dim(far_rows, group ^ 1, 0, keepdims=False)
    far_code = place_of(mine // NB, chip, core, chips)
    needed = place_of(theirs // NB, chip, 1 - core, chips) == PICKED
    sent = jnp.where(needed, place_of(theirs // NB, chip, core, chips), PICKED)
    picked = swap_cores(pick(jnp.stack([sent, theirs % NB]).astype(i32), [sibling] + flow_a + flow_b))

    self_code = jnp.zeros((NB, 1), i32)
    self_key = jnp.arange(NB, dtype=i32)[:, None]
    codes = jnp.concatenate([self_code, near_code, far_code.reshape(NB, EXP)], axis=1).reshape(-1)
    slots = jnp.concatenate([self_key, local % NB, (mine % NB).reshape(NB, EXP)], axis=1).reshape(-1)
    far_key = (NEAR + first_of(mine)).reshape(NB, EXP)
    targets = jnp.concatenate([self_key, near_key, far_key], axis=1).reshape(-1)
    leads = first_of(targets) == jnp.arange(ENTRIES, dtype=i32)
    table = jnp.stack([codes, slots, targets, leads.astype(i32)]).astype(i32)
    attended, grad_queries, near_terms, far_terms = attend(
        table,
        queries.reshape(NB, BS, D),
        cotangent.reshape(NB, BS, D),
        own,
        near,
        [sibling] + flow_a + flow_b,
        picked,
    )

    sibling_terms = swap_cores(far_terms)
    steps = [(4, 0), (3, 1), (3, 0), (2, 1), (2, 0), (1, 1), (1, 0)]
    direction = 1 - 2 * core
    wanted = []
    for distance, side in steps:
        cluster = ((chip + direction * distance) % chips) * 2 + jnp.where(side == 0, core, 1 - core)
        wanted += [cluster * NB, cluster * NB + 1]
    wanted += [group * NB, group * NB + 1]
    wanted = jnp.stack(wanted).astype(i32)
    hits = jnp.stack([slot_in(mine, wanted), slot_in(theirs, wanted)])
    start_a, start_b = spread(hits[:, : 2 * NB], far_terms, sibling_terms)
    a3, b2, a2, b1, a1 = spread(hits[:, 2 * NB : 7 * NB], far_terms, sibling_terms)

    def joined(x, y):
        return (x.astype(F32) + y.astype(F32)).astype(BF)

    back_a = ring_step(start_a)
    back_b = ring_step(start_b)
    back_a = ring_step(joined(back_a, a3))
    back_b = ring_step(joined(back_b, b2))
    back_a = ring_step(joined(back_a, a2))
    back_b = ring_step(joined(back_b, b1))
    back_a = ring_step(joined(back_a, a1))
    back_b = swap_cores(back_b)

    returned = [shifted(near_terms[NB + t], -offset) for t, offset in enumerate(OFFSETS)]
    back_slots = jnp.stack([given[W + offset] for offset in OFFSETS])
    last = jnp.concatenate([back_slots, hits[1, 7 * NB :]]).astype(i32)
    grad_keys, grad_values = close(last, near_terms[:NB], sibling_terms, back_a, back_b, returned)
    return (attended.reshape(NB * BS, D), grad_queries.reshape(NB * BS, D), grad_keys, grad_values)


def solution(mesh):
    rows = P(("group", "dom"), None)
    return jax.shard_map(
        on_device,
        mesh=mesh,
        in_specs=(rows, rows, rows, rows, P("group", None), P("dom", None, None)),
        out_specs=(rows, rows, rows, rows),
        check_vma=False,
    )
```

time: 358 us -> 227 us (0.63)
  the two profiles are of different devices: /device:TPU:57 before, /device:TPU:44 now
where the time goes in v1:
time: 227 us; the launch traced here: 226 us
  starting transfers between devices  105 us (46%)
  waiting for transfers between devices  63 us (28%)
  Pallas kernels  30 us (13%)
  local copies, waits for them, and re-layouts  12.8 us (6%)
  between operations  9.03 us (4%)
  other arithmetic  5.71 us (3%)
    ppermute x14, starting transfers between devices, ring_step(): lax.ppermute(array, 'group', [(g, (g + (2 if g % 2 == 0 else -2)) % size)...  55.8 us
    ppermute x14, waiting for transfers between devices, ring_step(): lax.ppermute(array, 'group', [(g, (g + (2 if g % 2 == 0 else -2)) % size)...  44.9 us
    ppermute x8, starting transfers between devices, shifted(): lax.ppermute(array, 'dom', [(i, i + by) for i in range(size) if 0 <= i +...  26.3 us
    ppermute x4, starting transfers between devices, swap_cores(): return lax.ppermute(array, 'group', [(g, g ^ 1) for g in range(size)])  23 us
    pallas_call x1, Pallas kernels, attend(): pl.pallas_call(attend_kernel, out_shape=(jax.ShapeDtypeStruct((NB, BS, D)...  16.5 us
    ppermute x8, waiting for transfers between devices, shifted(): lax.ppermute(array, 'dom', [(i, i + by) for i in range(size) if 0 <= i +...  13.3 us
    unnamed x40, local copies, waits for them, and re-layouts  11.1 us
    pallas_call x1, Pallas kernels, pick(): pl.pallas_call(pick_kernel, out_shape=jax.ShapeDtypeStruct((FAR, 2, BS, D...  9.9 us
  transfers between devices with their start and end apart: 26, of which 14 were waited for; matrix products, arithmetic and copies ran while one was open for 3% of the time, Pallas kernels for 5%

profile of v1, /device:TPU:44, one launch (start us, length us, event | category | flops | bytes accessed | tf_op | source)
XLA Modules:
  0.0 225.6 jit_solution(1811039571310283710)
XLA Ops:
  0.6 1.1 pad_maximum_fusion.refs_0_
  1.7 1.9 collective-permute-start.4
  3.7 4.3 %collective-permute-start.5 = (bf16[2,256,512]{2,1,0:T(8,128)(2,1)S(1)}, bf16[2,256,512]{2,1,0:T(8,128)(2,1)S(1)}, u32[]{:S(2)}, u32[]{:S(2)}) collective-permute-start(bf16[2,256,512]{2,1,0:T(8,128)(2,1)S(1)} %pad_maximum_fusion.refs_0_), channel_id=1, source_target_pairs={{0,64},{32,480},{64,128},{96,32},{128,192},{160,96},{192,256},{224... | collective-permute-start | bytes 1572872 | tf_op jit(solution)/shard_map/ppermute | solution.py:36
  8.0 0.8 copy-done.12
  8.8 4.3 %collective-permute-start.9 = (bf16[2,256,512]{2,1,0:T(8,128)(2,1)S(1)}, bf16[2,256,512]{2,1,0:T(8,128)(2,1)S(1)}, u32[]{:S(2)}, u32[]{:S(2)}) collective-permute-start(bf16[2,256,512]{2,1,0:T(8,128)(2,1)S(1)} %collective-permute-done.4.refs_0_.refs_5_), channel_id=1, source_target_pairs={{0,64},{32,480},{64,128},{96,32},{128,192},{160,96},{192,256},{224... | collective-permute-start | bytes 1572872 | tf_op jit(solution)/shard_map/ppermute | solution.py:36
  13.0 8.7 %collective-permute-done.5.refs_1_.refs_6_ = bf16[2,256,512]{2,1,0:T(8,128)(2,1)S(1)} collective-permute-done((bf16[2,256,512]{2,1,0:T(8,128)(2,1)S(1)}, bf16[2,256,512]{2,1,0:T(8,128)(2,1)S(1)}, u32[]{:S(2)}, u32[]{:S(2)}) %collective-permute-start.5) | collective-permute-done | bytes 524320 | tf_op jit(solution)/shard_map/ppermute | solution.py:36
  21.8 1.9 collective-permute-start.6
  23.7 3.7 %collective-permute-done.9.refs_5_.refs_10_ = bf16[2,256,512]{2,1,0:T(8,128)(2,1)S(1)} collective-permute-done((bf16[2,256,512]{2,1,0:T(8,128)(2,1)S(1)}, bf16[2,256,512]{2,1,0:T(8,128)(2,1)S(1)}, u32[]{:S(2)}, u32[]{:S(2)}) %collective-permute-start.9) | collective-permute-done | bytes 524320 | tf_op jit(solution)/shard_map/ppermute | solution.py:36
  27.4 1.9 collective-permute-start.10
  29.3 4.7 %collective-permute-done.6.refs_2_.refs_7_ = bf16[2,256,512]{2,1,0:T(8,128)(2,1)S(1)} collective-permute-done((bf16[2,256,512]{2,1,0:T(8,128)(2,1)S(1)}, bf16[2,256,512]{2,1,0:T(8,128)(2,1)S(1)}, u32[]{:S(2)}, u32[]{:S(2)}) %collective-permute-start.6) | collective-permute-done | bytes 524320 | tf_op jit(solution)/shard_map/ppermute | solution.py:36
  34.0 1.9 collective-permute-start.7
  36.0 3.7 %collective-permute-done.10.refs_6_.refs_11_ = bf16[2,256,512]{2,1,0:T(8,128)(2,1)S(1)} collective-permute-done((bf16[2,256,512]{2,1,0:T(8,128)(2,1)S(1)}, bf16[2,256,512]{2,1,0:T(8,128)(2,1)S(1)}, u32[]{:S(2)}, u32[]{:S(2)}) %collective-permute-start.10) | collective-permute-done | bytes 524320 | tf_op jit(solution)/shard_map/ppermute | solution.py:36
  39.7 1.9 collective-permute-start.11
  41.6 4.7 %collective-permute-done.7.refs_3_.refs_8_ = bf16[2,256,512]{2,1,0:T(8,128)(2,1)S(1)} collective-permute-done((bf16[2,256,512]{2,1,0:T(8,128)(2,1)S(1)}, bf16[2,256,512]{2,1,0:T(8,128)(2,1)S(1)}, u32[]{:S(2)}, u32[]{:S(2)}) %collective-permute-start.7) | collective-permute-done | bytes 524320 | tf_op jit(solution)/shard_map/ppermute | solution.py:36
  46.3 1.9 collective-permute-start.8
  48.2 0.8 copy.18
  49.3 0.6 fusion.23
  57.7 2.3 %fusion.1 = (bf16[2,128,512]{2,1,0:T(8,128)(2,1)}, bf16[2,128,512]{2,1,0:T(8,128)(2,1)}, bf16[2,128,512]{2,1,0:T(8,128)(2,1)}, bf16[2,128,512]{2,1,0:T(8,128)(2,1)}) fusion(s32[]{:T(128)S(6)} %select_n.306, bf16[1,2,128,512]{3,2,0,1:T(8,128)(2,1)} %bitcast.68, bf16[1,2,128,512]{3,2,0,1:T(8,128)(2,1)} %bitcast.66, s32[]{:T(128)S(6)} %select_n.303, ...), kind=kLoop, calls=%fused_computation.15 | loop fusion | flops 524288 | bytes 1572880 | tf_op jit(solution)/shard_map/jit(dynamic_index_in_dim)/squeeze | solution.py:306
  60.0 2.4 %collective-permute-start = (bf16[2,128,512]{2,1,0:T(8,128)(2,1)}, bf16[2,128,512]{2,1,0:T(8,128)(2,1)}, u32[]{:S(2)}, u32[]{:S(2)}) collective-permute-start(bf16[2,128,512]{2,1,0:T(8,128)(2,1)} %get-tuple-element.42), channel_id=1, source_target_pairs={{2,0},{3,1},{4,2},{5,3},{6,4},{7,5},{8,6},{9,7},{10,8},{11,9},{12,... | collective-permute-start | bytes 786440 | tf_op jit(solution)/shard_map/ppermute | solution.py:46
  62.4 4.8 %collective-permute-start.1 = (bf16[2,128,512]{2,1,0:T(8,128)(2,1)}, bf16[2,128,512]{2,1,0:T(8,128)(2,1)}, u32[]{:S(2)}, u32[]{:S(2)}) collective-permute-start(bf16[2,128,512]{2,1,0:T(8,128)(2,1)} %get-tuple-element.43), channel_id=1, source_target_pairs={{1,0},{2,1},{3,2},{4,3},{5,4},{6,5},{7,6},{8,7},{9,8},{10,9},{11,1... | collective-permute-start | bytes 786440 | tf_op jit(solution)/shard_map/ppermute | solution.py:46
  67.3 1.9 collective-permute-start.2
  69.5 0.6 pad_add_fusion.4.table
  70.1 5.0 %collective-permute-start.3 = (bf16[2,128,512]{2,1,0:T(8,128)(2,1)}, bf16[2,128,512]{2,1,0:T(8,128)(2,1)}, u32[]{:S(2)}, u32[]{:S(2)}) collective-permute-start(bf16[2,128,512]{2,1,0:T(8,128)(2,1)} %get-tuple-element.41), channel_id=1, source_target_pairs={{0,2},{1,3},{2,4},{3,5},{4,6},{5,7},{6,8},{7,9},{8,10},{9,11},{10,... | collective-permute-start | bytes 786440 | tf_op jit(solution)/shard_map/ppermute | solution.py:46
  75.2 9.9 %shard_map.93 = bf16[6,2,128,512]{3,2,1,0:T(8,128)(2,1)} custom-call(s32[2,6]{1,0:T(2,128)} %pad_add_fusion.4.table, bf16[2,256,512]{2,1,0:T(8,128)(2,1)} %copy-done, bf16[2,256,512]{2,1,0:T(8,128)(2,1)} %copy-done.2, bf16[2,256,512]{2,1,0:T(8,128)(2,1)} %copy-done.6, bf16[2,256,512]{2,1,0:T(8,128)(2,1)} %copy-done.10, ...), custom_call_target="tpu_custom_call" | custom-call | bytes 6291456 | tf_op jit(solution)/shard_map/pallas_call | solution.py:91
  85.1 16.9 %collective-permute-start.12 = (bf16[6,2,128,512]{3,2,1,0:T(8,128)(2,1)}, bf16[6,2,128,512]{3,2,1,0:T(8,128)(2,1)S(1)}, u32[]{:S(2)}, u32[]{:S(2)}) collective-permute-start(bf16[6,2,128,512]{3,2,1,0:T(8,128)(2,1)} %shard_map.93), channel_id=1, source_target_pairs={{0,32},{32,0},{64,96},{96,64},{128,160},{160,128},{192,224},{224,1... | collective-permute-start | bytes 4718600 | tf_op jit(solution)/shard_map/ppermute | solution.py:41
  102.0 0.2 select_reduce_fusion.3
  102.9 0.2 select_reduce_fusion
  103.1 2.1 collective-permute-done.12.refs_13_
  105.3 1.0 copy-done.1
  106.3 1.0 copy-done.3
  107.3 1.0 copy-done.5
  108.4 1.0 copy-done.7
  109.4 1.0 copy-done.9
  110.5 1.0 copy-done.11
  111.5 1.0 copy-done.13
  112.6 0.9 copy-done.17
  113.5 16.5 %shard_map.94 = (bf16[2,128,512]{2,1,0:T(8,128)(2,1)}, bf16[2,128,512]{2,1,0:T(8,128)(2,1)}, bf16[6,2,128,512]{3,2,1,0:T(8,128)(2,1)S(1)}, bf16[6,2,128,512]{3,2,1,0:T(8,128)(2,1)S(1)}) custom-call(s32[4,14]{1,0:T(4,128)S(1)} %pad_add_fusion.table, bf16[2,128,512]{2,1,0:T(8,128)(2,1)S(1)} %bitcast.62, bf16[2,128,512]{2,1,0:T(8,128)(2,1)S(1)} %bitcast.63, ...), custom_call_target="tpu_custom_call" | custom-call | flops 1409286144 | bytes 12582912 | tf_op jit(solution)/shard_map/pallas_call | solution.py:200
  130.0 1.2 copy-done.14
  131.2 2.3 %collective-permute-start.13 = (bf16[6,2,128,512]{3,2,1,0:T(8,128)(2,1)S(1)}, bf16[6,2,128,512]{3,2,1,0:T(8,128)(2,1)S(1)}, u32[]{:S(2)}, u32[]{:S(2)}) collective-permute-start(bf16[6,2,128,512]{3,2,1,0:T(8,128)(2,1)S(1)} %get-tuple-element.20.mine), channel_id=1, source_target_pairs={{0,32},{32,0},{64,96},{96,64},{128,160},{160,128},{192,224},{224,1... | collective-permute-start | bytes 4718600 | tf_op jit(solution)/shard_map/ppermute | solution.py:41
  133.8 2.7 %collective-permute-done.13.theirs = bf16[6,2,128,512]{3,2,1,0:T(8,128)(2,1)S(1)} collective-permute-done((bf16[6,2,128,512]{3,2,1,0:T(8,128)(2,1)S(1)}, bf16[6,2,128,512]{3,2,1,0:T(8,128)(2,1)S(1)}, u32[]{:S(2)}, u32[]{:S(2)}) %collective-permute-start.13) | collective-permute-done | bytes 1572896 | tf_op jit(solution)/shard_map/ppermute | solution.py:41
  136.5 0.7 shard_map.95
  137.2 2.0 collective-permute-start.14
  139.2 1.9 collective-permute-start.18
  141.2 0.9 shard_map.96
  142.1 7.3 %collective-permute-done.14 = bf16[2,2,128,512]{3,2,1,0:T(8,128)(2,1)S(1)} collective-permute-done((bf16[2,2,128,512]{3,2,1,0:T(8,128)(2,1)S(1)}, bf16[2,2,128,512]{3,2,1,0:T(8,128)(2,1)S(1)}, u32[]{:S(2)}, u32[]{:S(2)}) %collective-permute-start.14) | collective-permute-done | bytes 524320 | tf_op jit(solution)/shard_map/ppermute | solution.py:36
  149.6 8.5 %collective-permute-start.15 = (bf16[2,2,128,512]{3,2,1,0:T(8,128)(2,1)S(1)}, bf16[2,2,128,512]{3,2,1,0:T(8,128)(2,1)S(1)}, u32[]{:S(2)}, u32[]{:S(2)}) collective-permute-start(bf16[2,2,128,512]{3,2,1,0:T(8,128)(2,1)S(1)} %add_convert_fusion.4), channel_id=1, source_target_pairs={{0,64},{32,480},{64,128},{96,32},{128,192},{160,96},{192,256},{224... | collective-permute-start | bytes 1572872 | tf_op jit(solution)/shard_map/ppermute | solution.py:36
  158.2 0.1 add_convert_fusion.1
  158.3 5.6 %collective-permute-start.19 = (bf16[2,2,128,512]{3,2,1,0:T(8,128)(2,1)S(1)}, bf16[2,2,128,512]{3,2,1,0:T(8,128)(2,1)S(1)}, u32[]{:S(2)}, u32[]{:S(2)}) collective-permute-start(bf16[2,2,128,512]{3,2,1,0:T(8,128)(2,1)S(1)} %add_convert_fusion.1), channel_id=1, source_target_pairs={{0,64},{32,480},{64,128},{96,32},{128,192},{160,96},{192,256},{224... | collective-permute-start | bytes 1572872 | tf_op jit(solution)/shard_map/ppermute | solution.py:36
  164.0 2.7 %collective-permute-done.15 = bf16[2,2,128,512]{3,2,1,0:T(8,128)(2,1)S(1)} collective-permute-done((bf16[2,2,128,512]{3,2,1,0:T(8,128)(2,1)S(1)}, bf16[2,2,128,512]{3,2,1,0:T(8,128)(2,1)S(1)}, u32[]{:S(2)}, u32[]{:S(2)}) %collective-permute-start.15) | collective-permute-done | bytes 524320 | tf_op jit(solution)/shard_map/ppermute | solution.py:36
  166.8 11.2 %collective-permute-start.16 = (bf16[2,2,128,512]{3,2,1,0:T(8,128)(2,1)S(1)}, bf16[2,2,128,512]{3,2,1,0:T(8,128)(2,1)S(1)}, u32[]{:S(2)}, u32[]{:S(2)}) collective-permute-start(bf16[2,2,128,512]{3,2,1,0:T(8,128)(2,1)S(1)} %add_convert_fusion.3), channel_id=1, source_target_pairs={{0,64},{32,480},{64,128},{96,32},{128,192},{160,96},{192,256},{224... | collective-permute-start | bytes 1572872 | tf_op jit(solution)/shard_map/ppermute | solution.py:36
  178.0 0.1 add_convert_fusion
  178.1 6.5 %collective-permute-start.20 = (bf16[2,2,128,512]{3,2,1,0:T(8,128)(2,1)S(1)}, bf16[2,2,128,512]{3,2,1,0:T(8,128)(2,1)S(1)}, u32[]{:S(2)}, u32[]{:S(2)}) collective-permute-start(bf16[2,2,128,512]{3,2,1,0:T(8,128)(2,1)S(1)} %add_convert_fusion), channel_id=1, source_target_pairs={{0,64},{32,480},{64,128},{96,32},{128,192},{160,96},{192,256},{224... | collective-permute-start | bytes 1572872 | tf_op jit(solution)/shard_map/ppermute | solution.py:36
  184.7 1.9 collective-permute-start.22
  186.7 5.7 %collective-permute-done.16 = bf16[2,2,128,512]{3,2,1,0:T(8,128)(2,1)S(1)} collective-permute-done((bf16[2,2,128,512]{3,2,1,0:T(8,128)(2,1)S(1)}, bf16[2,2,128,512]{3,2,1,0:T(8,128)(2,1)S(1)}, u32[]{:S(2)}, u32[]{:S(2)}) %collective-permute-start.16) | collective-permute-done | bytes 524320 | tf_op jit(solution)/shard_map/ppermute | solution.py:36
  192.5 1.9 collective-permute-start.17
  194.4 3.5 %collective-permute-done.20 = bf16[2,2,128,512]{3,2,1,0:T(8,128)(2,1)S(1)} collective-permute-done((bf16[2,2,128,512]{3,2,1,0:T(8,128)(2,1)S(1)}, bf16[2,2,128,512]{3,2,1,0:T(8,128)(2,1)S(1)}, u32[]{:S(2)}, u32[]{:S(2)}) %collective-permute-start.20) | collective-permute-done | bytes 524320 | tf_op jit(solution)/shard_map/ppermute | solution.py:36
  198.0 1.9 collective-permute-start.21
  200.0 3.1 %collective-permute-start.23 = (bf16[2,128,512]{2,1,0:T(8,128)(2,1)S(1)}, bf16[2,128,512]{2,1,0:T(8,128)(2,1)S(1)}, u32[]{:S(2)}, u32[]{:S(2)}) collective-permute-start(bf16[2,128,512]{2,1,0:T(8,128)(2,1)S(1)} %get-tuple-element.39), channel_id=1, source_target_pairs={{0,1},{1,2},{2,3},{3,4},{4,5},{5,6},{6,7},{7,8},{8,9},{9,10},{10,1... | collective-permute-start | bytes 786440 | tf_op jit(solution)/shard_map/ppermute | solution.py:46
  203.1 2.7 %collective-permute-start.24 = (bf16[2,128,512]{2,1,0:T(8,128)(2,1)S(1)}, bf16[2,128,512]{2,1,0:T(8,128)(2,1)S(1)}, u32[]{:S(2)}, u32[]{:S(2)}) collective-permute-start(bf16[2,128,512]{2,1,0:T(8,128)(2,1)S(1)} %get-tuple-element.38), channel_id=1, source_target_pairs={{1,0},{2,1},{3,2},{4,3},{5,4},{6,5},{7,6},{8,7},{9,8},{10,9},{11,1... | collective-permute-start | bytes 786440 | tf_op jit(solution)/shard_map/ppermute | solution.py:46
  205.8 4.4 %collective-permute-start.25 = (bf16[2,128,512]{2,1,0:T(8,128)(2,1)S(1)}, bf16[2,128,512]{2,1,0:T(8,128)(2,1)S(1)}, u32[]{:S(2)}, u32[]{:S(2)}) collective-permute-start(bf16[2,128,512]{2,1,0:T(8,128)(2,1)S(1)} %get-tuple-element.37), channel_id=1, source_target_pairs={{2,0},{3,1},{4,2},{5,3},{6,4},{7,5},{8,6},{9,7},{10,8},{11,9},{12,... | collective-permute-start | bytes 786440 | tf_op jit(solution)/shard_map/ppermute | solution.py:46
  210.4 0.2 collective-permute-done.23.refs_1_
  210.5 3.6 %collective-permute-done.24.refs_2_ = bf16[2,128,512]{2,1,0:T(8,128)(2,1)S(1)} collective-permute-done((bf16[2,128,512]{2,1,0:T(8,128)(2,1)S(1)}, bf16[2,128,512]{2,1,0:T(8,128)(2,1)S(1)}, u32[]{:S(2)}, u32[]{:S(2)}) %collective-permute-start.24) | collective-permute-done | bytes 262176 | tf_op jit(solution)/shard_map/ppermute | solution.py:46
  214.2 9.5 %collective-permute-done.25.refs_3_ = bf16[2,128,512]{2,1,0:T(8,128)(2,1)S(1)} collective-permute-done((bf16[2,128,512]{2,1,0:T(8,128)(2,1)S(1)}, bf16[2,128,512]{2,1,0:T(8,128)(2,1)S(1)}, u32[]{:S(2)}, u32[]{:S(2)}) %collective-permute-start.25) | collective-permute-done | bytes 262176 | tf_op jit(solution)/shard_map/ppermute | solution.py:46
  223.6 1.9 shard_map.97
  (74 shorter events, 2.3 us)
Async XLA Ops:
  0.6 68.6 %copy-start.18 = (s32[1,32,3]{1,0,2:T(1,128)S(1)}, s32[1,32,3]{1,0,2:T(1,128)}, u32[]{:S(2)}) copy-start(s32[1,32,3]{1,0,2:T(1,128)} %param.11) | copy-start | bytes 1156
  1.7 7.0 %collective-permute-start.4 = (bf16[2,256,512]{2,1,0:T(8,128)(2,1)S(1)}, bf16[2,256,512]{2,1,0:T(8,128)(2,1)S(1)}, u32[]{:S(2)}, u32[]{:S(2)}) collective-permute-start(bf16[2,256,512]{2,1,0:T(8,128)(2,1)S(1)} %pad_maximum_fusion.refs_0_), channel_id=1, source_target_pairs={{0,32},{32,0},{64,96},{96,64},{128,160},{160,128},{192,224},{224,1... | collective-permute-start | bytes 1572872 | tf_op jit(solution)/shard_map/ppermute | solution.py:41
  3.7 18.1 %collective-permute-start.5 = (bf16[2,256,512]{2,1,0:T(8,128)(2,1)S(1)}, bf16[2,256,512]{2,1,0:T(8,128)(2,1)S(1)}, u32[]{:S(2)}, u32[]{:S(2)}) collective-permute-start(bf16[2,256,512]{2,1,0:T(8,128)(2,1)S(1)} %pad_maximum_fusion.refs_0_), channel_id=1, source_target_pairs={{0,64},{32,480},{64,128},{96,32},{128,192},{160,96},{192,256},{224... | collective-permute-start | bytes 1572872 | tf_op jit(solution)/shard_map/ppermute | solution.py:36
  7.9 0.8 copy-start.12
  8.8 66.4 %copy-start = (bf16[2,256,512]{2,1,0:T(8,128)(2,1)}, bf16[2,256,512]{2,1,0:T(8,128)(2,1)S(1)}, u32[]{:S(2)}) copy-start(bf16[2,256,512]{2,1,0:T(8,128)(2,1)S(1)} %collective-permute-done.4.refs_0_.refs_5_) | copy-start | bytes 1572868
  8.8 18.6 %collective-permute-start.9 = (bf16[2,256,512]{2,1,0:T(8,128)(2,1)S(1)}, bf16[2,256,512]{2,1,0:T(8,128)(2,1)S(1)}, u32[]{:S(2)}, u32[]{:S(2)}) collective-permute-start(bf16[2,256,512]{2,1,0:T(8,128)(2,1)S(1)} %collective-permute-done.4.refs_0_.refs_5_), channel_id=1, source_target_pairs={{0,64},{32,480},{64,128},{96,32},{128,192},{160,96},{192,256},{224... | collective-permute-start | bytes 1572872 | tf_op jit(solution)/shard_map/ppermute | solution.py:36
  21.8 53.4 %copy-start.2 = (bf16[2,256,512]{2,1,0:T(8,128)(2,1)}, bf16[2,256,512]{2,1,0:T(8,128)(2,1)S(1)}, u32[]{:S(2)}) copy-start(bf16[2,256,512]{2,1,0:T(8,128)(2,1)S(1)} %collective-permute-done.5.refs_1_.refs_6_) | copy-start | bytes 1572868
  21.8 12.3 %collective-permute-start.6 = (bf16[2,256,512]{2,1,0:T(8,128)(2,1)S(1)}, bf16[2,256,512]{2,1,0:T(8,128)(2,1)S(1)}, u32[]{:S(2)}, u32[]{:S(2)}) collective-permute-start(bf16[2,256,512]{2,1,0:T(8,128)(2,1)S(1)} %collective-permute-done.5.refs_1_.refs_6_), channel_id=1, source_target_pairs={{0,64},{32,480},{64,128},{96,32},{128,192},{160,96},{192,256},{224... | collective-permute-start | bytes 1572872 | tf_op jit(solution)/shard_map/ppermute | solution.py:36
  27.4 47.8 %copy-start.4 = (bf16[2,256,512]{2,1,0:T(8,128)(2,1)}, bf16[2,256,512]{2,1,0:T(8,128)(2,1)S(1)}, u32[]{:S(2)}) copy-start(bf16[2,256,512]{2,1,0:T(8,128)(2,1)S(1)} %collective-permute-done.9.refs_5_.refs_10_) | copy-start | bytes 1572868
  27.4 12.3 %collective-permute-start.10 = (bf16[2,256,512]{2,1,0:T(8,128)(2,1)S(1)}, bf16[2,256,512]{2,1,0:T(8,128)(2,1)S(1)}, u32[]{:S(2)}, u32[]{:S(2)}) collective-permute-start(bf16[2,256,512]{2,1,0:T(8,128)(2,1)S(1)} %collective-permute-done.9.refs_5_.refs_10_), channel_id=1, source_target_pairs={{0,64},{32,480},{64,128},{96,32},{128,192},{160,96},{192,256},{224... | collective-permute-start | bytes 1572872 | tf_op jit(solution)/shard_map/ppermute | solution.py:36
  34.0 41.2 %copy-start.6 = (bf16[2,256,512]{2,1,0:T(8,128)(2,1)}, bf16[2,256,512]{2,1,0:T(8,128)(2,1)S(1)}, u32[]{:S(2)}) copy-start(bf16[2,256,512]{2,1,0:T(8,128)(2,1)S(1)} %collective-permute-done.6.refs_2_.refs_7_) | copy-start | bytes 1572868
  34.0 12.3 %collective-permute-start.7 = (bf16[2,256,512]{2,1,0:T(8,128)(2,1)S(1)}, bf16[2,256,512]{2,1,0:T(8,128)(2,1)S(1)}, u32[]{:S(2)}, u32[]{:S(2)}) collective-permute-start(bf16[2,256,512]{2,1,0:T(8,128)(2,1)S(1)} %collective-permute-done.6.refs_2_.refs_7_), channel_id=1, source_target_pairs={{0,64},{32,480},{64,128},{96,32},{128,192},{160,96},{192,256},{224... | collective-permute-start | bytes 1572872 | tf_op jit(solution)/shard_map/ppermute | solution.py:36
  39.7 35.6 %copy-start.8 = (bf16[2,256,512]{2,1,0:T(8,128)(2,1)}, bf16[2,256,512]{2,1,0:T(8,128)(2,1)S(1)}, u32[]{:S(2)}) copy-start(bf16[2,256,512]{2,1,0:T(8,128)(2,1)S(1)} %collective-permute-done.10.refs_6_.refs_11_) | copy-start | bytes 1572868
  39.7 30.5 %collective-permute-start.11 = (bf16[2,256,512]{2,1,0:T(8,128)(2,1)S(1)}, bf16[2,256,512]{2,1,0:T(8,128)(2,1)}, u32[]{:S(2)}, u32[]{:S(2)}) collective-permute-start(bf16[2,256,512]{2,1,0:T(8,128)(2,1)S(1)} %collective-permute-done.10.refs_6_.refs_11_), channel_id=1, source_target_pairs={{0,64},{32,480},{64,128},{96,32},{128,192},{160,96},{192,256},{224... | collective-permute-start | bytes 1572872 | tf_op jit(solution)/shard_map/ppermute | solution.py:36
  46.3 28.9 %copy-start.10 = (bf16[2,256,512]{2,1,0:T(8,128)(2,1)}, bf16[2,256,512]{2,1,0:T(8,128)(2,1)S(1)}, u32[]{:S(2)}) copy-start(bf16[2,256,512]{2,1,0:T(8,128)(2,1)S(1)} %collective-permute-done.7.refs_3_.refs_8_) | copy-start | bytes 1572868
  46.3 28.8 %collective-permute-start.8 = (bf16[2,256,512]{2,1,0:T(8,128)(2,1)S(1)}, bf16[2,256,512]{2,1,0:T(8,128)(2,1)}, u32[]{:S(2)}, u32[]{:S(2)}) collective-permute-start(bf16[2,256,512]{2,1,0:T(8,128)(2,1)S(1)} %collective-permute-done.7.refs_3_.refs_8_), channel_id=1, source_target_pairs={{0,64},{32,480},{64,128},{96,32},{128,192},{160,96},{192,256},{224... | collective-permute-start | bytes 1572872 | tf_op jit(solution)/shard_map/ppermute | solution.py:36
  60.0 43.1 %collective-permute-start = (bf16[2,128,512]{2,1,0:T(8,128)(2,1)}, bf16[2,128,512]{2,1,0:T(8,128)(2,1)}, u32[]{:S(2)}, u32[]{:S(2)}) collective-permute-start(bf16[2,128,512]{2,1,0:T(8,128)(2,1)} %get-tuple-element.42), channel_id=1, source_target_pairs={{2,0},{3,1},{4,2},{5,3},{6,4},{7,5},{8,6},{9,7},{10,8},{11,9},{12,... | collective-permute-start | bytes 786440 | tf_op jit(solution)/shard_map/ppermute | solution.py:46
  62.4 40.7 %collective-permute-start.1 = (bf16[2,128,512]{2,1,0:T(8,128)(2,1)}, bf16[2,128,512]{2,1,0:T(8,128)(2,1)}, u32[]{:S(2)}, u32[]{:S(2)}) collective-permute-start(bf16[2,128,512]{2,1,0:T(8,128)(2,1)} %get-tuple-element.43), channel_id=1, source_target_pairs={{1,0},{2,1},{3,2},{4,3},{5,4},{6,5},{7,6},{8,7},{9,8},{10,9},{11,1... | collective-permute-start | bytes 786440 | tf_op jit(solution)/shard_map/ppermute | solution.py:46
  67.3 35.8 %collective-permute-start.2 = (bf16[2,128,512]{2,1,0:T(8,128)(2,1)}, bf16[2,128,512]{2,1,0:T(8,128)(2,1)}, u32[]{:S(2)}, u32[]{:S(2)}) collective-permute-start(bf16[2,128,512]{2,1,0:T(8,128)(2,1)} %get-tuple-element.44), channel_id=1, source_target_pairs={{0,1},{1,2},{2,3},{3,4},{4,5},{5,6},{6,7},{7,8},{8,9},{9,10},{10,1... | collective-permute-start | bytes 786440 | tf_op jit(solution)/shard_map/ppermute | solution.py:46
  70.1 35.1 %copy-start.16 = (bf16[256,512]{1,0:T(8,128)(2,1)S(1)}, bf16[256,512]{1,0:T(8,128)(2,1)}, u32[]{:S(2)}) copy-start(bf16[256,512]{1,0:T(8,128)(2,1)} %param.6) | copy-start | bytes 786436
  70.1 33.0 %collective-permute-start.3 = (bf16[2,128,512]{2,1,0:T(8,128)(2,1)}, bf16[2,128,512]{2,1,0:T(8,128)(2,1)}, u32[]{:S(2)}, u32[]{:S(2)}) collective-permute-start(bf16[2,128,512]{2,1,0:T(8,128)(2,1)} %get-tuple-element.41), channel_id=1, source_target_pairs={{0,2},{1,3},{2,4},{3,5},{4,6},{5,7},{6,8},{7,9},{8,10},{9,11},{10,... | collective-permute-start | bytes 786440 | tf_op jit(solution)/shard_map/ppermute | solution.py:46
  85.1 20.1 %collective-permute-start.12 = (bf16[6,2,128,512]{3,2,1,0:T(8,128)(2,1)}, bf16[6,2,128,512]{3,2,1,0:T(8,128)(2,1)S(1)}, u32[]{:S(2)}, u32[]{:S(2)}) collective-permute-start(bf16[6,2,128,512]{3,2,1,0:T(8,128)(2,1)} %shard_map.93), channel_id=1, source_target_pairs={{0,32},{32,0},{64,96},{96,64},{128,160},{160,128},{192,224},{224,1... | collective-permute-start | bytes 4718600 | tf_op jit(solution)/shard_map/ppermute | solution.py:41
  105.3 1.0 copy-start.1
  106.3 1.0 copy-start.3
  107.3 1.0 copy-start.5
  108.4 1.0 copy-start.7
  109.4 1.0 copy-start.9
  110.5 1.0 copy-start.11
  111.5 1.0 copy-start.13
  112.6 0.9 copy-start.17
  130.0 1.2 copy-start.14
  131.2 5.3 %collective-permute-start.13 = (bf16[6,2,128,512]{3,2,1,0:T(8,128)(2,1)S(1)}, bf16[6,2,128,512]{3,2,1,0:T(8,128)(2,1)S(1)}, u32[]{:S(2)}, u32[]{:S(2)}) collective-permute-start(bf16[6,2,128,512]{3,2,1,0:T(8,128)(2,1)S(1)} %get-tuple-element.20.mine), channel_id=1, source_target_pairs={{0,32},{32,0},{64,96},{96,64},{128,160},{160,128},{192,224},{224,1... | collective-permute-start | bytes 4718600 | tf_op jit(solution)/shard_map/ppermute | solution.py:41
  137.2 12.3 %collective-permute-start.14 = (bf16[2,2,128,512]{3,2,1,0:T(8,128)(2,1)S(1)}, bf16[2,2,128,512]{3,2,1,0:T(8,128)(2,1)S(1)}, u32[]{:S(2)}, u32[]{:S(2)}) collective-permute-start(bf16[2,2,128,512]{3,2,1,0:T(8,128)(2,1)S(1)} %get-tuple-element.21), channel_id=1, source_target_pairs={{0,64},{32,480},{64,128},{96,32},{128,192},{160,96},{192,256},{224... | collective-permute-start | bytes 1572872 | tf_op jit(solution)/shard_map/ppermute | solution.py:36
  139.2 19.0 %collective-permute-start.18 = (bf16[2,2,128,512]{3,2,1,0:T(8,128)(2,1)S(1)}, bf16[2,2,128,512]{3,2,1,0:T(8,128)(2,1)S(1)}, u32[]{:S(2)}, u32[]{:S(2)}) collective-permute-start(bf16[2,2,128,512]{3,2,1,0:T(8,128)(2,1)S(1)} %get-tuple-element.25), channel_id=1, source_target_pairs={{0,64},{32,480},{64,128},{96,32},{128,192},{160,96},{192,256},{224... | collective-permute-start | bytes 1572872 | tf_op jit(solution)/shard_map/ppermute | solution.py:36
  149.6 17.0 %collective-permute-start.15 = (bf16[2,2,128,512]{3,2,1,0:T(8,128)(2,1)S(1)}, bf16[2,2,128,512]{3,2,1,0:T(8,128)(2,1)S(1)}, u32[]{:S(2)}, u32[]{:S(2)}) collective-permute-start(bf16[2,2,128,512]{3,2,1,0:T(8,128)(2,1)S(1)} %add_convert_fusion.4), channel_id=1, source_target_pairs={{0,64},{32,480},{64,128},{96,32},{128,192},{160,96},{192,256},{224... | collective-permute-start | bytes 1572872 | tf_op jit(solution)/shard_map/ppermute | solution.py:36
  158.3 19.7 %collective-permute-start.19 = (bf16[2,2,128,512]{3,2,1,0:T(8,128)(2,1)S(1)}, bf16[2,2,128,512]{3,2,1,0:T(8,128)(2,1)S(1)}, u32[]{:S(2)}, u32[]{:S(2)}) collective-permute-start(bf16[2,2,128,512]{3,2,1,0:T(8,128)(2,1)S(1)} %add_convert_fusion.1), channel_id=1, source_target_pairs={{0,64},{32,480},{64,128},{96,32},{128,192},{160,96},{192,256},{224... | collective-permute-start | bytes 1572872 | tf_op jit(solution)/shard_map/ppermute | solution.py:36
  166.7 18.0 %copy-start.15 = (bf16[6,2,128,512]{3,2,1,0:T(8,128)(2,1)S(1)}, bf16[6,2,128,512]{3,2,1,0:T(8,128)(2,1)}, u32[]{:S(2)}) copy-start(bf16[6,2,128,512]{3,2,1,0:T(8,128)(2,1)} %copy-done.14) | copy-start | bytes 4718596
  166.8 25.5 %collective-permute-start.16 = (bf16[2,2,128,512]{3,2,1,0:T(8,128)(2,1)S(1)}, bf16[2,2,128,512]{3,2,1,0:T(8,128)(2,1)S(1)}, u32[]{:S(2)}, u32[]{:S(2)}) collective-permute-start(bf16[2,2,128,512]{3,2,1,0:T(8,128)(2,1)S(1)} %add_convert_fusion.3), channel_id=1, source_target_pairs={{0,64},{32,480},{64,128},{96,32},{128,192},{160,96},{192,256},{224... | collective-permute-start | bytes 1572872 | tf_op jit(solution)/shard_map/ppermute | solution.py:36
  178.1 19.8 %collective-permute-start.20 = (bf16[2,2,128,512]{3,2,1,0:T(8,128)(2,1)S(1)}, bf16[2,2,128,512]{3,2,1,0:T(8,128)(2,1)S(1)}, u32[]{:S(2)}, u32[]{:S(2)}) collective-permute-start(bf16[2,2,128,512]{3,2,1,0:T(8,128)(2,1)S(1)} %add_convert_fusion), channel_id=1, source_target_pairs={{0,64},{32,480},{64,128},{96,32},{128,192},{160,96},{192,256},{224... | collective-permute-start | bytes 1572872 | tf_op jit(solution)/shard_map/ppermute | solution.py:36
  184.7 21.1 %collective-permute-start.22 = (bf16[2,128,512]{2,1,0:T(8,128)(2,1)S(1)}, bf16[2,128,512]{2,1,0:T(8,128)(2,1)S(1)}, u32[]{:S(2)}, u32[]{:S(2)}) collective-permute-start(bf16[2,128,512]{2,1,0:T(8,128)(2,1)S(1)} %get-tuple-element.40), channel_id=1, source_target_pairs={{0,2},{1,3},{2,4},{3,5},{4,6},{5,7},{6,8},{7,9},{8,10},{9,11},{10,... | collective-permute-start | bytes 786440 | tf_op jit(solution)/shard_map/ppermute | solution.py:46
  192.5 31.2 %collective-permute-start.17 = (bf16[2,2,128,512]{3,2,1,0:T(8,128)(2,1)S(1)}, bf16[2,2,128,512]{3,2,1,0:T(8,128)(2,1)S(1)}, u32[]{:S(2)}, u32[]{:S(2)}) collective-permute-start(bf16[2,2,128,512]{3,2,1,0:T(8,128)(2,1)S(1)} %add_convert_fusion.2), channel_id=1, source_target_pairs={{0,64},{32,480},{64,128},{96,32},{128,192},{160,96},{192,256},{224... | collective-permute-start | bytes 1572872 | tf_op jit(solution)/shard_map/ppermute | solution.py:36
  198.0 25.7 %collective-permute-start.21 = (bf16[2,2,128,512]{3,2,1,0:T(8,128)(2,1)S(1)}, bf16[2,2,128,512]{3,2,1,0:T(8,128)(2,1)S(1)}, u32[]{:S(2)}, u32[]{:S(2)}) collective-permute-start(bf16[2,2,128,512]{3,2,1,0:T(8,128)(2,1)S(1)} %collective-permute-done.20), channel_id=1, source_target_pairs={{0,32},{32,0},{64,96},{96,64},{128,160},{160,128},{192,224},{224,1... | collective-permute-start | bytes 1572872 | tf_op jit(solution)/shard_map/ppermute | solution.py:41
  200.0 10.6 %collective-permute-start.23 = (bf16[2,128,512]{2,1,0:T(8,128)(2,1)S(1)}, bf16[2,128,512]{2,1,0:T(8,128)(2,1)S(1)}, u32[]{:S(2)}, u32[]{:S(2)}) collective-permute-start(bf16[2,128,512]{2,1,0:T(8,128)(2,1)S(1)} %get-tuple-element.39), channel_id=1, source_target_pairs={{0,1},{1,2},{2,3},{3,4},{4,5},{5,6},{6,7},{7,8},{8,9},{9,10},{10,1... | collective-permute-start | bytes 786440 | tf_op jit(solution)/shard_map/ppermute | solution.py:46
  203.1 11.1 %collective-permute-start.24 = (bf16[2,128,512]{2,1,0:T(8,128)(2,1)S(1)}, bf16[2,128,512]{2,1,0:T(8,128)(2,1)S(1)}, u32[]{:S(2)}, u32[]{:S(2)}) collective-permute-start(bf16[2,128,512]{2,1,0:T(8,128)(2,1)S(1)} %get-tuple-element.38), channel_id=1, source_target_pairs={{1,0},{2,1},{3,2},{4,3},{5,4},{6,5},{7,6},{8,7},{9,8},{10,9},{11,1... | collective-permute-start | bytes 786440 | tf_op jit(solution)/shard_map/ppermute | solution.py:46
  205.8 17.8 %collective-permute-start.25 = (bf16[2,128,512]{2,1,0:T(8,128)(2,1)S(1)}, bf16[2,128,512]{2,1,0:T(8,128)(2,1)S(1)}, u32[]{:S(2)}, u32[]{:S(2)}) collective-permute-start(bf16[2,128,512]{2,1,0:T(8,128)(2,1)S(1)} %get-tuple-element.37), channel_id=1, source_target_pairs={{2,0},{3,1},{4,2},{5,3},{6,4},{7,5},{8,6},{9,7},{10,8},{11,9},{12,... | collective-permute-start | bytes 786440 | tf_op jit(solution)/shard_map/ppermute | solution.py:46

commit v2 on v1

--- a/solution.py
+++ b/solution.py
@@ -92,8 +92,9 @@
         pick_kernel,
         out_shape=jax.ShapeDtypeStruct((FAR, 2, BS, D), BF),
         in_specs=[SMEM] + [ANY] * 8,
-        out_specs=ANY,
+        out_specs=VMEM,
         scratch_shapes=[pltpu.SemaphoreType.DMA((FAR,))],
+        compiler_params=pltpu.CompilerParams(vmem_limit_bytes=4 * 2**20),
         cost_estimate=pl.CostEstimate(flops=0, bytes_accessed=6 * 2**20, transcendentals=0),
     )(table, *places)
 
@@ -212,7 +213,7 @@
             pltpu.VMEM((NEAR + FAR, 2, BS, D), F32),
             pltpu.SemaphoreType.DMA((NB,)),
         ],
-        compiler_params=pltpu.CompilerParams(vmem_limit_bytes=40 * 2**20),
+        compiler_params=pltpu.CompilerParams(vmem_limit_bytes=32 * 2**20),
         cost_estimate=pl.CostEstimate(
             flops=12 * NB * BS * ROWS * D, bytes_accessed=12 * 2**20, transcendentals=NB * 8 * BS * ROWS
         ),
@@ -249,7 +250,7 @@
         out_shape=tuple(jax.ShapeDtypeStruct((NB, 2, BS, D), BF) for _ in range(count)),
         in_specs=[SMEM, VMEM, VMEM],
         out_specs=(VMEM,) * count,
-        compiler_params=pltpu.CompilerParams(vmem_limit_bytes=24 * 2**20),
+        compiler_params=pltpu.CompilerParams(vmem_limit_bytes=12 * 2**20),
         cost_estimate=pl.CostEstimate(flops=0, bytes_accessed=(3 + count) * 2**19, transcendentals=0),
     )(table, mine, theirs)
 
@@ -274,7 +275,7 @@
         out_shape=(jax.ShapeDtypeStruct((NB * BS, D), BF),) * 2,
         in_specs=[SMEM] + [VMEM] * 8,
         out_specs=(VMEM, VMEM),
-        compiler_params=pltpu.CompilerParams(vmem_limit_bytes=24 * 2**20),
+        compiler_params=pltpu.CompilerParams(vmem_limit_bytes=12 * 2**20),
         cost_estimate=pl.CostEstimate(flops=2**22, bytes_accessed=6 * 2**20, transcendentals=0),
     )(table, near, theirs, from_a, from_b, *returned)
 
@@ -292,10 +293,6 @@
     flow_a = [ring_step(own)]
     sibling = swap_cores(own)
     flow_b = [ring_step(sibling)]
-    for _ in range(2):
-        flow_a.append(ring_step(flow_a[-1]))
-        flow_b.append(ring_step(flow_b[-1]))
-    flow_a.append(ring_step(flow_a[-1]))
 
     padded = jnp.pad(local_list, ((W * NB, W * NB), (0, 0)), constant_values=-1)
     around = lax.dynamic_slice_in_dim(padded, dom * NB, (2 * W + 1) * NB, 0).reshape(2 * W + 1, NB * LOC)
@@ -305,6 +302,12 @@
     for offset in OFFSETS:
         piece = lax.dynamic_index_in_dim(blocks, given[W + offset], 1, keepdims=False)
         near.append(shifted(piece, offset))
+    flow_a[0], near = lax.optimization_barrier((flow_a[0], near))
+    for _ in range(2):
+        flow_a.append(ring_step(flow_a[-1]))
+        flow_b.append(ring_step(flow_b[-1]))
+    flow_a.append(ring_step(flow_a[-1]))
+
     local = around[W].reshape(NB, LOC)
     holder = local // NB - dom
     near_code = jnp.where(holder == 0, 0, jnp.where(holder > 0, 3 - holder, 2 - holder))
@@ -352,8 +355,10 @@
     def joined(x, y):
         return (x.astype(F32) + y.astype(F32)).astype(BF)
 
+    returned = [shifted(near_terms[NB + t], -offset) for t, offset in enumerate(OFFSETS)]
     back_a = ring_step(start_a)
     back_b = ring_step(start_b)
+    back_a, returned = lax.optimization_barrier((back_a, returned))
     back_a = ring_step(joined(back_a, a3))
     back_b = ring_step(joined(back_b, b2))
     back_a = ring_step(joined(back_a, a2))
@@ -361,7 +366,6 @@
     back_a = ring_step(joined(back_a, a1))
     back_b = swap_cores(back_b)
 
-    returned = [shifted(near_terms[NB + t], -offset) for t, offset in enumerate(OFFSETS)]
     back_slots = jnp.stack([given[W + offset] for offset in OFFSETS])
     last = jnp.concatenate([back_slots, hits[1, 7 * NB :]]).astype(i32)
     grad_keys, grad_values = close(last, near_terms[:NB], sibling_terms, back_a, back_b, returned)

time: 227 us -> 204 us (0.90)
  the two profiles are of different devices: /device:TPU:44 before, /device:TPU:28 now
where the time goes in v2:
time: 204 us; the launch traced here: 203 us
  waiting for transfers between devices  77.6 us (38%)
  starting transfers between devices  74.4 us (36%)
  Pallas kernels  22.5 us (11%)
  local copies, waits for them, and re-layouts  16.3 us (8%)
  between operations  9.04 us (4%)
  other arithmetic  3.32 us (2%)
    ppermute x14, waiting for transfers between devices, ring_step(): lax.ppermute(array, 'group', [(g, (g + (2 if g % 2 == 0 else -2)) % size)...  53.5 us
    ppermute x8, starting transfers between devices, shifted(): lax.ppermute(array, 'dom', [(i, i + by) for i in range(size) if 0 <= i +...  31.4 us
    ppermute x14, starting transfers between devices, ring_step(): lax.ppermute(array, 'group', [(g, (g + (2 if g % 2 == 0 else -2)) % size)...  29.5 us
    pallas_call x1, Pallas kernels, attend(): pl.pallas_call(attend_kernel, out_shape=(jax.ShapeDtypeStruct((NB, BS, D)...  16.7 us
    ppermute x8, waiting for transfers between devices, shifted(): lax.ppermute(array, 'dom', [(i, i + by) for i in range(size) if 0 <= i +...  16.7 us
    unnamed x48, local copies, waits for them, and re-layouts  14.6 us
    ppermute x4, starting transfers between devices, swap_cores(): return lax.ppermute(array, 'group', [(g, g ^ 1) for g in range(size)])  13.6 us
    ppermute x4, waiting for transfers between devices, swap_cores(): return lax.ppermute(array, 'group', [(g, g ^ 1) for g in range(size)])  7.35 us
  transfers between devices with their start and end apart: 26, of which 17 were waited for; matrix products, arithmetic and copies ran while one was open for 1% of the time, Pallas kernels for 0%

profile of v2, /device:TPU:28, one launch (start us, length us, event | category | flops | bytes accessed | tf_op | source)
XLA Modules:
  0.0 203.1 jit_solution(17765032422581149478)
XLA Ops:
  0.7 0.8 copy.18
  10.2 1.5 fusion.1
  11.7 2.3 %collective-permute-start.1 = (bf16[2,128,512]{2,1,0:T(8,128)(2,1)S(1)}, bf16[2,128,512]{2,1,0:T(8,128)(2,1)S(1)}, u32[]{:S(2)}, u32[]{:S(2)}) collective-permute-start(bf16[2,128,512]{2,1,0:T(8,128)(2,1)S(1)} %get-tuple-element.62), channel_id=1, source_target_pairs={{2,0},{3,1},{4,2},{5,3},{6,4},{7,5},{8,6},{9,7},{10,8},{11,9},{12,... | collective-permute-start | bytes 786440 | tf_op jit(solution)/shard_map/ppermute | solution.py:46
  14.1 4.3 %collective-permute-start = (bf16[2,256,512]{2,1,0:T(8,128)(2,1)S(1)}, bf16[2,256,512]{2,1,0:T(8,128)(2,1)S(1)}, u32[]{:S(2)}, u32[]{:S(2)}) collective-permute-start(bf16[2,256,512]{2,1,0:T(8,128)(2,1)S(1)} %pad_maximum_fusion.refs_0_), channel_id=1, source_target_pairs={{0,64},{32,480},{64,128},{96,32},{128,192},{160,96},{192,256},{224... | collective-permute-start | bytes 1572872 | tf_op jit(solution)/shard_map/ppermute | solution.py:36
  18.4 7.9 %collective-permute-start.5 = (bf16[2,256,512]{2,1,0:T(8,128)(2,1)S(1)}, bf16[2,256,512]{2,1,0:T(8,128)(2,1)S(1)}, u32[]{:S(2)}, u32[]{:S(2)}) collective-permute-start(bf16[2,256,512]{2,1,0:T(8,128)(2,1)S(1)} %pad_maximum_fusion.refs_0_), channel_id=1, source_target_pairs={{0,32},{32,0},{64,96},{96,64},{128,160},{160,128},{192,224},{224,1... | collective-permute-start | bytes 1572872 | tf_op jit(solution)/shard_map/ppermute | solution.py:41
  26.2 0.8 copy-done.6
  27.0 3.9 %collective-permute-start.2 = (bf16[2,128,512]{2,1,0:T(8,128)(2,1)S(1)}, bf16[2,128,512]{2,1,0:T(8,128)(2,1)S(1)}, u32[]{:S(2)}, u32[]{:S(2)}) collective-permute-start(bf16[2,128,512]{2,1,0:T(8,128)(2,1)S(1)} %get-tuple-element.63), channel_id=1, source_target_pairs={{1,0},{2,1},{3,2},{4,3},{5,4},{6,5},{7,6},{8,7},{9,8},{10,9},{11,1... | collective-permute-start | bytes 786440 | tf_op jit(solution)/shard_map/ppermute | solution.py:46
  31.0 2.0 collective-permute-start.3
  33.7 6.9 %collective-permute-start.4 = (bf16[2,128,512]{2,1,0:T(8,128)(2,1)S(1)}, bf16[2,128,512]{2,1,0:T(8,128)(2,1)S(1)}, u32[]{:S(2)}, u32[]{:S(2)}) collective-permute-start(bf16[2,128,512]{2,1,0:T(8,128)(2,1)S(1)} %get-tuple-element.61), channel_id=1, source_target_pairs={{0,2},{1,3},{2,4},{3,5},{4,6},{5,7},{6,8},{7,9},{8,10},{9,11},{10,... | collective-permute-start | bytes 786440 | tf_op jit(solution)/shard_map/ppermute | solution.py:46
  40.6 0.7 copy-done.14
  41.3 0.7 copy-done.16
  42.0 5.6 %collective-permute-done.4.refs_4_ = bf16[2,128,512]{2,1,0:T(8,128)(2,1)S(1)} collective-permute-done((bf16[2,128,512]{2,1,0:T(8,128)(2,1)S(1)}, bf16[2,128,512]{2,1,0:T(8,128)(2,1)S(1)}, u32[]{:S(2)}, u32[]{:S(2)}) %collective-permute-start.4) | collective-permute-done | bytes 262176 | tf_op jit(solution)/shard_map/ppermute | solution.py:46
  47.6 0.7 copy-done.18
  48.3 1.9 collective-permute-start.6
  50.3 1.9 collective-permute-start.9
  52.2 8.4 %collective-permute-done.6.refs_2_.refs_7_ = bf16[2,256,512]{2,1,0:T(8,128)(2,1)S(1)} collective-permute-done((bf16[2,256,512]{2,1,0:T(8,128)(2,1)S(1)}, bf16[2,256,512]{2,1,0:T(8,128)(2,1)S(1)}, u32[]{:S(2)}, u32[]{:S(2)}) %collective-permute-start.6) | collective-permute-done | bytes 524320 | tf_op jit(solution)/shard_map/ppermute | solution.py:36
  60.6 1.9 collective-permute-start.7
  62.5 3.7 %collective-permute-done.9.refs_5_.refs_10_ = bf16[2,256,512]{2,1,0:T(8,128)(2,1)S(1)} collective-permute-done((bf16[2,256,512]{2,1,0:T(8,128)(2,1)S(1)}, bf16[2,256,512]{2,1,0:T(8,128)(2,1)S(1)}, u32[]{:S(2)}, u32[]{:S(2)}) %collective-permute-start.9) | collective-permute-done | bytes 524320 | tf_op jit(solution)/shard_map/ppermute | solution.py:36
  66.2 1.9 collective-permute-start.10
  68.2 4.7 %collective-permute-done.7.refs_3_.refs_8_ = bf16[2,256,512]{2,1,0:T(8,128)(2,1)S(1)} collective-permute-done((bf16[2,256,512]{2,1,0:T(8,128)(2,1)S(1)}, bf16[2,256,512]{2,1,0:T(8,128)(2,1)S(1)}, u32[]{:S(2)}, u32[]{:S(2)}) %collective-permute-start.7) | collective-permute-done | bytes 524320 | tf_op jit(solution)/shard_map/ppermute | solution.py:36
  72.9 1.9 collective-permute-start.8
  74.8 3.7 %collective-permute-done.10.refs_6_.refs_11_ = bf16[2,256,512]{2,1,0:T(8,128)(2,1)S(1)} collective-permute-done((bf16[2,256,512]{2,1,0:T(8,128)(2,1)S(1)}, bf16[2,256,512]{2,1,0:T(8,128)(2,1)S(1)}, u32[]{:S(2)}, u32[]{:S(2)}) %collective-permute-start.10) | collective-permute-done | bytes 524320 | tf_op jit(solution)/shard_map/ppermute | solution.py:36
  78.5 1.9 collective-permute-start.11
  80.8 4.5 %collective-permute-done.8.refs_4_.refs_9_ = bf16[2,256,512]{2,1,0:T(8,128)(2,1)} collective-permute-done((bf16[2,256,512]{2,1,0:T(8,128)(2,1)S(1)}, bf16[2,256,512]{2,1,0:T(8,128)(2,1)}, u32[]{:S(2)}, u32[]{:S(2)}) %collective-permute-start.8) | collective-permute-done | bytes 524320 | tf_op jit(solution)/shard_map/ppermute | solution.py:36
  85.3 5.6 %collective-permute-done.11.refs_7_.refs_12_ = bf16[2,256,512]{2,1,0:T(8,128)(2,1)} collective-permute-done((bf16[2,256,512]{2,1,0:T(8,128)(2,1)S(1)}, bf16[2,256,512]{2,1,0:T(8,128)(2,1)}, u32[]{:S(2)}, u32[]{:S(2)}) %collective-permute-start.11) | collective-permute-done | bytes 524320 | tf_op jit(solution)/shard_map/ppermute | solution.py:36
  90.9 2.1 %shard_map.93 = bf16[6,2,128,512]{3,2,1,0:T(8,128)(2,1)} custom-call(s32[2,6]{1,0:T(2,128)S(1)} %pad_add_fusion.4.table, bf16[2,256,512]{2,1,0:T(8,128)(2,1)S(1)} %collective-permute-done.5.refs_0_.refs_5_, bf16[2,256,512]{2,1,0:T(8,128)(2,1)S(1)} %collective-permute-done.refs_1_.refs_6_, bf16[2,256,512]{2,1,0:T(8,128)(2,1)S(1)} %collective-permute-done.6.refs_2_.refs_7_, ...), custom_call_target="tpu_custom_call" | custom-call | bytes 6291456 | tf_op jit(solution)/shard_map/pallas_call | solution.py:91
  93.1 1.9 collective-permute-start.12
  96.0 2.7 %collective-permute-done.12.refs_13_ = bf16[6,2,128,512]{3,2,1,0:T(8,128)(2,1)} collective-permute-done((bf16[6,2,128,512]{3,2,1,0:T(8,128)(2,1)}, bf16[6,2,128,512]{3,2,1,0:T(8,128)(2,1)}, u32[]{:S(2)}, u32[]{:S(2)}) %collective-permute-start.12) | collective-permute-done | bytes 1572896 | tf_op jit(solution)/shard_map/ppermute | solution.py:41
  98.7 1.0 copy-done.1
  99.7 1.0 copy-done.3
  100.8 1.0 copy-done.5
  101.8 1.0 copy-done.7
  102.9 0.9 copy-done.11
  103.8 0.9 copy-done.13
  104.8 0.9 copy-done.15
  105.7 0.9 copy-done.17
  106.7 0.9 copy-done.19
  107.6 16.7 %shard_map.94 = (bf16[2,128,512]{2,1,0:T(8,128)(2,1)}, bf16[2,128,512]{2,1,0:T(8,128)(2,1)}, bf16[6,2,128,512]{3,2,1,0:T(8,128)(2,1)S(1)}, bf16[6,2,128,512]{3,2,1,0:T(8,128)(2,1)S(1)}) custom-call(s32[4,14]{1,0:T(4,128)S(1)} %pad_add_fusion.table, bf16[2,128,512]{2,1,0:T(8,128)(2,1)S(1)} %bitcast.62, bf16[2,128,512]{2,1,0:T(8,128)(2,1)S(1)} %bitcast.63, ...), custom_call_target="tpu_custom_call" | custom-call | flops 1409286144 | bytes 12582912 | tf_op jit(solution)/shard_map/pallas_call | solution.py:201
  124.4 1.2 copy-done.8
  125.6 1.9 collective-permute-start.13
  127.8 3.1 %collective-permute-done.13.theirs = bf16[6,2,128,512]{3,2,1,0:T(8,128)(2,1)S(1)} collective-permute-done((bf16[6,2,128,512]{3,2,1,0:T(8,128)(2,1)S(1)}, bf16[6,2,128,512]{3,2,1,0:T(8,128)(2,1)S(1)}, u32[]{:S(2)}, u32[]{:S(2)}) %collective-permute-start.13) | collective-permute-done | bytes 1572896 | tf_op jit(solution)/shard_map/ppermute | solution.py:41
  130.8 0.7 shard_map.95
  131.6 1.9 collective-permute-start.14
  133.6 8.1 %collective-permute-start.15 = (bf16[2,128,512]{2,1,0:T(8,128)(2,1)S(1)}, bf16[2,128,512]{2,1,0:T(8,128)(2,1)S(1)}, u32[]{:S(2)}, u32[]{:S(2)}) collective-permute-start(bf16[2,128,512]{2,1,0:T(8,128)(2,1)S(1)} %get-tuple-element.60), channel_id=1, source_target_pairs={{0,2},{1,3},{2,4},{3,5},{4,6},{5,7},{6,8},{7,9},{8,10},{9,11},{10,... | collective-permute-start | bytes 786440 | tf_op jit(solution)/shard_map/ppermute | solution.py:46
  141.7 4.2 %collective-permute-start.16 = (bf16[2,128,512]{2,1,0:T(8,128)(2,1)S(1)}, bf16[2,128,512]{2,1,0:T(8,128)(2,1)S(1)}, u32[]{:S(2)}, u32[]{:S(2)}) collective-permute-start(bf16[2,128,512]{2,1,0:T(8,128)(2,1)S(1)} %get-tuple-element.59), channel_id=1, source_target_pairs={{0,1},{1,2},{2,3},{3,4},{4,5},{5,6},{6,7},{7,8},{8,9},{9,10},{10,1... | collective-permute-start | bytes 786440 | tf_op jit(solution)/shard_map/ppermute | solution.py:46
  146.0 1.9 collective-permute-start.17
  147.9 1.9 collective-permute-start.18
  149.8 1.9 collective-permute-start.22
  151.8 0.9 shard_map.96
  152.8 4.3 %collective-permute-done.17.refs_2_ = bf16[2,128,512]{2,1,0:T(8,128)(2,1)S(1)} collective-permute-done((bf16[2,128,512]{2,1,0:T(8,128)(2,1)S(1)}, bf16[2,128,512]{2,1,0:T(8,128)(2,1)S(1)}, u32[]{:S(2)}, u32[]{:S(2)}) %collective-permute-start.17) | collective-permute-done | bytes 262176 | tf_op jit(solution)/shard_map/ppermute | solution.py:46
  157.1 6.8 %collective-permute-done.18.refs_3_ = bf16[2,128,512]{2,1,0:T(8,128)(2,1)S(1)} collective-permute-done((bf16[2,128,512]{2,1,0:T(8,128)(2,1)S(1)}, bf16[2,128,512]{2,1,0:T(8,128)(2,1)S(1)}, u32[]{:S(2)}, u32[]{:S(2)}) %collective-permute-start.18) | collective-permute-done | bytes 262176 | tf_op jit(solution)/shard_map/ppermute | solution.py:46
  164.0 1.9 collective-permute-start.19
  166.1 2.2 %collective-permute-start.23 = (bf16[2,2,128,512]{3,2,1,0:T(8,128)(2,1)S(1)}, bf16[2,2,128,512]{3,2,1,0:T(8,128)(2,1)S(1)}, u32[]{:S(2)}, u32[]{:S(2)}) collective-permute-start(bf16[2,2,128,512]{3,2,1,0:T(8,128)(2,1)S(1)} %add_convert_fusion.1), channel_id=1, source_target_pairs={{0,64},{32,480},{64,128},{96,32},{128,192},{160,96},{192,256},{224... | collective-permute-start | bytes 1572872 | tf_op jit(solution)/shard_map/ppermute | solution.py:36
  168.3 8.0 %collective-permute-done.19 = bf16[2,2,128,512]{3,2,1,0:T(8,128)(2,1)S(1)} collective-permute-done((bf16[2,2,128,512]{3,2,1,0:T(8,128)(2,1)S(1)}, bf16[2,2,128,512]{3,2,1,0:T(8,128)(2,1)S(1)}, u32[]{:S(2)}, u32[]{:S(2)}) %collective-permute-start.19) | collective-permute-done | bytes 524320 | tf_op jit(solution)/shard_map/ppermute | solution.py:36
  176.5 1.9 collective-permute-start.20
  178.4 3.5 %collective-permute-done.23 = bf16[2,2,128,512]{3,2,1,0:T(8,128)(2,1)S(1)} collective-permute-done((bf16[2,2,128,512]{3,2,1,0:T(8,128)(2,1)S(1)}, bf16[2,2,128,512]{3,2,1,0:T(8,128)(2,1)S(1)}, u32[]{:S(2)}, u32[]{:S(2)}) %collective-permute-start.23) | collective-permute-done | bytes 524320 | tf_op jit(solution)/shard_map/ppermute | solution.py:36
  182.1 1.9 collective-permute-start.24
  184.0 4.7 %collective-permute-done.20 = bf16[2,2,128,512]{3,2,1,0:T(8,128)(2,1)S(1)} collective-permute-done((bf16[2,2,128,512]{3,2,1,0:T(8,128)(2,1)S(1)}, bf16[2,2,128,512]{3,2,1,0:T(8,128)(2,1)S(1)}, u32[]{:S(2)}, u32[]{:S(2)}) %collective-permute-start.20) | collective-permute-done | bytes 524320 | tf_op jit(solution)/shard_map/ppermute | solution.py:36
  188.9 1.9 collective-permute-start.21
  190.8 3.5 %collective-permute-done.24 = bf16[2,2,128,512]{3,2,1,0:T(8,128)(2,1)S(1)} collective-permute-done((bf16[2,2,128,512]{3,2,1,0:T(8,128)(2,1)S(1)}, bf16[2,2,128,512]{3,2,1,0:T(8,128)(2,1)S(1)}, u32[]{:S(2)}, u32[]{:S(2)}) %collective-permute-start.24) | collective-permute-done | bytes 524320 | tf_op jit(solution)/shard_map/ppermute | solution.py:36
  194.4 1.9 collective-permute-start.25
  196.6 1.6 collective-permute-done.25.from_b
  198.2 3.0 %collective-permute-done.21.from_a = bf16[2,2,128,512]{3,2,1,0:T(8,128)(2,1)S(1)} collective-permute-done((bf16[2,2,128,512]{3,2,1,0:T(8,128)(2,1)S(1)}, bf16[2,2,128,512]{3,2,1,0:T(8,128)(2,1)S(1)}, u32[]{:S(2)}, u32[]{:S(2)}) %collective-permute-start.21) | collective-permute-done | bytes 524320 | tf_op jit(solution)/shard_map/ppermute | solution.py:36
  201.2 1.9 shard_map.97
  (82 shorter events, 4.4 us)
Async XLA Ops:
  0.6 13.4 %copy-start.21 = (bf16[256,512]{1,0:T(8,128)(2,1)S(1)}, bf16[256,512]{1,0:T(8,128)(2,1)}, u32[]{:S(2)}) copy-start(bf16[256,512]{1,0:T(8,128)(2,1)} %param.7) | copy-start | bytes 786436
  0.6 13.4 %copy-start.20 = (bf16[256,512]{1,0:T(8,128)(2,1)S(1)}, bf16[256,512]{1,0:T(8,128)(2,1)}, u32[]{:S(2)}) copy-start(bf16[256,512]{1,0:T(8,128)(2,1)} %param.8) | copy-start | bytes 786436
  0.7 79.8 %copy-start.22 = (s32[1,32,3]{1,0,2:T(1,128)S(1)}, s32[1,32,3]{1,0,2:T(1,128)}, u32[]{:S(2)}) copy-start(s32[1,32,3]{1,0,2:T(1,128)} %param.11) | copy-start | bytes 1156
  11.7 21.3 %collective-permute-start.1 = (bf16[2,128,512]{2,1,0:T(8,128)(2,1)S(1)}, bf16[2,128,512]{2,1,0:T(8,128)(2,1)S(1)}, u32[]{:S(2)}, u32[]{:S(2)}) collective-permute-start(bf16[2,128,512]{2,1,0:T(8,128)(2,1)S(1)} %get-tuple-element.62), channel_id=1, source_target_pairs={{2,0},{3,1},{4,2},{5,3},{6,4},{7,5},{8,6},{9,7},{10,8},{11,9},{12,... | collective-permute-start | bytes 786440 | tf_op jit(solution)/shard_map/ppermute | solution.py:46
  14.1 34.3 %collective-permute-start = (bf16[2,256,512]{2,1,0:T(8,128)(2,1)S(1)}, bf16[2,256,512]{2,1,0:T(8,128)(2,1)S(1)}, u32[]{:S(2)}, u32[]{:S(2)}) collective-permute-start(bf16[2,256,512]{2,1,0:T(8,128)(2,1)S(1)} %pad_maximum_fusion.refs_0_), channel_id=1, source_target_pairs={{0,64},{32,480},{64,128},{96,32},{128,192},{160,96},{192,256},{224... | collective-permute-start | bytes 1572872 | tf_op jit(solution)/shard_map/ppermute | solution.py:36
  18.4 31.9 %collective-permute-start.5 = (bf16[2,256,512]{2,1,0:T(8,128)(2,1)S(1)}, bf16[2,256,512]{2,1,0:T(8,128)(2,1)S(1)}, u32[]{:S(2)}, u32[]{:S(2)}) collective-permute-start(bf16[2,256,512]{2,1,0:T(8,128)(2,1)S(1)} %pad_maximum_fusion.refs_0_), channel_id=1, source_target_pairs={{0,32},{32,0},{64,96},{96,64},{128,160},{160,128},{192,224},{224,1... | collective-permute-start | bytes 1572872 | tf_op jit(solution)/shard_map/ppermute | solution.py:41
  26.2 0.8 copy-start.6
  27.0 13.6 %collective-permute-start.2 = (bf16[2,128,512]{2,1,0:T(8,128)(2,1)S(1)}, bf16[2,128,512]{2,1,0:T(8,128)(2,1)S(1)}, u32[]{:S(2)}, u32[]{:S(2)}) collective-permute-start(bf16[2,128,512]{2,1,0:T(8,128)(2,1)S(1)} %get-tuple-element.63), channel_id=1, source_target_pairs={{1,0},{2,1},{3,2},{4,3},{5,4},{6,5},{7,6},{8,7},{9,8},{10,9},{11,1... | collective-permute-start | bytes 786440 | tf_op jit(solution)/shard_map/ppermute | solution.py:46
  31.0 10.4 %collective-permute-start.3 = (bf16[2,128,512]{2,1,0:T(8,128)(2,1)S(1)}, bf16[2,128,512]{2,1,0:T(8,128)(2,1)S(1)}, u32[]{:S(2)}, u32[]{:S(2)}) collective-permute-start(bf16[2,128,512]{2,1,0:T(8,128)(2,1)S(1)} %get-tuple-element.64), channel_id=1, source_target_pairs={{0,1},{1,2},{2,3},{3,4},{4,5},{5,6},{6,7},{7,8},{8,9},{9,10},{10,1... | collective-permute-start | bytes 786440 | tf_op jit(solution)/shard_map/ppermute | solution.py:46
  33.0 0.7 copy-start.12
  33.7 14.0 %collective-permute-start.4 = (bf16[2,128,512]{2,1,0:T(8,128)(2,1)S(1)}, bf16[2,128,512]{2,1,0:T(8,128)(2,1)S(1)}, u32[]{:S(2)}, u32[]{:S(2)}) collective-permute-start(bf16[2,128,512]{2,1,0:T(8,128)(2,1)S(1)} %get-tuple-element.61), channel_id=1, source_target_pairs={{0,2},{1,3},{2,4},{3,5},{4,6},{5,7},{6,8},{7,9},{8,10},{9,11},{10,... | collective-permute-start | bytes 786440 | tf_op jit(solution)/shard_map/ppermute | solution.py:46
  40.6 0.7 copy-start.14
  41.3 0.7 copy-start.16
  47.6 0.7 copy-start.18
  48.3 12.3 %collective-permute-start.6 = (bf16[2,256,512]{2,1,0:T(8,128)(2,1)S(1)}, bf16[2,256,512]{2,1,0:T(8,128)(2,1)S(1)}, u32[]{:S(2)}, u32[]{:S(2)}) collective-permute-start(bf16[2,256,512]{2,1,0:T(8,128)(2,1)S(1)} %collective-permute-done.refs_1_.refs_6_), channel_id=1, source_target_pairs={{0,64},{32,480},{64,128},{96,32},{128,192},{160,96},{192,256},{224... | collective-permute-start | bytes 1572872 | tf_op jit(solution)/shard_map/ppermute | solution.py:36
  50.3 16.0 %collective-permute-start.9 = (bf16[2,256,512]{2,1,0:T(8,128)(2,1)S(1)}, bf16[2,256,512]{2,1,0:T(8,128)(2,1)S(1)}, u32[]{:S(2)}, u32[]{:S(2)}) collective-permute-start(bf16[2,256,512]{2,1,0:T(8,128)(2,1)S(1)} %collective-permute-done.5.refs_0_.refs_5_), channel_id=1, source_target_pairs={{0,64},{32,480},{64,128},{96,32},{128,192},{160,96},{192,256},{224... | collective-permute-start | bytes 1572872 | tf_op jit(solution)/shard_map/ppermute | solution.py:36
  60.6 12.3 %collective-permute-start.7 = (bf16[2,256,512]{2,1,0:T(8,128)(2,1)S(1)}, bf16[2,256,512]{2,1,0:T(8,128)(2,1)S(1)}, u32[]{:S(2)}, u32[]{:S(2)}) collective-permute-start(bf16[2,256,512]{2,1,0:T(8,128)(2,1)S(1)} %collective-permute-done.6.refs_2_.refs_7_), channel_id=1, source_target_pairs={{0,64},{32,480},{64,128},{96,32},{128,192},{160,96},{192,256},{224... | collective-permute-start | bytes 1572872 | tf_op jit(solution)/shard_map/ppermute | solution.py:36
  66.2 26.8 %copy-start = (bf16[2,256,512]{2,1,0:T(8,128)(2,1)}, bf16[2,256,512]{2,1,0:T(8,128)(2,1)S(1)}, u32[]{:S(2)}) copy-start(bf16[2,256,512]{2,1,0:T(8,128)(2,1)S(1)} %collective-permute-done.9.refs_5_.refs_10_) | copy-start | bytes 1572868
  66.2 12.3 %collective-permute-start.10 = (bf16[2,256,512]{2,1,0:T(8,128)(2,1)S(1)}, bf16[2,256,512]{2,1,0:T(8,128)(2,1)S(1)}, u32[]{:S(2)}, u32[]{:S(2)}) collective-permute-start(bf16[2,256,512]{2,1,0:T(8,128)(2,1)S(1)} %collective-permute-done.9.refs_5_.refs_10_), channel_id=1, source_target_pairs={{0,64},{32,480},{64,128},{96,32},{128,192},{160,96},{192,256},{224... | collective-permute-start | bytes 1572872 | tf_op jit(solution)/shard_map/ppermute | solution.py:36
  72.9 20.1 %copy-start.2 = (bf16[2,256,512]{2,1,0:T(8,128)(2,1)}, bf16[2,256,512]{2,1,0:T(8,128)(2,1)S(1)}, u32[]{:S(2)}) copy-start(bf16[2,256,512]{2,1,0:T(8,128)(2,1)S(1)} %collective-permute-done.7.refs_3_.refs_8_) | copy-start | bytes 1572868
  72.9 12.4 %collective-permute-start.8 = (bf16[2,256,512]{2,1,0:T(8,128)(2,1)S(1)}, bf16[2,256,512]{2,1,0:T(8,128)(2,1)}, u32[]{:S(2)}, u32[]{:S(2)}) collective-permute-start(bf16[2,256,512]{2,1,0:T(8,128)(2,1)S(1)} %collective-permute-done.7.refs_3_.refs_8_), channel_id=1, source_target_pairs={{0,64},{32,480},{64,128},{96,32},{128,192},{160,96},{192,256},{224... | collective-permute-start | bytes 1572872 | tf_op jit(solution)/shard_map/ppermute | solution.py:36
  78.5 14.5 %copy-start.4 = (bf16[2,256,512]{2,1,0:T(8,128)(2,1)}, bf16[2,256,512]{2,1,0:T(8,128)(2,1)S(1)}, u32[]{:S(2)}) copy-start(bf16[2,256,512]{2,1,0:T(8,128)(2,1)S(1)} %collective-permute-done.10.refs_6_.refs_11_) | copy-start | bytes 1572868
  78.5 12.4 %collective-permute-start.11 = (bf16[2,256,512]{2,1,0:T(8,128)(2,1)S(1)}, bf16[2,256,512]{2,1,0:T(8,128)(2,1)}, u32[]{:S(2)}, u32[]{:S(2)}) collective-permute-start(bf16[2,256,512]{2,1,0:T(8,128)(2,1)S(1)} %collective-permute-done.10.refs_6_.refs_11_), channel_id=1, source_target_pairs={{0,64},{32,480},{64,128},{96,32},{128,192},{160,96},{192,256},{224... | collective-permute-start | bytes 1572872 | tf_op jit(solution)/shard_map/ppermute | solution.py:36
  80.8 17.9 %copy-start.10 = (bf16[256,512]{1,0:T(8,128)(2,1)S(1)}, bf16[256,512]{1,0:T(8,128)(2,1)}, u32[]{:S(2)}) copy-start(bf16[256,512]{1,0:T(8,128)(2,1)} %param.6) | copy-start | bytes 786436
  93.1 5.6 %collective-permute-start.12 = (bf16[6,2,128,512]{3,2,1,0:T(8,128)(2,1)}, bf16[6,2,128,512]{3,2,1,0:T(8,128)(2,1)}, u32[]{:S(2)}, u32[]{:S(2)}) collective-permute-start(bf16[6,2,128,512]{3,2,1,0:T(8,128)(2,1)} %shard_map.93), channel_id=1, source_target_pairs={{0,32},{32,0},{64,96},{96,64},{128,160},{160,128},{192,224},{224,1... | collective-permute-start | bytes 4718600 | tf_op jit(solution)/shard_map/ppermute | solution.py:41
  98.7 1.0 copy-start.1
  99.7 1.0 copy-start.3
  100.8 1.0 copy-start.5
  101.8 1.0 copy-start.7
  102.9 0.9 copy-start.11
  103.8 0.9 copy-start.13
  104.8 0.9 copy-start.15
  105.7 0.9 copy-start.17
  106.7 0.9 copy-start.19
  124.4 1.2 copy-start.8
  125.6 5.3 %collective-permute-start.13 = (bf16[6,2,128,512]{3,2,1,0:T(8,128)(2,1)S(1)}, bf16[6,2,128,512]{3,2,1,0:T(8,128)(2,1)S(1)}, u32[]{:S(2)}, u32[]{:S(2)}) collective-permute-start(bf16[6,2,128,512]{3,2,1,0:T(8,128)(2,1)S(1)} %get-tuple-element.35.mine), channel_id=1, source_target_pairs={{0,32},{32,0},{64,96},{96,64},{128,160},{160,128},{192,224},{224,1... | collective-permute-start | bytes 4718600 | tf_op jit(solution)/shard_map/ppermute | solution.py:41
  130.8 2.6 %copy-start.9 = (bf16[6,2,128,512]{3,2,1,0:T(8,128)(2,1)S(1)}, bf16[6,2,128,512]{3,2,1,0:T(8,128)(2,1)}, u32[]{:S(2)}) copy-start(bf16[6,2,128,512]{3,2,1,0:T(8,128)(2,1)} %copy-done.8) | copy-start | bytes 4718596
  131.6 32.3 %collective-permute-start.14 = (bf16[2,2,128,512]{3,2,1,0:T(8,128)(2,1)S(1)}, bf16[2,2,128,512]{3,2,1,0:T(8,128)(2,1)S(1)}, u32[]{:S(2)}, u32[]{:S(2)}) collective-permute-start(bf16[2,2,128,512]{3,2,1,0:T(8,128)(2,1)S(1)} %get-tuple-element.36), channel_id=1, source_target_pairs={{0,64},{32,480},{64,128},{96,32},{128,192},{160,96},{192,256},{224... | collective-permute-start | bytes 1572872 | tf_op jit(solution)/shard_map/ppermute | solution.py:36
  133.6 16.2 %collective-permute-start.15 = (bf16[2,128,512]{2,1,0:T(8,128)(2,1)S(1)}, bf16[2,128,512]{2,1,0:T(8,128)(2,1)S(1)}, u32[]{:S(2)}, u32[]{:S(2)}) collective-permute-start(bf16[2,128,512]{2,1,0:T(8,128)(2,1)S(1)} %get-tuple-element.60), channel_id=1, source_target_pairs={{0,2},{1,3},{2,4},{3,5},{4,6},{5,7},{6,8},{7,9},{8,10},{9,11},{10,... | collective-permute-start | bytes 786440 | tf_op jit(solution)/shard_map/ppermute | solution.py:46
  141.7 11.1 %collective-permute-start.16 = (bf16[2,128,512]{2,1,0:T(8,128)(2,1)S(1)}, bf16[2,128,512]{2,1,0:T(8,128)(2,1)S(1)}, u32[]{:S(2)}, u32[]{:S(2)}) collective-permute-start(bf16[2,128,512]{2,1,0:T(8,128)(2,1)S(1)} %get-tuple-element.59), channel_id=1, source_target_pairs={{0,1},{1,2},{2,3},{3,4},{4,5},{5,6},{6,7},{7,8},{8,9},{9,10},{10,1... | collective-permute-start | bytes 786440 | tf_op jit(solution)/shard_map/ppermute | solution.py:46
  146.0 11.1 %collective-permute-start.17 = (bf16[2,128,512]{2,1,0:T(8,128)(2,1)S(1)}, bf16[2,128,512]{2,1,0:T(8,128)(2,1)S(1)}, u32[]{:S(2)}, u32[]{:S(2)}) collective-permute-start(bf16[2,128,512]{2,1,0:T(8,128)(2,1)S(1)} %get-tuple-element.58), channel_id=1, source_target_pairs={{1,0},{2,1},{3,2},{4,3},{5,4},{6,5},{7,6},{8,7},{9,8},{10,9},{11,1... | collective-permute-start | bytes 786440 | tf_op jit(solution)/shard_map/ppermute | solution.py:46
  147.9 16.0 %collective-permute-start.18 = (bf16[2,128,512]{2,1,0:T(8,128)(2,1)S(1)}, bf16[2,128,512]{2,1,0:T(8,128)(2,1)S(1)}, u32[]{:S(2)}, u32[]{:S(2)}) collective-permute-start(bf16[2,128,512]{2,1,0:T(8,128)(2,1)S(1)} %get-tuple-element.57), channel_id=1, source_target_pairs={{2,0},{3,1},{4,2},{5,3},{6,4},{7,5},{8,6},{9,7},{10,8},{11,9},{12,... | collective-permute-start | bytes 786440 | tf_op jit(solution)/shard_map/ppermute | solution.py:46
  149.8 16.1 %collective-permute-start.22 = (bf16[2,2,128,512]{3,2,1,0:T(8,128)(2,1)S(1)}, bf16[2,2,128,512]{3,2,1,0:T(8,128)(2,1)S(1)}, u32[]{:S(2)}, u32[]{:S(2)}) collective-permute-start(bf16[2,2,128,512]{3,2,1,0:T(8,128)(2,1)S(1)} %get-tuple-element.41), channel_id=1, source_target_pairs={{0,64},{32,480},{64,128},{96,32},{128,192},{160,96},{192,256},{224... | collective-permute-start | bytes 1572872 | tf_op jit(solution)/shard_map/ppermute | solution.py:36
  164.0 12.3 %collective-permute-start.19 = (bf16[2,2,128,512]{3,2,1,0:T(8,128)(2,1)S(1)}, bf16[2,2,128,512]{3,2,1,0:T(8,128)(2,1)S(1)}, u32[]{:S(2)}, u32[]{:S(2)}) collective-permute-start(bf16[2,2,128,512]{3,2,1,0:T(8,128)(2,1)S(1)} %add_convert_fusion.4), channel_id=1, source_target_pairs={{0,64},{32,480},{64,128},{96,32},{128,192},{160,96},{192,256},{224... | collective-permute-start | bytes 1572872 | tf_op jit(solution)/shard_map/ppermute | solution.py:36
  166.1 15.8 %collective-permute-start.23 = (bf16[2,2,128,512]{3,2,1,0:T(8,128)(2,1)S(1)}, bf16[2,2,128,512]{3,2,1,0:T(8,128)(2,1)S(1)}, u32[]{:S(2)}, u32[]{:S(2)}) collective-permute-start(bf16[2,2,128,512]{3,2,1,0:T(8,128)(2,1)S(1)} %add_convert_fusion.1), channel_id=1, source_target_pairs={{0,64},{32,480},{64,128},{96,32},{128,192},{160,96},{192,256},{224... | collective-permute-start | bytes 1572872 | tf_op jit(solution)/shard_map/ppermute | solution.py:36
  176.5 12.3 %collective-permute-start.20 = (bf16[2,2,128,512]{3,2,1,0:T(8,128)(2,1)S(1)}, bf16[2,2,128,512]{3,2,1,0:T(8,128)(2,1)S(1)}, u32[]{:S(2)}, u32[]{:S(2)}) collective-permute-start(bf16[2,2,128,512]{3,2,1,0:T(8,128)(2,1)S(1)} %add_convert_fusion.3), channel_id=1, source_target_pairs={{0,64},{32,480},{64,128},{96,32},{128,192},{160,96},{192,256},{224... | collective-permute-start | bytes 1572872 | tf_op jit(solution)/shard_map/ppermute | solution.py:36
  182.1 12.3 %collective-permute-start.24 = (bf16[2,2,128,512]{3,2,1,0:T(8,128)(2,1)S(1)}, bf16[2,2,128,512]{3,2,1,0:T(8,128)(2,1)S(1)}, u32[]{:S(2)}, u32[]{:S(2)}) collective-permute-start(bf16[2,2,128,512]{3,2,1,0:T(8,128)(2,1)S(1)} %add_convert_fusion), channel_id=1, source_target_pairs={{0,64},{32,480},{64,128},{96,32},{128,192},{160,96},{192,256},{224... | collective-permute-start | bytes 1572872 | tf_op jit(solution)/shard_map/ppermute | solution.py:36
  188.9 12.3 %collective-permute-start.21 = (bf16[2,2,128,512]{3,2,1,0:T(8,128)(2,1)S(1)}, bf16[2,2,128,512]{3,2,1,0:T(8,128)(2,1)S(1)}, u32[]{:S(2)}, u32[]{:S(2)}) collective-permute-start(bf16[2,2,128,512]{3,2,1,0:T(8,128)(2,1)S(1)} %add_convert_fusion.2), channel_id=1, source_target_pairs={{0,64},{32,480},{64,128},{96,32},{128,192},{160,96},{192,256},{224... | collective-permute-start | bytes 1572872 | tf_op jit(solution)/shard_map/ppermute | solution.py:36
  194.4 3.8 %collective-permute-start.25 = (bf16[2,2,128,512]{3,2,1,0:T(8,128)(2,1)S(1)}, bf16[2,2,128,512]{3,2,1,0:T(8,128)(2,1)S(1)}, u32[]{:S(2)}, u32[]{:S(2)}) collective-permute-start(bf16[2,2,128,512]{3,2,1,0:T(8,128)(2,1)S(1)} %collective-permute-done.24), channel_id=1, source_target_pairs={{0,32},{32,0},{64,96},{96,64},{128,160},{160,128},{192,224},{224,1... | collective-permute-start | bytes 1572872 | tf_op jit(solution)/shard_map/ppermute | solution.py:41

commit v3 on v2

--- a/solution.py
+++ b/solution.py
@@ -24,7 +24,7 @@
 F32 = jnp.float32
 OFFSETS = (-2, -1, 1, 2)
 
-ANY = pl.BlockSpec(memory_space=pl.ANY)
+HBM = pl.BlockSpec(memory_space=pltpu.HBM)
 VMEM = pl.BlockSpec(memory_space=pltpu.VMEM)
 SMEM = pl.BlockSpec(memory_space=pltpu.SMEM)
 
@@ -91,12 +91,37 @@
     return pl.pallas_call(
         pick_kernel,
         out_shape=jax.ShapeDtypeStruct((FAR, 2, BS, D), BF),
-        in_specs=[SMEM] + [ANY] * 8,
+        in_specs=[SMEM] + [HBM] * 8,
         out_specs=VMEM,
         scratch_shapes=[pltpu.SemaphoreType.DMA((FAR,))],
         compiler_params=pltpu.CompilerParams(vmem_limit_bytes=4 * 2**20),
         cost_estimate=pl.CostEstimate(flops=0, bytes_accessed=6 * 2**20, transcendentals=0),
     )(table, *places)
+
+
+def offer_kernel(table, keys, values, *refs):
+    outs, sem = refs[: 2 * W], refs[2 * W]
+    copies = []
+    for t, out in enumerate(outs):
+        rows = pl.ds(pl.multiple_of(table[t] * BS, BS), BS)
+        for half, source in enumerate((keys, values)):
+            copies.append(pltpu.make_async_copy(source.at[rows, :], out.at[half], sem.at[t, half]))
+    for copy in copies:
+        copy.start()
+    for copy in copies:
+        copy.wait()
+
+
+def offer(table, keys, values):
+    return pl.pallas_call(
+        offer_kernel,
+        out_shape=(jax.ShapeDtypeStruct((2, BS, D), BF),) * (2 * W),
+        in_specs=[SMEM, HBM, HBM],
+        out_specs=(VMEM,) * (2 * W),
+        scratch_shapes=[pltpu.SemaphoreType.DMA((2 * W, 2))],
+        compiler_params=pltpu.CompilerParams(vmem_limit_bytes=4 * 2**20),
+        cost_estimate=pl.CostEstimate(flops=0, bytes_accessed=2 * 2**20, transcendentals=0),
+    )(table, keys, values)
 
 
 def attend_pair(step, table, q_ref, g_ref, listed, att_ref, gq_ref, totals):
@@ -136,23 +161,17 @@
     grad_value = jnp.dot(weights_low, grad2, preferred_element_type=F32)
     for j in range(KB):
         slot = table[2, s * KB + j]
-        leads = table[3, s * KB + j]
+        again = table[3, s * KB + j] == 0
         rows = slice(j * BS, (j + 1) * BS)
-
-        @pl.when(leads == 1)
-        def _():
-            totals[slot, 0, :, cols] = grad_key[rows]
-            totals[slot, 1, :, cols] = grad_value[rows]
-
-        @pl.when(leads == 0)
-        def _():
-            totals[slot, 0, :, cols] += grad_key[rows]
-            totals[slot, 1, :, cols] += grad_value[rows]
+        for half, term in enumerate((grad_key, grad_value)):
+            before = totals[slot, half, :, cols]
+            totals[slot, half, :, cols] = jnp.where(again, before, 0.0) + term[rows]
 
 
 def attend_kernel(table, q_ref, g_ref, *refs):
     own, near, places, picked = refs[0], refs[1:5], refs[5:13], refs[13]
-    att_ref, gq_ref, near_out, far_out, listed, totals, sem = refs[14:]
+    att_ref, gq_ref, own_out, far_out = refs[14:18]
+    near_out, (listed, totals, sem) = refs[18:22], refs[22:]
 
     def bring(source, s, j):
         pltpu.make_async_copy(source, listed.at[s, :, pl.ds(j * BS, BS), :], sem.at[s]).start()
@@ -192,8 +211,10 @@
         attend_pair(step, table, q_ref, g_ref, listed, att_ref, gq_ref, totals)
         return carry
 
-    lax.fori_loop(0, NB * PAIRS, body, 0)
-    near_out[...] = totals[:NEAR].astype(BF)
+    lax.fori_loop(0, NB * PAIRS, body, 0, unroll=4)
+    own_out[...] = totals[:NB].astype(BF)
+    for t in range(2 * W):
+        near_out[t][...] = totals[NB + t].astype(BF)
     far_out[...] = totals[NEAR:].astype(BF)
 
 
@@ -203,11 +224,12 @@
         out_shape=(
             jax.ShapeDtypeStruct((NB, BS, D), BF),
             jax.ShapeDtypeStruct((NB, BS, D), BF),
-            jax.ShapeDtypeStruct((NEAR, 2, BS, D), BF),
+            jax.ShapeDtypeStruct((NB, 2, BS, D), BF),
             jax.ShapeDtypeStruct((FAR, 2, BS, D), BF),
-        ),
-        in_specs=[SMEM, VMEM, VMEM] + [ANY] * 14,
-        out_specs=(VMEM, VMEM, VMEM, VMEM),
+        )
+        + (jax.ShapeDtypeStruct((2, BS, D), BF),) * (2 * W),
+        in_specs=[SMEM, VMEM, VMEM] + [HBM] * 14,
+        out_specs=(VMEM,) * (4 + 2 * W),
         scratch_shapes=[
             pltpu.VMEM((NB, 2, ROWS, D), BF),
             pltpu.VMEM((NEAR + FAR, 2, BS, D), F32),
@@ -292,22 +314,11 @@
     own = jnp.stack([keys, values])
     flow_a = [ring_step(own)]
     sibling = swap_cores(own)
-    flow_b = [ring_step(sibling)]
 
     padded = jnp.pad(local_list, ((W * NB, W * NB), (0, 0)), constant_values=-1)
     around = lax.dynamic_slice_in_dim(padded, dom * NB, (2 * W + 1) * NB, 0).reshape(2 * W + 1, NB * LOC)
     given = jnp.max(jnp.where(around // NB == dom, around % NB, 0), axis=1).astype(i32)
-    blocks = own.reshape(2, NB, BS, D)
-    near = []
-    for offset in OFFSETS:
-        piece = lax.dynamic_index_in_dim(blocks, given[W + offset], 1, keepdims=False)
-        near.append(shifted(piece, offset))
-    flow_a[0], near = lax.optimization_barrier((flow_a[0], near))
-    for _ in range(2):
-        flow_a.append(ring_step(flow_a[-1]))
-        flow_b.append(ring_step(flow_b[-1]))
-    flow_a.append(ring_step(flow_a[-1]))
-
+    given = jnp.concatenate([given[:W], given[W + 1 :]])
     local = around[W].reshape(NB, LOC)
     holder = local // NB - dom
     near_code = jnp.where(holder == 0, 0, jnp.where(holder > 0, 3 - holder, 2 - holder))
@@ -319,7 +330,7 @@
     far_code = place_of(mine // NB, chip, core, chips)
     needed = place_of(theirs // NB, chip, 1 - core, chips) == PICKED
     sent = jnp.where(needed, place_of(theirs // NB, chip, core, chips), PICKED)
-    picked = swap_cores(pick(jnp.stack([sent, theirs % NB]).astype(i32), [sibling] + flow_a + flow_b))
+    pick_table = jnp.stack([sent, theirs % NB]).astype(i32)
 
     self_code = jnp.zeros((NB, 1), i32)
     self_key = jnp.arange(NB, dtype=i32)[:, None]
@@ -329,17 +340,6 @@
     targets = jnp.concatenate([self_key, near_key, far_key], axis=1).reshape(-1)
     leads = first_of(targets) == jnp.arange(ENTRIES, dtype=i32)
     table = jnp.stack([codes, slots, targets, leads.astype(i32)]).astype(i32)
-    attended, grad_queries, near_terms, far_terms = attend(
-        table,
-        queries.reshape(NB, BS, D),
-        cotangent.reshape(NB, BS, D),
-        own,
-        near,
-        [sibling] + flow_a + flow_b,
-        picked,
-    )
-
-    sibling_terms = swap_cores(far_terms)
     steps = [(4, 0), (3, 1), (3, 0), (2, 1), (2, 0), (1, 1), (1, 0)]
     direction = 1 - 2 * core
     wanted = []
@@ -349,26 +349,57 @@
     wanted += [group * NB, group * NB + 1]
     wanted = jnp.stack(wanted).astype(i32)
     hits = jnp.stack([slot_in(mine, wanted), slot_in(theirs, wanted)])
-    start_a, start_b = spread(hits[:, : 2 * NB], far_terms, sibling_terms)
-    a3, b2, a2, b1, a1 = spread(hits[:, 2 * NB : 7 * NB], far_terms, sibling_terms)
+    last = jnp.concatenate([given, hits[1, 7 * NB :]]).astype(i32)
+    tables = (given, pick_table, table, hits[:, : 2 * NB], hits[:, 2 * NB : 7 * NB], last)
+    flow_a[0], sibling, tables = lax.optimization_barrier((flow_a[0], sibling, tables))
+    given, pick_table, table, hits_first, hits_rest, last = tables
+
+    offered = offer(given, keys, values)
+    flow_b = [ring_step(sibling)]
+    near = [None, None, shifted(offered[2], OFFSETS[2]), shifted(offered[3], OFFSETS[3])]
+    flow_a[0], near[2], near[3] = lax.optimization_barrier((flow_a[0], near[2], near[3]))
+    flow_a.append(ring_step(flow_a[0]))
+    behind = lax.optimization_barrier((offered[0], offered[1], near[2], near[3]))
+    near = [shifted(behind[0], OFFSETS[0]), shifted(behind[1], OFFSETS[1]), behind[2], behind[3]]
+    flow_b.append(ring_step(flow_b[0]))
+    flow_a[1], near = lax.optimization_barrier((flow_a[1], near))
+    flow_a.append(ring_step(flow_a[1]))
+    flow_b.append(ring_step(flow_b[1]))
+    flow_a.append(ring_step(flow_a[2]))
+
+    picked = swap_cores(pick(pick_table, [sibling] + flow_a + flow_b))
+    attended, grad_queries, own_terms, far_terms, *near_terms = attend(
+        table,
+        queries.reshape(NB, BS, D),
+        cotangent.reshape(NB, BS, D),
+        own,
+        near,
+        [sibling] + flow_a + flow_b,
+        picked,
+    )
+
+    sibling_terms = swap_cores(far_terms)
+    start_a, start_b = spread(hits_first, far_terms, sibling_terms)
+    a3, b2, a2, b1, a1 = spread(hits_rest, far_terms, sibling_terms)
 
     def joined(x, y):
         return (x.astype(F32) + y.astype(F32)).astype(BF)
 
-    returned = [shifted(near_terms[NB + t], -offset) for t, offset in enumerate(OFFSETS)]
     back_a = ring_step(start_a)
     back_b = ring_step(start_b)
-    back_a, returned = lax.optimization_barrier((back_a, returned))
+    returned = [shifted(near_terms[t], -OFFSETS[t]) for t in (0, 1)]
+    back_a, *returned = lax.optimization_barrier((back_a, *returned))
     back_a = ring_step(joined(back_a, a3))
     back_b = ring_step(joined(back_b, b2))
+    back_a, *behind = lax.optimization_barrier((back_a, near_terms[2], near_terms[3], *returned))
+    returned = behind[2:] + [shifted(behind[t - 2], -OFFSETS[t]) for t in (2, 3)]
     back_a = ring_step(joined(back_a, a2))
     back_b = ring_step(joined(back_b, b1))
+    back_a, *returned = lax.optimization_barrier((back_a, *returned))
     back_a = ring_step(joined(back_a, a1))
     back_b = swap_cores(back_b)
 
-    back_slots = jnp.stack([given[W + offset] for offset in OFFSETS])
-    last = jnp.concatenate([back_slots, hits[1, 7 * NB :]]).astype(i32)
-    grad_keys, grad_values = close(last, near_terms[:NB], sibling_terms, back_a, back_b, returned)
+    grad_keys, grad_values = close(last, own_terms, sibling_terms, back_a, back_b, returned)
     return (attended.reshape(NB * BS, D), grad_queries.reshape(NB * BS, D), grad_keys, grad_values)
 
 

time: 204 us -> 179 us (0.88)
  the two profiles are of different devices: /device:TPU:28 before, /device:TPU:30 now
where the time goes in v3:
time: 179 us; the launch traced here: 178 us
  waiting for transfers between devices  82 us (46%)
  starting transfers between devices  69.2 us (39%)
  Pallas kernels  20.4 us (11%)
  other arithmetic  2.99 us (2%)
  local copies, waits for them, and re-layouts  2.52 us (1%)
    ppermute x14, waiting for transfers between devices, ring_step(): lax.ppermute(array, 'group', [(g, (g + (2 if g % 2 == 0 else -2)) % size)...  45.4 us
    ppermute x8, starting transfers between devices, shifted(): lax.ppermute(array, 'dom', [(i, i + by) for i in range(size) if 0 <= i +...  31.4 us
    ppermute x14, starting transfers between devices, ring_step(): lax.ppermute(array, 'group', [(g, (g + (2 if g % 2 == 0 else -2)) % size)...  30 us
    ppermute x8, waiting for transfers between devices, shifted(): lax.ppermute(array, 'dom', [(i, i + by) for i in range(size) if 0 <= i +...  29.9 us
    pallas_call x1, Pallas kernels, attend(): pl.pallas_call(attend_kernel, out_shape=(jax.ShapeDtypeStruct((NB, BS, D)...  13.5 us
    ppermute x4, starting transfers between devices, swap_cores(): return lax.ppermute(array, 'group', [(g, g ^ 1) for g in range(size)])  7.81 us
    ppermute x4, waiting for transfers between devices, swap_cores(): return lax.ppermute(array, 'group', [(g, g ^ 1) for g in range(size)])  6.63 us
  transfers between devices with their start and end apart: 26, of which 17 were waited for; matrix products, arithmetic and copies ran while one was open for 2% of the time, Pallas kernels for 1%

profile of v3, /device:TPU:30, one launch (start us, length us, event | category | flops | bytes accessed | tf_op | source)
XLA Modules:
  0.0 178.3 jit_solution(2352583322301106416)
XLA Ops:
  0.7 1.1 pad_maximum_fusion.refs_0_
  1.8 1.9 %collective-permute-start.1 = (bf16[2,256,512]{2,1,0:T(8,128)(2,1)S(1)}, bf16[2,256,512]{2,1,0:T(8,128)(2,1)S(1)}, u32[]{:S(2)}, u32[]{:S(2)}) collective-permute-start(bf16[2,256,512]{2,1,0:T(8,128)(2,1)S(1)} %pad_maximum_fusion.refs_0_), channel_id=1, source_target_pairs={{0,32},{32,0},{64,96},{96,64},{128,160},{160,128},{192,224},{224,1... | collective-permute-start | bytes 1572872 | tf_op jit(solution)/shard_map/ppermute | solution.py:41
  3.7 4.3 %collective-permute-start = (bf16[2,256,512]{2,1,0:T(8,128)(2,1)S(1)}, bf16[2,256,512]{2,1,0:T(8,128)(2,1)S(1)}, u32[]{:S(2)}, u32[]{:S(2)}) collective-permute-start(bf16[2,256,512]{2,1,0:T(8,128)(2,1)S(1)} %pad_maximum_fusion.refs_0_), channel_id=1, source_target_pairs={{0,64},{32,480},{64,128},{96,32},{128,192},{160,96},{192,256},{224... | collective-permute-start | bytes 1572872 | tf_op jit(solution)/shard_map/ppermute | solution.py:36
  8.1 0.8 copy.15
  9.0 0.2 select_reduce_fusion.3
  9.2 0.1 add.212
  9.4 0.8 copy.14
  10.1 0.1 fusion.2
  10.6 0.1 stack.95
  10.7 0.1 select_reduce_fusion.2
  11.3 0.1 reduce_max.18
  11.6 0.2 select_reduce_fusion
  11.8 10.0 %collective-permute-done.refs_1_.refs_6_ = bf16[2,256,512]{2,1,0:T(8,128)(2,1)S(1)} collective-permute-done((bf16[2,256,512]{2,1,0:T(8,128)(2,1)S(1)}, bf16[2,256,512]{2,1,0:T(8,128)(2,1)S(1)}, u32[]{:S(2)}, u32[]{:S(2)}) %collective-permute-start) | collective-permute-done | bytes 524320 | tf_op jit(solution)/shard_map/ppermute | solution.py:36
  21.8 2.0 %shard_map.93 = (bf16[2,128,512]{2,1,0:T(8,128)(2,1)S(1)}, bf16[2,128,512]{2,1,0:T(8,128)(2,1)S(1)}, bf16[2,128,512]{2,1,0:T(8,128)(2,1)S(1)}, bf16[2,128,512]{2,1,0:T(8,128)(2,1)S(1)}) custom-call(s32[4]{0:T(128)S(1)} %pad_add_fusion.6.table, bf16[256,512]{1,0:T(8,128)(2,1)S(1)} %copy-done.1, bf16[256,512]{1,0:T(8,128)(2,1)S(1)} %copy-done), custom_call_target="tpu_custom_call" | custom-call | bytes 2097152 | tf_op jit(solution)/shard_map/pallas_call | solution.py:116
  23.8 4.6 %collective-permute-start.2 = (bf16[2,128,512]{2,1,0:T(8,128)(2,1)S(1)}, bf16[2,128,512]{2,1,0:T(8,128)(2,1)S(1)}, u32[]{:S(2)}, u32[]{:S(2)}) collective-permute-start(bf16[2,128,512]{2,1,0:T(8,128)(2,1)S(1)} %get-tuple-element.61), channel_id=1, source_target_pairs={{0,1},{1,2},{2,3},{3,4},{4,5},{5,6},{6,7},{7,8},{8,9},{9,10},{10,1... | collective-permute-start | bytes 786440 | tf_op jit(solution)/shard_map/ppermute | solution.py:46
  28.4 4.3 %collective-permute-start.3 = (bf16[2,128,512]{2,1,0:T(8,128)(2,1)S(1)}, bf16[2,128,512]{2,1,0:T(8,128)(2,1)S(1)}, u32[]{:S(2)}, u32[]{:S(2)}) collective-permute-start(bf16[2,128,512]{2,1,0:T(8,128)(2,1)S(1)} %get-tuple-element.62), channel_id=1, source_target_pairs={{0,2},{1,3},{2,4},{3,5},{4,6},{5,7},{6,8},{7,9},{8,10},{9,11},{10,... | collective-permute-start | bytes 786440 | tf_op jit(solution)/shard_map/ppermute | solution.py:46
  32.8 1.9 %collective-permute-start.9 = (bf16[2,256,512]{2,1,0:T(8,128)(2,1)S(1)}, bf16[2,256,512]{2,1,0:T(8,128)(2,1)S(1)}, u32[]{:S(2)}, u32[]{:S(2)}) collective-permute-start(bf16[2,256,512]{2,1,0:T(8,128)(2,1)S(1)} %collective-permute-done.1.refs_0_.refs_5_), channel_id=1, source_target_pairs={{0,64},{32,480},{64,128},{96,32},{128,192},{160,96},{192,256},{224... | collective-permute-start | bytes 1572872 | tf_op jit(solution)/shard_map/ppermute | solution.py:36
  34.7 4.0 %collective-permute-done.2.refs_3_ = bf16[2,128,512]{2,1,0:T(8,128)(2,1)S(1)} collective-permute-done((bf16[2,128,512]{2,1,0:T(8,128)(2,1)S(1)}, bf16[2,128,512]{2,1,0:T(8,128)(2,1)S(1)}, u32[]{:S(2)}, u32[]{:S(2)}) %collective-permute-start.2) | collective-permute-done | bytes 262176 | tf_op jit(solution)/shard_map/ppermute | solution.py:46
  38.7 0.2 collective-permute-done.3.refs_4_
  38.9 1.9 %collective-permute-start.4 = (bf16[2,256,512]{2,1,0:T(8,128)(2,1)S(1)}, bf16[2,256,512]{2,1,0:T(8,128)(2,1)S(1)}, u32[]{:S(2)}, u32[]{:S(2)}) collective-permute-start(bf16[2,256,512]{2,1,0:T(8,128)(2,1)S(1)} %collective-permute-done.refs_1_.refs_6_), channel_id=1, source_target_pairs={{0,64},{32,480},{64,128},{96,32},{128,192},{160,96},{192,256},{224... | collective-permute-start | bytes 1572872 | tf_op jit(solution)/shard_map/ppermute | solution.py:36
  40.9 4.7 %collective-permute-start.5 = (bf16[2,128,512]{2,1,0:T(8,128)(2,1)S(1)}, bf16[2,128,512]{2,1,0:T(8,128)(2,1)S(1)}, u32[]{:S(2)}, u32[]{:S(2)}) collective-permute-start(bf16[2,128,512]{2,1,0:T(8,128)(2,1)S(1)} %get-tuple-element.68), channel_id=1, source_target_pairs={{2,0},{3,1},{4,2},{5,3},{6,4},{7,5},{8,6},{9,7},{10,8},{11,9},{12,... | collective-permute-start | bytes 786440 | tf_op jit(solution)/shard_map/ppermute | solution.py:46
  45.6 2.5 %collective-permute-start.6 = (bf16[2,128,512]{2,1,0:T(8,128)(2,1)S(1)}, bf16[2,128,512]{2,1,0:T(8,128)(2,1)S(1)}, u32[]{:S(2)}, u32[]{:S(2)}) collective-permute-start(bf16[2,128,512]{2,1,0:T(8,128)(2,1)S(1)} %get-tuple-element.69), channel_id=1, source_target_pairs={{1,0},{2,1},{3,2},{4,3},{5,4},{6,5},{7,6},{8,7},{9,8},{10,9},{11,1... | collective-permute-start | bytes 786440 | tf_op jit(solution)/shard_map/ppermute | solution.py:46
  48.1 1.9 %collective-permute-start.10 = (bf16[2,256,512]{2,1,0:T(8,128)(2,1)S(1)}, bf16[2,256,512]{2,1,0:T(8,128)(2,1)S(1)}, u32[]{:S(2)}, u32[]{:S(2)}) collective-permute-start(bf16[2,256,512]{2,1,0:T(8,128)(2,1)S(1)} %collective-permute-done.9.refs_5_.refs_10_), channel_id=1, source_target_pairs={{0,64},{32,480},{64,128},{96,32},{128,192},{160,96},{192,256},{224... | collective-permute-start | bytes 1572872 | tf_op jit(solution)/shard_map/ppermute | solution.py:36
  50.0 4.0 %collective-permute-done.5.refs_1_ = bf16[2,128,512]{2,1,0:T(8,128)(2,1)S(1)} collective-permute-done((bf16[2,128,512]{2,1,0:T(8,128)(2,1)S(1)}, bf16[2,128,512]{2,1,0:T(8,128)(2,1)S(1)}, u32[]{:S(2)}, u32[]{:S(2)}) %collective-permute-start.5) | collective-permute-done | bytes 262176 | tf_op jit(solution)/shard_map/ppermute | solution.py:46
  54.0 6.4 %collective-permute-done.6.refs_2_ = bf16[2,128,512]{2,1,0:T(8,128)(2,1)S(1)} collective-permute-done((bf16[2,128,512]{2,1,0:T(8,128)(2,1)S(1)}, bf16[2,128,512]{2,1,0:T(8,128)(2,1)S(1)}, u32[]{:S(2)}, u32[]{:S(2)}) %collective-permute-start.6) | collective-permute-done | bytes 262176 | tf_op jit(solution)/shard_map/ppermute | solution.py:46
  60.4 1.9 %collective-permute-start.7 = (bf16[2,256,512]{2,1,0:T(8,128)(2,1)S(1)}, bf16[2,256,512]{2,1,0:T(8,128)(2,1)S(1)}, u32[]{:S(2)}, u32[]{:S(2)}) collective-permute-start(bf16[2,256,512]{2,1,0:T(8,128)(2,1)S(1)} %collective-permute-done.4.refs_2_.refs_7_), channel_id=1, source_target_pairs={{0,64},{32,480},{64,128},{96,32},{128,192},{160,96},{192,256},{224... | collective-permute-start | bytes 1572872 | tf_op jit(solution)/shard_map/ppermute | solution.py:36
  62.4 1.9 %collective-permute-start.11 = (bf16[2,256,512]{2,1,0:T(8,128)(2,1)S(1)}, bf16[2,256,512]{2,1,0:T(8,128)(2,1)S(1)}, u32[]{:S(2)}, u32[]{:S(2)}) collective-permute-start(bf16[2,256,512]{2,1,0:T(8,128)(2,1)S(1)} %collective-permute-done.10.refs_6_.refs_11_), channel_id=1, source_target_pairs={{0,64},{32,480},{64,128},{96,32},{128,192},{160,96},{192,256},{224... | collective-permute-start | bytes 1572872 | tf_op jit(solution)/shard_map/ppermute | solution.py:36
  64.3 9.1 %collective-permute-done.7.refs_3_.refs_8_ = bf16[2,256,512]{2,1,0:T(8,128)(2,1)S(1)} collective-permute-done((bf16[2,256,512]{2,1,0:T(8,128)(2,1)S(1)}, bf16[2,256,512]{2,1,0:T(8,128)(2,1)S(1)}, u32[]{:S(2)}, u32[]{:S(2)}) %collective-permute-start.7) | collective-permute-done | bytes 524320 | tf_op jit(solution)/shard_map/ppermute | solution.py:36
  73.4 1.9 %collective-permute-start.8 = (bf16[2,256,512]{2,1,0:T(8,128)(2,1)S(1)}, bf16[2,256,512]{2,1,0:T(8,128)(2,1)S(1)}, u32[]{:S(2)}, u32[]{:S(2)}) collective-permute-start(bf16[2,256,512]{2,1,0:T(8,128)(2,1)S(1)} %collective-permute-done.7.refs_3_.refs_8_), channel_id=1, source_target_pairs={{0,64},{32,480},{64,128},{96,32},{128,192},{160,96},{192,256},{224... | collective-permute-start | bytes 1572872 | tf_op jit(solution)/shard_map/ppermute | solution.py:36
  75.3 3.7 %collective-permute-done.11.refs_7_.refs_12_ = bf16[2,256,512]{2,1,0:T(8,128)(2,1)S(1)} collective-permute-done((bf16[2,256,512]{2,1,0:T(8,128)(2,1)S(1)}, bf16[2,256,512]{2,1,0:T(8,128)(2,1)S(1)}, u32[]{:S(2)}, u32[]{:S(2)}) %collective-permute-start.11) | collective-permute-done | bytes 524320 | tf_op jit(solution)/shard_map/ppermute | solution.py:36
  79.0 6.7 %collective-permute-done.8.refs_4_.refs_9_ = bf16[2,256,512]{2,1,0:T(8,128)(2,1)S(1)} collective-permute-done((bf16[2,256,512]{2,1,0:T(8,128)(2,1)S(1)}, bf16[2,256,512]{2,1,0:T(8,128)(2,1)S(1)}, u32[]{:S(2)}, u32[]{:S(2)}) %collective-permute-start.8) | collective-permute-done | bytes 524320 | tf_op jit(solution)/shard_map/ppermute | solution.py:36
  85.7 1.0 shard_map.94
  86.7 1.9 %collective-permute-start.12 = (bf16[6,2,128,512]{3,2,1,0:T(8,128)(2,1)S(1)}, bf16[6,2,128,512]{3,2,1,0:T(8,128)(2,1)S(1)}, u32[]{:S(2)}, u32[]{:S(2)}) collective-permute-start(bf16[6,2,128,512]{3,2,1,0:T(8,128)(2,1)S(1)} %shard_map.94), channel_id=1, source_target_pairs={{0,32},{32,0},{64,96},{96,64},{128,160},{160,128},{192,224},{224,1... | collective-permute-start | bytes 4718600 | tf_op jit(solution)/shard_map/ppermute | solution.py:41
  88.7 3.4 %collective-permute-done.12.refs_13_ = bf16[6,2,128,512]{3,2,1,0:T(8,128)(2,1)S(1)} collective-permute-done((bf16[6,2,128,512]{3,2,1,0:T(8,128)(2,1)S(1)}, bf16[6,2,128,512]{3,2,1,0:T(8,128)(2,1)S(1)}, u32[]{:S(2)}, u32[]{:S(2)}) %collective-permute-start.12) | collective-permute-done | bytes 1572896 | tf_op jit(solution)/shard_map/ppermute | solution.py:41
  92.1 13.5 %shard_map.95 = (bf16[2,128,512]{2,1,0:T(8,128)(2,1)}, bf16[2,128,512]{2,1,0:T(8,128)(2,1)}, bf16[2,2,128,512]{3,2,1,0:T(8,128)(2,1)S(1)}, bf16[6,2,128,512]{3,2...) custom-call(s32[4,14]{1,0:T(4,128)S(1)} %pad_add_fusion.table, ...), custom_call_target="tpu_custom_call" | custom-call | flops 1409286144 | bytes 12582912 | tf_op jit(solution)/shard_map/pallas_call | solution.py:222
  105.6 2.1 %collective-permute-start.13 = (bf16[6,2,128,512]{3,2,1,0:T(8,128)(2,1)S(1)}, bf16[6,2,128,512]{3,2,1,0:T(8,128)(2,1)S(1)}, u32[]{:S(2)}, u32[]{:S(2)}) collective-permute-start(bf16[6,2,128,512]{3,2,1,0:T(8,128)(2,1)S(1)} %get-tuple-element.83.mine), channel_id=1, source_target_pairs={{0,32},{32,0},{64,96},{96,64},{128,160},{160,128},{192,224},{224,1... | collective-permute-start | bytes 4718600 | tf_op jit(solution)/shard_map/ppermute | solution.py:41
  107.7 3.2 %collective-permute-done.13.theirs = bf16[6,2,128,512]{3,2,1,0:T(8,128)(2,1)S(1)} collective-permute-done((bf16[6,2,128,512]{3,2,1,0:T(8,128)(2,1)S(1)}, bf16[6,2,128,512]{3,2,1,0:T(8,128)(2,1)S(1)}, u32[]{:S(2)}, u32[]{:S(2)}) %collective-permute-start.13) | collective-permute-done | bytes 1572896 | tf_op jit(solution)/shard_map/ppermute | solution.py:41
  110.9 0.9 shard_map.96
  111.8 1.9 %collective-permute-start.14 = (bf16[2,2,128,512]{3,2,1,0:T(8,128)(2,1)S(1)}, bf16[2,2,128,512]{3,2,1,0:T(8,128)(2,1)S(1)}, u32[]{:S(2)}, u32[]{:S(2)}) collective-permute-start(bf16[2,2,128,512]{3,2,1,0:T(8,128)(2,1)S(1)} %get-tuple-element.85), channel_id=1, source_target_pairs={{0,64},{32,480},{64,128},{96,32},{128,192},{160,96},{192,256},{224... | collective-permute-start | bytes 1572872 | tf_op jit(solution)/shard_map/ppermute | solution.py:36
  113.8 6.0 %collective-permute-start.15 = (bf16[2,128,512]{2,1,0:T(8,128)(2,1)S(1)}, bf16[2,128,512]{2,1,0:T(8,128)(2,1)S(1)}, u32[]{:S(2)}, u32[]{:S(2)}) collective-permute-start(bf16[2,128,512]{2,1,0:T(8,128)(2,1)S(1)} %get-tuple-element.86), channel_id=1, source_target_pairs={{0,2},{1,3},{2,4},{3,5},{4,6},{5,7},{6,8},{7,9},{8,10},{9,11},{10,... | collective-permute-start | bytes 786440 | tf_op jit(solution)/shard_map/ppermute | solution.py:46
  119.8 2.1 %collective-permute-start.16 = (bf16[2,128,512]{2,1,0:T(8,128)(2,1)S(1)}, bf16[2,128,512]{2,1,0:T(8,128)(2,1)S(1)}, u32[]{:S(2)}, u32[]{:S(2)}) collective-permute-start(bf16[2,128,512]{2,1,0:T(8,128)(2,1)S(1)} %get-tuple-element.87), channel_id=1, source_target_pairs={{0,1},{1,2},{2,3},{3,4},{4,5},{5,6},{6,7},{7,8},{8,9},{9,10},{10,1... | collective-permute-start | bytes 786440 | tf_op jit(solution)/shard_map/ppermute | solution.py:46
  121.9 1.9 %collective-permute-start.22 = (bf16[2,2,128,512]{3,2,1,0:T(8,128)(2,1)S(1)}, bf16[2,2,128,512]{3,2,1,0:T(8,128)(2,1)S(1)}, u32[]{:S(2)}, u32[]{:S(2)}) collective-permute-start(bf16[2,2,128,512]{3,2,1,0:T(8,128)(2,1)S(1)} %get-tuple-element.103), channel_id=1, source_target_pairs={{0,64},{32,480},{64,128},{96,32},{128,192},{160,96},{192,256},{224... | collective-permute-start | bytes 1572872 | tf_op jit(solution)/shard_map/ppermute | solution.py:36
  123.9 1.0 shard_map.97
  124.9 1.6 collective-permute-done.15.refs_0_
  126.4 4.9 %collective-permute-done.16.refs_1_ = bf16[2,128,512]{2,1,0:T(8,128)(2,1)S(1)} collective-permute-done((bf16[2,128,512]{2,1,0:T(8,128)(2,1)S(1)}, bf16[2,128,512]{2,1,0:T(8,128)(2,1)S(1)}, u32[]{:S(2)}, u32[]{:S(2)}) %collective-permute-start.16) | collective-permute-done | bytes 262176 | tf_op jit(solution)/shard_map/ppermute | solution.py:46
  131.3 0.1 add_convert_fusion.4
  131.5 1.9 %collective-permute-start.17 = (bf16[2,2,128,512]{3,2,1,0:T(8,128)(2,1)S(1)}, bf16[2,2,128,512]{3,2,1,0:T(8,128)(2,1)S(1)}, u32[]{:S(2)}, u32[]{:S(2)}) collective-permute-start(bf16[2,2,128,512]{3,2,1,0:T(8,128)(2,1)S(1)} %add_convert_fusion.4), channel_id=1, source_target_pairs={{0,64},{32,480},{64,128},{96,32},{128,192},{160,96},{192,256},{224... | collective-permute-start | bytes 1572872 | tf_op jit(solution)/shard_map/ppermute | solution.py:36
  133.4 0.8 collective-permute-done.22
  134.2 0.1 add_convert_fusion.1
  134.4 1.9 %collective-permute-start.23 = (bf16[2,2,128,512]{3,2,1,0:T(8,128)(2,1)S(1)}, bf16[2,2,128,512]{3,2,1,0:T(8,128)(2,1)S(1)}, u32[]{:S(2)}, u32[]{:S(2)}) collective-permute-start(bf16[2,2,128,512]{3,2,1,0:T(8,128)(2,1)S(1)} %add_convert_fusion.1), channel_id=1, source_target_pairs={{0,64},{32,480},{64,128},{96,32},{128,192},{160,96},{192,256},{224... | collective-permute-start | bytes 1572872 | tf_op jit(solution)/shard_map/ppermute | solution.py:36
  136.3 7.4 %collective-permute-done.17 = bf16[2,2,128,512]{3,2,1,0:T(8,128)(2,1)S(1)} collective-permute-done((bf16[2,2,128,512]{3,2,1,0:T(8,128)(2,1)S(1)}, bf16[2,2,128,512]{3,2,1,0:T(8,128)(2,1)S(1)}, u32[]{:S(2)}, u32[]{:S(2)}) %collective-permute-start.17) | collective-permute-done | bytes 524320 | tf_op jit(solution)/shard_map/ppermute | solution.py:36
  143.7 0.1 add_convert_fusion.3
  143.9 1.9 %collective-permute-start.18 = (bf16[2,2,128,512]{3,2,1,0:T(8,128)(2,1)S(1)}, bf16[2,2,128,512]{3,2,1,0:T(8,128)(2,1)S(1)}, u32[]{:S(2)}, u32[]{:S(2)}) collective-permute-start(bf16[2,2,128,512]{3,2,1,0:T(8,128)(2,1)S(1)} %add_convert_fusion.3), channel_id=1, source_target_pairs={{0,64},{32,480},{64,128},{96,32},{128,192},{160,96},{192,256},{224... | collective-permute-start | bytes 1572872 | tf_op jit(solution)/shard_map/ppermute | solution.py:36
  145.8 1.9 %collective-permute-start.19 = (bf16[2,128,512]{2,1,0:T(8,128)(2,1)S(1)}, bf16[2,128,512]{2,1,0:T(8,128)(2,1)S(1)}, u32[]{:S(2)}, u32[]{:S(2)}) collective-permute-start(bf16[2,128,512]{2,1,0:T(8,128)(2,1)S(1)} %get-tuple-element.99), channel_id=1, source_target_pairs={{1,0},{2,1},{3,2},{4,3},{5,4},{6,5},{7,6},{8,7},{9,8},{10,9},{11,1... | collective-permute-start | bytes 786440 | tf_op jit(solution)/shard_map/ppermute | solution.py:46
  147.7 5.2 %collective-permute-start.20 = (bf16[2,128,512]{2,1,0:T(8,128)(2,1)S(1)}, bf16[2,128,512]{2,1,0:T(8,128)(2,1)S(1)}, u32[]{:S(2)}, u32[]{:S(2)}) collective-permute-start(bf16[2,128,512]{2,1,0:T(8,128)(2,1)S(1)} %get-tuple-element.100), channel_id=1, source_target_pairs={{2,0},{3,1},{4,2},{5,3},{6,4},{7,5},{8,6},{9,7},{10,8},{11,9},{12,... | collective-permute-start | bytes 786440 | tf_op jit(solution)/shard_map/ppermute | solution.py:46
  153.0 0.1 add_convert_fusion
  153.1 1.9 %collective-permute-start.24 = (bf16[2,2,128,512]{3,2,1,0:T(8,128)(2,1)S(1)}, bf16[2,2,128,512]{3,2,1,0:T(8,128)(2,1)S(1)}, u32[]{:S(2)}, u32[]{:S(2)}) collective-permute-start(bf16[2,2,128,512]{3,2,1,0:T(8,128)(2,1)S(1)} %add_convert_fusion), channel_id=1, source_target_pairs={{0,64},{32,480},{64,128},{96,32},{128,192},{160,96},{192,256},{224... | collective-permute-start | bytes 1572872 | tf_op jit(solution)/shard_map/ppermute | solution.py:36
  155.0 7.2 %collective-permute-done.19.refs_2_ = bf16[2,128,512]{2,1,0:T(8,128)(2,1)S(1)} collective-permute-done((bf16[2,128,512]{2,1,0:T(8,128)(2,1)S(1)}, bf16[2,128,512]{2,1,0:T(8,128)(2,1)S(1)}, u32[]{:S(2)}, u32[]{:S(2)}) %collective-permute-start.19) | collective-permute-done | bytes 262176 | tf_op jit(solution)/shard_map/ppermute | solution.py:46
  162.2 1.6 collective-permute-done.20.refs_3_
  163.9 0.1 add_convert_fusion.2
  164.0 2.7 %collective-permute-start.21 = (bf16[2,2,128,512]{3,2,1,0:T(8,128)(2,1)S(1)}, bf16[2,2,128,512]{3,2,1,0:T(8,128)(2,1)S(1)}, u32[]{:S(2)}, u32[]{:S(2)}) collective-permute-start(bf16[2,2,128,512]{3,2,1,0:T(8,128)(2,1)S(1)} %add_convert_fusion.2), channel_id=1, source_target_pairs={{0,64},{32,480},{64,128},{96,32},{128,192},{160,96},{192,256},{224... | collective-permute-start | bytes 1572872 | tf_op jit(solution)/shard_map/ppermute | solution.py:36
  166.7 1.9 %collective-permute-start.25 = (bf16[2,2,128,512]{3,2,1,0:T(8,128)(2,1)S(1)}, bf16[2,2,128,512]{3,2,1,0:T(8,128)(2,1)S(1)}, u32[]{:S(2)}, u32[]{:S(2)}) collective-permute-start(bf16[2,2,128,512]{3,2,1,0:T(8,128)(2,1)S(1)} %collective-permute-done.24), channel_id=1, source_target_pairs={{0,32},{32,0},{64,96},{96,64},{128,160},{160,128},{192,224},{224,1... | collective-permute-start | bytes 1572872 | tf_op jit(solution)/shard_map/ppermute | solution.py:41
  168.6 7.7 %collective-permute-done.21.from_a = bf16[2,2,128,512]{3,2,1,0:T(8,128)(2,1)S(1)} collective-permute-done((bf16[2,2,128,512]{3,2,1,0:T(8,128)(2,1)S(1)}, bf16[2,2,128,512]{3,2,1,0:T(8,128)(2,1)S(1)}, u32[]{:S(2)}, u32[]{:S(2)}) %collective-permute-start.21) | collective-permute-done | bytes 524320 | tf_op jit(solution)/shard_map/ppermute | solution.py:36
  176.3 2.0 %shard_map.98 = (bf16[256,512]{1,0:T(8,128)(2,1)}, bf16[256,512]{1,0:T(8,128)(2,1)}) custom-call(s32[6]{0:T(128)S(1)} %pad_add_fusion.7.table, bf16[2,2,128,512]{3,2,1,0:T(8,128)(2,1)S(1)} %get-tuple-element.82.near, bf16[6,2,128,512]{3,2,1,0:T(8,128)(2,1)S(1)} %collective-permute-done.13.theirs, ...), custom_call_target="tpu_custom_call" | custom-call | flops 4194304 | bytes 6291456 | tf_op jit(solution)/shard_map/pallas_call | solution.py:295
  (42 shorter events, 1.3 us)
Async XLA Ops:
  0.6 21.2 %copy-start.1 = (bf16[256,512]{1,0:T(8,128)(2,1)S(1)}, bf16[256,512]{1,0:T(8,128)(2,1)}, u32[]{:S(2)}) copy-start(bf16[256,512]{1,0:T(8,128)(2,1)} %keys.1) | copy-start | bytes 786436
  0.6 21.2 %copy-start = (bf16[256,512]{1,0:T(8,128)(2,1)S(1)}, bf16[256,512]{1,0:T(8,128)(2,1)}, u32[]{:S(2)}) copy-start(bf16[256,512]{1,0:T(8,128)(2,1)} %values.1) | copy-start | bytes 786436
  1.8 10.0 %collective-permute-start.1 = (bf16[2,256,512]{2,1,0:T(8,128)(2,1)S(1)}, bf16[2,256,512]{2,1,0:T(8,128)(2,1)S(1)}, u32[]{:S(2)}, u32[]{:S(2)}) collective-permute-start(bf16[2,256,512]{2,1,0:T(8,128)(2,1)S(1)} %pad_maximum_fusion.refs_0_), channel_id=1, source_target_pairs={{0,32},{32,0},{64,96},{96,64},{128,160},{160,128},{192,224},{224,1... | collective-permute-start | bytes 1572872 | tf_op jit(solution)/shard_map/ppermute | solution.py:41
  3.7 18.1 %collective-permute-start = (bf16[2,256,512]{2,1,0:T(8,128)(2,1)S(1)}, bf16[2,256,512]{2,1,0:T(8,128)(2,1)S(1)}, u32[]{:S(2)}, u32[]{:S(2)}) collective-permute-start(bf16[2,256,512]{2,1,0:T(8,128)(2,1)S(1)} %pad_maximum_fusion.refs_0_), channel_id=1, source_target_pairs={{0,64},{32,480},{64,128},{96,32},{128,192},{160,96},{192,256},{224... | collective-permute-start | bytes 1572872 | tf_op jit(solution)/shard_map/ppermute | solution.py:36
  23.8 14.9 %collective-permute-start.2 = (bf16[2,128,512]{2,1,0:T(8,128)(2,1)S(1)}, bf16[2,128,512]{2,1,0:T(8,128)(2,1)S(1)}, u32[]{:S(2)}, u32[]{:S(2)}) collective-permute-start(bf16[2,128,512]{2,1,0:T(8,128)(2,1)S(1)} %get-tuple-element.61), channel_id=1, source_target_pairs={{0,1},{1,2},{2,3},{3,4},{4,5},{5,6},{6,7},{7,8},{8,9},{9,10},{10,1... | collective-permute-start | bytes 786440 | tf_op jit(solution)/shard_map/ppermute | solution.py:46
  28.4 10.5 %collective-permute-start.3 = (bf16[2,128,512]{2,1,0:T(8,128)(2,1)S(1)}, bf16[2,128,512]{2,1,0:T(8,128)(2,1)S(1)}, u32[]{:S(2)}, u32[]{:S(2)}) collective-permute-start(bf16[2,128,512]{2,1,0:T(8,128)(2,1)S(1)} %get-tuple-element.62), channel_id=1, source_target_pairs={{0,2},{1,3},{2,4},{3,5},{4,6},{5,7},{6,8},{7,9},{8,10},{9,11},{10,... | collective-permute-start | bytes 786440 | tf_op jit(solution)/shard_map/ppermute | solution.py:46
  32.8 15.3 %collective-permute-start.9 = (bf16[2,256,512]{2,1,0:T(8,128)(2,1)S(1)}, bf16[2,256,512]{2,1,0:T(8,128)(2,1)S(1)}, u32[]{:S(2)}, u32[]{:S(2)}) collective-permute-start(bf16[2,256,512]{2,1,0:T(8,128)(2,1)S(1)} %collective-permute-done.1.refs_0_.refs_5_), channel_id=1, source_target_pairs={{0,64},{32,480},{64,128},{96,32},{128,192},{160,96},{192,256},{224... | collective-permute-start | bytes 1572872 | tf_op jit(solution)/shard_map/ppermute | solution.py:36
  38.9 21.5 %collective-permute-start.4 = (bf16[2,256,512]{2,1,0:T(8,128)(2,1)S(1)}, bf16[2,256,512]{2,1,0:T(8,128)(2,1)S(1)}, u32[]{:S(2)}, u32[]{:S(2)}) collective-permute-start(bf16[2,256,512]{2,1,0:T(8,128)(2,1)S(1)} %collective-permute-done.refs_1_.refs_6_), channel_id=1, source_target_pairs={{0,64},{32,480},{64,128},{96,32},{128,192},{160,96},{192,256},{224... | collective-permute-start | bytes 1572872 | tf_op jit(solution)/shard_map/ppermute | solution.py:36
  40.9 51.2 %copy-start.2 = (bf16[256,512]{1,0:T(8,128)(2,1)S(1)}, bf16[256,512]{1,0:T(8,128)(2,1)}, u32[]{:S(2)}) copy-start(bf16[256,512]{1,0:T(8,128)(2,1)} %param.6) | copy-start | bytes 786436
  40.9 51.2 %copy-start.3 = (bf16[256,512]{1,0:T(8,128)(2,1)S(1)}, bf16[256,512]{1,0:T(8,128)(2,1)}, u32[]{:S(2)}) copy-start(bf16[256,512]{1,0:T(8,128)(2,1)} %param.9) | copy-start | bytes 786436
  40.9 13.1 %collective-permute-start.5 = (bf16[2,128,512]{2,1,0:T(8,128)(2,1)S(1)}, bf16[2,128,512]{2,1,0:T(8,128)(2,1)S(1)}, u32[]{:S(2)}, u32[]{:S(2)}) collective-permute-start(bf16[2,128,512]{2,1,0:T(8,128)(2,1)S(1)} %get-tuple-element.68), channel_id=1, source_target_pairs={{2,0},{3,1},{4,2},{5,3},{6,4},{7,5},{8,6},{9,7},{10,8},{11,9},{12,... | collective-permute-start | bytes 786440 | tf_op jit(solution)/shard_map/ppermute | solution.py:46
  45.6 14.9 %collective-permute-start.6 = (bf16[2,128,512]{2,1,0:T(8,128)(2,1)S(1)}, bf16[2,128,512]{2,1,0:T(8,128)(2,1)S(1)}, u32[]{:S(2)}, u32[]{:S(2)}) collective-permute-start(bf16[2,128,512]{2,1,0:T(8,128)(2,1)S(1)} %get-tuple-element.69), channel_id=1, source_target_pairs={{1,0},{2,1},{3,2},{4,3},{5,4},{6,5},{7,6},{8,7},{9,8},{10,9},{11,1... | collective-permute-start | bytes 786440 | tf_op jit(solution)/shard_map/ppermute | solution.py:46
  48.1 14.3 %collective-permute-start.10 = (bf16[2,256,512]{2,1,0:T(8,128)(2,1)S(1)}, bf16[2,256,512]{2,1,0:T(8,128)(2,1)S(1)}, u32[]{:S(2)}, u32[]{:S(2)}) collective-permute-start(bf16[2,256,512]{2,1,0:T(8,128)(2,1)S(1)} %collective-permute-done.9.refs_5_.refs_10_), channel_id=1, source_target_pairs={{0,64},{32,480},{64,128},{96,32},{128,192},{160,96},{192,256},{224... | collective-permute-start | bytes 1572872 | tf_op jit(solution)/shard_map/ppermute | solution.py:36
  60.4 13.0 %collective-permute-start.7 = (bf16[2,256,512]{2,1,0:T(8,128)(2,1)S(1)}, bf16[2,256,512]{2,1,0:T(8,128)(2,1)S(1)}, u32[]{:S(2)}, u32[]{:S(2)}) collective-permute-start(bf16[2,256,512]{2,1,0:T(8,128)(2,1)S(1)} %collective-permute-done.4.refs_2_.refs_7_), channel_id=1, source_target_pairs={{0,64},{32,480},{64,128},{96,32},{128,192},{160,96},{192,256},{224... | collective-permute-start | bytes 1572872 | tf_op jit(solution)/shard_map/ppermute | solution.py:36
  62.4 16.7 %collective-permute-start.11 = (bf16[2,256,512]{2,1,0:T(8,128)(2,1)S(1)}, bf16[2,256,512]{2,1,0:T(8,128)(2,1)S(1)}, u32[]{:S(2)}, u32[]{:S(2)}) collective-permute-start(bf16[2,256,512]{2,1,0:T(8,128)(2,1)S(1)} %collective-permute-done.10.refs_6_.refs_11_), channel_id=1, source_target_pairs={{0,64},{32,480},{64,128},{96,32},{128,192},{160,96},{192,256},{224... | collective-permute-start | bytes 1572872 | tf_op jit(solution)/shard_map/ppermute | solution.py:36
  73.4 12.3 %collective-permute-start.8 = (bf16[2,256,512]{2,1,0:T(8,128)(2,1)S(1)}, bf16[2,256,512]{2,1,0:T(8,128)(2,1)S(1)}, u32[]{:S(2)}, u32[]{:S(2)}) collective-permute-start(bf16[2,256,512]{2,1,0:T(8,128)(2,1)S(1)} %collective-permute-done.7.refs_3_.refs_8_), channel_id=1, source_target_pairs={{0,64},{32,480},{64,128},{96,32},{128,192},{160,96},{192,256},{224... | collective-permute-start | bytes 1572872 | tf_op jit(solution)/shard_map/ppermute | solution.py:36
  86.7 5.3 %collective-permute-start.12 = (bf16[6,2,128,512]{3,2,1,0:T(8,128)(2,1)S(1)}, bf16[6,2,128,512]{3,2,1,0:T(8,128)(2,1)S(1)}, u32[]{:S(2)}, u32[]{:S(2)}) collective-permute-start(bf16[6,2,128,512]{3,2,1,0:T(8,128)(2,1)S(1)} %shard_map.94), channel_id=1, source_target_pairs={{0,32},{32,0},{64,96},{96,64},{128,160},{160,128},{192,224},{224,1... | collective-permute-start | bytes 4718600 | tf_op jit(solution)/shard_map/ppermute | solution.py:41
  105.6 5.3 %collective-permute-start.13 = (bf16[6,2,128,512]{3,2,1,0:T(8,128)(2,1)S(1)}, bf16[6,2,128,512]{3,2,1,0:T(8,128)(2,1)S(1)}, u32[]{:S(2)}, u32[]{:S(2)}) collective-permute-start(bf16[6,2,128,512]{3,2,1,0:T(8,128)(2,1)S(1)} %get-tuple-element.83.mine), channel_id=1, source_target_pairs={{0,32},{32,0},{64,96},{96,64},{128,160},{160,128},{192,224},{224,1... | collective-permute-start | bytes 4718600 | tf_op jit(solution)/shard_map/ppermute | solution.py:41
  111.8 19.5 %collective-permute-start.14 = (bf16[2,2,128,512]{3,2,1,0:T(8,128)(2,1)S(1)}, bf16[2,2,128,512]{3,2,1,0:T(8,128)(2,1)S(1)}, u32[]{:S(2)}, u32[]{:S(2)}) collective-permute-start(bf16[2,2,128,512]{3,2,1,0:T(8,128)(2,1)S(1)} %get-tuple-element.85), channel_id=1, source_target_pairs={{0,64},{32,480},{64,128},{96,32},{128,192},{160,96},{192,256},{224... | collective-permute-start | bytes 1572872 | tf_op jit(solution)/shard_map/ppermute | solution.py:36
  113.8 12.7 %collective-permute-start.15 = (bf16[2,128,512]{2,1,0:T(8,128)(2,1)S(1)}, bf16[2,128,512]{2,1,0:T(8,128)(2,1)S(1)}, u32[]{:S(2)}, u32[]{:S(2)}) collective-permute-start(bf16[2,128,512]{2,1,0:T(8,128)(2,1)S(1)} %get-tuple-element.86), channel_id=1, source_target_pairs={{0,2},{1,3},{2,4},{3,5},{4,6},{5,7},{6,8},{7,9},{8,10},{9,11},{10,... | collective-permute-start | bytes 786440 | tf_op jit(solution)/shard_map/ppermute | solution.py:46
  119.8 11.5 %collective-permute-start.16 = (bf16[2,128,512]{2,1,0:T(8,128)(2,1)S(1)}, bf16[2,128,512]{2,1,0:T(8,128)(2,1)S(1)}, u32[]{:S(2)}, u32[]{:S(2)}) collective-permute-start(bf16[2,128,512]{2,1,0:T(8,128)(2,1)S(1)} %get-tuple-element.87), channel_id=1, source_target_pairs={{0,1},{1,2},{2,3},{3,4},{4,5},{5,6},{6,7},{7,8},{8,9},{9,10},{10,1... | collective-permute-start | bytes 786440 | tf_op jit(solution)/shard_map/ppermute | solution.py:46
  121.9 12.3 %collective-permute-start.22 = (bf16[2,2,128,512]{3,2,1,0:T(8,128)(2,1)S(1)}, bf16[2,2,128,512]{3,2,1,0:T(8,128)(2,1)S(1)}, u32[]{:S(2)}, u32[]{:S(2)}) collective-permute-start(bf16[2,2,128,512]{3,2,1,0:T(8,128)(2,1)S(1)} %get-tuple-element.103), channel_id=1, source_target_pairs={{0,64},{32,480},{64,128},{96,32},{128,192},{160,96},{192,256},{224... | collective-permute-start | bytes 1572872 | tf_op jit(solution)/shard_map/ppermute | solution.py:36
  131.5 12.3 %collective-permute-start.17 = (bf16[2,2,128,512]{3,2,1,0:T(8,128)(2,1)S(1)}, bf16[2,2,128,512]{3,2,1,0:T(8,128)(2,1)S(1)}, u32[]{:S(2)}, u32[]{:S(2)}) collective-permute-start(bf16[2,2,128,512]{3,2,1,0:T(8,128)(2,1)S(1)} %add_convert_fusion.4), channel_id=1, source_target_pairs={{0,64},{32,480},{64,128},{96,32},{128,192},{160,96},{192,256},{224... | collective-permute-start | bytes 1572872 | tf_op jit(solution)/shard_map/ppermute | solution.py:36
  134.4 18.6 %collective-permute-start.23 = (bf16[2,2,128,512]{3,2,1,0:T(8,128)(2,1)S(1)}, bf16[2,2,128,512]{3,2,1,0:T(8,128)(2,1)S(1)}, u32[]{:S(2)}, u32[]{:S(2)}) collective-permute-start(bf16[2,2,128,512]{3,2,1,0:T(8,128)(2,1)S(1)} %add_convert_fusion.1), channel_id=1, source_target_pairs={{0,64},{32,480},{64,128},{96,32},{128,192},{160,96},{192,256},{224... | collective-permute-start | bytes 1572872 | tf_op jit(solution)/shard_map/ppermute | solution.py:36
  143.9 20.0 %collective-permute-start.18 = (bf16[2,2,128,512]{3,2,1,0:T(8,128)(2,1)S(1)}, bf16[2,2,128,512]{3,2,1,0:T(8,128)(2,1)S(1)}, u32[]{:S(2)}, u32[]{:S(2)}) collective-permute-start(bf16[2,2,128,512]{3,2,1,0:T(8,128)(2,1)S(1)} %add_convert_fusion.3), channel_id=1, source_target_pairs={{0,64},{32,480},{64,128},{96,32},{128,192},{160,96},{192,256},{224... | collective-permute-start | bytes 1572872 | tf_op jit(solution)/shard_map/ppermute | solution.py:36
  145.8 16.4 %collective-permute-start.19 = (bf16[2,128,512]{2,1,0:T(8,128)(2,1)S(1)}, bf16[2,128,512]{2,1,0:T(8,128)(2,1)S(1)}, u32[]{:S(2)}, u32[]{:S(2)}) collective-permute-start(bf16[2,128,512]{2,1,0:T(8,128)(2,1)S(1)} %get-tuple-element.99), channel_id=1, source_target_pairs={{1,0},{2,1},{3,2},{4,3},{5,4},{6,5},{7,6},{8,7},{9,8},{10,9},{11,1... | collective-permute-start | bytes 786440 | tf_op jit(solution)/shard_map/ppermute | solution.py:46
  147.7 16.1 %collective-permute-start.20 = (bf16[2,128,512]{2,1,0:T(8,128)(2,1)S(1)}, bf16[2,128,512]{2,1,0:T(8,128)(2,1)S(1)}, u32[]{:S(2)}, u32[]{:S(2)}) collective-permute-start(bf16[2,128,512]{2,1,0:T(8,128)(2,1)S(1)} %get-tuple-element.100), channel_id=1, source_target_pairs={{2,0},{3,1},{4,2},{5,3},{6,4},{7,5},{8,6},{9,7},{10,8},{11,9},{12,... | collective-permute-start | bytes 786440 | tf_op jit(solution)/shard_map/ppermute | solution.py:46
  153.1 13.6 %collective-permute-start.24 = (bf16[2,2,128,512]{3,2,1,0:T(8,128)(2,1)S(1)}, bf16[2,2,128,512]{3,2,1,0:T(8,128)(2,1)S(1)}, u32[]{:S(2)}, u32[]{:S(2)}) collective-permute-start(bf16[2,2,128,512]{3,2,1,0:T(8,128)(2,1)S(1)} %add_convert_fusion), channel_id=1, source_target_pairs={{0,64},{32,480},{64,128},{96,32},{128,192},{160,96},{192,256},{224... | collective-permute-start | bytes 1572872 | tf_op jit(solution)/shard_map/ppermute | solution.py:36
  164.0 12.3 %collective-permute-start.21 = (bf16[2,2,128,512]{3,2,1,0:T(8,128)(2,1)S(1)}, bf16[2,2,128,512]{3,2,1,0:T(8,128)(2,1)S(1)}, u32[]{:S(2)}, u32[]{:S(2)}) collective-permute-start(bf16[2,2,128,512]{3,2,1,0:T(8,128)(2,1)S(1)} %add_convert_fusion.2), channel_id=1, source_target_pairs={{0,64},{32,480},{64,128},{96,32},{128,192},{160,96},{192,256},{224... | collective-permute-start | bytes 1572872 | tf_op jit(solution)/shard_map/ppermute | solution.py:36
  166.7 9.6 %collective-permute-start.25 = (bf16[2,2,128,512]{3,2,1,0:T(8,128)(2,1)S(1)}, bf16[2,2,128,512]{3,2,1,0:T(8,128)(2,1)S(1)}, u32[]{:S(2)}, u32[]{:S(2)}) collective-permute-start(bf16[2,2,128,512]{3,2,1,0:T(8,128)(2,1)S(1)} %collective-permute-done.24), channel_id=1, source_target_pairs={{0,32},{32,0},{64,96},{96,64},{128,160},{160,128},{192,224},{224,1... | collective-permute-start | bytes 1572872 | tf_op jit(solution)/shard_map/ppermute | solution.py:41

commit v4 on v3

--- a/solution.py
+++ b/solution.py
@@ -351,20 +351,22 @@
     hits = jnp.stack([slot_in(mine, wanted), slot_in(theirs, wanted)])
     last = jnp.concatenate([given, hits[1, 7 * NB :]]).astype(i32)
     tables = (given, pick_table, table, hits[:, : 2 * NB], hits[:, 2 * NB : 7 * NB], last)
-    flow_a[0], sibling, tables = lax.optimization_barrier((flow_a[0], sibling, tables))
+    sibling, tables = lax.optimization_barrier((sibling, tables))
     given, pick_table, table, hits_first, hits_rest, last = tables
 
+    flow_b = [ring_step(sibling)]
+    flow_a.append(ring_step(flow_a[0]))
     offered = offer(given, keys, values)
-    flow_b = [ring_step(sibling)]
-    near = [None, None, shifted(offered[2], OFFSETS[2]), shifted(offered[3], OFFSETS[3])]
-    flow_a[0], near[2], near[3] = lax.optimization_barrier((flow_a[0], near[2], near[3]))
-    flow_a.append(ring_step(flow_a[0]))
-    behind = lax.optimization_barrier((offered[0], offered[1], near[2], near[3]))
-    near = [shifted(behind[0], OFFSETS[0]), shifted(behind[1], OFFSETS[1]), behind[2], behind[3]]
     flow_b.append(ring_step(flow_b[0]))
-    flow_a[1], near = lax.optimization_barrier((flow_a[1], near))
+    up = [shifted(offered[t], OFFSETS[t]) for t in (2, 3)]
+    flow_a[1], *up = lax.optimization_barrier((flow_a[1], *up))
     flow_a.append(ring_step(flow_a[1]))
+    behind = lax.optimization_barrier((offered[0], offered[1], *up))
+    up = list(behind[2:])
+    down = [shifted(behind[t], OFFSETS[t]) for t in (0, 1)]
+    near = down + up
     flow_b.append(ring_step(flow_b[1]))
+    flow_a[2], near = lax.optimization_barrier((flow_a[2], near))
     flow_a.append(ring_step(flow_a[2]))
 
     picked = swap_cores(pick(pick_table, [sibling] + flow_a + flow_b))
@@ -387,15 +389,13 @@
 
     back_a = ring_step(start_a)
     back_b = ring_step(start_b)
-    returned = [shifted(near_terms[t], -OFFSETS[t]) for t in (0, 1)]
-    back_a, *returned = lax.optimization_barrier((back_a, *returned))
     back_a = ring_step(joined(back_a, a3))
     back_b = ring_step(joined(back_b, b2))
+    returned = [shifted(near_terms[t], -OFFSETS[t]) for t in (0, 1)]
     back_a, *behind = lax.optimization_barrier((back_a, near_terms[2], near_terms[3], *returned))
     returned = behind[2:] + [shifted(behind[t - 2], -OFFSETS[t]) for t in (2, 3)]
     back_a = ring_step(joined(back_a, a2))
     back_b = ring_step(joined(back_b, b1))
-    back_a, *returned = lax.optimization_barrier((back_a, *returned))
     back_a = ring_step(joined(back_a, a1))
     back_b = swap_cores(back_b)
 

time: 179 us -> 184 us (1.028)
  the two profiles are of different devices: /device:TPU:30 before, /device:TPU:29 now
where the time goes in v4:
time: 184 us; the launch traced here: 183 us
  starting transfers between devices  86.6 us (47%)
  waiting for transfers between devices  69.3 us (38%)
  Pallas kernels  20.4 us (11%)
  other arithmetic  3 us (2%)
  local copies, waits for them, and re-layouts  2.52 us (1%)
    ppermute x14, starting transfers between devices, ring_step(): lax.ppermute(array, 'group', [(g, (g + (2 if g % 2 == 0 else -2)) % size)...  41.4 us
    ppermute x8, waiting for transfers between devices, shifted(): lax.ppermute(array, 'dom', [(i, i + by) for i in range(size) if 0 <= i +...  37 us
    ppermute x8, starting transfers between devices, shifted(): lax.ppermute(array, 'dom', [(i, i + by) for i in range(size) if 0 <= i +...  29.6 us
    ppermute x14, waiting for transfers between devices, ring_step(): lax.ppermute(array, 'group', [(g, (g + (2 if g % 2 == 0 else -2)) % size)...  26.3 us
    ppermute x4, starting transfers between devices, swap_cores(): return lax.ppermute(array, 'group', [(g, g ^ 1) for g in range(size)])  15.6 us
    pallas_call x1, Pallas kernels, attend(): pl.pallas_call(attend_kernel, out_shape=(jax.ShapeDtypeStruct((NB, BS, D)...  13.5 us
    ppermute x4, waiting for transfers between devices, swap_cores(): return lax.ppermute(array, 'group', [(g, g ^ 1) for g in range(size)])  6.03 us
  transfers between devices with their start and end apart: 26, of which 16 were waited for; matrix products, arithmetic and copies ran while one was open for 2% of the time, Pallas kernels for 2%

profile of v4, /device:TPU:29, one launch (start us, length us, event | category | flops | bytes accessed | tf_op | source)
XLA Modules:
  0.0 183.0 jit_solution(7853978869874772457)
XLA Ops:
  0.7 1.1 pad_maximum_fusion.refs_0_
  1.8 10.7 %collective-permute-start.1 = (bf16[2,256,512]{2,1,0:T(8,128)(2,1)S(1)}, bf16[2,256,512]{2,1,0:T(8,128)(2,1)S(1)}, u32[]{:S(2)}, u32[]{:S(2)}) collective-permute-start(bf16[2,256,512]{2,1,0:T(8,128)(2,1)S(1)} %pad_maximum_fusion.refs_0_), channel_id=1, source_target_pairs={{0,64},{32,480},{64,128},{96,32},{128,192},{160,96},{192,256},{224... | collective-permute-start | bytes 1572872 | tf_op jit(solution)/shard_map/ppermute | solution.py:36
  12.5 1.9 %collective-permute-start = (bf16[2,256,512]{2,1,0:T(8,128)(2,1)S(1)}, bf16[2,256,512]{2,1,0:T(8,128)(2,1)S(1)}, u32[]{:S(2)}, u32[]{:S(2)}) collective-permute-start(bf16[2,256,512]{2,1,0:T(8,128)(2,1)S(1)} %pad_maximum_fusion.refs_0_), channel_id=1, source_target_pairs={{0,32},{32,0},{64,96},{96,64},{128,160},{160,128},{192,224},{224,1... | collective-permute-start | bytes 1572872 | tf_op jit(solution)/shard_map/ppermute | solution.py:41
  14.5 0.8 copy.15
  15.4 0.2 select_reduce_fusion.3
  15.6 0.1 add.212
  15.8 0.8 copy.14
  16.5 0.1 fusion.2
  17.0 0.1 stack_reshape.9
  17.2 0.2 select_reduce_fusion
  17.5 0.1 reduce_max.18
  17.7 0.1 stack.95
  17.8 0.1 select_reduce_fusion.2
  18.1 0.5 collective-permute-done.1.refs_1_.refs_6_
  18.6 5.0 %collective-permute-start.2 = (bf16[2,256,512]{2,1,0:T(8,128)(2,1)S(1)}, bf16[2,256,512]{2,1,0:T(8,128)(2,1)S(1)}, u32[]{:S(2)}, u32[]{:S(2)}) collective-permute-start(bf16[2,256,512]{2,1,0:T(8,128)(2,1)S(1)} %collective-permute-done.1.refs_1_.refs_6_), channel_id=1, source_target_pairs={{0,64},{32,480},{64,128},{96,32},{128,192},{160,96},{192,256},{224... | collective-permute-start | bytes 1572872 | tf_op jit(solution)/shard_map/ppermute | solution.py:36
  23.7 1.9 %collective-permute-start.9 = (bf16[2,256,512]{2,1,0:T(8,128)(2,1)S(1)}, bf16[2,256,512]{2,1,0:T(8,128)(2,1)S(1)}, u32[]{:S(2)}, u32[]{:S(2)}) collective-permute-start(bf16[2,256,512]{2,1,0:T(8,128)(2,1)S(1)} %collective-permute-done.refs_0_.refs_5_), channel_id=1, source_target_pairs={{0,64},{32,480},{64,128},{96,32},{128,192},{160,96},{192,256},{224... | collective-permute-start | bytes 1572872 | tf_op jit(solution)/shard_map/ppermute | solution.py:36
  25.7 2.0 %shard_map.93 = (bf16[2,128,512]{2,1,0:T(8,128)(2,1)S(1)}, bf16[2,128,512]{2,1,0:T(8,128)(2,1)S(1)}, bf16[2,128,512]{2,1,0:T(8,128)(2,1)S(1)}, bf16[2,128,512]{2,1,0:T(8,128)(2,1)S(1)}) custom-call(s32[4]{0:T(128)S(1)} %pad_add_fusion.6.table, bf16[256,512]{1,0:T(8,128)(2,1)S(1)} %copy-done.1, bf16[256,512]{1,0:T(8,128)(2,1)S(1)} %copy-done), custom_call_target="tpu_custom_call" | custom-call | bytes 2097152 | tf_op jit(solution)/shard_map/pallas_call | solution.py:116
  27.7 2.8 %collective-permute-start.3 = (bf16[2,128,512]{2,1,0:T(8,128)(2,1)S(1)}, bf16[2,128,512]{2,1,0:T(8,128)(2,1)S(1)}, u32[]{:S(2)}, u32[]{:S(2)}) collective-permute-start(bf16[2,128,512]{2,1,0:T(8,128)(2,1)S(1)} %get-tuple-element.51), channel_id=1, source_target_pairs={{0,1},{1,2},{2,3},{3,4},{4,5},{5,6},{6,7},{7,8},{8,9},{9,10},{10,1... | collective-permute-start | bytes 786440 | tf_op jit(solution)/shard_map/ppermute | solution.py:46
  30.5 4.7 %collective-permute-start.4 = (bf16[2,128,512]{2,1,0:T(8,128)(2,1)S(1)}, bf16[2,128,512]{2,1,0:T(8,128)(2,1)S(1)}, u32[]{:S(2)}, u32[]{:S(2)}) collective-permute-start(bf16[2,128,512]{2,1,0:T(8,128)(2,1)S(1)} %get-tuple-element.52), channel_id=1, source_target_pairs={{0,2},{1,3},{2,4},{3,5},{4,6},{5,7},{6,8},{7,9},{8,10},{9,11},{10,... | collective-permute-start | bytes 786440 | tf_op jit(solution)/shard_map/ppermute | solution.py:46
  35.2 3.9 %collective-permute-done.3.refs_3_ = bf16[2,128,512]{2,1,0:T(8,128)(2,1)S(1)} collective-permute-done((bf16[2,128,512]{2,1,0:T(8,128)(2,1)S(1)}, bf16[2,128,512]{2,1,0:T(8,128)(2,1)S(1)}, u32[]{:S(2)}, u32[]{:S(2)}) %collective-permute-start.3) | collective-permute-done | bytes 262176 | tf_op jit(solution)/shard_map/ppermute | solution.py:46
  39.0 3.7 %collective-permute-done.4.refs_4_ = bf16[2,128,512]{2,1,0:T(8,128)(2,1)S(1)} collective-permute-done((bf16[2,128,512]{2,1,0:T(8,128)(2,1)S(1)}, bf16[2,128,512]{2,1,0:T(8,128)(2,1)S(1)}, u32[]{:S(2)}, u32[]{:S(2)}) %collective-permute-start.4) | collective-permute-done | bytes 262176 | tf_op jit(solution)/shard_map/ppermute | solution.py:46
  42.7 1.9 %collective-permute-start.5 = (bf16[2,256,512]{2,1,0:T(8,128)(2,1)S(1)}, bf16[2,256,512]{2,1,0:T(8,128)(2,1)S(1)}, u32[]{:S(2)}, u32[]{:S(2)}) collective-permute-start(bf16[2,256,512]{2,1,0:T(8,128)(2,1)S(1)} %collective-permute-done.2.refs_2_.refs_7_), channel_id=1, source_target_pairs={{0,64},{32,480},{64,128},{96,32},{128,192},{160,96},{192,256},{224... | collective-permute-start | bytes 1572872 | tf_op jit(solution)/shard_map/ppermute | solution.py:36
  44.6 1.9 %collective-permute-start.10 = (bf16[2,256,512]{2,1,0:T(8,128)(2,1)S(1)}, bf16[2,256,512]{2,1,0:T(8,128)(2,1)S(1)}, u32[]{:S(2)}, u32[]{:S(2)}) collective-permute-start(bf16[2,256,512]{2,1,0:T(8,128)(2,1)S(1)} %collective-permute-done.9.refs_5_.refs_10_), channel_id=1, source_target_pairs={{0,64},{32,480},{64,128},{96,32},{128,192},{160,96},{192,256},{224... | collective-permute-start | bytes 1572872 | tf_op jit(solution)/shard_map/ppermute | solution.py:36
  46.6 4.2 %collective-permute-start.6 = (bf16[2,128,512]{2,1,0:T(8,128)(2,1)S(1)}, bf16[2,128,512]{2,1,0:T(8,128)(2,1)S(1)}, u32[]{:S(2)}, u32[]{:S(2)}) collective-permute-start(bf16[2,128,512]{2,1,0:T(8,128)(2,1)S(1)} %get-tuple-element.58), channel_id=1, source_target_pairs={{2,0},{3,1},{4,2},{5,3},{6,4},{7,5},{8,6},{9,7},{10,8},{11,9},{12,... | collective-permute-start | bytes 786440 | tf_op jit(solution)/shard_map/ppermute | solution.py:46
  50.8 1.9 %collective-permute-start.7 = (bf16[2,128,512]{2,1,0:T(8,128)(2,1)S(1)}, bf16[2,128,512]{2,1,0:T(8,128)(2,1)S(1)}, u32[]{:S(2)}, u32[]{:S(2)}) collective-permute-start(bf16[2,128,512]{2,1,0:T(8,128)(2,1)S(1)} %get-tuple-element.59), channel_id=1, source_target_pairs={{1,0},{2,1},{3,2},{4,3},{5,4},{6,5},{7,6},{8,7},{9,8},{10,9},{11,1... | collective-permute-start | bytes 786440 | tf_op jit(solution)/shard_map/ppermute | solution.py:46
  52.8 5.7 %collective-permute-done.6.refs_1_ = bf16[2,128,512]{2,1,0:T(8,128)(2,1)S(1)} collective-permute-done((bf16[2,128,512]{2,1,0:T(8,128)(2,1)S(1)}, bf16[2,128,512]{2,1,0:T(8,128)(2,1)S(1)}, u32[]{:S(2)}, u32[]{:S(2)}) %collective-permute-start.6) | collective-permute-done | bytes 262176 | tf_op jit(solution)/shard_map/ppermute | solution.py:46
  58.5 4.7 %collective-permute-done.7.refs_2_ = bf16[2,128,512]{2,1,0:T(8,128)(2,1)S(1)} collective-permute-done((bf16[2,128,512]{2,1,0:T(8,128)(2,1)S(1)}, bf16[2,128,512]{2,1,0:T(8,128)(2,1)S(1)}, u32[]{:S(2)}, u32[]{:S(2)}) %collective-permute-start.7) | collective-permute-done | bytes 262176 | tf_op jit(solution)/shard_map/ppermute | solution.py:46
  63.2 1.9 %collective-permute-start.11 = (bf16[2,256,512]{2,1,0:T(8,128)(2,1)S(1)}, bf16[2,256,512]{2,1,0:T(8,128)(2,1)S(1)}, u32[]{:S(2)}, u32[]{:S(2)}) collective-permute-start(bf16[2,256,512]{2,1,0:T(8,128)(2,1)S(1)} %collective-permute-done.10.refs_6_.refs_11_), channel_id=1, source_target_pairs={{0,64},{32,480},{64,128},{96,32},{128,192},{160,96},{192,256},{224... | collective-permute-start | bytes 1572872 | tf_op jit(solution)/shard_map/ppermute | solution.py:36
  65.1 1.9 %collective-permute-start.8 = (bf16[2,256,512]{2,1,0:T(8,128)(2,1)S(1)}, bf16[2,256,512]{2,1,0:T(8,128)(2,1)S(1)}, u32[]{:S(2)}, u32[]{:S(2)}) collective-permute-start(bf16[2,256,512]{2,1,0:T(8,128)(2,1)S(1)} %collective-permute-done.5.refs_3_.refs_8_), channel_id=1, source_target_pairs={{0,64},{32,480},{64,128},{96,32},{128,192},{160,96},{192,256},{224... | collective-permute-start | bytes 1572872 | tf_op jit(solution)/shard_map/ppermute | solution.py:36
  67.0 6.8 %collective-permute-done.11.refs_7_.refs_12_ = bf16[2,256,512]{2,1,0:T(8,128)(2,1)S(1)} collective-permute-done((bf16[2,256,512]{2,1,0:T(8,128)(2,1)S(1)}, bf16[2,256,512]{2,1,0:T(8,128)(2,1)S(1)}, u32[]{:S(2)}, u32[]{:S(2)}) %collective-permute-start.11) | collective-permute-done | bytes 524320 | tf_op jit(solution)/shard_map/ppermute | solution.py:36
  73.8 5.6 %collective-permute-done.8.refs_4_.refs_9_ = bf16[2,256,512]{2,1,0:T(8,128)(2,1)S(1)} collective-permute-done((bf16[2,256,512]{2,1,0:T(8,128)(2,1)S(1)}, bf16[2,256,512]{2,1,0:T(8,128)(2,1)S(1)}, u32[]{:S(2)}, u32[]{:S(2)}) %collective-permute-start.8) | collective-permute-done | bytes 524320 | tf_op jit(solution)/shard_map/ppermute | solution.py:36
  79.4 1.1 shard_map.94
  80.5 5.5 %collective-permute-start.12 = (bf16[6,2,128,512]{3,2,1,0:T(8,128)(2,1)S(1)}, bf16[6,2,128,512]{3,2,1,0:T(8,128)(2,1)S(1)}, u32[]{:S(2)}, u32[]{:S(2)}) collective-permute-start(bf16[6,2,128,512]{3,2,1,0:T(8,128)(2,1)S(1)} %shard_map.94), channel_id=1, source_target_pairs={{0,32},{32,0},{64,96},{96,64},{128,160},{160,128},{192,224},{224,1... | collective-permute-start | bytes 4718600 | tf_op jit(solution)/shard_map/ppermute | solution.py:41
  86.1 3.0 %collective-permute-done.12.refs_13_ = bf16[6,2,128,512]{3,2,1,0:T(8,128)(2,1)S(1)} collective-permute-done((bf16[6,2,128,512]{3,2,1,0:T(8,128)(2,1)S(1)}, bf16[6,2,128,512]{3,2,1,0:T(8,128)(2,1)S(1)}, u32[]{:S(2)}, u32[]{:S(2)}) %collective-permute-start.12) | collective-permute-done | bytes 1572896 | tf_op jit(solution)/shard_map/ppermute | solution.py:41
  89.1 13.5 %shard_map.95 = (bf16[2,128,512]{2,1,0:T(8,128)(2,1)}, bf16[2,128,512]{2,1,0:T(8,128)(2,1)}, bf16[2,2,128,512]{3,2,1,0:T(8,128)(2,1)S(1)}, bf16[6,2,128,512]{3,2...) custom-call(s32[4,14]{1,0:T(4,128)S(1)} %pad_add_fusion.table, ...), custom_call_target="tpu_custom_call" | custom-call | flops 1409286144 | bytes 12582912 | tf_op jit(solution)/shard_map/pallas_call | solution.py:222
  102.6 2.3 %collective-permute-start.13 = (bf16[6,2,128,512]{3,2,1,0:T(8,128)(2,1)S(1)}, bf16[6,2,128,512]{3,2,1,0:T(8,128)(2,1)S(1)}, u32[]{:S(2)}, u32[]{:S(2)}) collective-permute-start(bf16[6,2,128,512]{3,2,1,0:T(8,128)(2,1)S(1)} %get-tuple-element.73.mine), channel_id=1, source_target_pairs={{0,32},{32,0},{64,96},{96,64},{128,160},{160,128},{192,224},{224,1... | collective-permute-start | bytes 4718600 | tf_op jit(solution)/shard_map/ppermute | solution.py:41
  104.9 3.0 %collective-permute-done.13.theirs = bf16[6,2,128,512]{3,2,1,0:T(8,128)(2,1)S(1)} collective-permute-done((bf16[6,2,128,512]{3,2,1,0:T(8,128)(2,1)S(1)}, bf16[6,2,128,512]{3,2,1,0:T(8,128)(2,1)S(1)}, u32[]{:S(2)}, u32[]{:S(2)}) %collective-permute-start.13) | collective-permute-done | bytes 1572896 | tf_op jit(solution)/shard_map/ppermute | solution.py:41
  107.9 0.9 shard_map.96
  108.9 1.9 %collective-permute-start.14 = (bf16[2,2,128,512]{3,2,1,0:T(8,128)(2,1)S(1)}, bf16[2,2,128,512]{3,2,1,0:T(8,128)(2,1)S(1)}, u32[]{:S(2)}, u32[]{:S(2)}) collective-permute-start(bf16[2,2,128,512]{3,2,1,0:T(8,128)(2,1)S(1)} %get-tuple-element.75), channel_id=1, source_target_pairs={{0,64},{32,480},{64,128},{96,32},{128,192},{160,96},{192,256},{224... | collective-permute-start | bytes 1572872 | tf_op jit(solution)/shard_map/ppermute | solution.py:36
  110.8 1.9 %collective-permute-start.20 = (bf16[2,2,128,512]{3,2,1,0:T(8,128)(2,1)S(1)}, bf16[2,2,128,512]{3,2,1,0:T(8,128)(2,1)S(1)}, u32[]{:S(2)}, u32[]{:S(2)}) collective-permute-start(bf16[2,2,128,512]{3,2,1,0:T(8,128)(2,1)S(1)} %get-tuple-element.85), channel_id=1, source_target_pairs={{0,64},{32,480},{64,128},{96,32},{128,192},{160,96},{192,256},{224... | collective-permute-start | bytes 1572872 | tf_op jit(solution)/shard_map/ppermute | solution.py:36
  112.7 0.9 shard_map.97
  113.7 5.4 %collective-permute-done.14 = bf16[2,2,128,512]{3,2,1,0:T(8,128)(2,1)S(1)} collective-permute-done((bf16[2,2,128,512]{3,2,1,0:T(8,128)(2,1)S(1)}, bf16[2,2,128,512]{3,2,1,0:T(8,128)(2,1)S(1)}, u32[]{:S(2)}, u32[]{:S(2)}) %collective-permute-start.14) | collective-permute-done | bytes 524320 | tf_op jit(solution)/shard_map/ppermute | solution.py:36
  119.1 0.1 add_convert_fusion.4
  119.2 2.8 %collective-permute-start.15 = (bf16[2,2,128,512]{3,2,1,0:T(8,128)(2,1)S(1)}, bf16[2,2,128,512]{3,2,1,0:T(8,128)(2,1)S(1)}, u32[]{:S(2)}, u32[]{:S(2)}) collective-permute-start(bf16[2,2,128,512]{3,2,1,0:T(8,128)(2,1)S(1)} %add_convert_fusion.4), channel_id=1, source_target_pairs={{0,64},{32,480},{64,128},{96,32},{128,192},{160,96},{192,256},{224... | collective-permute-start | bytes 1572872 | tf_op jit(solution)/shard_map/ppermute | solution.py:36
  122.1 3.5 %collective-permute-start.16 = (bf16[2,128,512]{2,1,0:T(8,128)(2,1)S(1)}, bf16[2,128,512]{2,1,0:T(8,128)(2,1)S(1)}, u32[]{:S(2)}, u32[]{:S(2)}) collective-permute-start(bf16[2,128,512]{2,1,0:T(8,128)(2,1)S(1)} %get-tuple-element.80), channel_id=1, source_target_pairs={{0,2},{1,3},{2,4},{3,5},{4,6},{5,7},{6,8},{7,9},{8,10},{9,11},{10,... | collective-permute-start | bytes 786440 | tf_op jit(solution)/shard_map/ppermute | solution.py:46
  125.6 6.3 %collective-permute-start.17 = (bf16[2,128,512]{2,1,0:T(8,128)(2,1)S(1)}, bf16[2,128,512]{2,1,0:T(8,128)(2,1)S(1)}, u32[]{:S(2)}, u32[]{:S(2)}) collective-permute-start(bf16[2,128,512]{2,1,0:T(8,128)(2,1)S(1)} %get-tuple-element.81), channel_id=1, source_target_pairs={{0,1},{1,2},{2,3},{3,4},{4,5},{5,6},{6,7},{7,8},{8,9},{9,10},{10,1... | collective-permute-start | bytes 786440 | tf_op jit(solution)/shard_map/ppermute | solution.py:46
  132.0 0.1 add_convert_fusion.1
  132.1 1.9 %collective-permute-start.21 = (bf16[2,2,128,512]{3,2,1,0:T(8,128)(2,1)S(1)}, bf16[2,2,128,512]{3,2,1,0:T(8,128)(2,1)S(1)}, u32[]{:S(2)}, u32[]{:S(2)}) collective-permute-start(bf16[2,2,128,512]{3,2,1,0:T(8,128)(2,1)S(1)} %add_convert_fusion.1), channel_id=1, source_target_pairs={{0,64},{32,480},{64,128},{96,32},{128,192},{160,96},{192,256},{224... | collective-permute-start | bytes 1572872 | tf_op jit(solution)/shard_map/ppermute | solution.py:36
  134.0 5.0 %collective-permute-done.17.refs_1_ = bf16[2,128,512]{2,1,0:T(8,128)(2,1)S(1)} collective-permute-done((bf16[2,128,512]{2,1,0:T(8,128)(2,1)S(1)}, bf16[2,128,512]{2,1,0:T(8,128)(2,1)S(1)}, u32[]{:S(2)}, u32[]{:S(2)}) %collective-permute-start.17) | collective-permute-done | bytes 262176 | tf_op jit(solution)/shard_map/ppermute | solution.py:46
  139.0 0.1 add_convert_fusion.3
  139.2 1.9 %collective-permute-start.18 = (bf16[2,2,128,512]{3,2,1,0:T(8,128)(2,1)S(1)}, bf16[2,2,128,512]{3,2,1,0:T(8,128)(2,1)S(1)}, u32[]{:S(2)}, u32[]{:S(2)}) collective-permute-start(bf16[2,2,128,512]{3,2,1,0:T(8,128)(2,1)S(1)} %add_convert_fusion.3), channel_id=1, source_target_pairs={{0,64},{32,480},{64,128},{96,32},{128,192},{160,96},{192,256},{224... | collective-permute-start | bytes 1572872 | tf_op jit(solution)/shard_map/ppermute | solution.py:36
  141.1 1.2 collective-permute-done.21
  142.3 0.1 add_convert_fusion
  142.5 2.8 %collective-permute-start.22 = (bf16[2,2,128,512]{3,2,1,0:T(8,128)(2,1)S(1)}, bf16[2,2,128,512]{3,2,1,0:T(8,128)(2,1)S(1)}, u32[]{:S(2)}, u32[]{:S(2)}) collective-permute-start(bf16[2,2,128,512]{3,2,1,0:T(8,128)(2,1)S(1)} %add_convert_fusion), channel_id=1, source_target_pairs={{0,64},{32,480},{64,128},{96,32},{128,192},{160,96},{192,256},{224... | collective-permute-start | bytes 1572872 | tf_op jit(solution)/shard_map/ppermute | solution.py:36
  145.3 4.1 %collective-permute-done.18 = bf16[2,2,128,512]{3,2,1,0:T(8,128)(2,1)S(1)} collective-permute-done((bf16[2,2,128,512]{3,2,1,0:T(8,128)(2,1)S(1)}, bf16[2,2,128,512]{3,2,1,0:T(8,128)(2,1)S(1)}, u32[]{:S(2)}, u32[]{:S(2)}) %collective-permute-start.18) | collective-permute-done | bytes 524320 | tf_op jit(solution)/shard_map/ppermute | solution.py:36
  149.4 0.1 add_convert_fusion.2
  149.5 2.8 %collective-permute-start.19 = (bf16[2,2,128,512]{3,2,1,0:T(8,128)(2,1)S(1)}, bf16[2,2,128,512]{3,2,1,0:T(8,128)(2,1)S(1)}, u32[]{:S(2)}, u32[]{:S(2)}) collective-permute-start(bf16[2,2,128,512]{3,2,1,0:T(8,128)(2,1)S(1)} %add_convert_fusion.2), channel_id=1, source_target_pairs={{0,64},{32,480},{64,128},{96,32},{128,192},{160,96},{192,256},{224... | collective-permute-start | bytes 1572872 | tf_op jit(solution)/shard_map/ppermute | solution.py:36
  152.4 2.6 %collective-permute-done.22 = bf16[2,2,128,512]{3,2,1,0:T(8,128)(2,1)S(1)} collective-permute-done((bf16[2,2,128,512]{3,2,1,0:T(8,128)(2,1)S(1)}, bf16[2,2,128,512]{3,2,1,0:T(8,128)(2,1)S(1)}, u32[]{:S(2)}, u32[]{:S(2)}) %collective-permute-start.22) | collective-permute-done | bytes 524320 | tf_op jit(solution)/shard_map/ppermute | solution.py:36
  155.0 5.8 %collective-permute-start.23 = (bf16[2,2,128,512]{3,2,1,0:T(8,128)(2,1)S(1)}, bf16[2,2,128,512]{3,2,1,0:T(8,128)(2,1)S(1)}, u32[]{:S(2)}, u32[]{:S(2)}) collective-permute-start(bf16[2,2,128,512]{3,2,1,0:T(8,128)(2,1)S(1)} %collective-permute-done.22), channel_id=1, source_target_pairs={{0,32},{32,0},{64,96},{96,64},{128,160},{160,128},{192,224},{224,1... | collective-permute-start | bytes 1572872 | tf_op jit(solution)/shard_map/ppermute | solution.py:41
  160.8 1.9 %collective-permute-start.24 = (bf16[2,128,512]{2,1,0:T(8,128)(2,1)S(1)}, bf16[2,128,512]{2,1,0:T(8,128)(2,1)S(1)}, u32[]{:S(2)}, u32[]{:S(2)}) collective-permute-start(bf16[2,128,512]{2,1,0:T(8,128)(2,1)S(1)} %get-tuple-element.90), channel_id=1, source_target_pairs={{1,0},{2,1},{3,2},{4,3},{5,4},{6,5},{7,6},{8,7},{9,8},{10,9},{11,1... | collective-permute-start | bytes 786440 | tf_op jit(solution)/shard_map/ppermute | solution.py:46
  162.7 4.2 %collective-permute-start.25 = (bf16[2,128,512]{2,1,0:T(8,128)(2,1)S(1)}, bf16[2,128,512]{2,1,0:T(8,128)(2,1)S(1)}, u32[]{:S(2)}, u32[]{:S(2)}) collective-permute-start(bf16[2,128,512]{2,1,0:T(8,128)(2,1)S(1)} %get-tuple-element.91), channel_id=1, source_target_pairs={{2,0},{3,1},{4,2},{5,3},{6,4},{7,5},{8,6},{9,7},{10,8},{11,9},{12,... | collective-permute-start | bytes 786440 | tf_op jit(solution)/shard_map/ppermute | solution.py:46
  166.9 3.7 %collective-permute-done.24.refs_2_ = bf16[2,128,512]{2,1,0:T(8,128)(2,1)S(1)} collective-permute-done((bf16[2,128,512]{2,1,0:T(8,128)(2,1)S(1)}, bf16[2,128,512]{2,1,0:T(8,128)(2,1)S(1)}, u32[]{:S(2)}, u32[]{:S(2)}) %collective-permute-start.24) | collective-permute-done | bytes 262176 | tf_op jit(solution)/shard_map/ppermute | solution.py:46
  170.6 10.4 %collective-permute-done.25.refs_3_ = bf16[2,128,512]{2,1,0:T(8,128)(2,1)S(1)} collective-permute-done((bf16[2,128,512]{2,1,0:T(8,128)(2,1)S(1)}, bf16[2,128,512]{2,1,0:T(8,128)(2,1)S(1)}, u32[]{:S(2)}, u32[]{:S(2)}) %collective-permute-start.25) | collective-permute-done | bytes 262176 | tf_op jit(solution)/shard_map/ppermute | solution.py:46
  181.0 2.0 %shard_map.98 = (bf16[256,512]{1,0:T(8,128)(2,1)}, bf16[256,512]{1,0:T(8,128)(2,1)}) custom-call(s32[6]{0:T(128)S(1)} %pad_add_fusion.7.table, bf16[2,2,128,512]{3,2,1,0:T(8,128)(2,1)S(1)} %get-tuple-element.72.near, bf16[6,2,128,512]{3,2,1,0:T(8,128)(2,1)S(1)} %collective-permute-done.13.theirs, ...), custom_call_target="tpu_custom_call" | custom-call | flops 4194304 | bytes 6291456 | tf_op jit(solution)/shard_map/pallas_call | solution.py:295
  (42 shorter events, 1.2 us)
Async XLA Ops:
  0.6 25.0 %copy-start.1 = (bf16[256,512]{1,0:T(8,128)(2,1)S(1)}, bf16[256,512]{1,0:T(8,128)(2,1)}, u32[]{:S(2)}) copy-start(bf16[256,512]{1,0:T(8,128)(2,1)} %keys.1) | copy-start | bytes 786436
  0.6 25.0 %copy-start = (bf16[256,512]{1,0:T(8,128)(2,1)S(1)}, bf16[256,512]{1,0:T(8,128)(2,1)}, u32[]{:S(2)}) copy-start(bf16[256,512]{1,0:T(8,128)(2,1)} %values.1) | copy-start | bytes 786436
  1.8 16.8 %collective-permute-start.1 = (bf16[2,256,512]{2,1,0:T(8,128)(2,1)S(1)}, bf16[2,256,512]{2,1,0:T(8,128)(2,1)S(1)}, u32[]{:S(2)}, u32[]{:S(2)}) collective-permute-start(bf16[2,256,512]{2,1,0:T(8,128)(2,1)S(1)} %pad_maximum_fusion.refs_0_), channel_id=1, source_target_pairs={{0,64},{32,480},{64,128},{96,32},{128,192},{160,96},{192,256},{224... | collective-permute-start | bytes 1572872 | tf_op jit(solution)/shard_map/ppermute | solution.py:36
  12.5 11.3 %collective-permute-start = (bf16[2,256,512]{2,1,0:T(8,128)(2,1)S(1)}, bf16[2,256,512]{2,1,0:T(8,128)(2,1)S(1)}, u32[]{:S(2)}, u32[]{:S(2)}) collective-permute-start(bf16[2,256,512]{2,1,0:T(8,128)(2,1)S(1)} %pad_maximum_fusion.refs_0_), channel_id=1, source_target_pairs={{0,32},{32,0},{64,96},{96,64},{128,160},{160,128},{192,224},{224,1... | collective-permute-start | bytes 1572872 | tf_op jit(solution)/shard_map/ppermute | solution.py:41
  18.6 24.1 %collective-permute-start.2 = (bf16[2,256,512]{2,1,0:T(8,128)(2,1)S(1)}, bf16[2,256,512]{2,1,0:T(8,128)(2,1)S(1)}, u32[]{:S(2)}, u32[]{:S(2)}) collective-permute-start(bf16[2,256,512]{2,1,0:T(8,128)(2,1)S(1)} %collective-permute-done.1.refs_1_.refs_6_), channel_id=1, source_target_pairs={{0,64},{32,480},{64,128},{96,32},{128,192},{160,96},{192,256},{224... | collective-permute-start | bytes 1572872 | tf_op jit(solution)/shard_map/ppermute | solution.py:36
  23.7 20.9 %collective-permute-start.9 = (bf16[2,256,512]{2,1,0:T(8,128)(2,1)S(1)}, bf16[2,256,512]{2,1,0:T(8,128)(2,1)S(1)}, u32[]{:S(2)}, u32[]{:S(2)}) collective-permute-start(bf16[2,256,512]{2,1,0:T(8,128)(2,1)S(1)} %collective-permute-done.refs_0_.refs_5_), channel_id=1, source_target_pairs={{0,64},{32,480},{64,128},{96,32},{128,192},{160,96},{192,256},{224... | collective-permute-start | bytes 1572872 | tf_op jit(solution)/shard_map/ppermute | solution.py:36
  27.7 11.4 %collective-permute-start.3 = (bf16[2,128,512]{2,1,0:T(8,128)(2,1)S(1)}, bf16[2,128,512]{2,1,0:T(8,128)(2,1)S(1)}, u32[]{:S(2)}, u32[]{:S(2)}) collective-permute-start(bf16[2,128,512]{2,1,0:T(8,128)(2,1)S(1)} %get-tuple-element.51), channel_id=1, source_target_pairs={{0,1},{1,2},{2,3},{3,4},{4,5},{5,6},{6,7},{7,8},{8,9},{9,10},{10,1... | collective-permute-start | bytes 786440 | tf_op jit(solution)/shard_map/ppermute | solution.py:46
  30.5 12.2 %collective-permute-start.4 = (bf16[2,128,512]{2,1,0:T(8,128)(2,1)S(1)}, bf16[2,128,512]{2,1,0:T(8,128)(2,1)S(1)}, u32[]{:S(2)}, u32[]{:S(2)}) collective-permute-start(bf16[2,128,512]{2,1,0:T(8,128)(2,1)S(1)} %get-tuple-element.52), channel_id=1, source_target_pairs={{0,2},{1,3},{2,4},{3,5},{4,6},{5,7},{6,8},{7,9},{8,10},{9,11},{10,... | collective-permute-start | bytes 786440 | tf_op jit(solution)/shard_map/ppermute | solution.py:46
  42.7 20.5 %collective-permute-start.5 = (bf16[2,256,512]{2,1,0:T(8,128)(2,1)S(1)}, bf16[2,256,512]{2,1,0:T(8,128)(2,1)S(1)}, u32[]{:S(2)}, u32[]{:S(2)}) collective-permute-start(bf16[2,256,512]{2,1,0:T(8,128)(2,1)S(1)} %collective-permute-done.2.refs_2_.refs_7_), channel_id=1, source_target_pairs={{0,64},{32,480},{64,128},{96,32},{128,192},{160,96},{192,256},{224... | collective-permute-start | bytes 1572872 | tf_op jit(solution)/shard_map/ppermute | solution.py:36
  44.6 18.6 %collective-permute-start.10 = (bf16[2,256,512]{2,1,0:T(8,128)(2,1)S(1)}, bf16[2,256,512]{2,1,0:T(8,128)(2,1)S(1)}, u32[]{:S(2)}, u32[]{:S(2)}) collective-permute-start(bf16[2,256,512]{2,1,0:T(8,128)(2,1)S(1)} %collective-permute-done.9.refs_5_.refs_10_), channel_id=1, source_target_pairs={{0,64},{32,480},{64,128},{96,32},{128,192},{160,96},{192,256},{224... | collective-permute-start | bytes 1572872 | tf_op jit(solution)/shard_map/ppermute | solution.py:36
  46.6 42.5 %copy-start.2 = (bf16[256,512]{1,0:T(8,128)(2,1)S(1)}, bf16[256,512]{1,0:T(8,128)(2,1)}, u32[]{:S(2)}) copy-start(bf16[256,512]{1,0:T(8,128)(2,1)} %param.6) | copy-start | bytes 786436
  46.6 42.5 %copy-start.3 = (bf16[256,512]{1,0:T(8,128)(2,1)S(1)}, bf16[256,512]{1,0:T(8,128)(2,1)}, u32[]{:S(2)}) copy-start(bf16[256,512]{1,0:T(8,128)(2,1)} %param.9) | copy-start | bytes 786436
  46.6 11.9 %collective-permute-start.6 = (bf16[2,128,512]{2,1,0:T(8,128)(2,1)S(1)}, bf16[2,128,512]{2,1,0:T(8,128)(2,1)S(1)}, u32[]{:S(2)}, u32[]{:S(2)}) collective-permute-start(bf16[2,128,512]{2,1,0:T(8,128)(2,1)S(1)} %get-tuple-element.58), channel_id=1, source_target_pairs={{2,0},{3,1},{4,2},{5,3},{6,4},{7,5},{8,6},{9,7},{10,8},{11,9},{12,... | collective-permute-start | bytes 786440 | tf_op jit(solution)/shard_map/ppermute | solution.py:46
  50.8 12.3 %collective-permute-start.7 = (bf16[2,128,512]{2,1,0:T(8,128)(2,1)S(1)}, bf16[2,128,512]{2,1,0:T(8,128)(2,1)S(1)}, u32[]{:S(2)}, u32[]{:S(2)}) collective-permute-start(bf16[2,128,512]{2,1,0:T(8,128)(2,1)S(1)} %get-tuple-element.59), channel_id=1, source_target_pairs={{1,0},{2,1},{3,2},{4,3},{5,4},{6,5},{7,6},{8,7},{9,8},{10,9},{11,1... | collective-permute-start | bytes 786440 | tf_op jit(solution)/shard_map/ppermute | solution.py:46
  63.2 10.6 %collective-permute-start.11 = (bf16[2,256,512]{2,1,0:T(8,128)(2,1)S(1)}, bf16[2,256,512]{2,1,0:T(8,128)(2,1)S(1)}, u32[]{:S(2)}, u32[]{:S(2)}) collective-permute-start(bf16[2,256,512]{2,1,0:T(8,128)(2,1)S(1)} %collective-permute-done.10.refs_6_.refs_11_), channel_id=1, source_target_pairs={{0,64},{32,480},{64,128},{96,32},{128,192},{160,96},{192,256},{224... | collective-permute-start | bytes 1572872 | tf_op jit(solution)/shard_map/ppermute | solution.py:36
  65.1 14.3 %collective-permute-start.8 = (bf16[2,256,512]{2,1,0:T(8,128)(2,1)S(1)}, bf16[2,256,512]{2,1,0:T(8,128)(2,1)S(1)}, u32[]{:S(2)}, u32[]{:S(2)}) collective-permute-start(bf16[2,256,512]{2,1,0:T(8,128)(2,1)S(1)} %collective-permute-done.5.refs_3_.refs_8_), channel_id=1, source_target_pairs={{0,64},{32,480},{64,128},{96,32},{128,192},{160,96},{192,256},{224... | collective-permute-start | bytes 1572872 | tf_op jit(solution)/shard_map/ppermute | solution.py:36
  80.5 8.6 %collective-permute-start.12 = (bf16[6,2,128,512]{3,2,1,0:T(8,128)(2,1)S(1)}, bf16[6,2,128,512]{3,2,1,0:T(8,128)(2,1)S(1)}, u32[]{:S(2)}, u32[]{:S(2)}) collective-permute-start(bf16[6,2,128,512]{3,2,1,0:T(8,128)(2,1)S(1)} %shard_map.94), channel_id=1, source_target_pairs={{0,32},{32,0},{64,96},{96,64},{128,160},{160,128},{192,224},{224,1... | collective-permute-start | bytes 4718600 | tf_op jit(solution)/shard_map/ppermute | solution.py:41
  102.6 5.3 %collective-permute-start.13 = (bf16[6,2,128,512]{3,2,1,0:T(8,128)(2,1)S(1)}, bf16[6,2,128,512]{3,2,1,0:T(8,128)(2,1)S(1)}, u32[]{:S(2)}, u32[]{:S(2)}) collective-permute-start(bf16[6,2,128,512]{3,2,1,0:T(8,128)(2,1)S(1)} %get-tuple-element.73.mine), channel_id=1, source_target_pairs={{0,32},{32,0},{64,96},{96,64},{128,160},{160,128},{192,224},{224,1... | collective-permute-start | bytes 4718600 | tf_op jit(solution)/shard_map/ppermute | solution.py:41
  108.9 10.2 %collective-permute-start.14 = (bf16[2,2,128,512]{3,2,1,0:T(8,128)(2,1)S(1)}, bf16[2,2,128,512]{3,2,1,0:T(8,128)(2,1)S(1)}, u32[]{:S(2)}, u32[]{:S(2)}) collective-permute-start(bf16[2,2,128,512]{3,2,1,0:T(8,128)(2,1)S(1)} %get-tuple-element.75), channel_id=1, source_target_pairs={{0,64},{32,480},{64,128},{96,32},{128,192},{160,96},{192,256},{224... | collective-permute-start | bytes 1572872 | tf_op jit(solution)/shard_map/ppermute | solution.py:36
  110.8 21.1 %collective-permute-start.20 = (bf16[2,2,128,512]{3,2,1,0:T(8,128)(2,1)S(1)}, bf16[2,2,128,512]{3,2,1,0:T(8,128)(2,1)S(1)}, u32[]{:S(2)}, u32[]{:S(2)}) collective-permute-start(bf16[2,2,128,512]{3,2,1,0:T(8,128)(2,1)S(1)} %get-tuple-element.85), channel_id=1, source_target_pairs={{0,64},{32,480},{64,128},{96,32},{128,192},{160,96},{192,256},{224... | collective-permute-start | bytes 1572872 | tf_op jit(solution)/shard_map/ppermute | solution.py:36
  119.2 19.8 %collective-permute-start.15 = (bf16[2,2,128,512]{3,2,1,0:T(8,128)(2,1)S(1)}, bf16[2,2,128,512]{3,2,1,0:T(8,128)(2,1)S(1)}, u32[]{:S(2)}, u32[]{:S(2)}) collective-permute-start(bf16[2,2,128,512]{3,2,1,0:T(8,128)(2,1)S(1)} %add_convert_fusion.4), channel_id=1, source_target_pairs={{0,64},{32,480},{64,128},{96,32},{128,192},{160,96},{192,256},{224... | collective-permute-start | bytes 1572872 | tf_op jit(solution)/shard_map/ppermute | solution.py:36
  122.1 11.9 %collective-permute-start.16 = (bf16[2,128,512]{2,1,0:T(8,128)(2,1)S(1)}, bf16[2,128,512]{2,1,0:T(8,128)(2,1)S(1)}, u32[]{:S(2)}, u32[]{:S(2)}) collective-permute-start(bf16[2,128,512]{2,1,0:T(8,128)(2,1)S(1)} %get-tuple-element.80), channel_id=1, source_target_pairs={{0,2},{1,3},{2,4},{3,5},{4,6},{5,7},{6,8},{7,9},{8,10},{9,11},{10,... | collective-permute-start | bytes 786440 | tf_op jit(solution)/shard_map/ppermute | solution.py:46
  125.6 13.4 %collective-permute-start.17 = (bf16[2,128,512]{2,1,0:T(8,128)(2,1)S(1)}, bf16[2,128,512]{2,1,0:T(8,128)(2,1)S(1)}, u32[]{:S(2)}, u32[]{:S(2)}) collective-permute-start(bf16[2,128,512]{2,1,0:T(8,128)(2,1)S(1)} %get-tuple-element.81), channel_id=1, source_target_pairs={{0,1},{1,2},{2,3},{3,4},{4,5},{5,6},{6,7},{7,8},{8,9},{9,10},{10,1... | collective-permute-start | bytes 786440 | tf_op jit(solution)/shard_map/ppermute | solution.py:46
  132.1 10.2 %collective-permute-start.21 = (bf16[2,2,128,512]{3,2,1,0:T(8,128)(2,1)S(1)}, bf16[2,2,128,512]{3,2,1,0:T(8,128)(2,1)S(1)}, u32[]{:S(2)}, u32[]{:S(2)}) collective-permute-start(bf16[2,2,128,512]{3,2,1,0:T(8,128)(2,1)S(1)} %add_convert_fusion.1), channel_id=1, source_target_pairs={{0,64},{32,480},{64,128},{96,32},{128,192},{160,96},{192,256},{224... | collective-permute-start | bytes 1572872 | tf_op jit(solution)/shard_map/ppermute | solution.py:36
  139.2 10.2 %collective-permute-start.18 = (bf16[2,2,128,512]{3,2,1,0:T(8,128)(2,1)S(1)}, bf16[2,2,128,512]{3,2,1,0:T(8,128)(2,1)S(1)}, u32[]{:S(2)}, u32[]{:S(2)}) collective-permute-start(bf16[2,2,128,512]{3,2,1,0:T(8,128)(2,1)S(1)} %add_convert_fusion.3), channel_id=1, source_target_pairs={{0,64},{32,480},{64,128},{96,32},{128,192},{160,96},{192,256},{224... | collective-permute-start | bytes 1572872 | tf_op jit(solution)/shard_map/ppermute | solution.py:36
  142.5 12.5 %collective-permute-start.22 = (bf16[2,2,128,512]{3,2,1,0:T(8,128)(2,1)S(1)}, bf16[2,2,128,512]{3,2,1,0:T(8,128)(2,1)S(1)}, u32[]{:S(2)}, u32[]{:S(2)}) collective-permute-start(bf16[2,2,128,512]{3,2,1,0:T(8,128)(2,1)S(1)} %add_convert_fusion), channel_id=1, source_target_pairs={{0,64},{32,480},{64,128},{96,32},{128,192},{160,96},{192,256},{224... | collective-permute-start | bytes 1572872 | tf_op jit(solution)/shard_map/ppermute | solution.py:36
  149.5 31.5 %collective-permute-start.19 = (bf16[2,2,128,512]{3,2,1,0:T(8,128)(2,1)S(1)}, bf16[2,2,128,512]{3,2,1,0:T(8,128)(2,1)S(1)}, u32[]{:S(2)}, u32[]{:S(2)}) collective-permute-start(bf16[2,2,128,512]{3,2,1,0:T(8,128)(2,1)S(1)} %add_convert_fusion.2), channel_id=1, source_target_pairs={{0,64},{32,480},{64,128},{96,32},{128,192},{160,96},{192,256},{224... | collective-permute-start | bytes 1572872 | tf_op jit(solution)/shard_map/ppermute | solution.py:36
  155.0 26.0 %collective-permute-start.23 = (bf16[2,2,128,512]{3,2,1,0:T(8,128)(2,1)S(1)}, bf16[2,2,128,512]{3,2,1,0:T(8,128)(2,1)S(1)}, u32[]{:S(2)}, u32[]{:S(2)}) collective-permute-start(bf16[2,2,128,512]{3,2,1,0:T(8,128)(2,1)S(1)} %collective-permute-done.22), channel_id=1, source_target_pairs={{0,32},{32,0},{64,96},{96,64},{128,160},{160,128},{192,224},{224,1... | collective-permute-start | bytes 1572872 | tf_op jit(solution)/shard_map/ppermute | solution.py:41
  160.8 9.8 %collective-permute-start.24 = (bf16[2,128,512]{2,1,0:T(8,128)(2,1)S(1)}, bf16[2,128,512]{2,1,0:T(8,128)(2,1)S(1)}, u32[]{:S(2)}, u32[]{:S(2)}) collective-permute-start(bf16[2,128,512]{2,1,0:T(8,128)(2,1)S(1)} %get-tuple-element.90), channel_id=1, source_target_pairs={{1,0},{2,1},{3,2},{4,3},{5,4},{6,5},{7,6},{8,7},{9,8},{10,9},{11,1... | collective-permute-start | bytes 786440 | tf_op jit(solution)/shard_map/ppermute | solution.py:46
  162.7 18.3 %collective-permute-start.25 = (bf16[2,128,512]{2,1,0:T(8,128)(2,1)S(1)}, bf16[2,128,512]{2,1,0:T(8,128)(2,1)S(1)}, u32[]{:S(2)}, u32[]{:S(2)}) collective-permute-start(bf16[2,128,512]{2,1,0:T(8,128)(2,1)S(1)} %get-tuple-element.91), channel_id=1, source_target_pairs={{2,0},{3,1},{4,2},{5,3},{6,4},{7,5},{8,6},{9,7},{10,8},{11,9},{12,... | collective-permute-start | bytes 786440 | tf_op jit(solution)/shard_map/ppermute | solution.py:46

commit v5 on v4

--- a/solution.py
+++ b/solution.py
@@ -22,7 +22,6 @@
 PAIRS = D // 128
 BF = jnp.bfloat16
 F32 = jnp.float32
-OFFSETS = (-2, -1, 1, 2)
 
 HBM = pl.BlockSpec(memory_space=pltpu.HBM)
 VMEM = pl.BlockSpec(memory_space=pltpu.VMEM)
@@ -41,9 +40,15 @@
     return lax.ppermute(array, "group", [(g, g ^ 1) for g in range(size)])
 
 
-def shifted(array, by):
-    size = lax.axis_size("dom")
-    return lax.ppermute(array, "dom", [(i, i + by) for i in range(size) if 0 <= i + by < size])
+def dom_step(array, by):
+    groups, doms = lax.axis_size("group"), lax.axis_size("dom")
+    pairs = []
+    for g in range(groups):
+        for i in range(doms):
+            to = i + (by if g % 2 == 0 else -by)
+            if 0 <= to < doms:
+                pairs.append((g * doms + i, g * doms + to))
+    return lax.ppermute(array, ("group", "dom"), pairs)
 
 
 def place_of(cluster, chip, core, chips):
@@ -100,12 +105,13 @@
 
 
 def offer_kernel(table, keys, values, *refs):
-    outs, sem = refs[: 2 * W], refs[2 * W]
+    outs, sem = refs[:2], refs[2]
     copies = []
-    for t, out in enumerate(outs):
+    for t in range(2 * W):
         rows = pl.ds(pl.multiple_of(table[t] * BS, BS), BS)
         for half, source in enumerate((keys, values)):
-            copies.append(pltpu.make_async_copy(source.at[rows, :], out.at[half], sem.at[t, half]))
+            target = outs[t // W].at[t % W, half]
+            copies.append(pltpu.make_async_copy(source.at[rows, :], target, sem.at[t, half]))
     for copy in copies:
         copy.start()
     for copy in copies:
@@ -115,9 +121,9 @@
 def offer(table, keys, values):
     return pl.pallas_call(
         offer_kernel,
-        out_shape=(jax.ShapeDtypeStruct((2, BS, D), BF),) * (2 * W),
+        out_shape=(jax.ShapeDtypeStruct((W, 2, BS, D), BF),) * 2,
         in_specs=[SMEM, HBM, HBM],
-        out_specs=(VMEM,) * (2 * W),
+        out_specs=(VMEM,) * 2,
         scratch_shapes=[pltpu.SemaphoreType.DMA((2 * W, 2))],
         compiler_params=pltpu.CompilerParams(vmem_limit_bytes=4 * 2**20),
         cost_estimate=pl.CostEstimate(flops=0, bytes_accessed=2 * 2**20, transcendentals=0),
@@ -169,9 +175,9 @@
 
 
 def attend_kernel(table, q_ref, g_ref, *refs):
-    own, near, places, picked = refs[0], refs[1:5], refs[5:13], refs[13]
-    att_ref, gq_ref, own_out, far_out = refs[14:18]
-    near_out, (listed, totals, sem) = refs[18:22], refs[22:]
+    own, (one, two, other), places, picked = refs[0], refs[1:4], refs[4:12], refs[12]
+    near = (one.at[0], two.at[0], other.at[0], other.at[1])
+    att_ref, gq_ref, own_out, far_out, keep_out, give_out, listed, totals, sem = refs[13:]
 
     def bring(source, s, j):
         pltpu.make_async_copy(source, listed.at[s, :, pl.ds(j * BS, BS), :], sem.at[s]).start()
@@ -213,8 +219,8 @@
 
     lax.fori_loop(0, NB * PAIRS, body, 0, unroll=4)
     own_out[...] = totals[:NB].astype(BF)
-    for t in range(2 * W):
-        near_out[t][...] = totals[NB + t].astype(BF)
+    keep_out[...] = totals[NB : NB + W].astype(BF)
+    give_out[...] = totals[NB + W : NEAR].astype(BF)
     far_out[...] = totals[NEAR:].astype(BF)
 
 
@@ -227,9 +233,9 @@
             jax.ShapeDtypeStruct((NB, 2, BS, D), BF),
             jax.ShapeDtypeStruct((FAR, 2, BS, D), BF),
         )
-        + (jax.ShapeDtypeStruct((2, BS, D), BF),) * (2 * W),
-        in_specs=[SMEM, VMEM, VMEM] + [HBM] * 14,
-        out_specs=(VMEM,) * (4 + 2 * W),
+        + (jax.ShapeDtypeStruct((W, 2, BS, D), BF),) * 2,
+        in_specs=[SMEM, VMEM, VMEM] + [HBM] * 13,
+        out_specs=(VMEM,) * 6,
         scratch_shapes=[
             pltpu.VMEM((NB, 2, ROWS, D), BF),
             pltpu.VMEM((NEAR + FAR, 2, BS, D), F32),
@@ -278,7 +284,8 @@
 
 
 def close_kernel(table, near, theirs, from_a, from_b, *refs):
-    returned, (gk_ref, gv_ref) = refs[:4], refs[4:]
+    (one, two, other), (gk_ref, gv_ref) = refs[:3], refs[3:]
+    returned = (one.at[0], two.at[0], other.at[0], other.at[1])
     for s in range(NB):
         for half, out in enumerate((gk_ref, gv_ref)):
             total = near[s, half].astype(F32)
@@ -295,7 +302,7 @@
     return pl.pallas_call(
         close_kernel,
         out_shape=(jax.ShapeDtypeStruct((NB * BS, D), BF),) * 2,
-        in_specs=[SMEM] + [VMEM] * 8,
+        in_specs=[SMEM] + [VMEM] * 7,
         out_specs=(VMEM, VMEM),
         compiler_params=pltpu.CompilerParams(vmem_limit_bytes=12 * 2**20),
         cost_estimate=pl.CostEstimate(flops=2**22, bytes_accessed=6 * 2**20, transcendentals=0),
@@ -318,10 +325,12 @@
     padded = jnp.pad(local_list, ((W * NB, W * NB), (0, 0)), constant_values=-1)
     around = lax.dynamic_slice_in_dim(padded, dom * NB, (2 * W + 1) * NB, 0).reshape(2 * W + 1, NB * LOC)
     given = jnp.max(jnp.where(around // NB == dom, around % NB, 0), axis=1).astype(i32)
-    given = jnp.concatenate([given[:W], given[W + 1 :]])
+    up, down = given[W + 1 :], given[:W][::-1]
+    given = jnp.where(core == 0, jnp.concatenate([up, down]), jnp.concatenate([down, up]))
     local = around[W].reshape(NB, LOC)
     holder = local // NB - dom
-    near_code = jnp.where(holder == 0, 0, jnp.where(holder > 0, 3 - holder, 2 - holder))
+    direct = (holder < 0) == (core == 0)
+    near_code = jnp.where(holder == 0, 0, jnp.abs(holder) + jnp.where(direct, 0, W))
     near_key = jnp.where(holder == 0, local % NB, NB - 1 + near_code)
 
     far_rows = far_list[0].reshape(groups, FAR)
@@ -356,21 +365,21 @@
 
     flow_b = [ring_step(sibling)]
     flow_a.append(ring_step(flow_a[0]))
-    offered = offer(given, keys, values)
+    keep, give = offer(given, keys, values)
+    given_here = swap_cores(give)
     flow_b.append(ring_step(flow_b[0]))
-    up = [shifted(offered[t], OFFSETS[t]) for t in (2, 3)]
-    flow_a[1], *up = lax.optimization_barrier((flow_a[1], *up))
+    one = dom_step(jnp.stack([keep[0], given_here[0]]), 1)
+    flow_a[1], one = lax.optimization_barrier((flow_a[1], one))
     flow_a.append(ring_step(flow_a[1]))
-    behind = lax.optimization_barrier((offered[0], offered[1], *up))
-    up = list(behind[2:])
-    down = [shifted(behind[t], OFFSETS[t]) for t in (0, 1)]
-    near = down + up
+    keep, given_here, flow_b[1] = lax.optimization_barrier((keep, given_here, flow_b[1]))
+    two = dom_step(jnp.stack([keep[1], given_here[1]]), 2)
     flow_b.append(ring_step(flow_b[1]))
-    flow_a[2], near = lax.optimization_barrier((flow_a[2], near))
+    flow_a[2], two = lax.optimization_barrier((flow_a[2], two))
     flow_a.append(ring_step(flow_a[2]))
+    near = (one, two, swap_cores(jnp.stack([one[1], two[1]])))
 
     picked = swap_cores(pick(pick_table, [sibling] + flow_a + flow_b))
-    attended, grad_queries, own_terms, far_terms, *near_terms = attend(
+    attended, grad_queries, own_terms, far_terms, keep, give = attend(
         table,
         queries.reshape(NB, BS, D),
         cotangent.reshape(NB, BS, D),
@@ -389,14 +398,19 @@
 
     back_a = ring_step(start_a)
     back_b = ring_step(start_b)
+    give, a3 = lax.optimization_barrier((give, a3))
+    given_here = swap_cores(give)
     back_a = ring_step(joined(back_a, a3))
     back_b = ring_step(joined(back_b, b2))
-    returned = [shifted(near_terms[t], -OFFSETS[t]) for t in (0, 1)]
-    back_a, *behind = lax.optimization_barrier((back_a, near_terms[2], near_terms[3], *returned))
-    returned = behind[2:] + [shifted(behind[t - 2], -OFFSETS[t]) for t in (2, 3)]
+    two = dom_step(jnp.stack([keep[1], given_here[1]]), -2)
+    back_a, two = lax.optimization_barrier((back_a, two))
     back_a = ring_step(joined(back_a, a2))
+    keep, given_here, back_b = lax.optimization_barrier((keep, given_here, back_b))
+    one = dom_step(jnp.stack([keep[0], given_here[0]]), -1)
     back_b = ring_step(joined(back_b, b1))
+    back_a, one = lax.optimization_barrier((back_a, one))
     back_a = ring_step(joined(back_a, a1))
+    returned = (one, two, swap_cores(jnp.stack([one[1], two[1]])))
     back_b = swap_cores(back_b)
 
     grad_keys, grad_values = close(last, own_terms, sibling_terms, back_a, back_b, returned)

time: 184 us -> 168 us (0.913)
  the two profiles are of different devices: /device:TPU:29 before, /device:TPU:30 now
where the time goes in v5:
time: 168 us; the launch traced here: 167 us
  starting transfers between devices  76.4 us (45%)
  waiting for transfers between devices  62.7 us (37%)
  Pallas kernels  20.2 us (12%)
  other arithmetic  3.3 us (2%)
  local copies, waits for them, and re-layouts  2.84 us (2%)
    ppermute x14, waiting for transfers between devices, ring_step(): lax.ppermute(array, 'group', [(g, (g + (2 if g % 2 == 0 else -2)) % size)...  39.1 us
    ppermute x14, starting transfers between devices, ring_step(): lax.ppermute(array, 'group', [(g, (g + (2 if g % 2 == 0 else -2)) % size)...  35.4 us
    ppermute x8, starting transfers between devices, swap_cores(): return lax.ppermute(array, 'group', [(g, g ^ 1) for g in range(size)])  27.2 us
    ppermute x4, waiting for transfers between devices, dom_step(): return lax.ppermute(array, ('group', 'dom'), pairs)  19 us
    ppermute x4, starting transfers between devices, dom_step(): return lax.ppermute(array, ('group', 'dom'), pairs)  13.8 us
    pallas_call x1, Pallas kernels, attend(): pl.pallas_call(attend_kernel, out_shape=(jax.ShapeDtypeStruct((NB, BS, D)...  13.5 us
    ppermute x8, waiting for transfers between devices, swap_cores(): return lax.ppermute(array, 'group', [(g, g ^ 1) for g in range(size)])  4.53 us
  transfers between devices with their start and end apart: 26, of which 15 were waited for; matrix products, arithmetic and copies ran while one was open for 3% of the time, Pallas kernels for 2%

profile of v5, /device:TPU:30, one launch (start us, length us, event | category | flops | bytes accessed | tf_op | source)
XLA Modules:
  0.0 166.8 jit_solution(2746339776464408051)
XLA Ops:
  0.7 1.1 pad_maximum_fusion.refs_0_
  1.8 4.3 %collective-permute-start.1 = (bf16[2,256,512]{2,1,0:T(8,128)(2,1)S(1)}, bf16[2,256,512]{2,1,0:T(8,128)(2,1)S(1)}, u32[]{:S(2)}, u32[]{:S(2)}) collective-permute-start(bf16[2,256,512]{2,1,0:T(8,128)(2,1)S(1)} %pad_maximum_fusion.refs_0_), channel_id=1, source_target_pairs={{0,64},{32,480},{64,128},{96,32},{128,192},{160,96},{192,256},{224... | collective-permute-start | bytes 1572872 | tf_op jit(solution)/shard_map/ppermute | solution.py:35
  6.1 8.1 %collective-permute-start = (bf16[2,256,512]{2,1,0:T(8,128)(2,1)S(1)}, bf16[2,256,512]{2,1,0:T(8,128)(2,1)S(1)}, u32[]{:S(2)}, u32[]{:S(2)}) collective-permute-start(bf16[2,256,512]{2,1,0:T(8,128)(2,1)S(1)} %pad_maximum_fusion.refs_0_), channel_id=1, source_target_pairs={{0,32},{32,0},{64,96},{96,64},{128,160},{160,128},{192,224},{224,1... | collective-permute-start | bytes 1572872 | tf_op jit(solution)/shard_map/ppermute | solution.py:40
  14.3 0.8 copy.15
  15.2 0.2 select_reduce_fusion.3
  15.4 0.1 add.216
  15.6 0.8 copy.14
  16.3 0.1 fusion.2
  16.6 0.1 eq.193
  16.8 0.1 stack.113
  16.9 0.1 select_reduce_fusion.2
  17.5 0.1 reduce_max.18
  17.7 0.1 rev.3
  17.9 0.2 select_reduce_fusion
  18.1 1.9 %collective-permute-start.6 = (bf16[2,256,512]{2,1,0:T(8,128)(2,1)S(1)}, bf16[2,256,512]{2,1,0:T(8,128)(2,1)S(1)}, u32[]{:S(2)}, u32[]{:S(2)}) collective-permute-start(bf16[2,256,512]{2,1,0:T(8,128)(2,1)S(1)} %collective-permute-done.refs_0_.refs_4_), channel_id=1, source_target_pairs={{0,64},{32,480},{64,128},{96,32},{128,192},{160,96},{192,256},{224... | collective-permute-start | bytes 1572872 | tf_op jit(solution)/shard_map/ppermute | solution.py:35
  20.1 2.0 %shard_map.93 = (bf16[2,2,128,512]{3,2,1,0:T(8,128)(2,1)S(1)}, bf16[2,2,128,512]{3,2,1,0:T(8,128)(2,1)S(1)}) custom-call(s32[4]{0:T(128)S(1)} %broadcast_select_fusion.2.table, bf16[256,512]{1,0:T(8,128)(2,1)S(1)} %copy-done.1, bf16[256,512]{1,0:T(8,128)(2,1)S(1)} %copy-done), custom_call_target="tpu_custom_call" | custom-call | bytes 2097152 | tf_op jit(solution)/shard_map/pallas_call | solution.py:122
  22.1 2.6 %collective-permute-start.3 = (bf16[2,2,128,512]{3,2,1,0:T(8,128)(2,1)S(1)}, bf16[2,2,128,512]{3,2,1,0:T(8,128)(2,1)S(1)}, u32[]{:S(2)}, u32[]{:S(2)}) collective-permute-start(bf16[2,2,128,512]{3,2,1,0:T(8,128)(2,1)S(1)} %get-tuple-element.47), channel_id=1, source_target_pairs={{0,32},{32,0},{64,96},{96,64},{128,160},{160,128},{192,224},{224,1... | collective-permute-start | bytes 1572872 | tf_op jit(solution)/shard_map/ppermute | solution.py:40
  24.7 3.0 %collective-permute-start.2 = (bf16[2,256,512]{2,1,0:T(8,128)(2,1)S(1)}, bf16[2,256,512]{2,1,0:T(8,128)(2,1)S(1)}, u32[]{:S(2)}, u32[]{:S(2)}) collective-permute-start(bf16[2,256,512]{2,1,0:T(8,128)(2,1)S(1)} %collective-permute-done.1.refs_1_.refs_5_), channel_id=1, source_target_pairs={{0,64},{32,480},{64,128},{96,32},{128,192},{160,96},{192,256},{224... | collective-permute-start | bytes 1572872 | tf_op jit(solution)/shard_map/ppermute | solution.py:35
  27.7 2.7 %collective-permute-done.6.refs_5_.refs_9_ = bf16[2,256,512]{2,1,0:T(8,128)(2,1)S(1)} collective-permute-done((bf16[2,256,512]{2,1,0:T(8,128)(2,1)S(1)}, bf16[2,256,512]{2,1,0:T(8,128)(2,1)S(1)}, u32[]{:S(2)}, u32[]{:S(2)}) %collective-permute-start.6) | collective-permute-done | bytes 524320 | tf_op jit(solution)/shard_map/ppermute | solution.py:35
  30.4 1.9 %collective-permute-start.7 = (bf16[2,256,512]{2,1,0:T(8,128)(2,1)S(1)}, bf16[2,256,512]{2,1,0:T(8,128)(2,1)S(1)}, u32[]{:S(2)}, u32[]{:S(2)}) collective-permute-start(bf16[2,256,512]{2,1,0:T(8,128)(2,1)S(1)} %collective-permute-done.6.refs_5_.refs_9_), channel_id=1, source_target_pairs={{0,64},{32,480},{64,128},{96,32},{128,192},{160,96},{192,256},{224... | collective-permute-start | bytes 1572872 | tf_op jit(solution)/shard_map/ppermute | solution.py:35
  32.4 4.6 %collective-permute-start.4 = (bf16[2,2,128,512]{3,2,1,0:T(8,128)(2,1)S(1)}, bf16[2,2,128,512]{3,2,1,0:T(8,128)(2,1)S(1)}, u32[]{:S(2)}, u32[]{:S(2)}) collective-permute-start(bf16[2,2,128,512]{3,2,1,0:T(8,128)(2,1)S(1)} %pad_maximum_fusion.1), channel_id=1, source_target_pairs={{0,1},{1,2},{2,3},{3,4},{4,5},{5,6},{6,7},{7,8},{8,9},{9,10},{10,1... | collective-permute-start | bytes 1572872 | tf_op jit(solution)/shard_map/ppermute | solution.py:51
  37.1 5.6 %collective-permute-done.7.refs_6_.refs_10_ = bf16[2,256,512]{2,1,0:T(8,128)(2,1)S(1)} collective-permute-done((bf16[2,256,512]{2,1,0:T(8,128)(2,1)S(1)}, bf16[2,256,512]{2,1,0:T(8,128)(2,1)S(1)}, u32[]{:S(2)}, u32[]{:S(2)}) %collective-permute-start.7) | collective-permute-done | bytes 524320 | tf_op jit(solution)/shard_map/ppermute | solution.py:35
  42.8 1.0 collective-permute-done.4.refs_1_
  43.7 1.9 %collective-permute-start.5 = (bf16[2,256,512]{2,1,0:T(8,128)(2,1)S(1)}, bf16[2,256,512]{2,1,0:T(8,128)(2,1)S(1)}, u32[]{:S(2)}, u32[]{:S(2)}) collective-permute-start(bf16[2,256,512]{2,1,0:T(8,128)(2,1)S(1)} %collective-permute-done.2.refs_2_.refs_6_), channel_id=1, source_target_pairs={{0,64},{32,480},{64,128},{96,32},{128,192},{160,96},{192,256},{224... | collective-permute-start | bytes 1572872 | tf_op jit(solution)/shard_map/ppermute | solution.py:35
  45.7 5.3 %collective-permute-start.8 = (bf16[2,2,128,512]{3,2,1,0:T(8,128)(2,1)S(1)}, bf16[2,2,128,512]{3,2,1,0:T(8,128)(2,1)S(1)}, u32[]{:S(2)}, u32[]{:S(2)}) collective-permute-start(bf16[2,2,128,512]{3,2,1,0:T(8,128)(2,1)S(1)} %pad_maximum_fusion.2), channel_id=1, source_target_pairs={{0,2},{1,3},{2,4},{3,5},{4,6},{5,7},{6,8},{7,9},{8,10},{9,11},{10,... | collective-permute-start | bytes 1572872 | tf_op jit(solution)/shard_map/ppermute | solution.py:51
  51.0 3.0 %collective-permute-start.11 = (bf16[2,256,512]{2,1,0:T(8,128)(2,1)S(1)}, bf16[2,256,512]{2,1,0:T(8,128)(2,1)S(1)}, u32[]{:S(2)}, u32[]{:S(2)}) collective-permute-start(bf16[2,256,512]{2,1,0:T(8,128)(2,1)S(1)} %collective-permute-done.7.refs_6_.refs_10_), channel_id=1, source_target_pairs={{0,64},{32,480},{64,128},{96,32},{128,192},{160,96},{192,256},{224... | collective-permute-start | bytes 1572872 | tf_op jit(solution)/shard_map/ppermute | solution.py:35
  54.0 2.0 %collective-permute-done.5.refs_3_.refs_7_ = bf16[2,256,512]{2,1,0:T(8,128)(2,1)S(1)} collective-permute-done((bf16[2,256,512]{2,1,0:T(8,128)(2,1)S(1)}, bf16[2,256,512]{2,1,0:T(8,128)(2,1)S(1)}, u32[]{:S(2)}, u32[]{:S(2)}) %collective-permute-start.5) | collective-permute-done | bytes 524320 | tf_op jit(solution)/shard_map/ppermute | solution.py:35
  56.0 7.9 %collective-permute-done.8.refs_2_ = bf16[2,2,128,512]{3,2,1,0:T(8,128)(2,1)S(1)} collective-permute-done((bf16[2,2,128,512]{3,2,1,0:T(8,128)(2,1)S(1)}, bf16[2,2,128,512]{3,2,1,0:T(8,128)(2,1)S(1)}, u32[]{:S(2)}, u32[]{:S(2)}) %collective-permute-start.8) | collective-permute-done | bytes 524320 | tf_op jit(solution)/shard_map/ppermute | solution.py:51
  63.9 3.0 %collective-permute-start.10 = (bf16[2,256,512]{2,1,0:T(8,128)(2,1)S(1)}, bf16[2,256,512]{2,1,0:T(8,128)(2,1)S(1)}, u32[]{:S(2)}, u32[]{:S(2)}) collective-permute-start(bf16[2,256,512]{2,1,0:T(8,128)(2,1)S(1)} %collective-permute-done.5.refs_3_.refs_7_), channel_id=1, source_target_pairs={{0,64},{32,480},{64,128},{96,32},{128,192},{160,96},{192,256},{224... | collective-permute-start | bytes 1572872 | tf_op jit(solution)/shard_map/ppermute | solution.py:35
  66.9 9.3 %collective-permute-done.10.refs_4_.refs_8_ = bf16[2,256,512]{2,1,0:T(8,128)(2,1)S(1)} collective-permute-done((bf16[2,256,512]{2,1,0:T(8,128)(2,1)S(1)}, bf16[2,256,512]{2,1,0:T(8,128)(2,1)S(1)}, u32[]{:S(2)}, u32[]{:S(2)}) %collective-permute-start.10) | collective-permute-done | bytes 524320 | tf_op jit(solution)/shard_map/ppermute | solution.py:35
  76.2 1.1 shard_map.94
  77.3 2.1 %collective-permute-start.12 = (bf16[6,2,128,512]{3,2,1,0:T(8,128)(2,1)S(1)}, bf16[6,2,128,512]{3,2,1,0:T(8,128)(2,1)S(1)}, u32[]{:S(2)}, u32[]{:S(2)}) collective-permute-start(bf16[6,2,128,512]{3,2,1,0:T(8,128)(2,1)S(1)} %shard_map.94), channel_id=1, source_target_pairs={{0,32},{32,0},{64,96},{96,64},{128,160},{160,128},{192,224},{224,1... | collective-permute-start | bytes 4718600 | tf_op jit(solution)/shard_map/ppermute | solution.py:40
  79.5 2.4 %collective-permute-start.9 = (bf16[2,2,128,512]{3,2,1,0:T(8,128)(2,1)S(1)}, bf16[2,2,128,512]{3,2,1,0:T(8,128)(2,1)S(1)}, u32[]{:S(2)}, u32[]{:S(2)}) collective-permute-start(bf16[2,2,128,512]{3,2,1,0:T(8,128)(2,1)S(1)} %pad_maximum_fusion.3), channel_id=1, source_target_pairs={{0,32},{32,0},{64,96},{96,64},{128,160},{160,128},{192,224},{224,1... | collective-permute-start | bytes 1572872 | tf_op jit(solution)/shard_map/ppermute | solution.py:40
  81.9 1.6 collective-permute-done.9.refs_3_
  83.5 13.5 %shard_map.95 = (bf16[2,128,512]{2,1,0:T(8,128)(2,1)}, bf16[2,128,512]{2,1,0:T(8,128)(2,1)}, bf16[2,2,128,512]{3,2,1,0:T(8,128)(2,1)S(1)}, bf16[6,2,128,512]{3,2...) custom-call(s32[4,14]{1,0:T(4,128)S(1)} %pad_add_fusion.table, ...), custom_call_target="tpu_custom_call" | custom-call | flops 1409286144 | bytes 12582912 | tf_op jit(solution)/shard_map/pallas_call | solution.py:228
  97.0 2.4 %collective-permute-start.13 = (bf16[6,2,128,512]{3,2,1,0:T(8,128)(2,1)S(1)}, bf16[6,2,128,512]{3,2,1,0:T(8,128)(2,1)S(1)}, u32[]{:S(2)}, u32[]{:S(2)}) collective-permute-start(bf16[6,2,128,512]{3,2,1,0:T(8,128)(2,1)S(1)} %get-tuple-element.61.mine), channel_id=1, source_target_pairs={{0,32},{32,0},{64,96},{96,64},{128,160},{160,128},{192,224},{224,1... | collective-permute-start | bytes 4718600 | tf_op jit(solution)/shard_map/ppermute | solution.py:40
  99.4 2.9 %collective-permute-done.13.theirs = bf16[6,2,128,512]{3,2,1,0:T(8,128)(2,1)S(1)} collective-permute-done((bf16[6,2,128,512]{3,2,1,0:T(8,128)(2,1)S(1)}, bf16[6,2,128,512]{3,2,1,0:T(8,128)(2,1)S(1)}, u32[]{:S(2)}, u32[]{:S(2)}) %collective-permute-start.13) | collective-permute-done | bytes 1572896 | tf_op jit(solution)/shard_map/ppermute | solution.py:40
  102.3 0.7 shard_map.96
  103.1 1.9 %collective-permute-start.14 = (bf16[2,2,128,512]{3,2,1,0:T(8,128)(2,1)S(1)}, bf16[2,2,128,512]{3,2,1,0:T(8,128)(2,1)S(1)}, u32[]{:S(2)}, u32[]{:S(2)}) collective-permute-start(bf16[2,2,128,512]{3,2,1,0:T(8,128)(2,1)S(1)} %get-tuple-element.63), channel_id=1, source_target_pairs={{0,64},{32,480},{64,128},{96,32},{128,192},{160,96},{192,256},{224... | collective-permute-start | bytes 1572872 | tf_op jit(solution)/shard_map/ppermute | solution.py:35
  105.0 0.9 shard_map.97
  105.9 4.0 %collective-permute-start.16 = (bf16[2,2,128,512]{3,2,1,0:T(8,128)(2,1)S(1)}, bf16[2,2,128,512]{3,2,1,0:T(8,128)(2,1)S(1)}, u32[]{:S(2)}, u32[]{:S(2)}) collective-permute-start(bf16[2,2,128,512]{3,2,1,0:T(8,128)(2,1)S(1)} %get-tuple-element.69), channel_id=1, source_target_pairs={{0,32},{32,0},{64,96},{96,64},{128,160},{160,128},{192,224},{224,1... | collective-permute-start | bytes 1572872 | tf_op jit(solution)/shard_map/ppermute | solution.py:40
  109.9 2.3 %collective-permute-start.19 = (bf16[2,2,128,512]{3,2,1,0:T(8,128)(2,1)S(1)}, bf16[2,2,128,512]{3,2,1,0:T(8,128)(2,1)S(1)}, u32[]{:S(2)}, u32[]{:S(2)}) collective-permute-start(bf16[2,2,128,512]{3,2,1,0:T(8,128)(2,1)S(1)} %get-tuple-element.72), channel_id=1, source_target_pairs={{0,64},{32,480},{64,128},{96,32},{128,192},{160,96},{192,256},{224... | collective-permute-start | bytes 1572872 | tf_op jit(solution)/shard_map/ppermute | solution.py:35
  112.2 3.1 %collective-permute-done.14 = bf16[2,2,128,512]{3,2,1,0:T(8,128)(2,1)S(1)} collective-permute-done((bf16[2,2,128,512]{3,2,1,0:T(8,128)(2,1)S(1)}, bf16[2,2,128,512]{3,2,1,0:T(8,128)(2,1)S(1)}, u32[]{:S(2)}, u32[]{:S(2)}) %collective-permute-start.14) | collective-permute-done | bytes 524320 | tf_op jit(solution)/shard_map/ppermute | solution.py:35
  115.3 0.1 add_convert_fusion.4
  115.5 1.9 %collective-permute-start.15 = (bf16[2,2,128,512]{3,2,1,0:T(8,128)(2,1)S(1)}, bf16[2,2,128,512]{3,2,1,0:T(8,128)(2,1)S(1)}, u32[]{:S(2)}, u32[]{:S(2)}) collective-permute-start(bf16[2,2,128,512]{3,2,1,0:T(8,128)(2,1)S(1)} %add_convert_fusion.4), channel_id=1, source_target_pairs={{0,64},{32,480},{64,128},{96,32},{128,192},{160,96},{192,256},{224... | collective-permute-start | bytes 1572872 | tf_op jit(solution)/shard_map/ppermute | solution.py:35
  117.5 1.9 %collective-permute-start.17 = (bf16[2,2,128,512]{3,2,1,0:T(8,128)(2,1)S(1)}, bf16[2,2,128,512]{3,2,1,0:T(8,128)(2,1)S(1)}, u32[]{:S(2)}, u32[]{:S(2)}) collective-permute-start(bf16[2,2,128,512]{3,2,1,0:T(8,128)(2,1)S(1)} %pad_maximum_fusion.4), channel_id=1, source_target_pairs={{2,0},{3,1},{4,2},{5,3},{6,4},{7,5},{8,6},{9,7},{10,8},{11,9},{12,... | collective-permute-start | bytes 1572872 | tf_op jit(solution)/shard_map/ppermute | solution.py:51
  119.4 2.8 %collective-permute-done.19 = bf16[2,2,128,512]{3,2,1,0:T(8,128)(2,1)S(1)} collective-permute-done((bf16[2,2,128,512]{3,2,1,0:T(8,128)(2,1)S(1)}, bf16[2,2,128,512]{3,2,1,0:T(8,128)(2,1)S(1)}, u32[]{:S(2)}, u32[]{:S(2)}) %collective-permute-start.19) | collective-permute-done | bytes 524320 | tf_op jit(solution)/shard_map/ppermute | solution.py:35
  122.2 0.1 add_convert_fusion.2
  122.3 1.9 %collective-permute-start.20 = (bf16[2,2,128,512]{3,2,1,0:T(8,128)(2,1)S(1)}, bf16[2,2,128,512]{3,2,1,0:T(8,128)(2,1)S(1)}, u32[]{:S(2)}, u32[]{:S(2)}) collective-permute-start(bf16[2,2,128,512]{3,2,1,0:T(8,128)(2,1)S(1)} %add_convert_fusion.2), channel_id=1, source_target_pairs={{0,64},{32,480},{64,128},{96,32},{128,192},{160,96},{192,256},{224... | collective-permute-start | bytes 1572872 | tf_op jit(solution)/shard_map/ppermute | solution.py:35
  124.3 3.5 %collective-permute-done.15 = bf16[2,2,128,512]{3,2,1,0:T(8,128)(2,1)S(1)} collective-permute-done((bf16[2,2,128,512]{3,2,1,0:T(8,128)(2,1)S(1)}, bf16[2,2,128,512]{3,2,1,0:T(8,128)(2,1)S(1)}, u32[]{:S(2)}, u32[]{:S(2)}) %collective-permute-start.15) | collective-permute-done | bytes 524320 | tf_op jit(solution)/shard_map/ppermute | solution.py:35
  127.8 4.5 %collective-permute-done.17.refs_1_ = bf16[2,2,128,512]{3,2,1,0:T(8,128)(2,1)S(1)} collective-permute-done((bf16[2,2,128,512]{3,2,1,0:T(8,128)(2,1)S(1)}, bf16[2,2,128,512]{3,2,1,0:T(8,128)(2,1)S(1)}, u32[]{:S(2)}, u32[]{:S(2)}) %collective-permute-start.17) | collective-permute-done | bytes 524320 | tf_op jit(solution)/shard_map/ppermute | solution.py:51
  132.3 0.1 add_convert_fusion.3
  132.4 3.1 %collective-permute-start.18 = (bf16[2,2,128,512]{3,2,1,0:T(8,128)(2,1)S(1)}, bf16[2,2,128,512]{3,2,1,0:T(8,128)(2,1)S(1)}, u32[]{:S(2)}, u32[]{:S(2)}) collective-permute-start(bf16[2,2,128,512]{3,2,1,0:T(8,128)(2,1)S(1)} %add_convert_fusion.3), channel_id=1, source_target_pairs={{0,64},{32,480},{64,128},{96,32},{128,192},{160,96},{192,256},{224... | collective-permute-start | bytes 1572872 | tf_op jit(solution)/shard_map/ppermute | solution.py:35
  135.6 1.9 %collective-permute-start.21 = (bf16[2,2,128,512]{3,2,1,0:T(8,128)(2,1)S(1)}, bf16[2,2,128,512]{3,2,1,0:T(8,128)(2,1)S(1)}, u32[]{:S(2)}, u32[]{:S(2)}) collective-permute-start(bf16[2,2,128,512]{3,2,1,0:T(8,128)(2,1)S(1)} %pad_maximum_fusion.5), channel_id=1, source_target_pairs={{1,0},{2,1},{3,2},{4,3},{5,4},{6,5},{7,6},{8,7},{9,8},{10,9},{11,1... | collective-permute-start | bytes 1572872 | tf_op jit(solution)/shard_map/ppermute | solution.py:51
  137.6 0.1 add_convert_fusion
  137.7 3.0 %collective-permute-start.23 = (bf16[2,2,128,512]{3,2,1,0:T(8,128)(2,1)S(1)}, bf16[2,2,128,512]{3,2,1,0:T(8,128)(2,1)S(1)}, u32[]{:S(2)}, u32[]{:S(2)}) collective-permute-start(bf16[2,2,128,512]{3,2,1,0:T(8,128)(2,1)S(1)} %add_convert_fusion), channel_id=1, source_target_pairs={{0,64},{32,480},{64,128},{96,32},{128,192},{160,96},{192,256},{224... | collective-permute-start | bytes 1572872 | tf_op jit(solution)/shard_map/ppermute | solution.py:35
  140.7 4.0 %collective-permute-done.18 = bf16[2,2,128,512]{3,2,1,0:T(8,128)(2,1)S(1)} collective-permute-done((bf16[2,2,128,512]{3,2,1,0:T(8,128)(2,1)S(1)}, bf16[2,2,128,512]{3,2,1,0:T(8,128)(2,1)S(1)}, u32[]{:S(2)}, u32[]{:S(2)}) %collective-permute-start.18) | collective-permute-done | bytes 524320 | tf_op jit(solution)/shard_map/ppermute | solution.py:35
  144.7 5.7 %collective-permute-done.21.refs_0_ = bf16[2,2,128,512]{3,2,1,0:T(8,128)(2,1)S(1)} collective-permute-done((bf16[2,2,128,512]{3,2,1,0:T(8,128)(2,1)S(1)}, bf16[2,2,128,512]{3,2,1,0:T(8,128)(2,1)S(1)}, u32[]{:S(2)}, u32[]{:S(2)}) %collective-permute-start.21) | collective-permute-done | bytes 524320 | tf_op jit(solution)/shard_map/ppermute | solution.py:51
  150.5 1.9 %collective-permute-start.25 = (bf16[2,2,128,512]{3,2,1,0:T(8,128)(2,1)S(1)}, bf16[2,2,128,512]{3,2,1,0:T(8,128)(2,1)S(1)}, u32[]{:S(2)}, u32[]{:S(2)}) collective-permute-start(bf16[2,2,128,512]{3,2,1,0:T(8,128)(2,1)S(1)} %pad_maximum_fusion.6), channel_id=1, source_target_pairs={{0,32},{32,0},{64,96},{96,64},{128,160},{160,128},{192,224},{224,1... | collective-permute-start | bytes 1572872 | tf_op jit(solution)/shard_map/ppermute | solution.py:40
  152.4 0.1 add_convert_fusion.1
  152.6 2.4 %collective-permute-start.22 = (bf16[2,2,128,512]{3,2,1,0:T(8,128)(2,1)S(1)}, bf16[2,2,128,512]{3,2,1,0:T(8,128)(2,1)S(1)}, u32[]{:S(2)}, u32[]{:S(2)}) collective-permute-start(bf16[2,2,128,512]{3,2,1,0:T(8,128)(2,1)S(1)} %add_convert_fusion.1), channel_id=1, source_target_pairs={{0,64},{32,480},{64,128},{96,32},{128,192},{160,96},{192,256},{224... | collective-permute-start | bytes 1572872 | tf_op jit(solution)/shard_map/ppermute | solution.py:35
  155.0 3.8 %collective-permute-start.24 = (bf16[2,2,128,512]{3,2,1,0:T(8,128)(2,1)S(1)}, bf16[2,2,128,512]{3,2,1,0:T(8,128)(2,1)S(1)}, u32[]{:S(2)}, u32[]{:S(2)}) collective-permute-start(bf16[2,2,128,512]{3,2,1,0:T(8,128)(2,1)S(1)} %collective-permute-done.23), channel_id=1, source_target_pairs={{0,32},{32,0},{64,96},{96,64},{128,160},{160,128},{192,224},{224,1... | collective-permute-start | bytes 1572872 | tf_op jit(solution)/shard_map/ppermute | solution.py:40
  158.8 6.0 %collective-permute-done.22.from_a = bf16[2,2,128,512]{3,2,1,0:T(8,128)(2,1)S(1)} collective-permute-done((bf16[2,2,128,512]{3,2,1,0:T(8,128)(2,1)S(1)}, bf16[2,2,128,512]{3,2,1,0:T(8,128)(2,1)S(1)}, u32[]{:S(2)}, u32[]{:S(2)}) %collective-permute-start.22) | collective-permute-done | bytes 524320 | tf_op jit(solution)/shard_map/ppermute | solution.py:35
  164.9 2.0 %shard_map.98 = (bf16[256,512]{1,0:T(8,128)(2,1)}, bf16[256,512]{1,0:T(8,128)(2,1)}) custom-call(s32[6]{0:T(128)S(1)} %pad_add_fusion.6.table, bf16[2,2,128,512]{3,2,1,0:T(8,128)(2,1)S(1)} %get-tuple-element.60.near, bf16[6,2,128,512]{3,2,1,0:T(8,128)(2,1)S(1)} %collective-permute-done.13.theirs, ...), custom_call_target="tpu_custom_call" | custom-call | flops 4194304 | bytes 6291456 | tf_op jit(solution)/shard_map/pallas_call | solution.py:302
  (61 shorter events, 1.7 us)
Async XLA Ops:
  0.6 19.4 %copy-start.1 = (bf16[256,512]{1,0:T(8,128)(2,1)S(1)}, bf16[256,512]{1,0:T(8,128)(2,1)}, u32[]{:S(2)}) copy-start(bf16[256,512]{1,0:T(8,128)(2,1)} %keys.1) | copy-start | bytes 786436
  0.6 19.4 %copy-start = (bf16[256,512]{1,0:T(8,128)(2,1)S(1)}, bf16[256,512]{1,0:T(8,128)(2,1)}, u32[]{:S(2)}) copy-start(bf16[256,512]{1,0:T(8,128)(2,1)} %values.1) | copy-start | bytes 786436
  1.8 22.9 %collective-permute-start.1 = (bf16[2,256,512]{2,1,0:T(8,128)(2,1)S(1)}, bf16[2,256,512]{2,1,0:T(8,128)(2,1)S(1)}, u32[]{:S(2)}, u32[]{:S(2)}) collective-permute-start(bf16[2,256,512]{2,1,0:T(8,128)(2,1)S(1)} %pad_maximum_fusion.refs_0_), channel_id=1, source_target_pairs={{0,64},{32,480},{64,128},{96,32},{128,192},{160,96},{192,256},{224... | collective-permute-start | bytes 1572872 | tf_op jit(solution)/shard_map/ppermute | solution.py:35
  6.1 12.1 %collective-permute-start = (bf16[2,256,512]{2,1,0:T(8,128)(2,1)S(1)}, bf16[2,256,512]{2,1,0:T(8,128)(2,1)S(1)}, u32[]{:S(2)}, u32[]{:S(2)}) collective-permute-start(bf16[2,256,512]{2,1,0:T(8,128)(2,1)S(1)} %pad_maximum_fusion.refs_0_), channel_id=1, source_target_pairs={{0,32},{32,0},{64,96},{96,64},{128,160},{160,128},{192,224},{224,1... | collective-permute-start | bytes 1572872 | tf_op jit(solution)/shard_map/ppermute | solution.py:40
  18.1 12.3 %collective-permute-start.6 = (bf16[2,256,512]{2,1,0:T(8,128)(2,1)S(1)}, bf16[2,256,512]{2,1,0:T(8,128)(2,1)S(1)}, u32[]{:S(2)}, u32[]{:S(2)}) collective-permute-start(bf16[2,256,512]{2,1,0:T(8,128)(2,1)S(1)} %collective-permute-done.refs_0_.refs_4_), channel_id=1, source_target_pairs={{0,64},{32,480},{64,128},{96,32},{128,192},{160,96},{192,256},{224... | collective-permute-start | bytes 1572872 | tf_op jit(solution)/shard_map/ppermute | solution.py:35
  22.1 10.3 %collective-permute-start.3 = (bf16[2,2,128,512]{3,2,1,0:T(8,128)(2,1)S(1)}, bf16[2,2,128,512]{3,2,1,0:T(8,128)(2,1)S(1)}, u32[]{:S(2)}, u32[]{:S(2)}) collective-permute-start(bf16[2,2,128,512]{3,2,1,0:T(8,128)(2,1)S(1)} %get-tuple-element.47), channel_id=1, source_target_pairs={{0,32},{32,0},{64,96},{96,64},{128,160},{160,128},{192,224},{224,1... | collective-permute-start | bytes 1572872 | tf_op jit(solution)/shard_map/ppermute | solution.py:40
  24.7 18.0 %collective-permute-start.2 = (bf16[2,256,512]{2,1,0:T(8,128)(2,1)S(1)}, bf16[2,256,512]{2,1,0:T(8,128)(2,1)S(1)}, u32[]{:S(2)}, u32[]{:S(2)}) collective-permute-start(bf16[2,256,512]{2,1,0:T(8,128)(2,1)S(1)} %collective-permute-done.1.refs_1_.refs_5_), channel_id=1, source_target_pairs={{0,64},{32,480},{64,128},{96,32},{128,192},{160,96},{192,256},{224... | collective-permute-start | bytes 1572872 | tf_op jit(solution)/shard_map/ppermute | solution.py:35
  30.4 12.3 %collective-permute-start.7 = (bf16[2,256,512]{2,1,0:T(8,128)(2,1)S(1)}, bf16[2,256,512]{2,1,0:T(8,128)(2,1)S(1)}, u32[]{:S(2)}, u32[]{:S(2)}) collective-permute-start(bf16[2,256,512]{2,1,0:T(8,128)(2,1)S(1)} %collective-permute-done.6.refs_5_.refs_9_), channel_id=1, source_target_pairs={{0,64},{32,480},{64,128},{96,32},{128,192},{160,96},{192,256},{224... | collective-permute-start | bytes 1572872 | tf_op jit(solution)/shard_map/ppermute | solution.py:35
  32.4 11.3 %collective-permute-start.4 = (bf16[2,2,128,512]{3,2,1,0:T(8,128)(2,1)S(1)}, bf16[2,2,128,512]{3,2,1,0:T(8,128)(2,1)S(1)}, u32[]{:S(2)}, u32[]{:S(2)}) collective-permute-start(bf16[2,2,128,512]{3,2,1,0:T(8,128)(2,1)S(1)} %pad_maximum_fusion.1), channel_id=1, source_target_pairs={{0,1},{1,2},{2,3},{3,4},{4,5},{5,6},{6,7},{7,8},{8,9},{9,10},{10,1... | collective-permute-start | bytes 1572872 | tf_op jit(solution)/shard_map/ppermute | solution.py:51
  43.7 12.3 %collective-permute-start.5 = (bf16[2,256,512]{2,1,0:T(8,128)(2,1)S(1)}, bf16[2,256,512]{2,1,0:T(8,128)(2,1)S(1)}, u32[]{:S(2)}, u32[]{:S(2)}) collective-permute-start(bf16[2,256,512]{2,1,0:T(8,128)(2,1)S(1)} %collective-permute-done.2.refs_2_.refs_6_), channel_id=1, source_target_pairs={{0,64},{32,480},{64,128},{96,32},{128,192},{160,96},{192,256},{224... | collective-permute-start | bytes 1572872 | tf_op jit(solution)/shard_map/ppermute | solution.py:35
  45.7 18.2 %collective-permute-start.8 = (bf16[2,2,128,512]{3,2,1,0:T(8,128)(2,1)S(1)}, bf16[2,2,128,512]{3,2,1,0:T(8,128)(2,1)S(1)}, u32[]{:S(2)}, u32[]{:S(2)}) collective-permute-start(bf16[2,2,128,512]{3,2,1,0:T(8,128)(2,1)S(1)} %pad_maximum_fusion.2), channel_id=1, source_target_pairs={{0,2},{1,3},{2,4},{3,5},{4,6},{5,7},{6,8},{7,9},{8,10},{9,11},{10,... | collective-permute-start | bytes 1572872 | tf_op jit(solution)/shard_map/ppermute | solution.py:51
  51.0 15.9 %collective-permute-start.11 = (bf16[2,256,512]{2,1,0:T(8,128)(2,1)S(1)}, bf16[2,256,512]{2,1,0:T(8,128)(2,1)S(1)}, u32[]{:S(2)}, u32[]{:S(2)}) collective-permute-start(bf16[2,256,512]{2,1,0:T(8,128)(2,1)S(1)} %collective-permute-done.7.refs_6_.refs_10_), channel_id=1, source_target_pairs={{0,64},{32,480},{64,128},{96,32},{128,192},{160,96},{192,256},{224... | collective-permute-start | bytes 1572872 | tf_op jit(solution)/shard_map/ppermute | solution.py:35
  63.9 12.3 %collective-permute-start.10 = (bf16[2,256,512]{2,1,0:T(8,128)(2,1)S(1)}, bf16[2,256,512]{2,1,0:T(8,128)(2,1)S(1)}, u32[]{:S(2)}, u32[]{:S(2)}) collective-permute-start(bf16[2,256,512]{2,1,0:T(8,128)(2,1)S(1)} %collective-permute-done.5.refs_3_.refs_7_), channel_id=1, source_target_pairs={{0,64},{32,480},{64,128},{96,32},{128,192},{160,96},{192,256},{224... | collective-permute-start | bytes 1572872 | tf_op jit(solution)/shard_map/ppermute | solution.py:35
  77.3 6.2 %copy-start.2 = (bf16[256,512]{1,0:T(8,128)(2,1)S(1)}, bf16[256,512]{1,0:T(8,128)(2,1)}, u32[]{:S(2)}) copy-start(bf16[256,512]{1,0:T(8,128)(2,1)} %param.6) | copy-start | bytes 786436
  77.3 6.2 %copy-start.3 = (bf16[256,512]{1,0:T(8,128)(2,1)S(1)}, bf16[256,512]{1,0:T(8,128)(2,1)}, u32[]{:S(2)}) copy-start(bf16[256,512]{1,0:T(8,128)(2,1)} %param.9) | copy-start | bytes 786436
  77.3 6.2 %collective-permute-start.12 = (bf16[6,2,128,512]{3,2,1,0:T(8,128)(2,1)S(1)}, bf16[6,2,128,512]{3,2,1,0:T(8,128)(2,1)S(1)}, u32[]{:S(2)}, u32[]{:S(2)}) collective-permute-start(bf16[6,2,128,512]{3,2,1,0:T(8,128)(2,1)S(1)} %shard_map.94), channel_id=1, source_target_pairs={{0,32},{32,0},{64,96},{96,64},{128,160},{160,128},{192,224},{224,1... | collective-permute-start | bytes 4718600 | tf_op jit(solution)/shard_map/ppermute | solution.py:40
  79.5 4.0 %collective-permute-start.9 = (bf16[2,2,128,512]{3,2,1,0:T(8,128)(2,1)S(1)}, bf16[2,2,128,512]{3,2,1,0:T(8,128)(2,1)S(1)}, u32[]{:S(2)}, u32[]{:S(2)}) collective-permute-start(bf16[2,2,128,512]{3,2,1,0:T(8,128)(2,1)S(1)} %pad_maximum_fusion.3), channel_id=1, source_target_pairs={{0,32},{32,0},{64,96},{96,64},{128,160},{160,128},{192,224},{224,1... | collective-permute-start | bytes 1572872 | tf_op jit(solution)/shard_map/ppermute | solution.py:40
  97.0 5.3 %collective-permute-start.13 = (bf16[6,2,128,512]{3,2,1,0:T(8,128)(2,1)S(1)}, bf16[6,2,128,512]{3,2,1,0:T(8,128)(2,1)S(1)}, u32[]{:S(2)}, u32[]{:S(2)}) collective-permute-start(bf16[6,2,128,512]{3,2,1,0:T(8,128)(2,1)S(1)} %get-tuple-element.61.mine), channel_id=1, source_target_pairs={{0,32},{32,0},{64,96},{96,64},{128,160},{160,128},{192,224},{224,1... | collective-permute-start | bytes 4718600 | tf_op jit(solution)/shard_map/ppermute | solution.py:40
  103.1 12.3 %collective-permute-start.14 = (bf16[2,2,128,512]{3,2,1,0:T(8,128)(2,1)S(1)}, bf16[2,2,128,512]{3,2,1,0:T(8,128)(2,1)S(1)}, u32[]{:S(2)}, u32[]{:S(2)}) collective-permute-start(bf16[2,2,128,512]{3,2,1,0:T(8,128)(2,1)S(1)} %get-tuple-element.63), channel_id=1, source_target_pairs={{0,64},{32,480},{64,128},{96,32},{128,192},{160,96},{192,256},{224... | collective-permute-start | bytes 1572872 | tf_op jit(solution)/shard_map/ppermute | solution.py:35
  105.9 11.5 %collective-permute-start.16 = (bf16[2,2,128,512]{3,2,1,0:T(8,128)(2,1)S(1)}, bf16[2,2,128,512]{3,2,1,0:T(8,128)(2,1)S(1)}, u32[]{:S(2)}, u32[]{:S(2)}) collective-permute-start(bf16[2,2,128,512]{3,2,1,0:T(8,128)(2,1)S(1)} %get-tuple-element.69), channel_id=1, source_target_pairs={{0,32},{32,0},{64,96},{96,64},{128,160},{160,128},{192,224},{224,1... | collective-permute-start | bytes 1572872 | tf_op jit(solution)/shard_map/ppermute | solution.py:40
  109.9 12.3 %collective-permute-start.19 = (bf16[2,2,128,512]{3,2,1,0:T(8,128)(2,1)S(1)}, bf16[2,2,128,512]{3,2,1,0:T(8,128)(2,1)S(1)}, u32[]{:S(2)}, u32[]{:S(2)}) collective-permute-start(bf16[2,2,128,512]{3,2,1,0:T(8,128)(2,1)S(1)} %get-tuple-element.72), channel_id=1, source_target_pairs={{0,64},{32,480},{64,128},{96,32},{128,192},{160,96},{192,256},{224... | collective-permute-start | bytes 1572872 | tf_op jit(solution)/shard_map/ppermute | solution.py:35
  115.5 12.3 %collective-permute-start.15 = (bf16[2,2,128,512]{3,2,1,0:T(8,128)(2,1)S(1)}, bf16[2,2,128,512]{3,2,1,0:T(8,128)(2,1)S(1)}, u32[]{:S(2)}, u32[]{:S(2)}) collective-permute-start(bf16[2,2,128,512]{3,2,1,0:T(8,128)(2,1)S(1)} %add_convert_fusion.4), channel_id=1, source_target_pairs={{0,64},{32,480},{64,128},{96,32},{128,192},{160,96},{192,256},{224... | collective-permute-start | bytes 1572872 | tf_op jit(solution)/shard_map/ppermute | solution.py:35
  117.5 14.8 %collective-permute-start.17 = (bf16[2,2,128,512]{3,2,1,0:T(8,128)(2,1)S(1)}, bf16[2,2,128,512]{3,2,1,0:T(8,128)(2,1)S(1)}, u32[]{:S(2)}, u32[]{:S(2)}) collective-permute-start(bf16[2,2,128,512]{3,2,1,0:T(8,128)(2,1)S(1)} %pad_maximum_fusion.4), channel_id=1, source_target_pairs={{2,0},{3,1},{4,2},{5,3},{6,4},{7,5},{8,6},{9,7},{10,8},{11,9},{12,... | collective-permute-start | bytes 1572872 | tf_op jit(solution)/shard_map/ppermute | solution.py:51
  122.3 13.2 %collective-permute-start.20 = (bf16[2,2,128,512]{3,2,1,0:T(8,128)(2,1)S(1)}, bf16[2,2,128,512]{3,2,1,0:T(8,128)(2,1)S(1)}, u32[]{:S(2)}, u32[]{:S(2)}) collective-permute-start(bf16[2,2,128,512]{3,2,1,0:T(8,128)(2,1)S(1)} %add_convert_fusion.2), channel_id=1, source_target_pairs={{0,64},{32,480},{64,128},{96,32},{128,192},{160,96},{192,256},{224... | collective-permute-start | bytes 1572872 | tf_op jit(solution)/shard_map/ppermute | solution.py:35
  132.4 12.3 %collective-permute-start.18 = (bf16[2,2,128,512]{3,2,1,0:T(8,128)(2,1)S(1)}, bf16[2,2,128,512]{3,2,1,0:T(8,128)(2,1)S(1)}, u32[]{:S(2)}, u32[]{:S(2)}) collective-permute-start(bf16[2,2,128,512]{3,2,1,0:T(8,128)(2,1)S(1)} %add_convert_fusion.3), channel_id=1, source_target_pairs={{0,64},{32,480},{64,128},{96,32},{128,192},{160,96},{192,256},{224... | collective-permute-start | bytes 1572872 | tf_op jit(solution)/shard_map/ppermute | solution.py:35
  135.6 14.8 %collective-permute-start.21 = (bf16[2,2,128,512]{3,2,1,0:T(8,128)(2,1)S(1)}, bf16[2,2,128,512]{3,2,1,0:T(8,128)(2,1)S(1)}, u32[]{:S(2)}, u32[]{:S(2)}) collective-permute-start(bf16[2,2,128,512]{3,2,1,0:T(8,128)(2,1)S(1)} %pad_maximum_fusion.5), channel_id=1, source_target_pairs={{1,0},{2,1},{3,2},{4,3},{5,4},{6,5},{7,6},{8,7},{9,8},{10,9},{11,1... | collective-permute-start | bytes 1572872 | tf_op jit(solution)/shard_map/ppermute | solution.py:51
  137.7 17.3 %collective-permute-start.23 = (bf16[2,2,128,512]{3,2,1,0:T(8,128)(2,1)S(1)}, bf16[2,2,128,512]{3,2,1,0:T(8,128)(2,1)S(1)}, u32[]{:S(2)}, u32[]{:S(2)}) collective-permute-start(bf16[2,2,128,512]{3,2,1,0:T(8,128)(2,1)S(1)} %add_convert_fusion), channel_id=1, source_target_pairs={{0,64},{32,480},{64,128},{96,32},{128,192},{160,96},{192,256},{224... | collective-permute-start | bytes 1572872 | tf_op jit(solution)/shard_map/ppermute | solution.py:35
  150.5 8.3 %collective-permute-start.25 = (bf16[2,2,128,512]{3,2,1,0:T(8,128)(2,1)S(1)}, bf16[2,2,128,512]{3,2,1,0:T(8,128)(2,1)S(1)}, u32[]{:S(2)}, u32[]{:S(2)}) collective-permute-start(bf16[2,2,128,512]{3,2,1,0:T(8,128)(2,1)S(1)} %pad_maximum_fusion.6), channel_id=1, source_target_pairs={{0,32},{32,0},{64,96},{96,64},{128,160},{160,128},{192,224},{224,1... | collective-permute-start | bytes 1572872 | tf_op jit(solution)/shard_map/ppermute | solution.py:40
  152.6 12.3 %collective-permute-start.22 = (bf16[2,2,128,512]{3,2,1,0:T(8,128)(2,1)S(1)}, bf16[2,2,128,512]{3,2,1,0:T(8,128)(2,1)S(1)}, u32[]{:S(2)}, u32[]{:S(2)}) collective-permute-start(bf16[2,2,128,512]{3,2,1,0:T(8,128)(2,1)S(1)} %add_convert_fusion.1), channel_id=1, source_target_pairs={{0,64},{32,480},{64,128},{96,32},{128,192},{160,96},{192,256},{224... | collective-permute-start | bytes 1572872 | tf_op jit(solution)/shard_map/ppermute | solution.py:35
  155.0 9.9 %collective-permute-start.24 = (bf16[2,2,128,512]{3,2,1,0:T(8,128)(2,1)S(1)}, bf16[2,2,128,512]{3,2,1,0:T(8,128)(2,1)S(1)}, u32[]{:S(2)}, u32[]{:S(2)}) collective-permute-start(bf16[2,2,128,512]{3,2,1,0:T(8,128)(2,1)S(1)} %collective-permute-done.23), channel_id=1, source_target_pairs={{0,32},{32,0},{64,96},{96,64},{128,160},{160,128},{192,224},{224,1... | collective-permute-start | bytes 1572872 | tf_op jit(solution)/shard_map/ppermute | solution.py:40

commit v6 on v5

--- a/solution.py
+++ b/solution.py
@@ -210,14 +210,13 @@
                 def _():
                     bring(picked.at[s * EXP + j - 1 - LOC], s, j)
 
-    for s in range(NB):
-        pltpu.make_async_copy(listed.at[s], listed.at[s], sem.at[s]).wait()
-
     def body(step, carry):
         attend_pair(step, table, q_ref, g_ref, listed, att_ref, gq_ref, totals)
         return carry
 
-    lax.fori_loop(0, NB * PAIRS, body, 0, unroll=4)
+    for s in range(NB):
+        pltpu.make_async_copy(listed.at[s], listed.at[s], sem.at[s]).wait()
+        lax.fori_loop(s * PAIRS, (s + 1) * PAIRS, body, 0, unroll=PAIRS)
     own_out[...] = totals[:NB].astype(BF)
     keep_out[...] = totals[NB : NB + W].astype(BF)
     give_out[...] = totals[NB + W : NEAR].astype(BF)
@@ -368,14 +367,14 @@
     keep, give = offer(given, keys, values)
     given_here = swap_cores(give)
     flow_b.append(ring_step(flow_b[0]))
+    two = dom_step(jnp.stack([keep[1], given_here[1]]), 2)
+    flow_a.append(ring_step(flow_a[1]))
+    flow_b[1], two = lax.optimization_barrier((flow_b[1], two))
+    flow_b.append(ring_step(flow_b[1]))
+    keep, given_here, two = lax.optimization_barrier((keep, given_here, two))
     one = dom_step(jnp.stack([keep[0], given_here[0]]), 1)
-    flow_a[1], one = lax.optimization_barrier((flow_a[1], one))
-    flow_a.append(ring_step(flow_a[1]))
-    keep, given_here, flow_b[1] = lax.optimization_barrier((keep, given_here, flow_b[1]))
-    two = dom_step(jnp.stack([keep[1], given_here[1]]), 2)
-    flow_b.append(ring_step(flow_b[1]))
-    flow_a[2], two = lax.optimization_barrier((flow_a[2], two))
     flow_a.append(ring_step(flow_a[2]))
+    flow_a[3], one = lax.optimization_barrier((flow_a[3], one))
     near = (one, two, swap_cores(jnp.stack([one[1], two[1]])))
 
     picked = swap_cores(pick(pick_table, [sibling] + flow_a + flow_b))
@@ -390,6 +389,7 @@
     )
 
     sibling_terms = swap_cores(far_terms)
+    sibling_terms, give = lax.optimization_barrier((sibling_terms, give))
     start_a, start_b = spread(hits_first, far_terms, sibling_terms)
     a3, b2, a2, b1, a1 = spread(hits_rest, far_terms, sibling_terms)
 
@@ -398,20 +398,19 @@
 
     back_a = ring_step(start_a)
     back_b = ring_step(start_b)
-    give, a3 = lax.optimization_barrier((give, a3))
     given_here = swap_cores(give)
     back_a = ring_step(joined(back_a, a3))
+    two = dom_step(jnp.stack([keep[1], given_here[1]]), -2)
     back_b = ring_step(joined(back_b, b2))
-    two = dom_step(jnp.stack([keep[1], given_here[1]]), -2)
-    back_a, two = lax.optimization_barrier((back_a, two))
     back_a = ring_step(joined(back_a, a2))
-    keep, given_here, back_b = lax.optimization_barrier((keep, given_here, back_b))
+    back_b, two = lax.optimization_barrier((back_b, two))
+    back_b = ring_step(joined(back_b, b1))
+    keep, given_here, two = lax.optimization_barrier((keep, given_here, two))
     one = dom_step(jnp.stack([keep[0], given_here[0]]), -1)
-    back_b = ring_step(joined(back_b, b1))
-    back_a, one = lax.optimization_barrier((back_a, one))
     back_a = ring_step(joined(back_a, a1))
-    returned = (one, two, swap_cores(jnp.stack([one[1], two[1]])))
+    other, back_b = lax.optimization_barrier((jnp.stack([one[1], two[1]]), back_b))
     back_b = swap_cores(back_b)
+    returned = (one, two, swap_cores(other))
 
     grad_keys, grad_values = close(last, own_terms, sibling_terms, back_a, back_b, returned)
     return (attended.reshape(NB * BS, D), grad_queries.reshape(NB * BS, D), grad_keys, grad_values)

time: 168 us -> 157 us (0.935)
  the two profiles are of different devices: /device:TPU:30 before, /device:TPU:57 now
where the time goes in v6:
time: 157 us; the launch traced here: 156 us
  starting transfers between devices  89.9 us (57%)
  waiting for transfers between devices  37.8 us (24%)
  Pallas kernels  20.7 us (13%)
  other arithmetic  3.3 us (2%)
  local copies, waits for them, and re-layouts  2.83 us (2%)
    ppermute x14, starting transfers between devices, ring_step(): lax.ppermute(array, 'group', [(g, (g + (2 if g % 2 == 0 else -2)) % size)...  50.2 us
    ppermute x8, starting transfers between devices, swap_cores(): return lax.ppermute(array, 'group', [(g, g ^ 1) for g in range(size)])  25.4 us
    ppermute x4, waiting for transfers between devices, dom_step(): return lax.ppermute(array, ('group', 'dom'), pairs)  18.6 us
    ppermute x4, starting transfers between devices, dom_step(): return lax.ppermute(array, ('group', 'dom'), pairs)  14.2 us
    pallas_call x1, Pallas kernels, attend(): pl.pallas_call(attend_kernel, out_shape=(jax.ShapeDtypeStruct((NB, BS, D)...  13.8 us
    ppermute x14, waiting for transfers between devices, ring_step(): lax.ppermute(array, 'group', [(g, (g + (2 if g % 2 == 0 else -2)) % size)...  12.3 us
    ppermute x8, waiting for transfers between devices, swap_cores(): return lax.ppermute(array, 'group', [(g, g ^ 1) for g in range(size)])  6.91 us
  transfers between devices with their start and end apart: 26, of which 13 were waited for; matrix products, arithmetic and copies ran while one was open for 3% of the time, Pallas kernels for 2%

profile of v6, /device:TPU:57, one launch (start us, length us, event | category | flops | bytes accessed | tf_op | source)
XLA Modules:
  0.0 155.9 jit_solution(11785927833671553919)
XLA Ops:
  0.7 1.1 pad_maximum_fusion.refs_0_
  1.8 10.7 %collective-permute-start.1 = (bf16[2,256,512]{2,1,0:T(8,128)(2,1)S(1)}, bf16[2,256,512]{2,1,0:T(8,128)(2,1)S(1)}, u32[]{:S(2)}, u32[]{:S(2)}) collective-permute-start(bf16[2,256,512]{2,1,0:T(8,128)(2,1)S(1)} %pad_maximum_fusion.refs_0_), channel_id=1, source_target_pairs={{0,64},{32,480},{64,128},{96,32},{128,192},{160,96},{192,256},{224... | collective-permute-start | bytes 1572872 | tf_op jit(solution)/shard_map/ppermute | solution.py:35
  12.5 1.9 %collective-permute-start = (bf16[2,256,512]{2,1,0:T(8,128)(2,1)S(1)}, bf16[2,256,512]{2,1,0:T(8,128)(2,1)S(1)}, u32[]{:S(2)}, u32[]{:S(2)}) collective-permute-start(bf16[2,256,512]{2,1,0:T(8,128)(2,1)S(1)} %pad_maximum_fusion.refs_0_), channel_id=1, source_target_pairs={{0,32},{32,0},{64,96},{96,64},{128,160},{160,128},{192,224},{224,1... | collective-permute-start | bytes 1572872 | tf_op jit(solution)/shard_map/ppermute | solution.py:40
  14.6 0.8 copy.15
  15.4 0.2 select_reduce_fusion.3
  15.6 0.1 stack.113
  15.7 0.1 select_reduce_fusion.2
  15.9 0.1 add.216
  16.0 0.1 squeeze.8
  16.1 0.8 copy.14
  16.9 0.1 fusion.2
  17.1 0.1 eq.193
  17.2 0.2 select_reduce_fusion
  17.5 0.1 reduce_max.18
  17.7 0.1 rev.3
  18.0 0.1 stack_reshape.11
  18.4 2.0 %shard_map.93 = (bf16[2,2,128,512]{3,2,1,0:T(8,128)(2,1)S(1)}, bf16[2,2,128,512]{3,2,1,0:T(8,128)(2,1)S(1)}) custom-call(s32[4]{0:T(128)S(1)} %broadcast_select_fusion.2.table, bf16[256,512]{1,0:T(8,128)(2,1)S(1)} %copy-done.3, bf16[256,512]{1,0:T(8,128)(2,1)S(1)} %copy-done.2), custom_call_target="tpu_custom_call" | custom-call | bytes 2097152 | tf_op jit(solution)/shard_map/pallas_call | solution.py:122
  20.4 2.4 %collective-permute-start.5 = (bf16[2,2,128,512]{3,2,1,0:T(8,128)(2,1)S(1)}, bf16[2,2,128,512]{3,2,1,0:T(8,128)(2,1)S(1)}, u32[]{:S(2)}, u32[]{:S(2)}) collective-permute-start(bf16[2,2,128,512]{3,2,1,0:T(8,128)(2,1)S(1)} %get-tuple-element.47), channel_id=1, source_target_pairs={{0,32},{32,0},{64,96},{96,64},{128,160},{160,128},{192,224},{224,1... | collective-permute-start | bytes 1572872 | tf_op jit(solution)/shard_map/ppermute | solution.py:40
  22.8 2.2 %collective-permute-start.6 = (bf16[2,256,512]{2,1,0:T(8,128)(2,1)S(1)}, bf16[2,256,512]{2,1,0:T(8,128)(2,1)S(1)}, u32[]{:S(2)}, u32[]{:S(2)}) collective-permute-start(bf16[2,256,512]{2,1,0:T(8,128)(2,1)S(1)} %collective-permute-done.refs_0_.refs_4_), channel_id=1, source_target_pairs={{0,64},{32,480},{64,128},{96,32},{128,192},{160,96},{192,256},{224... | collective-permute-start | bytes 1572872 | tf_op jit(solution)/shard_map/ppermute | solution.py:35
  25.0 3.6 %collective-permute-start.2 = (bf16[2,256,512]{2,1,0:T(8,128)(2,1)S(1)}, bf16[2,256,512]{2,1,0:T(8,128)(2,1)S(1)}, u32[]{:S(2)}, u32[]{:S(2)}) collective-permute-start(bf16[2,256,512]{2,1,0:T(8,128)(2,1)S(1)} %collective-permute-done.1.refs_1_.refs_5_), channel_id=1, source_target_pairs={{0,64},{32,480},{64,128},{96,32},{128,192},{160,96},{192,256},{224... | collective-permute-start | bytes 1572872 | tf_op jit(solution)/shard_map/ppermute | solution.py:35
  28.7 4.3 %collective-permute-done.6.refs_5_.refs_9_ = bf16[2,256,512]{2,1,0:T(8,128)(2,1)S(1)} collective-permute-done((bf16[2,256,512]{2,1,0:T(8,128)(2,1)S(1)}, bf16[2,256,512]{2,1,0:T(8,128)(2,1)S(1)}, u32[]{:S(2)}, u32[]{:S(2)}) %collective-permute-start.6) | collective-permute-done | bytes 524320 | tf_op jit(solution)/shard_map/ppermute | solution.py:35
  33.0 3.1 %collective-permute-start.7 = (bf16[2,256,512]{2,1,0:T(8,128)(2,1)S(1)}, bf16[2,256,512]{2,1,0:T(8,128)(2,1)S(1)}, u32[]{:S(2)}, u32[]{:S(2)}) collective-permute-start(bf16[2,256,512]{2,1,0:T(8,128)(2,1)S(1)} %collective-permute-done.6.refs_5_.refs_9_), channel_id=1, source_target_pairs={{0,64},{32,480},{64,128},{96,32},{128,192},{160,96},{192,256},{224... | collective-permute-start | bytes 1572872 | tf_op jit(solution)/shard_map/ppermute | solution.py:35
  36.1 5.4 %collective-permute-start.8 = (bf16[2,2,128,512]{3,2,1,0:T(8,128)(2,1)S(1)}, bf16[2,2,128,512]{3,2,1,0:T(8,128)(2,1)S(1)}, u32[]{:S(2)}, u32[]{:S(2)}) collective-permute-start(bf16[2,2,128,512]{3,2,1,0:T(8,128)(2,1)S(1)} %pad_maximum_fusion.1), channel_id=1, source_target_pairs={{0,2},{1,3},{2,4},{3,5},{4,6},{5,7},{6,8},{7,9},{8,10},{9,11},{10,... | collective-permute-start | bytes 1572872 | tf_op jit(solution)/shard_map/ppermute | solution.py:51
  41.6 2.6 %collective-permute-start.3 = (bf16[2,256,512]{2,1,0:T(8,128)(2,1)S(1)}, bf16[2,256,512]{2,1,0:T(8,128)(2,1)S(1)}, u32[]{:S(2)}, u32[]{:S(2)}) collective-permute-start(bf16[2,256,512]{2,1,0:T(8,128)(2,1)S(1)} %collective-permute-done.2.refs_2_.refs_6_), channel_id=1, source_target_pairs={{0,64},{32,480},{64,128},{96,32},{128,192},{160,96},{192,256},{224... | collective-permute-start | bytes 1572872 | tf_op jit(solution)/shard_map/ppermute | solution.py:35
  44.2 8.9 %collective-permute-done.8.refs_2_ = bf16[2,2,128,512]{3,2,1,0:T(8,128)(2,1)S(1)} collective-permute-done((bf16[2,2,128,512]{3,2,1,0:T(8,128)(2,1)S(1)}, bf16[2,2,128,512]{3,2,1,0:T(8,128)(2,1)S(1)}, u32[]{:S(2)}, u32[]{:S(2)}) %collective-permute-start.8) | collective-permute-done | bytes 524320 | tf_op jit(solution)/shard_map/ppermute | solution.py:51
  53.3 2.6 %collective-permute-start.4 = (bf16[2,256,512]{2,1,0:T(8,128)(2,1)S(1)}, bf16[2,256,512]{2,1,0:T(8,128)(2,1)S(1)}, u32[]{:S(2)}, u32[]{:S(2)}) collective-permute-start(bf16[2,256,512]{2,1,0:T(8,128)(2,1)S(1)} %collective-permute-done.3.refs_3_.refs_7_), channel_id=1, source_target_pairs={{0,64},{32,480},{64,128},{96,32},{128,192},{160,96},{192,256},{224... | collective-permute-start | bytes 1572872 | tf_op jit(solution)/shard_map/ppermute | solution.py:35
  55.9 2.9 %collective-permute-start.9 = (bf16[2,2,128,512]{3,2,1,0:T(8,128)(2,1)S(1)}, bf16[2,2,128,512]{3,2,1,0:T(8,128)(2,1)S(1)}, u32[]{:S(2)}, u32[]{:S(2)}) collective-permute-start(bf16[2,2,128,512]{3,2,1,0:T(8,128)(2,1)S(1)} %pad_maximum_fusion.2), channel_id=1, source_target_pairs={{0,1},{1,2},{2,3},{3,4},{4,5},{5,6},{6,7},{7,8},{8,9},{9,10},{10,1... | collective-permute-start | bytes 1572872 | tf_op jit(solution)/shard_map/ppermute | solution.py:51
  58.8 2.2 %collective-permute-start.11 = (bf16[2,256,512]{2,1,0:T(8,128)(2,1)S(1)}, bf16[2,256,512]{2,1,0:T(8,128)(2,1)S(1)}, u32[]{:S(2)}, u32[]{:S(2)}) collective-permute-start(bf16[2,256,512]{2,1,0:T(8,128)(2,1)S(1)} %collective-permute-done.7.refs_6_.refs_10_), channel_id=1, source_target_pairs={{0,64},{32,480},{64,128},{96,32},{128,192},{160,96},{192,256},{224... | collective-permute-start | bytes 1572872 | tf_op jit(solution)/shard_map/ppermute | solution.py:35
  61.0 2.5 %collective-permute-done.4.refs_4_.refs_8_ = bf16[2,256,512]{2,1,0:T(8,128)(2,1)S(1)} collective-permute-done((bf16[2,256,512]{2,1,0:T(8,128)(2,1)S(1)}, bf16[2,256,512]{2,1,0:T(8,128)(2,1)S(1)}, u32[]{:S(2)}, u32[]{:S(2)}) %collective-permute-start.4) | collective-permute-done | bytes 524320 | tf_op jit(solution)/shard_map/ppermute | solution.py:35
  63.5 2.7 %collective-permute-done.9.refs_1_ = bf16[2,2,128,512]{3,2,1,0:T(8,128)(2,1)S(1)} collective-permute-done((bf16[2,2,128,512]{3,2,1,0:T(8,128)(2,1)S(1)}, bf16[2,2,128,512]{3,2,1,0:T(8,128)(2,1)S(1)}, u32[]{:S(2)}, u32[]{:S(2)}) %collective-permute-start.9) | collective-permute-done | bytes 524320 | tf_op jit(solution)/shard_map/ppermute | solution.py:51
  66.1 3.0 %collective-permute-done.11.refs_7_.refs_11_ = bf16[2,256,512]{2,1,0:T(8,128)(2,1)S(1)} collective-permute-done((bf16[2,256,512]{2,1,0:T(8,128)(2,1)S(1)}, bf16[2,256,512]{2,1,0:T(8,128)(2,1)S(1)}, u32[]{:S(2)}, u32[]{:S(2)}) %collective-permute-start.11) | collective-permute-done | bytes 524320 | tf_op jit(solution)/shard_map/ppermute | solution.py:35
  69.1 1.1 shard_map.94
  70.2 5.0 %collective-permute-start.12 = (bf16[6,2,128,512]{3,2,1,0:T(8,128)(2,1)S(1)}, bf16[6,2,128,512]{3,2,1,0:T(8,128)(2,1)S(1)}, u32[]{:S(2)}, u32[]{:S(2)}) collective-permute-start(bf16[6,2,128,512]{3,2,1,0:T(8,128)(2,1)S(1)} %shard_map.94), channel_id=1, source_target_pairs={{0,32},{32,0},{64,96},{96,64},{128,160},{160,128},{192,224},{224,1... | collective-permute-start | bytes 4718600 | tf_op jit(solution)/shard_map/ppermute | solution.py:40
  75.4 1.9 %collective-permute-start.10 = (bf16[2,2,128,512]{3,2,1,0:T(8,128)(2,1)S(1)}, bf16[2,2,128,512]{3,2,1,0:T(8,128)(2,1)S(1)}, u32[]{:S(2)}, u32[]{:S(2)}) collective-permute-start(bf16[2,2,128,512]{3,2,1,0:T(8,128)(2,1)S(1)} %pad_maximum_fusion.3), channel_id=1, source_target_pairs={{0,32},{32,0},{64,96},{96,64},{128,160},{160,128},{192,224},{224,1... | collective-permute-start | bytes 1572872 | tf_op jit(solution)/shard_map/ppermute | solution.py:40
  77.3 1.9 %collective-permute-done.10.refs_3_ = bf16[2,2,128,512]{3,2,1,0:T(8,128)(2,1)S(1)} collective-permute-done((bf16[2,2,128,512]{3,2,1,0:T(8,128)(2,1)S(1)}, bf16[2,2,128,512]{3,2,1,0:T(8,128)(2,1)S(1)}, u32[]{:S(2)}, u32[]{:S(2)}) %collective-permute-start.10) | collective-permute-done | bytes 524320 | tf_op jit(solution)/shard_map/ppermute | solution.py:40
  79.2 13.8 %shard_map.95 = (bf16[2,128,512]{2,1,0:T(8,128)(2,1)}, bf16[2,128,512]{2,1,0:T(8,128)(2,1)}, bf16[2,2,128,512]{3,2,1,0:T(8,128)(2,1)S(1)}, bf16[6,2,128,512]{3,2...) custom-call(s32[4,14]{1,0:T(4,128)S(1)} %pad_add_fusion.table, ...), custom_call_target="tpu_custom_call" | custom-call | flops 1409286144 | bytes 12582912 | tf_op jit(solution)/shard_map/pallas_call | solution.py:227
  93.0 2.1 %collective-permute-start.13 = (bf16[6,2,128,512]{3,2,1,0:T(8,128)(2,1)S(1)}, bf16[6,2,128,512]{3,2,1,0:T(8,128)(2,1)S(1)}, u32[]{:S(2)}, u32[]{:S(2)}) collective-permute-start(bf16[6,2,128,512]{3,2,1,0:T(8,128)(2,1)S(1)} %get-tuple-element.61.mine), channel_id=1, source_target_pairs={{0,32},{32,0},{64,96},{96,64},{128,160},{160,128},{192,224},{224,1... | collective-permute-start | bytes 4718600 | tf_op jit(solution)/shard_map/ppermute | solution.py:40
  95.1 3.2 %collective-permute-done.13.theirs = bf16[6,2,128,512]{3,2,1,0:T(8,128)(2,1)S(1)} collective-permute-done((bf16[6,2,128,512]{3,2,1,0:T(8,128)(2,1)S(1)}, bf16[6,2,128,512]{3,2,1,0:T(8,128)(2,1)S(1)}, u32[]{:S(2)}, u32[]{:S(2)}) %collective-permute-start.13) | collective-permute-done | bytes 1572896 | tf_op jit(solution)/shard_map/ppermute | solution.py:40
  98.3 0.8 shard_map.96
  99.1 2.5 %collective-permute-start.14 = (bf16[2,2,128,512]{3,2,1,0:T(8,128)(2,1)S(1)}, bf16[2,2,128,512]{3,2,1,0:T(8,128)(2,1)S(1)}, u32[]{:S(2)}, u32[]{:S(2)}) collective-permute-start(bf16[2,2,128,512]{3,2,1,0:T(8,128)(2,1)S(1)} %get-tuple-element.65), channel_id=1, source_target_pairs={{0,64},{32,480},{64,128},{96,32},{128,192},{160,96},{192,256},{224... | collective-permute-start | bytes 1572872 | tf_op jit(solution)/shard_map/ppermute | solution.py:35
  101.5 1.9 %collective-permute-start.18 = (bf16[2,2,128,512]{3,2,1,0:T(8,128)(2,1)S(1)}, bf16[2,2,128,512]{3,2,1,0:T(8,128)(2,1)S(1)}, u32[]{:S(2)}, u32[]{:S(2)}) collective-permute-start(bf16[2,2,128,512]{3,2,1,0:T(8,128)(2,1)S(1)} %get-tuple-element.71), channel_id=1, source_target_pairs={{0,32},{32,0},{64,96},{96,64},{128,160},{160,128},{192,224},{224,1... | collective-permute-start | bytes 1572872 | tf_op jit(solution)/shard_map/ppermute | solution.py:40
  103.5 4.5 %collective-permute-start.19 = (bf16[2,2,128,512]{3,2,1,0:T(8,128)(2,1)S(1)}, bf16[2,2,128,512]{3,2,1,0:T(8,128)(2,1)S(1)}, u32[]{:S(2)}, u32[]{:S(2)}) collective-permute-start(bf16[2,2,128,512]{3,2,1,0:T(8,128)(2,1)S(1)} %get-tuple-element.72), channel_id=1, source_target_pairs={{0,64},{32,480},{64,128},{96,32},{128,192},{160,96},{192,256},{224... | collective-permute-start | bytes 1572872 | tf_op jit(solution)/shard_map/ppermute | solution.py:35
  108.0 1.2 shard_map.97
  109.1 0.1 collective-permute-done.14
  109.3 0.1 add_convert_fusion.4
  109.4 3.4 %collective-permute-start.15 = (bf16[2,2,128,512]{3,2,1,0:T(8,128)(2,1)S(1)}, bf16[2,2,128,512]{3,2,1,0:T(8,128)(2,1)S(1)}, u32[]{:S(2)}, u32[]{:S(2)}) collective-permute-start(bf16[2,2,128,512]{3,2,1,0:T(8,128)(2,1)S(1)} %add_convert_fusion.4), channel_id=1, source_target_pairs={{0,64},{32,480},{64,128},{96,32},{128,192},{160,96},{192,256},{224... | collective-permute-start | bytes 1572872 | tf_op jit(solution)/shard_map/ppermute | solution.py:35
  112.9 4.0 %collective-permute-start.21 = (bf16[2,2,128,512]{3,2,1,0:T(8,128)(2,1)S(1)}, bf16[2,2,128,512]{3,2,1,0:T(8,128)(2,1)S(1)}, u32[]{:S(2)}, u32[]{:S(2)}) collective-permute-start(bf16[2,2,128,512]{3,2,1,0:T(8,128)(2,1)S(1)} %pad_maximum_fusion.4), channel_id=1, source_target_pairs={{2,0},{3,1},{4,2},{5,3},{6,4},{7,5},{8,6},{9,7},{10,8},{11,9},{12,... | collective-permute-start | bytes 1572872 | tf_op jit(solution)/shard_map/ppermute | solution.py:51
  116.9 0.1 add_convert_fusion.1
  117.1 2.2 %collective-permute-start.20 = (bf16[2,2,128,512]{3,2,1,0:T(8,128)(2,1)S(1)}, bf16[2,2,128,512]{3,2,1,0:T(8,128)(2,1)S(1)}, u32[]{:S(2)}, u32[]{:S(2)}) collective-permute-start(bf16[2,2,128,512]{3,2,1,0:T(8,128)(2,1)S(1)} %add_convert_fusion.1), channel_id=1, source_target_pairs={{0,64},{32,480},{64,128},{96,32},{128,192},{160,96},{192,256},{224... | collective-permute-start | bytes 1572872 | tf_op jit(solution)/shard_map/ppermute | solution.py:35
  119.2 1.3 collective-permute-done.15
  120.5 0.1 add_convert_fusion.3
  120.7 4.2 %collective-permute-start.16 = (bf16[2,2,128,512]{3,2,1,0:T(8,128)(2,1)S(1)}, bf16[2,2,128,512]{3,2,1,0:T(8,128)(2,1)S(1)}, u32[]{:S(2)}, u32[]{:S(2)}) collective-permute-start(bf16[2,2,128,512]{3,2,1,0:T(8,128)(2,1)S(1)} %add_convert_fusion.3), channel_id=1, source_target_pairs={{0,64},{32,480},{64,128},{96,32},{128,192},{160,96},{192,256},{224... | collective-permute-start | bytes 1572872 | tf_op jit(solution)/shard_map/ppermute | solution.py:35
  124.8 1.4 collective-permute-done.21.refs_1_
  126.2 1.1 collective-permute-done.20
  127.4 1.9 %collective-permute-start.22 = (bf16[2,2,128,512]{3,2,1,0:T(8,128)(2,1)S(1)}, bf16[2,2,128,512]{3,2,1,0:T(8,128)(2,1)S(1)}, u32[]{:S(2)}, u32[]{:S(2)}) collective-permute-start(bf16[2,2,128,512]{3,2,1,0:T(8,128)(2,1)S(1)} %pad_maximum_fusion.5), channel_id=1, source_target_pairs={{1,0},{2,1},{3,2},{4,3},{5,4},{6,5},{7,6},{8,7},{9,8},{10,9},{11,1... | collective-permute-start | bytes 1572872 | tf_op jit(solution)/shard_map/ppermute | solution.py:51
  129.3 0.1 add_convert_fusion
  129.5 3.6 %collective-permute-start.23 = (bf16[2,2,128,512]{3,2,1,0:T(8,128)(2,1)S(1)}, bf16[2,2,128,512]{3,2,1,0:T(8,128)(2,1)S(1)}, u32[]{:S(2)}, u32[]{:S(2)}) collective-permute-start(bf16[2,2,128,512]{3,2,1,0:T(8,128)(2,1)S(1)} %add_convert_fusion), channel_id=1, source_target_pairs={{0,64},{32,480},{64,128},{96,32},{128,192},{160,96},{192,256},{224... | collective-permute-start | bytes 1572872 | tf_op jit(solution)/shard_map/ppermute | solution.py:35
  133.1 0.1 add_convert_fusion.2
  133.2 3.0 %collective-permute-start.17 = (bf16[2,2,128,512]{3,2,1,0:T(8,128)(2,1)S(1)}, bf16[2,2,128,512]{3,2,1,0:T(8,128)(2,1)S(1)}, u32[]{:S(2)}, u32[]{:S(2)}) collective-permute-start(bf16[2,2,128,512]{3,2,1,0:T(8,128)(2,1)S(1)} %add_convert_fusion.2), channel_id=1, source_target_pairs={{0,64},{32,480},{64,128},{96,32},{128,192},{160,96},{192,256},{224... | collective-permute-start | bytes 1572872 | tf_op jit(solution)/shard_map/ppermute | solution.py:35
  136.3 5.7 %collective-permute-done.22.refs_0_ = bf16[2,2,128,512]{3,2,1,0:T(8,128)(2,1)S(1)} collective-permute-done((bf16[2,2,128,512]{3,2,1,0:T(8,128)(2,1)S(1)}, bf16[2,2,128,512]{3,2,1,0:T(8,128)(2,1)S(1)}, u32[]{:S(2)}, u32[]{:S(2)}) %collective-permute-start.22) | collective-permute-done | bytes 524320 | tf_op jit(solution)/shard_map/ppermute | solution.py:51
  142.0 8.1 %collective-permute-start.24 = (bf16[2,2,128,512]{3,2,1,0:T(8,128)(2,1)S(1)}, bf16[2,2,128,512]{3,2,1,0:T(8,128)(2,1)S(1)}, u32[]{:S(2)}, u32[]{:S(2)}) collective-permute-start(bf16[2,2,128,512]{3,2,1,0:T(8,128)(2,1)S(1)} %collective-permute-done.23), channel_id=1, source_target_pairs={{0,32},{32,0},{64,96},{96,64},{128,160},{160,128},{192,224},{224,1... | collective-permute-start | bytes 1572872 | tf_op jit(solution)/shard_map/ppermute | solution.py:40
  150.2 1.9 %collective-permute-start.25 = (bf16[2,2,128,512]{3,2,1,0:T(8,128)(2,1)S(1)}, bf16[2,2,128,512]{3,2,1,0:T(8,128)(2,1)S(1)}, u32[]{:S(2)}, u32[]{:S(2)}) collective-permute-start(bf16[2,2,128,512]{3,2,1,0:T(8,128)(2,1)S(1)} %pad_maximum_fusion.6), channel_id=1, source_target_pairs={{0,32},{32,0},{64,96},{96,64},{128,160},{160,128},{192,224},{224,1... | collective-permute-start | bytes 1572872 | tf_op jit(solution)/shard_map/ppermute | solution.py:40
  152.1 1.9 %collective-permute-done.25.refs_2_ = bf16[2,2,128,512]{3,2,1,0:T(8,128)(2,1)S(1)} collective-permute-done((bf16[2,2,128,512]{3,2,1,0:T(8,128)(2,1)S(1)}, bf16[2,2,128,512]{3,2,1,0:T(8,128)(2,1)S(1)}, u32[]{:S(2)}, u32[]{:S(2)}) %collective-permute-start.25) | collective-permute-done | bytes 524320 | tf_op jit(solution)/shard_map/ppermute | solution.py:40
  154.0 1.9 %shard_map.98 = (bf16[256,512]{1,0:T(8,128)(2,1)}, bf16[256,512]{1,0:T(8,128)(2,1)}) custom-call(s32[6]{0:T(128)S(1)} %pad_add_fusion.6.table, bf16[2,2,128,512]{3,2,1,0:T(8,128)(2,1)S(1)} %get-tuple-element.60.near, bf16[6,2,128,512]{3,2,1,0:T(8,128)(2,1)S(1)} %collective-permute-done.13.theirs, ...), custom_call_target="tpu_custom_call" | custom-call | flops 4194304 | bytes 6291456 | tf_op jit(solution)/shard_map/pallas_call | solution.py:301
  (66 shorter events, 1.6 us)
Async XLA Ops:
  0.6 17.7 %copy-start.3 = (bf16[256,512]{1,0:T(8,128)(2,1)S(1)}, bf16[256,512]{1,0:T(8,128)(2,1)}, u32[]{:S(2)}) copy-start(bf16[256,512]{1,0:T(8,128)(2,1)} %keys.1) | copy-start | bytes 786436
  0.6 17.7 %copy-start.2 = (bf16[256,512]{1,0:T(8,128)(2,1)S(1)}, bf16[256,512]{1,0:T(8,128)(2,1)}, u32[]{:S(2)}) copy-start(bf16[256,512]{1,0:T(8,128)(2,1)} %values.1) | copy-start | bytes 786436
  1.8 23.2 %collective-permute-start.1 = (bf16[2,256,512]{2,1,0:T(8,128)(2,1)S(1)}, bf16[2,256,512]{2,1,0:T(8,128)(2,1)S(1)}, u32[]{:S(2)}, u32[]{:S(2)}) collective-permute-start(bf16[2,256,512]{2,1,0:T(8,128)(2,1)S(1)} %pad_maximum_fusion.refs_0_), channel_id=1, source_target_pairs={{0,64},{32,480},{64,128},{96,32},{128,192},{160,96},{192,256},{224... | collective-permute-start | bytes 1572872 | tf_op jit(solution)/shard_map/ppermute | solution.py:35
  12.5 5.9 %collective-permute-start = (bf16[2,256,512]{2,1,0:T(8,128)(2,1)S(1)}, bf16[2,256,512]{2,1,0:T(8,128)(2,1)S(1)}, u32[]{:S(2)}, u32[]{:S(2)}) collective-permute-start(bf16[2,256,512]{2,1,0:T(8,128)(2,1)S(1)} %pad_maximum_fusion.refs_0_), channel_id=1, source_target_pairs={{0,32},{32,0},{64,96},{96,64},{128,160},{160,128},{192,224},{224,1... | collective-permute-start | bytes 1572872 | tf_op jit(solution)/shard_map/ppermute | solution.py:40
  20.4 8.2 %collective-permute-start.5 = (bf16[2,2,128,512]{3,2,1,0:T(8,128)(2,1)S(1)}, bf16[2,2,128,512]{3,2,1,0:T(8,128)(2,1)S(1)}, u32[]{:S(2)}, u32[]{:S(2)}) collective-permute-start(bf16[2,2,128,512]{3,2,1,0:T(8,128)(2,1)S(1)} %get-tuple-element.47), channel_id=1, source_target_pairs={{0,32},{32,0},{64,96},{96,64},{128,160},{160,128},{192,224},{224,1... | collective-permute-start | bytes 1572872 | tf_op jit(solution)/shard_map/ppermute | solution.py:40
  22.8 10.2 %collective-permute-start.6 = (bf16[2,256,512]{2,1,0:T(8,128)(2,1)S(1)}, bf16[2,256,512]{2,1,0:T(8,128)(2,1)S(1)}, u32[]{:S(2)}, u32[]{:S(2)}) collective-permute-start(bf16[2,256,512]{2,1,0:T(8,128)(2,1)S(1)} %collective-permute-done.refs_0_.refs_4_), channel_id=1, source_target_pairs={{0,64},{32,480},{64,128},{96,32},{128,192},{160,96},{192,256},{224... | collective-permute-start | bytes 1572872 | tf_op jit(solution)/shard_map/ppermute | solution.py:35
  25.0 16.6 %collective-permute-start.2 = (bf16[2,256,512]{2,1,0:T(8,128)(2,1)S(1)}, bf16[2,256,512]{2,1,0:T(8,128)(2,1)S(1)}, u32[]{:S(2)}, u32[]{:S(2)}) collective-permute-start(bf16[2,256,512]{2,1,0:T(8,128)(2,1)S(1)} %collective-permute-done.1.refs_1_.refs_5_), channel_id=1, source_target_pairs={{0,64},{32,480},{64,128},{96,32},{128,192},{160,96},{192,256},{224... | collective-permute-start | bytes 1572872 | tf_op jit(solution)/shard_map/ppermute | solution.py:35
  33.0 11.2 %collective-permute-start.7 = (bf16[2,256,512]{2,1,0:T(8,128)(2,1)S(1)}, bf16[2,256,512]{2,1,0:T(8,128)(2,1)S(1)}, u32[]{:S(2)}, u32[]{:S(2)}) collective-permute-start(bf16[2,256,512]{2,1,0:T(8,128)(2,1)S(1)} %collective-permute-done.6.refs_5_.refs_9_), channel_id=1, source_target_pairs={{0,64},{32,480},{64,128},{96,32},{128,192},{160,96},{192,256},{224... | collective-permute-start | bytes 1572872 | tf_op jit(solution)/shard_map/ppermute | solution.py:35
  36.1 17.0 %collective-permute-start.8 = (bf16[2,2,128,512]{3,2,1,0:T(8,128)(2,1)S(1)}, bf16[2,2,128,512]{3,2,1,0:T(8,128)(2,1)S(1)}, u32[]{:S(2)}, u32[]{:S(2)}) collective-permute-start(bf16[2,2,128,512]{3,2,1,0:T(8,128)(2,1)S(1)} %pad_maximum_fusion.1), channel_id=1, source_target_pairs={{0,2},{1,3},{2,4},{3,5},{4,6},{5,7},{6,8},{7,9},{8,10},{9,11},{10,... | collective-permute-start | bytes 1572872 | tf_op jit(solution)/shard_map/ppermute | solution.py:51
  41.6 11.7 %collective-permute-start.3 = (bf16[2,256,512]{2,1,0:T(8,128)(2,1)S(1)}, bf16[2,256,512]{2,1,0:T(8,128)(2,1)S(1)}, u32[]{:S(2)}, u32[]{:S(2)}) collective-permute-start(bf16[2,256,512]{2,1,0:T(8,128)(2,1)S(1)} %collective-permute-done.2.refs_2_.refs_6_), channel_id=1, source_target_pairs={{0,64},{32,480},{64,128},{96,32},{128,192},{160,96},{192,256},{224... | collective-permute-start | bytes 1572872 | tf_op jit(solution)/shard_map/ppermute | solution.py:35
  53.3 10.2 %collective-permute-start.4 = (bf16[2,256,512]{2,1,0:T(8,128)(2,1)S(1)}, bf16[2,256,512]{2,1,0:T(8,128)(2,1)S(1)}, u32[]{:S(2)}, u32[]{:S(2)}) collective-permute-start(bf16[2,256,512]{2,1,0:T(8,128)(2,1)S(1)} %collective-permute-done.3.refs_3_.refs_7_), channel_id=1, source_target_pairs={{0,64},{32,480},{64,128},{96,32},{128,192},{160,96},{192,256},{224... | collective-permute-start | bytes 1572872 | tf_op jit(solution)/shard_map/ppermute | solution.py:35
  55.9 10.2 %collective-permute-start.9 = (bf16[2,2,128,512]{3,2,1,0:T(8,128)(2,1)S(1)}, bf16[2,2,128,512]{3,2,1,0:T(8,128)(2,1)S(1)}, u32[]{:S(2)}, u32[]{:S(2)}) collective-permute-start(bf16[2,2,128,512]{3,2,1,0:T(8,128)(2,1)S(1)} %pad_maximum_fusion.2), channel_id=1, source_target_pairs={{0,1},{1,2},{2,3},{3,4},{4,5},{5,6},{6,7},{7,8},{8,9},{9,10},{10,1... | collective-permute-start | bytes 1572872 | tf_op jit(solution)/shard_map/ppermute | solution.py:51
  58.8 10.3 %collective-permute-start.11 = (bf16[2,256,512]{2,1,0:T(8,128)(2,1)S(1)}, bf16[2,256,512]{2,1,0:T(8,128)(2,1)S(1)}, u32[]{:S(2)}, u32[]{:S(2)}) collective-permute-start(bf16[2,256,512]{2,1,0:T(8,128)(2,1)S(1)} %collective-permute-done.7.refs_6_.refs_10_), channel_id=1, source_target_pairs={{0,64},{32,480},{64,128},{96,32},{128,192},{160,96},{192,256},{224... | collective-permute-start | bytes 1572872 | tf_op jit(solution)/shard_map/ppermute | solution.py:35
  70.2 9.0 %copy-start.4 = (bf16[256,512]{1,0:T(8,128)(2,1)S(1)}, bf16[256,512]{1,0:T(8,128)(2,1)}, u32[]{:S(2)}) copy-start(bf16[256,512]{1,0:T(8,128)(2,1)} %param.6) | copy-start | bytes 786436
  70.2 9.0 %copy-start.5 = (bf16[256,512]{1,0:T(8,128)(2,1)S(1)}, bf16[256,512]{1,0:T(8,128)(2,1)}, u32[]{:S(2)}) copy-start(bf16[256,512]{1,0:T(8,128)(2,1)} %param.9) | copy-start | bytes 786436
  70.2 9.0 %collective-permute-start.12 = (bf16[6,2,128,512]{3,2,1,0:T(8,128)(2,1)S(1)}, bf16[6,2,128,512]{3,2,1,0:T(8,128)(2,1)S(1)}, u32[]{:S(2)}, u32[]{:S(2)}) collective-permute-start(bf16[6,2,128,512]{3,2,1,0:T(8,128)(2,1)S(1)} %shard_map.94), channel_id=1, source_target_pairs={{0,32},{32,0},{64,96},{96,64},{128,160},{160,128},{192,224},{224,1... | collective-permute-start | bytes 4718600 | tf_op jit(solution)/shard_map/ppermute | solution.py:40
  75.4 3.8 %collective-permute-start.10 = (bf16[2,2,128,512]{3,2,1,0:T(8,128)(2,1)S(1)}, bf16[2,2,128,512]{3,2,1,0:T(8,128)(2,1)S(1)}, u32[]{:S(2)}, u32[]{:S(2)}) collective-permute-start(bf16[2,2,128,512]{3,2,1,0:T(8,128)(2,1)S(1)} %pad_maximum_fusion.3), channel_id=1, source_target_pairs={{0,32},{32,0},{64,96},{96,64},{128,160},{160,128},{192,224},{224,1... | collective-permute-start | bytes 1572872 | tf_op jit(solution)/shard_map/ppermute | solution.py:40
  93.0 5.3 %collective-permute-start.13 = (bf16[6,2,128,512]{3,2,1,0:T(8,128)(2,1)S(1)}, bf16[6,2,128,512]{3,2,1,0:T(8,128)(2,1)S(1)}, u32[]{:S(2)}, u32[]{:S(2)}) collective-permute-start(bf16[6,2,128,512]{3,2,1,0:T(8,128)(2,1)S(1)} %get-tuple-element.61.mine), channel_id=1, source_target_pairs={{0,32},{32,0},{64,96},{96,64},{128,160},{160,128},{192,224},{224,1... | collective-permute-start | bytes 4718600 | tf_op jit(solution)/shard_map/ppermute | solution.py:40
  99.1 10.2 %collective-permute-start.14 = (bf16[2,2,128,512]{3,2,1,0:T(8,128)(2,1)S(1)}, bf16[2,2,128,512]{3,2,1,0:T(8,128)(2,1)S(1)}, u32[]{:S(2)}, u32[]{:S(2)}) collective-permute-start(bf16[2,2,128,512]{3,2,1,0:T(8,128)(2,1)S(1)} %get-tuple-element.65), channel_id=1, source_target_pairs={{0,64},{32,480},{64,128},{96,32},{128,192},{160,96},{192,256},{224... | collective-permute-start | bytes 1572872 | tf_op jit(solution)/shard_map/ppermute | solution.py:35
  101.5 11.3 %collective-permute-start.18 = (bf16[2,2,128,512]{3,2,1,0:T(8,128)(2,1)S(1)}, bf16[2,2,128,512]{3,2,1,0:T(8,128)(2,1)S(1)}, u32[]{:S(2)}, u32[]{:S(2)}) collective-permute-start(bf16[2,2,128,512]{3,2,1,0:T(8,128)(2,1)S(1)} %get-tuple-element.71), channel_id=1, source_target_pairs={{0,32},{32,0},{64,96},{96,64},{128,160},{160,128},{192,224},{224,1... | collective-permute-start | bytes 1572872 | tf_op jit(solution)/shard_map/ppermute | solution.py:40
  103.5 13.4 %collective-permute-start.19 = (bf16[2,2,128,512]{3,2,1,0:T(8,128)(2,1)S(1)}, bf16[2,2,128,512]{3,2,1,0:T(8,128)(2,1)S(1)}, u32[]{:S(2)}, u32[]{:S(2)}) collective-permute-start(bf16[2,2,128,512]{3,2,1,0:T(8,128)(2,1)S(1)} %get-tuple-element.72), channel_id=1, source_target_pairs={{0,64},{32,480},{64,128},{96,32},{128,192},{160,96},{192,256},{224... | collective-permute-start | bytes 1572872 | tf_op jit(solution)/shard_map/ppermute | solution.py:35
  109.4 11.1 %collective-permute-start.15 = (bf16[2,2,128,512]{3,2,1,0:T(8,128)(2,1)S(1)}, bf16[2,2,128,512]{3,2,1,0:T(8,128)(2,1)S(1)}, u32[]{:S(2)}, u32[]{:S(2)}) collective-permute-start(bf16[2,2,128,512]{3,2,1,0:T(8,128)(2,1)S(1)} %add_convert_fusion.4), channel_id=1, source_target_pairs={{0,64},{32,480},{64,128},{96,32},{128,192},{160,96},{192,256},{224... | collective-permute-start | bytes 1572872 | tf_op jit(solution)/shard_map/ppermute | solution.py:35
  112.9 13.3 %collective-permute-start.21 = (bf16[2,2,128,512]{3,2,1,0:T(8,128)(2,1)S(1)}, bf16[2,2,128,512]{3,2,1,0:T(8,128)(2,1)S(1)}, u32[]{:S(2)}, u32[]{:S(2)}) collective-permute-start(bf16[2,2,128,512]{3,2,1,0:T(8,128)(2,1)S(1)} %pad_maximum_fusion.4), channel_id=1, source_target_pairs={{2,0},{3,1},{4,2},{5,3},{6,4},{7,5},{8,6},{9,7},{10,8},{11,9},{12,... | collective-permute-start | bytes 1572872 | tf_op jit(solution)/shard_map/ppermute | solution.py:51
  117.1 10.2 %collective-permute-start.20 = (bf16[2,2,128,512]{3,2,1,0:T(8,128)(2,1)S(1)}, bf16[2,2,128,512]{3,2,1,0:T(8,128)(2,1)S(1)}, u32[]{:S(2)}, u32[]{:S(2)}) collective-permute-start(bf16[2,2,128,512]{3,2,1,0:T(8,128)(2,1)S(1)} %add_convert_fusion.1), channel_id=1, source_target_pairs={{0,64},{32,480},{64,128},{96,32},{128,192},{160,96},{192,256},{224... | collective-permute-start | bytes 1572872 | tf_op jit(solution)/shard_map/ppermute | solution.py:35
  120.7 12.4 %collective-permute-start.16 = (bf16[2,2,128,512]{3,2,1,0:T(8,128)(2,1)S(1)}, bf16[2,2,128,512]{3,2,1,0:T(8,128)(2,1)S(1)}, u32[]{:S(2)}, u32[]{:S(2)}) collective-permute-start(bf16[2,2,128,512]{3,2,1,0:T(8,128)(2,1)S(1)} %add_convert_fusion.3), channel_id=1, source_target_pairs={{0,64},{32,480},{64,128},{96,32},{128,192},{160,96},{192,256},{224... | collective-permute-start | bytes 1572872 | tf_op jit(solution)/shard_map/ppermute | solution.py:35
  126.2 6.8 %copy-start = (bf16[2,2,128,512]{3,2,1,0:T(8,128)(2,1)}, bf16[2,2,128,512]{3,2,1,0:T(8,128)(2,1)S(1)}, u32[]{:S(2)}) copy-start(bf16[2,2,128,512]{3,2,1,0:T(8,128)(2,1)S(1)} %collective-permute-done.21.refs_1_) | copy-start | bytes 1572868
  127.4 14.5 %collective-permute-start.22 = (bf16[2,2,128,512]{3,2,1,0:T(8,128)(2,1)S(1)}, bf16[2,2,128,512]{3,2,1,0:T(8,128)(2,1)S(1)}, u32[]{:S(2)}, u32[]{:S(2)}) collective-permute-start(bf16[2,2,128,512]{3,2,1,0:T(8,128)(2,1)S(1)} %pad_maximum_fusion.5), channel_id=1, source_target_pairs={{1,0},{2,1},{3,2},{4,3},{5,4},{6,5},{7,6},{8,7},{9,8},{10,9},{11,1... | collective-permute-start | bytes 1572872 | tf_op jit(solution)/shard_map/ppermute | solution.py:51
  129.5 12.6 %collective-permute-start.23 = (bf16[2,2,128,512]{3,2,1,0:T(8,128)(2,1)S(1)}, bf16[2,2,128,512]{3,2,1,0:T(8,128)(2,1)S(1)}, u32[]{:S(2)}, u32[]{:S(2)}) collective-permute-start(bf16[2,2,128,512]{3,2,1,0:T(8,128)(2,1)S(1)} %add_convert_fusion), channel_id=1, source_target_pairs={{0,64},{32,480},{64,128},{96,32},{128,192},{160,96},{192,256},{224... | collective-permute-start | bytes 1572872 | tf_op jit(solution)/shard_map/ppermute | solution.py:35
  133.1 8.9 %slice-start = ((bf16[2,2,128,512]{3,2,1,0:T(8,128)(2,1)}), bf16[1,2,128,512]{3,2,1,0:T(8,128)(2,1)S(1)}, s32[]{:S(2)}) async-start(bf16[2,2,128,512]{3,2,1,0:T(8,128)(2,1)} %copy-done), calls=%async_computation | async-start | bytes 524288 | tf_op jit(solution)/shard_map/slice | solution.py:411
  133.1 20.9 %copy-start.1 = (bf16[2,2,128,512]{3,2,1,0:T(8,128)(2,1)S(1)}, bf16[2,2,128,512]{3,2,1,0:T(8,128)(2,1)}, u32[]{:S(2)}) copy-start(bf16[2,2,128,512]{3,2,1,0:T(8,128)(2,1)} %copy-done) | copy-start | bytes 1572868
  133.2 18.9 %collective-permute-start.17 = (bf16[2,2,128,512]{3,2,1,0:T(8,128)(2,1)S(1)}, bf16[2,2,128,512]{3,2,1,0:T(8,128)(2,1)S(1)}, u32[]{:S(2)}, u32[]{:S(2)}) collective-permute-start(bf16[2,2,128,512]{3,2,1,0:T(8,128)(2,1)S(1)} %add_convert_fusion.2), channel_id=1, source_target_pairs={{0,64},{32,480},{64,128},{96,32},{128,192},{160,96},{192,256},{224... | collective-permute-start | bytes 1572872 | tf_op jit(solution)/shard_map/ppermute | solution.py:35
  142.0 10.1 %collective-permute-start.24 = (bf16[2,2,128,512]{3,2,1,0:T(8,128)(2,1)S(1)}, bf16[2,2,128,512]{3,2,1,0:T(8,128)(2,1)S(1)}, u32[]{:S(2)}, u32[]{:S(2)}) collective-permute-start(bf16[2,2,128,512]{3,2,1,0:T(8,128)(2,1)S(1)} %collective-permute-done.23), channel_id=1, source_target_pairs={{0,32},{32,0},{64,96},{96,64},{128,160},{160,128},{192,224},{224,1... | collective-permute-start | bytes 1572872 | tf_op jit(solution)/shard_map/ppermute | solution.py:40
  150.2 3.8 %collective-permute-start.25 = (bf16[2,2,128,512]{3,2,1,0:T(8,128)(2,1)S(1)}, bf16[2,2,128,512]{3,2,1,0:T(8,128)(2,1)S(1)}, u32[]{:S(2)}, u32[]{:S(2)}) collective-permute-start(bf16[2,2,128,512]{3,2,1,0:T(8,128)(2,1)S(1)} %pad_maximum_fusion.6), channel_id=1, source_target_pairs={{0,32},{32,0},{64,96},{96,64},{128,160},{160,128},{192,224},{224,1... | collective-permute-start | bytes 1572872 | tf_op jit(solution)/shard_map/ppermute | solution.py:40

commit v7 on v6

--- a/solution.py
+++ b/solution.py
@@ -149,22 +149,22 @@
         return jnp.concatenate([both[:64, :128], both[64:, 128:]], axis=0)
 
     scores = lax.dot_general(keys, query2, last, preferred_element_type=F32)
+    grad_weights = lax.dot_general(values, grad2, last, preferred_element_type=F32)
     highest = jnp.max(scores, axis=0, keepdims=True)
     raised = jnp.exp2((scores - highest) * (0.125 * math.log2(math.e)))
     weights = raised * (1.0 / jnp.sum(raised, axis=0, keepdims=True))
     weights_low = weights.astype(BF)
+    grad_value = jnp.dot(weights_low, grad2, preferred_element_type=F32)
     mixture = own_heads(lax.dot_general(values, weights_low, first, preferred_element_type=F32))
     att_ref[s, :, cols] = mixture.T.astype(BF)
     product = mixture * grad.astype(F32).T
     carried = jnp.concatenate(
         [jnp.sum(product[:64], axis=0, keepdims=True), jnp.sum(product[64:], axis=0, keepdims=True)], axis=1
     )
-    grad_weights = lax.dot_general(values, grad2, last, preferred_element_type=F32)
     grad_scores = ((weights * (grad_weights - carried)) * 0.125).astype(BF)
     grad_query = own_heads(lax.dot_general(keys, grad_scores, first, preferred_element_type=F32))
     gq_ref[s, :, cols] = grad_query.T.astype(BF)
     grad_key = jnp.dot(grad_scores, query2, preferred_element_type=F32)
-    grad_value = jnp.dot(weights_low, grad2, preferred_element_type=F32)
     for j in range(KB):
         slot = table[2, s * KB + j]
         again = table[3, s * KB + j] == 0
@@ -216,7 +216,12 @@
 
     for s in range(NB):
         pltpu.make_async_copy(listed.at[s], listed.at[s], sem.at[s]).wait()
-        lax.fori_loop(s * PAIRS, (s + 1) * PAIRS, body, 0, unroll=PAIRS)
+
+    def body(step, carry):
+        attend_pair(step, table, q_ref, g_ref, listed, att_ref, gq_ref, totals)
+        return carry
+
+    lax.fori_loop(0, NB * PAIRS, body, 0, unroll=PAIRS)
     own_out[...] = totals[:NB].astype(BF)
     keep_out[...] = totals[NB : NB + W].astype(BF)
     give_out[...] = totals[NB + W : NEAR].astype(BF)
@@ -360,9 +365,9 @@
     last = jnp.concatenate([given, hits[1, 7 * NB :]]).astype(i32)
     tables = (given, pick_table, table, hits[:, : 2 * NB], hits[:, 2 * NB : 7 * NB], last)
     sibling, tables = lax.optimization_barrier((sibling, tables))
+    flow_b = [ring_step(sibling)]
     given, pick_table, table, hits_first, hits_rest, last = tables
 
-    flow_b = [ring_step(sibling)]
     flow_a.append(ring_step(flow_a[0]))
     keep, give = offer(given, keys, values)
     given_here = swap_cores(give)

time: 157 us -> 155 us (0.987)
  Pallas kernels: 20.7 us -> 19 us
    pallas_call x1, Pallas kernels: 13.8 us -> 12.1 us  [attend(): pl.pallas_call(attend_kernel, out_shape=(jax.ShapeDtypeStruct((NB, BS, D)...]
where the time goes in v7:
time: 155 us; the launch traced here: 154 us
  starting transfers between devices  89.9 us (58%)
  waiting for transfers between devices  37.9 us (24%)
  Pallas kernels  19 us (12%)
  other arithmetic  3.3 us (2%)
  local copies, waits for them, and re-layouts  2.83 us (2%)
    ppermute x14, starting transfers between devices, ring_step(): lax.ppermute(array, 'group', [(g, (g + (2 if g % 2 == 0 else -2)) % size)...  50.3 us
    ppermute x8, starting transfers between devices, swap_cores(): return lax.ppermute(array, 'group', [(g, g ^ 1) for g in range(size)])  25.4 us
    ppermute x4, waiting for transfers between devices, dom_step(): return lax.ppermute(array, ('group', 'dom'), pairs)  18.5 us
    ppermute x4, starting transfers between devices, dom_step(): return lax.ppermute(array, ('group', 'dom'), pairs)  14.2 us
    ppermute x14, waiting for transfers between devices, ring_step(): lax.ppermute(array, 'group', [(g, (g + (2 if g % 2 == 0 else -2)) % size)...  12.5 us
    pallas_call x1, Pallas kernels, attend(): pl.pallas_call(attend_kernel, out_shape=(jax.ShapeDtypeStruct((NB, BS, D)...  12.1 us
    ppermute x8, waiting for transfers between devices, swap_cores(): return lax.ppermute(array, 'group', [(g, g ^ 1) for g in range(size)])  6.91 us
  transfers between devices with their start and end apart: 26, of which 13 were waited for; matrix products, arithmetic and copies ran while one was open for 3% of the time, Pallas kernels for 2%

profile of v7, /device:TPU:57, one launch (start us, length us, event | category | flops | bytes accessed | tf_op | source)
XLA Modules:
  0.0 154.3 jit_solution(10593493997357504920)
XLA Ops:
  0.7 1.1 pad_maximum_fusion.refs_0_
  1.8 10.7 %collective-permute-start.1 = (bf16[2,256,512]{2,1,0:T(8,128)(2,1)S(1)}, bf16[2,256,512]{2,1,0:T(8,128)(2,1)S(1)}, u32[]{:S(2)}, u32[]{:S(2)}) collective-permute-start(bf16[2,256,512]{2,1,0:T(8,128)(2,1)S(1)} %pad_maximum_fusion.refs_0_), channel_id=1, source_target_pairs={{0,64},{32,480},{64,128},{96,32},{128,192},{160,96},{192,256},{224... | collective-permute-start | bytes 1572872 | tf_op jit(solution)/shard_map/ppermute | solution.py:35
  12.5 1.9 %collective-permute-start = (bf16[2,256,512]{2,1,0:T(8,128)(2,1)S(1)}, bf16[2,256,512]{2,1,0:T(8,128)(2,1)S(1)}, u32[]{:S(2)}, u32[]{:S(2)}) collective-permute-start(bf16[2,256,512]{2,1,0:T(8,128)(2,1)S(1)} %pad_maximum_fusion.refs_0_), channel_id=1, source_target_pairs={{0,32},{32,0},{64,96},{96,64},{128,160},{160,128},{192,224},{224,1... | collective-permute-start | bytes 1572872 | tf_op jit(solution)/shard_map/ppermute | solution.py:40
  14.6 0.8 copy.15
  15.4 0.2 select_reduce_fusion.3
  15.6 0.1 stack.113
  15.7 0.1 select_reduce_fusion.2
  15.9 0.1 add.216
  16.0 0.1 squeeze.8
  16.1 0.8 copy.14
  16.9 0.1 fusion.2
  17.1 0.1 eq.193
  17.2 0.2 select_reduce_fusion
  17.5 0.1 reduce_max.18
  17.7 0.1 rev.3
  18.0 0.1 stack_reshape.11
  18.4 2.0 %shard_map.93 = (bf16[2,2,128,512]{3,2,1,0:T(8,128)(2,1)S(1)}, bf16[2,2,128,512]{3,2,1,0:T(8,128)(2,1)S(1)}) custom-call(s32[4]{0:T(128)S(1)} %broadcast_select_fusion.2.table, bf16[256,512]{1,0:T(8,128)(2,1)S(1)} %copy-done.3, bf16[256,512]{1,0:T(8,128)(2,1)S(1)} %copy-done.2), custom_call_target="tpu_custom_call" | custom-call | bytes 2097152 | tf_op jit(solution)/shard_map/pallas_call | solution.py:122
  20.4 2.4 %collective-permute-start.5 = (bf16[2,2,128,512]{3,2,1,0:T(8,128)(2,1)S(1)}, bf16[2,2,128,512]{3,2,1,0:T(8,128)(2,1)S(1)}, u32[]{:S(2)}, u32[]{:S(2)}) collective-permute-start(bf16[2,2,128,512]{3,2,1,0:T(8,128)(2,1)S(1)} %get-tuple-element.47), channel_id=1, source_target_pairs={{0,32},{32,0},{64,96},{96,64},{128,160},{160,128},{192,224},{224,1... | collective-permute-start | bytes 1572872 | tf_op jit(solution)/shard_map/ppermute | solution.py:40
  22.8 2.2 %collective-permute-start.6 = (bf16[2,256,512]{2,1,0:T(8,128)(2,1)S(1)}, bf16[2,256,512]{2,1,0:T(8,128)(2,1)S(1)}, u32[]{:S(2)}, u32[]{:S(2)}) collective-permute-start(bf16[2,256,512]{2,1,0:T(8,128)(2,1)S(1)} %collective-permute-done.refs_0_.refs_4_), channel_id=1, source_target_pairs={{0,64},{32,480},{64,128},{96,32},{128,192},{160,96},{192,256},{224... | collective-permute-start | bytes 1572872 | tf_op jit(solution)/shard_map/ppermute | solution.py:35
  25.0 3.6 %collective-permute-start.2 = (bf16[2,256,512]{2,1,0:T(8,128)(2,1)S(1)}, bf16[2,256,512]{2,1,0:T(8,128)(2,1)S(1)}, u32[]{:S(2)}, u32[]{:S(2)}) collective-permute-start(bf16[2,256,512]{2,1,0:T(8,128)(2,1)S(1)} %collective-permute-done.1.refs_1_.refs_5_), channel_id=1, source_target_pairs={{0,64},{32,480},{64,128},{96,32},{128,192},{160,96},{192,256},{224... | collective-permute-start | bytes 1572872 | tf_op jit(solution)/shard_map/ppermute | solution.py:35
  28.7 4.3 %collective-permute-done.6.refs_5_.refs_9_ = bf16[2,256,512]{2,1,0:T(8,128)(2,1)S(1)} collective-permute-done((bf16[2,256,512]{2,1,0:T(8,128)(2,1)S(1)}, bf16[2,256,512]{2,1,0:T(8,128)(2,1)S(1)}, u32[]{:S(2)}, u32[]{:S(2)}) %collective-permute-start.6) | collective-permute-done | bytes 524320 | tf_op jit(solution)/shard_map/ppermute | solution.py:35
  33.0 3.1 %collective-permute-start.7 = (bf16[2,256,512]{2,1,0:T(8,128)(2,1)S(1)}, bf16[2,256,512]{2,1,0:T(8,128)(2,1)S(1)}, u32[]{:S(2)}, u32[]{:S(2)}) collective-permute-start(bf16[2,256,512]{2,1,0:T(8,128)(2,1)S(1)} %collective-permute-done.6.refs_5_.refs_9_), channel_id=1, source_target_pairs={{0,64},{32,480},{64,128},{96,32},{128,192},{160,96},{192,256},{224... | collective-permute-start | bytes 1572872 | tf_op jit(solution)/shard_map/ppermute | solution.py:35
  36.1 5.4 %collective-permute-start.8 = (bf16[2,2,128,512]{3,2,1,0:T(8,128)(2,1)S(1)}, bf16[2,2,128,512]{3,2,1,0:T(8,128)(2,1)S(1)}, u32[]{:S(2)}, u32[]{:S(2)}) collective-permute-start(bf16[2,2,128,512]{3,2,1,0:T(8,128)(2,1)S(1)} %pad_maximum_fusion.1), channel_id=1, source_target_pairs={{0,2},{1,3},{2,4},{3,5},{4,6},{5,7},{6,8},{7,9},{8,10},{9,11},{10,... | collective-permute-start | bytes 1572872 | tf_op jit(solution)/shard_map/ppermute | solution.py:51
  41.6 2.6 %collective-permute-start.3 = (bf16[2,256,512]{2,1,0:T(8,128)(2,1)S(1)}, bf16[2,256,512]{2,1,0:T(8,128)(2,1)S(1)}, u32[]{:S(2)}, u32[]{:S(2)}) collective-permute-start(bf16[2,256,512]{2,1,0:T(8,128)(2,1)S(1)} %collective-permute-done.2.refs_2_.refs_6_), channel_id=1, source_target_pairs={{0,64},{32,480},{64,128},{96,32},{128,192},{160,96},{192,256},{224... | collective-permute-start | bytes 1572872 | tf_op jit(solution)/shard_map/ppermute | solution.py:35
  44.2 8.9 %collective-permute-done.8.refs_2_ = bf16[2,2,128,512]{3,2,1,0:T(8,128)(2,1)S(1)} collective-permute-done((bf16[2,2,128,512]{3,2,1,0:T(8,128)(2,1)S(1)}, bf16[2,2,128,512]{3,2,1,0:T(8,128)(2,1)S(1)}, u32[]{:S(2)}, u32[]{:S(2)}) %collective-permute-start.8) | collective-permute-done | bytes 524320 | tf_op jit(solution)/shard_map/ppermute | solution.py:51
  53.3 2.6 %collective-permute-start.4 = (bf16[2,256,512]{2,1,0:T(8,128)(2,1)S(1)}, bf16[2,256,512]{2,1,0:T(8,128)(2,1)S(1)}, u32[]{:S(2)}, u32[]{:S(2)}) collective-permute-start(bf16[2,256,512]{2,1,0:T(8,128)(2,1)S(1)} %collective-permute-done.3.refs_3_.refs_7_), channel_id=1, source_target_pairs={{0,64},{32,480},{64,128},{96,32},{128,192},{160,96},{192,256},{224... | collective-permute-start | bytes 1572872 | tf_op jit(solution)/shard_map/ppermute | solution.py:35
  55.9 2.9 %collective-permute-start.9 = (bf16[2,2,128,512]{3,2,1,0:T(8,128)(2,1)S(1)}, bf16[2,2,128,512]{3,2,1,0:T(8,128)(2,1)S(1)}, u32[]{:S(2)}, u32[]{:S(2)}) collective-permute-start(bf16[2,2,128,512]{3,2,1,0:T(8,128)(2,1)S(1)} %pad_maximum_fusion.2), channel_id=1, source_target_pairs={{0,1},{1,2},{2,3},{3,4},{4,5},{5,6},{6,7},{7,8},{8,9},{9,10},{10,1... | collective-permute-start | bytes 1572872 | tf_op jit(solution)/shard_map/ppermute | solution.py:51
  58.8 2.2 %collective-permute-start.11 = (bf16[2,256,512]{2,1,0:T(8,128)(2,1)S(1)}, bf16[2,256,512]{2,1,0:T(8,128)(2,1)S(1)}, u32[]{:S(2)}, u32[]{:S(2)}) collective-permute-start(bf16[2,256,512]{2,1,0:T(8,128)(2,1)S(1)} %collective-permute-done.7.refs_6_.refs_10_), channel_id=1, source_target_pairs={{0,64},{32,480},{64,128},{96,32},{128,192},{160,96},{192,256},{224... | collective-permute-start | bytes 1572872 | tf_op jit(solution)/shard_map/ppermute | solution.py:35
  61.0 2.5 %collective-permute-done.4.refs_4_.refs_8_ = bf16[2,256,512]{2,1,0:T(8,128)(2,1)S(1)} collective-permute-done((bf16[2,256,512]{2,1,0:T(8,128)(2,1)S(1)}, bf16[2,256,512]{2,1,0:T(8,128)(2,1)S(1)}, u32[]{:S(2)}, u32[]{:S(2)}) %collective-permute-start.4) | collective-permute-done | bytes 524320 | tf_op jit(solution)/shard_map/ppermute | solution.py:35
  63.5 2.7 %collective-permute-done.9.refs_1_ = bf16[2,2,128,512]{3,2,1,0:T(8,128)(2,1)S(1)} collective-permute-done((bf16[2,2,128,512]{3,2,1,0:T(8,128)(2,1)S(1)}, bf16[2,2,128,512]{3,2,1,0:T(8,128)(2,1)S(1)}, u32[]{:S(2)}, u32[]{:S(2)}) %collective-permute-start.9) | collective-permute-done | bytes 524320 | tf_op jit(solution)/shard_map/ppermute | solution.py:51
  66.1 3.0 %collective-permute-done.11.refs_7_.refs_11_ = bf16[2,256,512]{2,1,0:T(8,128)(2,1)S(1)} collective-permute-done((bf16[2,256,512]{2,1,0:T(8,128)(2,1)S(1)}, bf16[2,256,512]{2,1,0:T(8,128)(2,1)S(1)}, u32[]{:S(2)}, u32[]{:S(2)}) %collective-permute-start.11) | collective-permute-done | bytes 524320 | tf_op jit(solution)/shard_map/ppermute | solution.py:35
  69.1 1.1 shard_map.94
  70.3 5.0 %collective-permute-start.12 = (bf16[6,2,128,512]{3,2,1,0:T(8,128)(2,1)S(1)}, bf16[6,2,128,512]{3,2,1,0:T(8,128)(2,1)S(1)}, u32[]{:S(2)}, u32[]{:S(2)}) collective-permute-start(bf16[6,2,128,512]{3,2,1,0:T(8,128)(2,1)S(1)} %shard_map.94), channel_id=1, source_target_pairs={{0,32},{32,0},{64,96},{96,64},{128,160},{160,128},{192,224},{224,1... | collective-permute-start | bytes 4718600 | tf_op jit(solution)/shard_map/ppermute | solution.py:40
  75.4 1.9 %collective-permute-start.10 = (bf16[2,2,128,512]{3,2,1,0:T(8,128)(2,1)S(1)}, bf16[2,2,128,512]{3,2,1,0:T(8,128)(2,1)S(1)}, u32[]{:S(2)}, u32[]{:S(2)}) collective-permute-start(bf16[2,2,128,512]{3,2,1,0:T(8,128)(2,1)S(1)} %pad_maximum_fusion.3), channel_id=1, source_target_pairs={{0,32},{32,0},{64,96},{96,64},{128,160},{160,128},{192,224},{224,1... | collective-permute-start | bytes 1572872 | tf_op jit(solution)/shard_map/ppermute | solution.py:40
  77.3 1.9 %collective-permute-done.10.refs_3_ = bf16[2,2,128,512]{3,2,1,0:T(8,128)(2,1)S(1)} collective-permute-done((bf16[2,2,128,512]{3,2,1,0:T(8,128)(2,1)S(1)}, bf16[2,2,128,512]{3,2,1,0:T(8,128)(2,1)S(1)}, u32[]{:S(2)}, u32[]{:S(2)}) %collective-permute-start.10) | collective-permute-done | bytes 524320 | tf_op jit(solution)/shard_map/ppermute | solution.py:40
  79.2 12.1 %shard_map.95 = (bf16[2,128,512]{2,1,0:T(8,128)(2,1)}, bf16[2,128,512]{2,1,0:T(8,128)(2,1)}, bf16[2,2,128,512]{3,2,1,0:T(8,128)(2,1)S(1)}, bf16[6,2,128,512]{3,2...) custom-call(s32[4,14]{1,0:T(4,128)S(1)} %pad_add_fusion.table, ...), custom_call_target="tpu_custom_call" | custom-call | flops 1409286144 | bytes 12582912 | tf_op jit(solution)/shard_map/pallas_call | solution.py:232
  91.3 2.1 %collective-permute-start.13 = (bf16[6,2,128,512]{3,2,1,0:T(8,128)(2,1)S(1)}, bf16[6,2,128,512]{3,2,1,0:T(8,128)(2,1)S(1)}, u32[]{:S(2)}, u32[]{:S(2)}) collective-permute-start(bf16[6,2,128,512]{3,2,1,0:T(8,128)(2,1)S(1)} %get-tuple-element.61.mine), channel_id=1, source_target_pairs={{0,32},{32,0},{64,96},{96,64},{128,160},{160,128},{192,224},{224,1... | collective-permute-start | bytes 4718600 | tf_op jit(solution)/shard_map/ppermute | solution.py:40
  93.4 3.2 %collective-permute-done.13.theirs = bf16[6,2,128,512]{3,2,1,0:T(8,128)(2,1)S(1)} collective-permute-done((bf16[6,2,128,512]{3,2,1,0:T(8,128)(2,1)S(1)}, bf16[6,2,128,512]{3,2,1,0:T(8,128)(2,1)S(1)}, u32[]{:S(2)}, u32[]{:S(2)}) %collective-permute-start.13) | collective-permute-done | bytes 1572896 | tf_op jit(solution)/shard_map/ppermute | solution.py:40
  96.6 0.9 shard_map.96
  97.5 2.5 %collective-permute-start.14 = (bf16[2,2,128,512]{3,2,1,0:T(8,128)(2,1)S(1)}, bf16[2,2,128,512]{3,2,1,0:T(8,128)(2,1)S(1)}, u32[]{:S(2)}, u32[]{:S(2)}) collective-permute-start(bf16[2,2,128,512]{3,2,1,0:T(8,128)(2,1)S(1)} %get-tuple-element.65), channel_id=1, source_target_pairs={{0,64},{32,480},{64,128},{96,32},{128,192},{160,96},{192,256},{224... | collective-permute-start | bytes 1572872 | tf_op jit(solution)/shard_map/ppermute | solution.py:35
  100.0 1.9 %collective-permute-start.18 = (bf16[2,2,128,512]{3,2,1,0:T(8,128)(2,1)S(1)}, bf16[2,2,128,512]{3,2,1,0:T(8,128)(2,1)S(1)}, u32[]{:S(2)}, u32[]{:S(2)}) collective-permute-start(bf16[2,2,128,512]{3,2,1,0:T(8,128)(2,1)S(1)} %get-tuple-element.71), channel_id=1, source_target_pairs={{0,32},{32,0},{64,96},{96,64},{128,160},{160,128},{192,224},{224,1... | collective-permute-start | bytes 1572872 | tf_op jit(solution)/shard_map/ppermute | solution.py:40
  101.9 4.5 %collective-permute-start.19 = (bf16[2,2,128,512]{3,2,1,0:T(8,128)(2,1)S(1)}, bf16[2,2,128,512]{3,2,1,0:T(8,128)(2,1)S(1)}, u32[]{:S(2)}, u32[]{:S(2)}) collective-permute-start(bf16[2,2,128,512]{3,2,1,0:T(8,128)(2,1)S(1)} %get-tuple-element.72), channel_id=1, source_target_pairs={{0,64},{32,480},{64,128},{96,32},{128,192},{160,96},{192,256},{224... | collective-permute-start | bytes 1572872 | tf_op jit(solution)/shard_map/ppermute | solution.py:35
  106.4 0.9 shard_map.97
  107.4 0.3 collective-permute-done.14
  107.7 0.1 add_convert_fusion.4
  107.8 3.4 %collective-permute-start.15 = (bf16[2,2,128,512]{3,2,1,0:T(8,128)(2,1)S(1)}, bf16[2,2,128,512]{3,2,1,0:T(8,128)(2,1)S(1)}, u32[]{:S(2)}, u32[]{:S(2)}) collective-permute-start(bf16[2,2,128,512]{3,2,1,0:T(8,128)(2,1)S(1)} %add_convert_fusion.4), channel_id=1, source_target_pairs={{0,64},{32,480},{64,128},{96,32},{128,192},{160,96},{192,256},{224... | collective-permute-start | bytes 1572872 | tf_op jit(solution)/shard_map/ppermute | solution.py:35
  111.4 4.0 %collective-permute-start.21 = (bf16[2,2,128,512]{3,2,1,0:T(8,128)(2,1)S(1)}, bf16[2,2,128,512]{3,2,1,0:T(8,128)(2,1)S(1)}, u32[]{:S(2)}, u32[]{:S(2)}) collective-permute-start(bf16[2,2,128,512]{3,2,1,0:T(8,128)(2,1)S(1)} %pad_maximum_fusion.4), channel_id=1, source_target_pairs={{2,0},{3,1},{4,2},{5,3},{6,4},{7,5},{8,6},{9,7},{10,8},{11,9},{12,... | collective-permute-start | bytes 1572872 | tf_op jit(solution)/shard_map/ppermute | solution.py:51
  115.4 0.1 add_convert_fusion.1
  115.5 2.2 %collective-permute-start.20 = (bf16[2,2,128,512]{3,2,1,0:T(8,128)(2,1)S(1)}, bf16[2,2,128,512]{3,2,1,0:T(8,128)(2,1)S(1)}, u32[]{:S(2)}, u32[]{:S(2)}) collective-permute-start(bf16[2,2,128,512]{3,2,1,0:T(8,128)(2,1)S(1)} %add_convert_fusion.1), channel_id=1, source_target_pairs={{0,64},{32,480},{64,128},{96,32},{128,192},{160,96},{192,256},{224... | collective-permute-start | bytes 1572872 | tf_op jit(solution)/shard_map/ppermute | solution.py:35
  117.7 1.2 collective-permute-done.15
  118.9 0.1 add_convert_fusion.3
  119.1 4.2 %collective-permute-start.16 = (bf16[2,2,128,512]{3,2,1,0:T(8,128)(2,1)S(1)}, bf16[2,2,128,512]{3,2,1,0:T(8,128)(2,1)S(1)}, u32[]{:S(2)}, u32[]{:S(2)}) collective-permute-start(bf16[2,2,128,512]{3,2,1,0:T(8,128)(2,1)S(1)} %add_convert_fusion.3), channel_id=1, source_target_pairs={{0,64},{32,480},{64,128},{96,32},{128,192},{160,96},{192,256},{224... | collective-permute-start | bytes 1572872 | tf_op jit(solution)/shard_map/ppermute | solution.py:35
  123.3 1.4 collective-permute-done.21.refs_1_
  124.7 1.1 collective-permute-done.20
  125.9 1.9 %collective-permute-start.22 = (bf16[2,2,128,512]{3,2,1,0:T(8,128)(2,1)S(1)}, bf16[2,2,128,512]{3,2,1,0:T(8,128)(2,1)S(1)}, u32[]{:S(2)}, u32[]{:S(2)}) collective-permute-start(bf16[2,2,128,512]{3,2,1,0:T(8,128)(2,1)S(1)} %pad_maximum_fusion.5), channel_id=1, source_target_pairs={{1,0},{2,1},{3,2},{4,3},{5,4},{6,5},{7,6},{8,7},{9,8},{10,9},{11,1... | collective-permute-start | bytes 1572872 | tf_op jit(solution)/shard_map/ppermute | solution.py:51
  127.8 0.1 add_convert_fusion
  127.9 3.6 %collective-permute-start.23 = (bf16[2,2,128,512]{3,2,1,0:T(8,128)(2,1)S(1)}, bf16[2,2,128,512]{3,2,1,0:T(8,128)(2,1)S(1)}, u32[]{:S(2)}, u32[]{:S(2)}) collective-permute-start(bf16[2,2,128,512]{3,2,1,0:T(8,128)(2,1)S(1)} %add_convert_fusion), channel_id=1, source_target_pairs={{0,64},{32,480},{64,128},{96,32},{128,192},{160,96},{192,256},{224... | collective-permute-start | bytes 1572872 | tf_op jit(solution)/shard_map/ppermute | solution.py:35
  131.6 0.1 add_convert_fusion.2
  131.7 3.0 %collective-permute-start.17 = (bf16[2,2,128,512]{3,2,1,0:T(8,128)(2,1)S(1)}, bf16[2,2,128,512]{3,2,1,0:T(8,128)(2,1)S(1)}, u32[]{:S(2)}, u32[]{:S(2)}) collective-permute-start(bf16[2,2,128,512]{3,2,1,0:T(8,128)(2,1)S(1)} %add_convert_fusion.2), channel_id=1, source_target_pairs={{0,64},{32,480},{64,128},{96,32},{128,192},{160,96},{192,256},{224... | collective-permute-start | bytes 1572872 | tf_op jit(solution)/shard_map/ppermute | solution.py:35
  134.7 5.6 %collective-permute-done.22.refs_0_ = bf16[2,2,128,512]{3,2,1,0:T(8,128)(2,1)S(1)} collective-permute-done((bf16[2,2,128,512]{3,2,1,0:T(8,128)(2,1)S(1)}, bf16[2,2,128,512]{3,2,1,0:T(8,128)(2,1)S(1)}, u32[]{:S(2)}, u32[]{:S(2)}) %collective-permute-start.22) | collective-permute-done | bytes 524320 | tf_op jit(solution)/shard_map/ppermute | solution.py:51
  140.4 8.2 %collective-permute-start.24 = (bf16[2,2,128,512]{3,2,1,0:T(8,128)(2,1)S(1)}, bf16[2,2,128,512]{3,2,1,0:T(8,128)(2,1)S(1)}, u32[]{:S(2)}, u32[]{:S(2)}) collective-permute-start(bf16[2,2,128,512]{3,2,1,0:T(8,128)(2,1)S(1)} %collective-permute-done.23), channel_id=1, source_target_pairs={{0,32},{32,0},{64,96},{96,64},{128,160},{160,128},{192,224},{224,1... | collective-permute-start | bytes 1572872 | tf_op jit(solution)/shard_map/ppermute | solution.py:40
  148.6 1.9 %collective-permute-start.25 = (bf16[2,2,128,512]{3,2,1,0:T(8,128)(2,1)S(1)}, bf16[2,2,128,512]{3,2,1,0:T(8,128)(2,1)S(1)}, u32[]{:S(2)}, u32[]{:S(2)}) collective-permute-start(bf16[2,2,128,512]{3,2,1,0:T(8,128)(2,1)S(1)} %pad_maximum_fusion.6), channel_id=1, source_target_pairs={{0,32},{32,0},{64,96},{96,64},{128,160},{160,128},{192,224},{224,1... | collective-permute-start | bytes 1572872 | tf_op jit(solution)/shard_map/ppermute | solution.py:40
  150.5 1.9 %collective-permute-done.25.refs_2_ = bf16[2,2,128,512]{3,2,1,0:T(8,128)(2,1)S(1)} collective-permute-done((bf16[2,2,128,512]{3,2,1,0:T(8,128)(2,1)S(1)}, bf16[2,2,128,512]{3,2,1,0:T(8,128)(2,1)S(1)}, u32[]{:S(2)}, u32[]{:S(2)}) %collective-permute-start.25) | collective-permute-done | bytes 524320 | tf_op jit(solution)/shard_map/ppermute | solution.py:40
  152.4 1.9 %shard_map.98 = (bf16[256,512]{1,0:T(8,128)(2,1)}, bf16[256,512]{1,0:T(8,128)(2,1)}) custom-call(s32[6]{0:T(128)S(1)} %pad_add_fusion.6.table, bf16[2,2,128,512]{3,2,1,0:T(8,128)(2,1)S(1)} %get-tuple-element.60.near, bf16[6,2,128,512]{3,2,1,0:T(8,128)(2,1)S(1)} %collective-permute-done.13.theirs, ...), custom_call_target="tpu_custom_call" | custom-call | flops 4194304 | bytes 6291456 | tf_op jit(solution)/shard_map/pallas_call | solution.py:306
  (66 shorter events, 1.6 us)
Async XLA Ops:
  0.6 17.7 %copy-start.3 = (bf16[256,512]{1,0:T(8,128)(2,1)S(1)}, bf16[256,512]{1,0:T(8,128)(2,1)}, u32[]{:S(2)}) copy-start(bf16[256,512]{1,0:T(8,128)(2,1)} %keys.1) | copy-start | bytes 786436
  0.6 17.7 %copy-start.2 = (bf16[256,512]{1,0:T(8,128)(2,1)S(1)}, bf16[256,512]{1,0:T(8,128)(2,1)}, u32[]{:S(2)}) copy-start(bf16[256,512]{1,0:T(8,128)(2,1)} %values.1) | copy-start | bytes 786436
  1.8 23.2 %collective-permute-start.1 = (bf16[2,256,512]{2,1,0:T(8,128)(2,1)S(1)}, bf16[2,256,512]{2,1,0:T(8,128)(2,1)S(1)}, u32[]{:S(2)}, u32[]{:S(2)}) collective-permute-start(bf16[2,256,512]{2,1,0:T(8,128)(2,1)S(1)} %pad_maximum_fusion.refs_0_), channel_id=1, source_target_pairs={{0,64},{32,480},{64,128},{96,32},{128,192},{160,96},{192,256},{224... | collective-permute-start | bytes 1572872 | tf_op jit(solution)/shard_map/ppermute | solution.py:35
  12.5 5.9 %collective-permute-start = (bf16[2,256,512]{2,1,0:T(8,128)(2,1)S(1)}, bf16[2,256,512]{2,1,0:T(8,128)(2,1)S(1)}, u32[]{:S(2)}, u32[]{:S(2)}) collective-permute-start(bf16[2,256,512]{2,1,0:T(8,128)(2,1)S(1)} %pad_maximum_fusion.refs_0_), channel_id=1, source_target_pairs={{0,32},{32,0},{64,96},{96,64},{128,160},{160,128},{192,224},{224,1... | collective-permute-start | bytes 1572872 | tf_op jit(solution)/shard_map/ppermute | solution.py:40
  20.4 8.2 %collective-permute-start.5 = (bf16[2,2,128,512]{3,2,1,0:T(8,128)(2,1)S(1)}, bf16[2,2,128,512]{3,2,1,0:T(8,128)(2,1)S(1)}, u32[]{:S(2)}, u32[]{:S(2)}) collective-permute-start(bf16[2,2,128,512]{3,2,1,0:T(8,128)(2,1)S(1)} %get-tuple-element.47), channel_id=1, source_target_pairs={{0,32},{32,0},{64,96},{96,64},{128,160},{160,128},{192,224},{224,1... | collective-permute-start | bytes 1572872 | tf_op jit(solution)/shard_map/ppermute | solution.py:40
  22.8 10.2 %collective-permute-start.6 = (bf16[2,256,512]{2,1,0:T(8,128)(2,1)S(1)}, bf16[2,256,512]{2,1,0:T(8,128)(2,1)S(1)}, u32[]{:S(2)}, u32[]{:S(2)}) collective-permute-start(bf16[2,256,512]{2,1,0:T(8,128)(2,1)S(1)} %collective-permute-done.refs_0_.refs_4_), channel_id=1, source_target_pairs={{0,64},{32,480},{64,128},{96,32},{128,192},{160,96},{192,256},{224... | collective-permute-start | bytes 1572872 | tf_op jit(solution)/shard_map/ppermute | solution.py:35
  25.0 16.6 %collective-permute-start.2 = (bf16[2,256,512]{2,1,0:T(8,128)(2,1)S(1)}, bf16[2,256,512]{2,1,0:T(8,128)(2,1)S(1)}, u32[]{:S(2)}, u32[]{:S(2)}) collective-permute-start(bf16[2,256,512]{2,1,0:T(8,128)(2,1)S(1)} %collective-permute-done.1.refs_1_.refs_5_), channel_id=1, source_target_pairs={{0,64},{32,480},{64,128},{96,32},{128,192},{160,96},{192,256},{224... | collective-permute-start | bytes 1572872 | tf_op jit(solution)/shard_map/ppermute | solution.py:35
  33.0 11.2 %collective-permute-start.7 = (bf16[2,256,512]{2,1,0:T(8,128)(2,1)S(1)}, bf16[2,256,512]{2,1,0:T(8,128)(2,1)S(1)}, u32[]{:S(2)}, u32[]{:S(2)}) collective-permute-start(bf16[2,256,512]{2,1,0:T(8,128)(2,1)S(1)} %collective-permute-done.6.refs_5_.refs_9_), channel_id=1, source_target_pairs={{0,64},{32,480},{64,128},{96,32},{128,192},{160,96},{192,256},{224... | collective-permute-start | bytes 1572872 | tf_op jit(solution)/shard_map/ppermute | solution.py:35
  36.1 17.0 %collective-permute-start.8 = (bf16[2,2,128,512]{3,2,1,0:T(8,128)(2,1)S(1)}, bf16[2,2,128,512]{3,2,1,0:T(8,128)(2,1)S(1)}, u32[]{:S(2)}, u32[]{:S(2)}) collective-permute-start(bf16[2,2,128,512]{3,2,1,0:T(8,128)(2,1)S(1)} %pad_maximum_fusion.1), channel_id=1, source_target_pairs={{0,2},{1,3},{2,4},{3,5},{4,6},{5,7},{6,8},{7,9},{8,10},{9,11},{10,... | collective-permute-start | bytes 1572872 | tf_op jit(solution)/shard_map/ppermute | solution.py:51
  41.6 11.7 %collective-permute-start.3 = (bf16[2,256,512]{2,1,0:T(8,128)(2,1)S(1)}, bf16[2,256,512]{2,1,0:T(8,128)(2,1)S(1)}, u32[]{:S(2)}, u32[]{:S(2)}) collective-permute-start(bf16[2,256,512]{2,1,0:T(8,128)(2,1)S(1)} %collective-permute-done.2.refs_2_.refs_6_), channel_id=1, source_target_pairs={{0,64},{32,480},{64,128},{96,32},{128,192},{160,96},{192,256},{224... | collective-permute-start | bytes 1572872 | tf_op jit(solution)/shard_map/ppermute | solution.py:35
  53.3 10.2 %collective-permute-start.4 = (bf16[2,256,512]{2,1,0:T(8,128)(2,1)S(1)}, bf16[2,256,512]{2,1,0:T(8,128)(2,1)S(1)}, u32[]{:S(2)}, u32[]{:S(2)}) collective-permute-start(bf16[2,256,512]{2,1,0:T(8,128)(2,1)S(1)} %collective-permute-done.3.refs_3_.refs_7_), channel_id=1, source_target_pairs={{0,64},{32,480},{64,128},{96,32},{128,192},{160,96},{192,256},{224... | collective-permute-start | bytes 1572872 | tf_op jit(solution)/shard_map/ppermute | solution.py:35
  55.9 10.2 %collective-permute-start.9 = (bf16[2,2,128,512]{3,2,1,0:T(8,128)(2,1)S(1)}, bf16[2,2,128,512]{3,2,1,0:T(8,128)(2,1)S(1)}, u32[]{:S(2)}, u32[]{:S(2)}) collective-permute-start(bf16[2,2,128,512]{3,2,1,0:T(8,128)(2,1)S(1)} %pad_maximum_fusion.2), channel_id=1, source_target_pairs={{0,1},{1,2},{2,3},{3,4},{4,5},{5,6},{6,7},{7,8},{8,9},{9,10},{10,1... | collective-permute-start | bytes 1572872 | tf_op jit(solution)/shard_map/ppermute | solution.py:51
  58.8 10.3 %collective-permute-start.11 = (bf16[2,256,512]{2,1,0:T(8,128)(2,1)S(1)}, bf16[2,256,512]{2,1,0:T(8,128)(2,1)S(1)}, u32[]{:S(2)}, u32[]{:S(2)}) collective-permute-start(bf16[2,256,512]{2,1,0:T(8,128)(2,1)S(1)} %collective-permute-done.7.refs_6_.refs_10_), channel_id=1, source_target_pairs={{0,64},{32,480},{64,128},{96,32},{128,192},{160,96},{192,256},{224... | collective-permute-start | bytes 1572872 | tf_op jit(solution)/shard_map/ppermute | solution.py:35
  70.2 8.9 %copy-start.4 = (bf16[256,512]{1,0:T(8,128)(2,1)S(1)}, bf16[256,512]{1,0:T(8,128)(2,1)}, u32[]{:S(2)}) copy-start(bf16[256,512]{1,0:T(8,128)(2,1)} %param.6) | copy-start | bytes 786436
  70.3 8.9 %copy-start.5 = (bf16[256,512]{1,0:T(8,128)(2,1)S(1)}, bf16[256,512]{1,0:T(8,128)(2,1)}, u32[]{:S(2)}) copy-start(bf16[256,512]{1,0:T(8,128)(2,1)} %param.9) | copy-start | bytes 786436
  70.3 8.9 %collective-permute-start.12 = (bf16[6,2,128,512]{3,2,1,0:T(8,128)(2,1)S(1)}, bf16[6,2,128,512]{3,2,1,0:T(8,128)(2,1)S(1)}, u32[]{:S(2)}, u32[]{:S(2)}) collective-permute-start(bf16[6,2,128,512]{3,2,1,0:T(8,128)(2,1)S(1)} %shard_map.94), channel_id=1, source_target_pairs={{0,32},{32,0},{64,96},{96,64},{128,160},{160,128},{192,224},{224,1... | collective-permute-start | bytes 4718600 | tf_op jit(solution)/shard_map/ppermute | solution.py:40
  75.4 3.8 %collective-permute-start.10 = (bf16[2,2,128,512]{3,2,1,0:T(8,128)(2,1)S(1)}, bf16[2,2,128,512]{3,2,1,0:T(8,128)(2,1)S(1)}, u32[]{:S(2)}, u32[]{:S(2)}) collective-permute-start(bf16[2,2,128,512]{3,2,1,0:T(8,128)(2,1)S(1)} %pad_maximum_fusion.3), channel_id=1, source_target_pairs={{0,32},{32,0},{64,96},{96,64},{128,160},{160,128},{192,224},{224,1... | collective-permute-start | bytes 1572872 | tf_op jit(solution)/shard_map/ppermute | solution.py:40
  91.3 5.3 %collective-permute-start.13 = (bf16[6,2,128,512]{3,2,1,0:T(8,128)(2,1)S(1)}, bf16[6,2,128,512]{3,2,1,0:T(8,128)(2,1)S(1)}, u32[]{:S(2)}, u32[]{:S(2)}) collective-permute-start(bf16[6,2,128,512]{3,2,1,0:T(8,128)(2,1)S(1)} %get-tuple-element.61.mine), channel_id=1, source_target_pairs={{0,32},{32,0},{64,96},{96,64},{128,160},{160,128},{192,224},{224,1... | collective-permute-start | bytes 4718600 | tf_op jit(solution)/shard_map/ppermute | solution.py:40
  97.5 10.2 %collective-permute-start.14 = (bf16[2,2,128,512]{3,2,1,0:T(8,128)(2,1)S(1)}, bf16[2,2,128,512]{3,2,1,0:T(8,128)(2,1)S(1)}, u32[]{:S(2)}, u32[]{:S(2)}) collective-permute-start(bf16[2,2,128,512]{3,2,1,0:T(8,128)(2,1)S(1)} %get-tuple-element.65), channel_id=1, source_target_pairs={{0,64},{32,480},{64,128},{96,32},{128,192},{160,96},{192,256},{224... | collective-permute-start | bytes 1572872 | tf_op jit(solution)/shard_map/ppermute | solution.py:35
  100.0 11.3 %collective-permute-start.18 = (bf16[2,2,128,512]{3,2,1,0:T(8,128)(2,1)S(1)}, bf16[2,2,128,512]{3,2,1,0:T(8,128)(2,1)S(1)}, u32[]{:S(2)}, u32[]{:S(2)}) collective-permute-start(bf16[2,2,128,512]{3,2,1,0:T(8,128)(2,1)S(1)} %get-tuple-element.71), channel_id=1, source_target_pairs={{0,32},{32,0},{64,96},{96,64},{128,160},{160,128},{192,224},{224,1... | collective-permute-start | bytes 1572872 | tf_op jit(solution)/shard_map/ppermute | solution.py:40
  101.9 13.5 %collective-permute-start.19 = (bf16[2,2,128,512]{3,2,1,0:T(8,128)(2,1)S(1)}, bf16[2,2,128,512]{3,2,1,0:T(8,128)(2,1)S(1)}, u32[]{:S(2)}, u32[]{:S(2)}) collective-permute-start(bf16[2,2,128,512]{3,2,1,0:T(8,128)(2,1)S(1)} %get-tuple-element.72), channel_id=1, source_target_pairs={{0,64},{32,480},{64,128},{96,32},{128,192},{160,96},{192,256},{224... | collective-permute-start | bytes 1572872 | tf_op jit(solution)/shard_map/ppermute | solution.py:35
  107.8 11.1 %collective-permute-start.15 = (bf16[2,2,128,512]{3,2,1,0:T(8,128)(2,1)S(1)}, bf16[2,2,128,512]{3,2,1,0:T(8,128)(2,1)S(1)}, u32[]{:S(2)}, u32[]{:S(2)}) collective-permute-start(bf16[2,2,128,512]{3,2,1,0:T(8,128)(2,1)S(1)} %add_convert_fusion.4), channel_id=1, source_target_pairs={{0,64},{32,480},{64,128},{96,32},{128,192},{160,96},{192,256},{224... | collective-permute-start | bytes 1572872 | tf_op jit(solution)/shard_map/ppermute | solution.py:35
  111.4 13.3 %collective-permute-start.21 = (bf16[2,2,128,512]{3,2,1,0:T(8,128)(2,1)S(1)}, bf16[2,2,128,512]{3,2,1,0:T(8,128)(2,1)S(1)}, u32[]{:S(2)}, u32[]{:S(2)}) collective-permute-start(bf16[2,2,128,512]{3,2,1,0:T(8,128)(2,1)S(1)} %pad_maximum_fusion.4), channel_id=1, source_target_pairs={{2,0},{3,1},{4,2},{5,3},{6,4},{7,5},{8,6},{9,7},{10,8},{11,9},{12,... | collective-permute-start | bytes 1572872 | tf_op jit(solution)/shard_map/ppermute | solution.py:51
  115.5 10.2 %collective-permute-start.20 = (bf16[2,2,128,512]{3,2,1,0:T(8,128)(2,1)S(1)}, bf16[2,2,128,512]{3,2,1,0:T(8,128)(2,1)S(1)}, u32[]{:S(2)}, u32[]{:S(2)}) collective-permute-start(bf16[2,2,128,512]{3,2,1,0:T(8,128)(2,1)S(1)} %add_convert_fusion.1), channel_id=1, source_target_pairs={{0,64},{32,480},{64,128},{96,32},{128,192},{160,96},{192,256},{224... | collective-permute-start | bytes 1572872 | tf_op jit(solution)/shard_map/ppermute | solution.py:35
  119.1 12.5 %collective-permute-start.16 = (bf16[2,2,128,512]{3,2,1,0:T(8,128)(2,1)S(1)}, bf16[2,2,128,512]{3,2,1,0:T(8,128)(2,1)S(1)}, u32[]{:S(2)}, u32[]{:S(2)}) collective-permute-start(bf16[2,2,128,512]{3,2,1,0:T(8,128)(2,1)S(1)} %add_convert_fusion.3), channel_id=1, source_target_pairs={{0,64},{32,480},{64,128},{96,32},{128,192},{160,96},{192,256},{224... | collective-permute-start | bytes 1572872 | tf_op jit(solution)/shard_map/ppermute | solution.py:35
  124.7 6.8 %copy-start = (bf16[2,2,128,512]{3,2,1,0:T(8,128)(2,1)}, bf16[2,2,128,512]{3,2,1,0:T(8,128)(2,1)S(1)}, u32[]{:S(2)}) copy-start(bf16[2,2,128,512]{3,2,1,0:T(8,128)(2,1)S(1)} %collective-permute-done.21.refs_1_) | copy-start | bytes 1572868
  125.9 14.5 %collective-permute-start.22 = (bf16[2,2,128,512]{3,2,1,0:T(8,128)(2,1)S(1)}, bf16[2,2,128,512]{3,2,1,0:T(8,128)(2,1)S(1)}, u32[]{:S(2)}, u32[]{:S(2)}) collective-permute-start(bf16[2,2,128,512]{3,2,1,0:T(8,128)(2,1)S(1)} %pad_maximum_fusion.5), channel_id=1, source_target_pairs={{1,0},{2,1},{3,2},{4,3},{5,4},{6,5},{7,6},{8,7},{9,8},{10,9},{11,1... | collective-permute-start | bytes 1572872 | tf_op jit(solution)/shard_map/ppermute | solution.py:51
  127.9 12.5 %collective-permute-start.23 = (bf16[2,2,128,512]{3,2,1,0:T(8,128)(2,1)S(1)}, bf16[2,2,128,512]{3,2,1,0:T(8,128)(2,1)S(1)}, u32[]{:S(2)}, u32[]{:S(2)}) collective-permute-start(bf16[2,2,128,512]{3,2,1,0:T(8,128)(2,1)S(1)} %add_convert_fusion), channel_id=1, source_target_pairs={{0,64},{32,480},{64,128},{96,32},{128,192},{160,96},{192,256},{224... | collective-permute-start | bytes 1572872 | tf_op jit(solution)/shard_map/ppermute | solution.py:35
  131.5 8.8 %slice-start = ((bf16[2,2,128,512]{3,2,1,0:T(8,128)(2,1)}), bf16[1,2,128,512]{3,2,1,0:T(8,128)(2,1)S(1)}, s32[]{:S(2)}) async-start(bf16[2,2,128,512]{3,2,1,0:T(8,128)(2,1)} %copy-done), calls=%async_computation | async-start | bytes 524288 | tf_op jit(solution)/shard_map/slice | solution.py:416
  131.6 20.8 %copy-start.1 = (bf16[2,2,128,512]{3,2,1,0:T(8,128)(2,1)S(1)}, bf16[2,2,128,512]{3,2,1,0:T(8,128)(2,1)}, u32[]{:S(2)}) copy-start(bf16[2,2,128,512]{3,2,1,0:T(8,128)(2,1)} %copy-done) | copy-start | bytes 1572868
  131.7 18.8 %collective-permute-start.17 = (bf16[2,2,128,512]{3,2,1,0:T(8,128)(2,1)S(1)}, bf16[2,2,128,512]{3,2,1,0:T(8,128)(2,1)S(1)}, u32[]{:S(2)}, u32[]{:S(2)}) collective-permute-start(bf16[2,2,128,512]{3,2,1,0:T(8,128)(2,1)S(1)} %add_convert_fusion.2), channel_id=1, source_target_pairs={{0,64},{32,480},{64,128},{96,32},{128,192},{160,96},{192,256},{224... | collective-permute-start | bytes 1572872 | tf_op jit(solution)/shard_map/ppermute | solution.py:35
  140.4 10.1 %collective-permute-start.24 = (bf16[2,2,128,512]{3,2,1,0:T(8,128)(2,1)S(1)}, bf16[2,2,128,512]{3,2,1,0:T(8,128)(2,1)S(1)}, u32[]{:S(2)}, u32[]{:S(2)}) collective-permute-start(bf16[2,2,128,512]{3,2,1,0:T(8,128)(2,1)S(1)} %collective-permute-done.23), channel_id=1, source_target_pairs={{0,32},{32,0},{64,96},{96,64},{128,160},{160,128},{192,224},{224,1... | collective-permute-start | bytes 1572872 | tf_op jit(solution)/shard_map/ppermute | solution.py:40
  148.6 3.8 %collective-permute-start.25 = (bf16[2,2,128,512]{3,2,1,0:T(8,128)(2,1)S(1)}, bf16[2,2,128,512]{3,2,1,0:T(8,128)(2,1)S(1)}, u32[]{:S(2)}, u32[]{:S(2)}) collective-permute-start(bf16[2,2,128,512]{3,2,1,0:T(8,128)(2,1)S(1)} %pad_maximum_fusion.6), channel_id=1, source_target_pairs={{0,32},{32,0},{64,96},{96,64},{128,160},{160,128},{192,224},{224,1... | collective-permute-start | bytes 1572872 | tf_op jit(solution)/shard_map/ppermute | solution.py:40

commit v8 on v7

--- a/solution.py
+++ b/solution.py
@@ -371,10 +371,10 @@
     flow_a.append(ring_step(flow_a[0]))
     keep, give = offer(given, keys, values)
     given_here = swap_cores(give)
+    two = dom_step(jnp.stack([keep[1], given_here[1]]), 2)
+    flow_b[0], two = lax.optimization_barrier((flow_b[0], two))
     flow_b.append(ring_step(flow_b[0]))
-    two = dom_step(jnp.stack([keep[1], given_here[1]]), 2)
     flow_a.append(ring_step(flow_a[1]))
-    flow_b[1], two = lax.optimization_barrier((flow_b[1], two))
     flow_b.append(ring_step(flow_b[1]))
     keep, given_here, two = lax.optimization_barrier((keep, given_here, two))
     one = dom_step(jnp.stack([keep[0], given_here[0]]), 1)

time: 155 us -> 154 us (level)
  waiting for transfers between devices: 37.9 us -> 32.4 us
  starting transfers between devices: 89.9 us -> 93.6 us
    ppermute x4, waiting for transfers between devices: 18.5 us -> 12.3 us  [dom_step(): return lax.ppermute(array, ('group', 'dom'), pairs)]
    ppermute x4, starting transfers between devices: 14.2 us -> 16.9 us  [dom_step(): return lax.ppermute(array, ('group', 'dom'), pairs)]
    ppermute x14, starting transfers between devices: 50.3 us -> 52.5 us  [ring_step(): lax.ppermute(array, 'group', [(g, (g + (2 if g % 2 == 0 else -2)) % size)...]
  transfers between devices with their start and end apart: 26 -> 26, of which waited for: 13 -> 15; matrix products, arithmetic and copies ran while one was open for 3% -> 3% of each run, Pallas kernels for 2% -> 2%
where the time goes in v8:
time: 154 us; the launch traced here: 152 us
  starting transfers between devices  93.6 us (61%)
  waiting for transfers between devices  32.4 us (21%)
  Pallas kernels  18.9 us (12%)
  other arithmetic  3.3 us (2%)
  local copies, waits for them, and re-layouts  2.83 us (2%)
    ppermute x14, starting transfers between devices, ring_step(): lax.ppermute(array, 'group', [(g, (g + (2 if g % 2 == 0 else -2)) % size)...  52.5 us
    ppermute x8, starting transfers between devices, swap_cores(): return lax.ppermute(array, 'group', [(g, g ^ 1) for g in range(size)])  24.2 us
    ppermute x4, starting transfers between devices, dom_step(): return lax.ppermute(array, ('group', 'dom'), pairs)  16.9 us
    ppermute x14, waiting for transfers between devices, ring_step(): lax.ppermute(array, 'group', [(g, (g + (2 if g % 2 == 0 else -2)) % size)...  13.2 us
    ppermute x4, waiting for transfers between devices, dom_step(): return lax.ppermute(array, ('group', 'dom'), pairs)  12.3 us
    pallas_call x1, Pallas kernels, attend(): pl.pallas_call(attend_kernel, out_shape=(jax.ShapeDtypeStruct((NB, BS, D)...  12.1 us
    ppermute x8, waiting for transfers between devices, swap_cores(): return lax.ppermute(array, 'group', [(g, g ^ 1) for g in range(size)])  6.91 us
  transfers between devices with their start and end apart: 26, of which 15 were waited for; matrix products, arithmetic and copies ran while one was open for 3% of the time, Pallas kernels for 2%

profile of v8, /device:TPU:57, one launch (start us, length us, event | category | flops | bytes accessed | tf_op | source)
XLA Modules:
  0.0 152.4 jit_solution(2668890786515219386)
XLA Ops:
  0.7 1.1 pad_maximum_fusion.refs_0_
  1.8 10.7 %collective-permute-start.1 = (bf16[2,256,512]{2,1,0:T(8,128)(2,1)S(1)}, bf16[2,256,512]{2,1,0:T(8,128)(2,1)S(1)}, u32[]{:S(2)}, u32[]{:S(2)}) collective-permute-start(bf16[2,256,512]{2,1,0:T(8,128)(2,1)S(1)} %pad_maximum_fusion.refs_0_), channel_id=1, source_target_pairs={{0,64},{32,480},{64,128},{96,32},{128,192},{160,96},{192,256},{224... | collective-permute-start | bytes 1572872 | tf_op jit(solution)/shard_map/ppermute | solution.py:35
  12.5 1.9 %collective-permute-start = (bf16[2,256,512]{2,1,0:T(8,128)(2,1)S(1)}, bf16[2,256,512]{2,1,0:T(8,128)(2,1)S(1)}, u32[]{:S(2)}, u32[]{:S(2)}) collective-permute-start(bf16[2,256,512]{2,1,0:T(8,128)(2,1)S(1)} %pad_maximum_fusion.refs_0_), channel_id=1, source_target_pairs={{0,32},{32,0},{64,96},{96,64},{128,160},{160,128},{192,224},{224,1... | collective-permute-start | bytes 1572872 | tf_op jit(solution)/shard_map/ppermute | solution.py:40
  14.5 0.8 copy.15
  15.4 0.2 select_reduce_fusion.3
  15.6 0.1 add.216
  15.8 0.8 copy.14
  16.5 0.1 fusion.2
  16.8 0.1 eq.193
  17.0 0.1 stack.113
  17.1 0.1 select_reduce_fusion.2
  17.6 0.1 reduce_max.18
  17.8 0.1 rev.3
  18.1 0.2 select_reduce_fusion
  18.3 2.0 %shard_map.93 = (bf16[2,2,128,512]{3,2,1,0:T(8,128)(2,1)S(1)}, bf16[2,2,128,512]{3,2,1,0:T(8,128)(2,1)S(1)}) custom-call(s32[4]{0:T(128)S(1)} %broadcast_select_fusion.2.table, bf16[256,512]{1,0:T(8,128)(2,1)S(1)} %copy-done.3, bf16[256,512]{1,0:T(8,128)(2,1)S(1)} %copy-done.2), custom_call_target="tpu_custom_call" | custom-call | bytes 2097152 | tf_op jit(solution)/shard_map/pallas_call | solution.py:122
  20.3 2.4 %collective-permute-start.5 = (bf16[2,2,128,512]{3,2,1,0:T(8,128)(2,1)S(1)}, bf16[2,2,128,512]{3,2,1,0:T(8,128)(2,1)S(1)}, u32[]{:S(2)}, u32[]{:S(2)}) collective-permute-start(bf16[2,2,128,512]{3,2,1,0:T(8,128)(2,1)S(1)} %get-tuple-element.47), channel_id=1, source_target_pairs={{0,32},{32,0},{64,96},{96,64},{128,160},{160,128},{192,224},{224,1... | collective-permute-start | bytes 1572872 | tf_op jit(solution)/shard_map/ppermute | solution.py:40
  22.8 2.2 %collective-permute-start.6 = (bf16[2,256,512]{2,1,0:T(8,128)(2,1)S(1)}, bf16[2,256,512]{2,1,0:T(8,128)(2,1)S(1)}, u32[]{:S(2)}, u32[]{:S(2)}) collective-permute-start(bf16[2,256,512]{2,1,0:T(8,128)(2,1)S(1)} %collective-permute-done.refs_0_.refs_4_), channel_id=1, source_target_pairs={{0,64},{32,480},{64,128},{96,32},{128,192},{160,96},{192,256},{224... | collective-permute-start | bytes 1572872 | tf_op jit(solution)/shard_map/ppermute | solution.py:35
  25.0 3.6 %collective-permute-start.2 = (bf16[2,256,512]{2,1,0:T(8,128)(2,1)S(1)}, bf16[2,256,512]{2,1,0:T(8,128)(2,1)S(1)}, u32[]{:S(2)}, u32[]{:S(2)}) collective-permute-start(bf16[2,256,512]{2,1,0:T(8,128)(2,1)S(1)} %collective-permute-done.1.refs_1_.refs_5_), channel_id=1, source_target_pairs={{0,64},{32,480},{64,128},{96,32},{128,192},{160,96},{192,256},{224... | collective-permute-start | bytes 1572872 | tf_op jit(solution)/shard_map/ppermute | solution.py:35
  28.6 5.4 %collective-permute-start.7 = (bf16[2,2,128,512]{3,2,1,0:T(8,128)(2,1)S(1)}, bf16[2,2,128,512]{3,2,1,0:T(8,128)(2,1)S(1)}, u32[]{:S(2)}, u32[]{:S(2)}) collective-permute-start(bf16[2,2,128,512]{3,2,1,0:T(8,128)(2,1)S(1)} %pad_maximum_fusion.1), channel_id=1, source_target_pairs={{0,2},{1,3},{2,4},{3,5},{4,6},{5,7},{6,8},{7,9},{8,10},{9,11},{10,... | collective-permute-start | bytes 1572872 | tf_op jit(solution)/shard_map/ppermute | solution.py:51
  34.1 4.5 %collective-permute-done.2.refs_2_.refs_6_ = bf16[2,256,512]{2,1,0:T(8,128)(2,1)S(1)} collective-permute-done((bf16[2,256,512]{2,1,0:T(8,128)(2,1)S(1)}, bf16[2,256,512]{2,1,0:T(8,128)(2,1)S(1)}, u32[]{:S(2)}, u32[]{:S(2)}) %collective-permute-start.2) | collective-permute-done | bytes 524320 | tf_op jit(solution)/shard_map/ppermute | solution.py:35
  38.6 3.4 %collective-permute-start.3 = (bf16[2,256,512]{2,1,0:T(8,128)(2,1)S(1)}, bf16[2,256,512]{2,1,0:T(8,128)(2,1)S(1)}, u32[]{:S(2)}, u32[]{:S(2)}) collective-permute-start(bf16[2,256,512]{2,1,0:T(8,128)(2,1)S(1)} %collective-permute-done.2.refs_2_.refs_6_), channel_id=1, source_target_pairs={{0,64},{32,480},{64,128},{96,32},{128,192},{160,96},{192,256},{224... | collective-permute-start | bytes 1572872 | tf_op jit(solution)/shard_map/ppermute | solution.py:35
  42.0 3.2 %collective-permute-done.7.refs_2_ = bf16[2,2,128,512]{3,2,1,0:T(8,128)(2,1)S(1)} collective-permute-done((bf16[2,2,128,512]{3,2,1,0:T(8,128)(2,1)S(1)}, bf16[2,2,128,512]{3,2,1,0:T(8,128)(2,1)S(1)}, u32[]{:S(2)}, u32[]{:S(2)}) %collective-permute-start.7) | collective-permute-done | bytes 524320 | tf_op jit(solution)/shard_map/ppermute | solution.py:51
  45.2 2.7 %collective-permute-start.10 = (bf16[2,256,512]{2,1,0:T(8,128)(2,1)S(1)}, bf16[2,256,512]{2,1,0:T(8,128)(2,1)S(1)}, u32[]{:S(2)}, u32[]{:S(2)}) collective-permute-start(bf16[2,256,512]{2,1,0:T(8,128)(2,1)S(1)} %collective-permute-done.6.refs_5_.refs_9_), channel_id=1, source_target_pairs={{0,64},{32,480},{64,128},{96,32},{128,192},{160,96},{192,256},{224... | collective-permute-start | bytes 1572872 | tf_op jit(solution)/shard_map/ppermute | solution.py:35
  48.0 0.8 collective-permute-done.3.refs_3_.refs_7_
  48.8 4.3 %collective-permute-start.4 = (bf16[2,256,512]{2,1,0:T(8,128)(2,1)S(1)}, bf16[2,256,512]{2,1,0:T(8,128)(2,1)S(1)}, u32[]{:S(2)}, u32[]{:S(2)}) collective-permute-start(bf16[2,256,512]{2,1,0:T(8,128)(2,1)S(1)} %collective-permute-done.3.refs_3_.refs_7_), channel_id=1, source_target_pairs={{0,64},{32,480},{64,128},{96,32},{128,192},{160,96},{192,256},{224... | collective-permute-start | bytes 1572872 | tf_op jit(solution)/shard_map/ppermute | solution.py:35
  53.1 5.2 %collective-permute-start.8 = (bf16[2,2,128,512]{3,2,1,0:T(8,128)(2,1)S(1)}, bf16[2,2,128,512]{3,2,1,0:T(8,128)(2,1)S(1)}, u32[]{:S(2)}, u32[]{:S(2)}) collective-permute-start(bf16[2,2,128,512]{3,2,1,0:T(8,128)(2,1)S(1)} %pad_maximum_fusion.2), channel_id=1, source_target_pairs={{0,1},{1,2},{2,3},{3,4},{4,5},{5,6},{6,7},{7,8},{8,9},{9,10},{10,1... | collective-permute-start | bytes 1572872 | tf_op jit(solution)/shard_map/ppermute | solution.py:51
  58.3 1.9 %collective-permute-start.11 = (bf16[2,256,512]{2,1,0:T(8,128)(2,1)S(1)}, bf16[2,256,512]{2,1,0:T(8,128)(2,1)S(1)}, u32[]{:S(2)}, u32[]{:S(2)}) collective-permute-start(bf16[2,256,512]{2,1,0:T(8,128)(2,1)S(1)} %collective-permute-done.10.refs_6_.refs_10_), channel_id=1, source_target_pairs={{0,64},{32,480},{64,128},{96,32},{128,192},{160,96},{192,256},{224... | collective-permute-start | bytes 1572872 | tf_op jit(solution)/shard_map/ppermute | solution.py:35
  60.2 0.8 collective-permute-done.4.refs_4_.refs_8_
  61.0 3.4 %collective-permute-done.8.refs_1_ = bf16[2,2,128,512]{3,2,1,0:T(8,128)(2,1)S(1)} collective-permute-done((bf16[2,2,128,512]{3,2,1,0:T(8,128)(2,1)S(1)}, bf16[2,2,128,512]{3,2,1,0:T(8,128)(2,1)S(1)}, u32[]{:S(2)}, u32[]{:S(2)}) %collective-permute-start.8) | collective-permute-done | bytes 524320 | tf_op jit(solution)/shard_map/ppermute | solution.py:51
  64.4 4.1 %collective-permute-done.11.refs_7_.refs_11_ = bf16[2,256,512]{2,1,0:T(8,128)(2,1)S(1)} collective-permute-done((bf16[2,256,512]{2,1,0:T(8,128)(2,1)S(1)}, bf16[2,256,512]{2,1,0:T(8,128)(2,1)S(1)}, u32[]{:S(2)}, u32[]{:S(2)}) %collective-permute-start.11) | collective-permute-done | bytes 524320 | tf_op jit(solution)/shard_map/ppermute | solution.py:35
  68.5 1.1 shard_map.94
  69.6 4.3 %collective-permute-start.12 = (bf16[6,2,128,512]{3,2,1,0:T(8,128)(2,1)S(1)}, bf16[6,2,128,512]{3,2,1,0:T(8,128)(2,1)S(1)}, u32[]{:S(2)}, u32[]{:S(2)}) collective-permute-start(bf16[6,2,128,512]{3,2,1,0:T(8,128)(2,1)S(1)} %shard_map.94), channel_id=1, source_target_pairs={{0,32},{32,0},{64,96},{96,64},{128,160},{160,128},{192,224},{224,1... | collective-permute-start | bytes 4718600 | tf_op jit(solution)/shard_map/ppermute | solution.py:40
  74.1 1.9 %collective-permute-start.9 = (bf16[2,2,128,512]{3,2,1,0:T(8,128)(2,1)S(1)}, bf16[2,2,128,512]{3,2,1,0:T(8,128)(2,1)S(1)}, u32[]{:S(2)}, u32[]{:S(2)}) collective-permute-start(bf16[2,2,128,512]{3,2,1,0:T(8,128)(2,1)S(1)} %pad_maximum_fusion.3), channel_id=1, source_target_pairs={{0,32},{32,0},{64,96},{96,64},{128,160},{160,128},{192,224},{224,1... | collective-permute-start | bytes 1572872 | tf_op jit(solution)/shard_map/ppermute | solution.py:40
  76.0 1.9 %collective-permute-done.9.refs_3_ = bf16[2,2,128,512]{3,2,1,0:T(8,128)(2,1)S(1)} collective-permute-done((bf16[2,2,128,512]{3,2,1,0:T(8,128)(2,1)S(1)}, bf16[2,2,128,512]{3,2,1,0:T(8,128)(2,1)S(1)}, u32[]{:S(2)}, u32[]{:S(2)}) %collective-permute-start.9) | collective-permute-done | bytes 524320 | tf_op jit(solution)/shard_map/ppermute | solution.py:40
  77.9 12.1 %shard_map.95 = (bf16[2,128,512]{2,1,0:T(8,128)(2,1)}, bf16[2,128,512]{2,1,0:T(8,128)(2,1)}, bf16[2,2,128,512]{3,2,1,0:T(8,128)(2,1)S(1)}, bf16[6,2,128,512]{3,2...) custom-call(s32[4,14]{1,0:T(4,128)S(1)} %pad_add_fusion.table, ...), custom_call_target="tpu_custom_call" | custom-call | flops 1409286144 | bytes 12582912 | tf_op jit(solution)/shard_map/pallas_call | solution.py:232
  90.0 2.1 %collective-permute-start.13 = (bf16[6,2,128,512]{3,2,1,0:T(8,128)(2,1)S(1)}, bf16[6,2,128,512]{3,2,1,0:T(8,128)(2,1)S(1)}, u32[]{:S(2)}, u32[]{:S(2)}) collective-permute-start(bf16[6,2,128,512]{3,2,1,0:T(8,128)(2,1)S(1)} %get-tuple-element.61.mine), channel_id=1, source_target_pairs={{0,32},{32,0},{64,96},{96,64},{128,160},{160,128},{192,224},{224,1... | collective-permute-start | bytes 4718600 | tf_op jit(solution)/shard_map/ppermute | solution.py:40
  92.1 3.2 %collective-permute-done.13.theirs = bf16[6,2,128,512]{3,2,1,0:T(8,128)(2,1)S(1)} collective-permute-done((bf16[6,2,128,512]{3,2,1,0:T(8,128)(2,1)S(1)}, bf16[6,2,128,512]{3,2,1,0:T(8,128)(2,1)S(1)}, u32[]{:S(2)}, u32[]{:S(2)}) %collective-permute-start.13) | collective-permute-done | bytes 1572896 | tf_op jit(solution)/shard_map/ppermute | solution.py:40
  95.3 0.9 shard_map.96
  96.2 3.4 %collective-permute-start.14 = (bf16[2,2,128,512]{3,2,1,0:T(8,128)(2,1)S(1)}, bf16[2,2,128,512]{3,2,1,0:T(8,128)(2,1)S(1)}, u32[]{:S(2)}, u32[]{:S(2)}) collective-permute-start(bf16[2,2,128,512]{3,2,1,0:T(8,128)(2,1)S(1)} %get-tuple-element.65), channel_id=1, source_target_pairs={{0,64},{32,480},{64,128},{96,32},{128,192},{160,96},{192,256},{224... | collective-permute-start | bytes 1572872 | tf_op jit(solution)/shard_map/ppermute | solution.py:35
  99.6 1.9 %collective-permute-start.18 = (bf16[2,2,128,512]{3,2,1,0:T(8,128)(2,1)S(1)}, bf16[2,2,128,512]{3,2,1,0:T(8,128)(2,1)S(1)}, u32[]{:S(2)}, u32[]{:S(2)}) collective-permute-start(bf16[2,2,128,512]{3,2,1,0:T(8,128)(2,1)S(1)} %get-tuple-element.71), channel_id=1, source_target_pairs={{0,32},{32,0},{64,96},{96,64},{128,160},{160,128},{192,224},{224,1... | collective-permute-start | bytes 1572872 | tf_op jit(solution)/shard_map/ppermute | solution.py:40
  101.5 3.6 %collective-permute-start.19 = (bf16[2,2,128,512]{3,2,1,0:T(8,128)(2,1)S(1)}, bf16[2,2,128,512]{3,2,1,0:T(8,128)(2,1)S(1)}, u32[]{:S(2)}, u32[]{:S(2)}) collective-permute-start(bf16[2,2,128,512]{3,2,1,0:T(8,128)(2,1)S(1)} %get-tuple-element.72), channel_id=1, source_target_pairs={{0,64},{32,480},{64,128},{96,32},{128,192},{160,96},{192,256},{224... | collective-permute-start | bytes 1572872 | tf_op jit(solution)/shard_map/ppermute | solution.py:35
  105.2 0.9 shard_map.97
  106.1 0.3 collective-permute-done.14
  106.4 0.1 add_convert_fusion.4
  106.6 4.3 %collective-permute-start.15 = (bf16[2,2,128,512]{3,2,1,0:T(8,128)(2,1)S(1)}, bf16[2,2,128,512]{3,2,1,0:T(8,128)(2,1)S(1)}, u32[]{:S(2)}, u32[]{:S(2)}) collective-permute-start(bf16[2,2,128,512]{3,2,1,0:T(8,128)(2,1)S(1)} %add_convert_fusion.4), channel_id=1, source_target_pairs={{0,64},{32,480},{64,128},{96,32},{128,192},{160,96},{192,256},{224... | collective-permute-start | bytes 1572872 | tf_op jit(solution)/shard_map/ppermute | solution.py:35
  111.0 4.3 %collective-permute-start.21 = (bf16[2,2,128,512]{3,2,1,0:T(8,128)(2,1)S(1)}, bf16[2,2,128,512]{3,2,1,0:T(8,128)(2,1)S(1)}, u32[]{:S(2)}, u32[]{:S(2)}) collective-permute-start(bf16[2,2,128,512]{3,2,1,0:T(8,128)(2,1)S(1)} %pad_maximum_fusion.4), channel_id=1, source_target_pairs={{2,0},{3,1},{4,2},{5,3},{6,4},{7,5},{8,6},{9,7},{10,8},{11,9},{12,... | collective-permute-start | bytes 1572872 | tf_op jit(solution)/shard_map/ppermute | solution.py:51
  115.4 0.1 add_convert_fusion.1
  115.5 1.9 %collective-permute-start.20 = (bf16[2,2,128,512]{3,2,1,0:T(8,128)(2,1)S(1)}, bf16[2,2,128,512]{3,2,1,0:T(8,128)(2,1)S(1)}, u32[]{:S(2)}, u32[]{:S(2)}) collective-permute-start(bf16[2,2,128,512]{3,2,1,0:T(8,128)(2,1)S(1)} %add_convert_fusion.1), channel_id=1, source_target_pairs={{0,64},{32,480},{64,128},{96,32},{128,192},{160,96},{192,256},{224... | collective-permute-start | bytes 1572872 | tf_op jit(solution)/shard_map/ppermute | solution.py:35
  117.4 0.2 collective-permute-done.15
  117.7 0.1 add_convert_fusion.3
  117.8 4.3 %collective-permute-start.16 = (bf16[2,2,128,512]{3,2,1,0:T(8,128)(2,1)S(1)}, bf16[2,2,128,512]{3,2,1,0:T(8,128)(2,1)S(1)}, u32[]{:S(2)}, u32[]{:S(2)}) collective-permute-start(bf16[2,2,128,512]{3,2,1,0:T(8,128)(2,1)S(1)} %add_convert_fusion.3), channel_id=1, source_target_pairs={{0,64},{32,480},{64,128},{96,32},{128,192},{160,96},{192,256},{224... | collective-permute-start | bytes 1572872 | tf_op jit(solution)/shard_map/ppermute | solution.py:35
  122.2 1.2 collective-permute-done.21.refs_1_
  123.4 2.3 %collective-permute-done.20 = bf16[2,2,128,512]{3,2,1,0:T(8,128)(2,1)S(1)} collective-permute-done((bf16[2,2,128,512]{3,2,1,0:T(8,128)(2,1)S(1)}, bf16[2,2,128,512]{3,2,1,0:T(8,128)(2,1)S(1)}, u32[]{:S(2)}, u32[]{:S(2)}) %collective-permute-start.20) | collective-permute-done | bytes 524320 | tf_op jit(solution)/shard_map/ppermute | solution.py:35
  125.8 1.9 %collective-permute-start.22 = (bf16[2,2,128,512]{3,2,1,0:T(8,128)(2,1)S(1)}, bf16[2,2,128,512]{3,2,1,0:T(8,128)(2,1)S(1)}, u32[]{:S(2)}, u32[]{:S(2)}) collective-permute-start(bf16[2,2,128,512]{3,2,1,0:T(8,128)(2,1)S(1)} %pad_maximum_fusion.5), channel_id=1, source_target_pairs={{1,0},{2,1},{3,2},{4,3},{5,4},{6,5},{7,6},{8,7},{9,8},{10,9},{11,1... | collective-permute-start | bytes 1572872 | tf_op jit(solution)/shard_map/ppermute | solution.py:51
  127.8 0.1 add_convert_fusion
  127.9 3.3 %collective-permute-start.23 = (bf16[2,2,128,512]{3,2,1,0:T(8,128)(2,1)S(1)}, bf16[2,2,128,512]{3,2,1,0:T(8,128)(2,1)S(1)}, u32[]{:S(2)}, u32[]{:S(2)}) collective-permute-start(bf16[2,2,128,512]{3,2,1,0:T(8,128)(2,1)S(1)} %add_convert_fusion), channel_id=1, source_target_pairs={{0,64},{32,480},{64,128},{96,32},{128,192},{160,96},{192,256},{224... | collective-permute-start | bytes 1572872 | tf_op jit(solution)/shard_map/ppermute | solution.py:35
  131.2 0.1 collective-permute-done.16
  131.3 0.1 add_convert_fusion.2
  131.5 3.0 %collective-permute-start.17 = (bf16[2,2,128,512]{3,2,1,0:T(8,128)(2,1)S(1)}, bf16[2,2,128,512]{3,2,1,0:T(8,128)(2,1)S(1)}, u32[]{:S(2)}, u32[]{:S(2)}) collective-permute-start(bf16[2,2,128,512]{3,2,1,0:T(8,128)(2,1)S(1)} %add_convert_fusion.2), channel_id=1, source_target_pairs={{0,64},{32,480},{64,128},{96,32},{128,192},{160,96},{192,256},{224... | collective-permute-start | bytes 1572872 | tf_op jit(solution)/shard_map/ppermute | solution.py:35
  134.5 4.5 %collective-permute-done.22.refs_0_ = bf16[2,2,128,512]{3,2,1,0:T(8,128)(2,1)S(1)} collective-permute-done((bf16[2,2,128,512]{3,2,1,0:T(8,128)(2,1)S(1)}, bf16[2,2,128,512]{3,2,1,0:T(8,128)(2,1)S(1)}, u32[]{:S(2)}, u32[]{:S(2)}) %collective-permute-start.22) | collective-permute-done | bytes 524320 | tf_op jit(solution)/shard_map/ppermute | solution.py:51
  139.1 7.6 %collective-permute-start.24 = (bf16[2,2,128,512]{3,2,1,0:T(8,128)(2,1)S(1)}, bf16[2,2,128,512]{3,2,1,0:T(8,128)(2,1)S(1)}, u32[]{:S(2)}, u32[]{:S(2)}) collective-permute-start(bf16[2,2,128,512]{3,2,1,0:T(8,128)(2,1)S(1)} %collective-permute-done.23), channel_id=1, source_target_pairs={{0,32},{32,0},{64,96},{96,64},{128,160},{160,128},{192,224},{224,1... | collective-permute-start | bytes 1572872 | tf_op jit(solution)/shard_map/ppermute | solution.py:40
  146.7 1.9 %collective-permute-start.25 = (bf16[2,2,128,512]{3,2,1,0:T(8,128)(2,1)S(1)}, bf16[2,2,128,512]{3,2,1,0:T(8,128)(2,1)S(1)}, u32[]{:S(2)}, u32[]{:S(2)}) collective-permute-start(bf16[2,2,128,512]{3,2,1,0:T(8,128)(2,1)S(1)} %pad_maximum_fusion.6), channel_id=1, source_target_pairs={{0,32},{32,0},{64,96},{96,64},{128,160},{160,128},{192,224},{224,1... | collective-permute-start | bytes 1572872 | tf_op jit(solution)/shard_map/ppermute | solution.py:40
  148.6 1.9 %collective-permute-done.25.refs_2_ = bf16[2,2,128,512]{3,2,1,0:T(8,128)(2,1)S(1)} collective-permute-done((bf16[2,2,128,512]{3,2,1,0:T(8,128)(2,1)S(1)}, bf16[2,2,128,512]{3,2,1,0:T(8,128)(2,1)S(1)}, u32[]{:S(2)}, u32[]{:S(2)}) %collective-permute-start.25) | collective-permute-done | bytes 524320 | tf_op jit(solution)/shard_map/ppermute | solution.py:40
  150.5 1.9 %shard_map.98 = (bf16[256,512]{1,0:T(8,128)(2,1)}, bf16[256,512]{1,0:T(8,128)(2,1)}) custom-call(s32[6]{0:T(128)S(1)} %pad_add_fusion.6.table, bf16[2,2,128,512]{3,2,1,0:T(8,128)(2,1)S(1)} %get-tuple-element.60.near, bf16[6,2,128,512]{3,2,1,0:T(8,128)(2,1)S(1)} %collective-permute-done.13.theirs, ...), custom_call_target="tpu_custom_call" | custom-call | flops 4194304 | bytes 6291456 | tf_op jit(solution)/shard_map/pallas_call | solution.py:306
  (66 shorter events, 1.7 us)
Async XLA Ops:
  0.6 17.7 %copy-start.3 = (bf16[256,512]{1,0:T(8,128)(2,1)S(1)}, bf16[256,512]{1,0:T(8,128)(2,1)}, u32[]{:S(2)}) copy-start(bf16[256,512]{1,0:T(8,128)(2,1)} %keys.1) | copy-start | bytes 786436
  0.6 17.7 %copy-start.2 = (bf16[256,512]{1,0:T(8,128)(2,1)S(1)}, bf16[256,512]{1,0:T(8,128)(2,1)}, u32[]{:S(2)}) copy-start(bf16[256,512]{1,0:T(8,128)(2,1)} %values.1) | copy-start | bytes 786436
  1.8 23.2 %collective-permute-start.1 = (bf16[2,256,512]{2,1,0:T(8,128)(2,1)S(1)}, bf16[2,256,512]{2,1,0:T(8,128)(2,1)S(1)}, u32[]{:S(2)}, u32[]{:S(2)}) collective-permute-start(bf16[2,256,512]{2,1,0:T(8,128)(2,1)S(1)} %pad_maximum_fusion.refs_0_), channel_id=1, source_target_pairs={{0,64},{32,480},{64,128},{96,32},{128,192},{160,96},{192,256},{224... | collective-permute-start | bytes 1572872 | tf_op jit(solution)/shard_map/ppermute | solution.py:35
  12.5 5.9 %collective-permute-start = (bf16[2,256,512]{2,1,0:T(8,128)(2,1)S(1)}, bf16[2,256,512]{2,1,0:T(8,128)(2,1)S(1)}, u32[]{:S(2)}, u32[]{:S(2)}) collective-permute-start(bf16[2,256,512]{2,1,0:T(8,128)(2,1)S(1)} %pad_maximum_fusion.refs_0_), channel_id=1, source_target_pairs={{0,32},{32,0},{64,96},{96,64},{128,160},{160,128},{192,224},{224,1... | collective-permute-start | bytes 1572872 | tf_op jit(solution)/shard_map/ppermute | solution.py:40
  20.3 8.2 %collective-permute-start.5 = (bf16[2,2,128,512]{3,2,1,0:T(8,128)(2,1)S(1)}, bf16[2,2,128,512]{3,2,1,0:T(8,128)(2,1)S(1)}, u32[]{:S(2)}, u32[]{:S(2)}) collective-permute-start(bf16[2,2,128,512]{3,2,1,0:T(8,128)(2,1)S(1)} %get-tuple-element.47), channel_id=1, source_target_pairs={{0,32},{32,0},{64,96},{96,64},{128,160},{160,128},{192,224},{224,1... | collective-permute-start | bytes 1572872 | tf_op jit(solution)/shard_map/ppermute | solution.py:40
  22.8 19.2 %collective-permute-start.6 = (bf16[2,256,512]{2,1,0:T(8,128)(2,1)S(1)}, bf16[2,256,512]{2,1,0:T(8,128)(2,1)S(1)}, u32[]{:S(2)}, u32[]{:S(2)}) collective-permute-start(bf16[2,256,512]{2,1,0:T(8,128)(2,1)S(1)} %collective-permute-done.refs_0_.refs_4_), channel_id=1, source_target_pairs={{0,64},{32,480},{64,128},{96,32},{128,192},{160,96},{192,256},{224... | collective-permute-start | bytes 1572872 | tf_op jit(solution)/shard_map/ppermute | solution.py:35
  25.0 13.6 %collective-permute-start.2 = (bf16[2,256,512]{2,1,0:T(8,128)(2,1)S(1)}, bf16[2,256,512]{2,1,0:T(8,128)(2,1)S(1)}, u32[]{:S(2)}, u32[]{:S(2)}) collective-permute-start(bf16[2,256,512]{2,1,0:T(8,128)(2,1)S(1)} %collective-permute-done.1.refs_1_.refs_5_), channel_id=1, source_target_pairs={{0,64},{32,480},{64,128},{96,32},{128,192},{160,96},{192,256},{224... | collective-permute-start | bytes 1572872 | tf_op jit(solution)/shard_map/ppermute | solution.py:35
  28.6 16.5 %collective-permute-start.7 = (bf16[2,2,128,512]{3,2,1,0:T(8,128)(2,1)S(1)}, bf16[2,2,128,512]{3,2,1,0:T(8,128)(2,1)S(1)}, u32[]{:S(2)}, u32[]{:S(2)}) collective-permute-start(bf16[2,2,128,512]{3,2,1,0:T(8,128)(2,1)S(1)} %pad_maximum_fusion.1), channel_id=1, source_target_pairs={{0,2},{1,3},{2,4},{3,5},{4,6},{5,7},{6,8},{7,9},{8,10},{9,11},{10,... | collective-permute-start | bytes 1572872 | tf_op jit(solution)/shard_map/ppermute | solution.py:51
  38.6 10.2 %collective-permute-start.3 = (bf16[2,256,512]{2,1,0:T(8,128)(2,1)S(1)}, bf16[2,256,512]{2,1,0:T(8,128)(2,1)S(1)}, u32[]{:S(2)}, u32[]{:S(2)}) collective-permute-start(bf16[2,256,512]{2,1,0:T(8,128)(2,1)S(1)} %collective-permute-done.2.refs_2_.refs_6_), channel_id=1, source_target_pairs={{0,64},{32,480},{64,128},{96,32},{128,192},{160,96},{192,256},{224... | collective-permute-start | bytes 1572872 | tf_op jit(solution)/shard_map/ppermute | solution.py:35
  45.2 13.1 %collective-permute-start.10 = (bf16[2,256,512]{2,1,0:T(8,128)(2,1)S(1)}, bf16[2,256,512]{2,1,0:T(8,128)(2,1)S(1)}, u32[]{:S(2)}, u32[]{:S(2)}) collective-permute-start(bf16[2,256,512]{2,1,0:T(8,128)(2,1)S(1)} %collective-permute-done.6.refs_5_.refs_9_), channel_id=1, source_target_pairs={{0,64},{32,480},{64,128},{96,32},{128,192},{160,96},{192,256},{224... | collective-permute-start | bytes 1572872 | tf_op jit(solution)/shard_map/ppermute | solution.py:35
  48.8 12.2 %collective-permute-start.4 = (bf16[2,256,512]{2,1,0:T(8,128)(2,1)S(1)}, bf16[2,256,512]{2,1,0:T(8,128)(2,1)S(1)}, u32[]{:S(2)}, u32[]{:S(2)}) collective-permute-start(bf16[2,256,512]{2,1,0:T(8,128)(2,1)S(1)} %collective-permute-done.3.refs_3_.refs_7_), channel_id=1, source_target_pairs={{0,64},{32,480},{64,128},{96,32},{128,192},{160,96},{192,256},{224... | collective-permute-start | bytes 1572872 | tf_op jit(solution)/shard_map/ppermute | solution.py:35
  53.1 11.3 %collective-permute-start.8 = (bf16[2,2,128,512]{3,2,1,0:T(8,128)(2,1)S(1)}, bf16[2,2,128,512]{3,2,1,0:T(8,128)(2,1)S(1)}, u32[]{:S(2)}, u32[]{:S(2)}) collective-permute-start(bf16[2,2,128,512]{3,2,1,0:T(8,128)(2,1)S(1)} %pad_maximum_fusion.2), channel_id=1, source_target_pairs={{0,1},{1,2},{2,3},{3,4},{4,5},{5,6},{6,7},{7,8},{8,9},{9,10},{10,1... | collective-permute-start | bytes 1572872 | tf_op jit(solution)/shard_map/ppermute | solution.py:51
  58.3 10.2 %collective-permute-start.11 = (bf16[2,256,512]{2,1,0:T(8,128)(2,1)S(1)}, bf16[2,256,512]{2,1,0:T(8,128)(2,1)S(1)}, u32[]{:S(2)}, u32[]{:S(2)}) collective-permute-start(bf16[2,256,512]{2,1,0:T(8,128)(2,1)S(1)} %collective-permute-done.10.refs_6_.refs_10_), channel_id=1, source_target_pairs={{0,64},{32,480},{64,128},{96,32},{128,192},{160,96},{192,256},{224... | collective-permute-start | bytes 1572872 | tf_op jit(solution)/shard_map/ppermute | solution.py:35
  69.6 8.3 %copy-start.4 = (bf16[256,512]{1,0:T(8,128)(2,1)S(1)}, bf16[256,512]{1,0:T(8,128)(2,1)}, u32[]{:S(2)}) copy-start(bf16[256,512]{1,0:T(8,128)(2,1)} %param.6) | copy-start | bytes 786436
  69.6 8.3 %copy-start.5 = (bf16[256,512]{1,0:T(8,128)(2,1)S(1)}, bf16[256,512]{1,0:T(8,128)(2,1)}, u32[]{:S(2)}) copy-start(bf16[256,512]{1,0:T(8,128)(2,1)} %param.9) | copy-start | bytes 786436
  69.6 8.3 %collective-permute-start.12 = (bf16[6,2,128,512]{3,2,1,0:T(8,128)(2,1)S(1)}, bf16[6,2,128,512]{3,2,1,0:T(8,128)(2,1)S(1)}, u32[]{:S(2)}, u32[]{:S(2)}) collective-permute-start(bf16[6,2,128,512]{3,2,1,0:T(8,128)(2,1)S(1)} %shard_map.94), channel_id=1, source_target_pairs={{0,32},{32,0},{64,96},{96,64},{128,160},{160,128},{192,224},{224,1... | collective-permute-start | bytes 4718600 | tf_op jit(solution)/shard_map/ppermute | solution.py:40
  74.1 3.8 %collective-permute-start.9 = (bf16[2,2,128,512]{3,2,1,0:T(8,128)(2,1)S(1)}, bf16[2,2,128,512]{3,2,1,0:T(8,128)(2,1)S(1)}, u32[]{:S(2)}, u32[]{:S(2)}) collective-permute-start(bf16[2,2,128,512]{3,2,1,0:T(8,128)(2,1)S(1)} %pad_maximum_fusion.3), channel_id=1, source_target_pairs={{0,32},{32,0},{64,96},{96,64},{128,160},{160,128},{192,224},{224,1... | collective-permute-start | bytes 1572872 | tf_op jit(solution)/shard_map/ppermute | solution.py:40
  90.0 5.3 %collective-permute-start.13 = (bf16[6,2,128,512]{3,2,1,0:T(8,128)(2,1)S(1)}, bf16[6,2,128,512]{3,2,1,0:T(8,128)(2,1)S(1)}, u32[]{:S(2)}, u32[]{:S(2)}) collective-permute-start(bf16[6,2,128,512]{3,2,1,0:T(8,128)(2,1)S(1)} %get-tuple-element.61.mine), channel_id=1, source_target_pairs={{0,32},{32,0},{64,96},{96,64},{128,160},{160,128},{192,224},{224,1... | collective-permute-start | bytes 4718600 | tf_op jit(solution)/shard_map/ppermute | solution.py:40
  96.2 10.2 %collective-permute-start.14 = (bf16[2,2,128,512]{3,2,1,0:T(8,128)(2,1)S(1)}, bf16[2,2,128,512]{3,2,1,0:T(8,128)(2,1)S(1)}, u32[]{:S(2)}, u32[]{:S(2)}) collective-permute-start(bf16[2,2,128,512]{3,2,1,0:T(8,128)(2,1)S(1)} %get-tuple-element.65), channel_id=1, source_target_pairs={{0,64},{32,480},{64,128},{96,32},{128,192},{160,96},{192,256},{224... | collective-permute-start | bytes 1572872 | tf_op jit(solution)/shard_map/ppermute | solution.py:35
  99.6 11.3 %collective-permute-start.18 = (bf16[2,2,128,512]{3,2,1,0:T(8,128)(2,1)S(1)}, bf16[2,2,128,512]{3,2,1,0:T(8,128)(2,1)S(1)}, u32[]{:S(2)}, u32[]{:S(2)}) collective-permute-start(bf16[2,2,128,512]{3,2,1,0:T(8,128)(2,1)S(1)} %get-tuple-element.71), channel_id=1, source_target_pairs={{0,32},{32,0},{64,96},{96,64},{128,160},{160,128},{192,224},{224,1... | collective-permute-start | bytes 1572872 | tf_op jit(solution)/shard_map/ppermute | solution.py:40
  101.5 13.8 %collective-permute-start.19 = (bf16[2,2,128,512]{3,2,1,0:T(8,128)(2,1)S(1)}, bf16[2,2,128,512]{3,2,1,0:T(8,128)(2,1)S(1)}, u32[]{:S(2)}, u32[]{:S(2)}) collective-permute-start(bf16[2,2,128,512]{3,2,1,0:T(8,128)(2,1)S(1)} %get-tuple-element.72), channel_id=1, source_target_pairs={{0,64},{32,480},{64,128},{96,32},{128,192},{160,96},{192,256},{224... | collective-permute-start | bytes 1572872 | tf_op jit(solution)/shard_map/ppermute | solution.py:35
  106.6 11.1 %collective-permute-start.15 = (bf16[2,2,128,512]{3,2,1,0:T(8,128)(2,1)S(1)}, bf16[2,2,128,512]{3,2,1,0:T(8,128)(2,1)S(1)}, u32[]{:S(2)}, u32[]{:S(2)}) collective-permute-start(bf16[2,2,128,512]{3,2,1,0:T(8,128)(2,1)S(1)} %add_convert_fusion.4), channel_id=1, source_target_pairs={{0,64},{32,480},{64,128},{96,32},{128,192},{160,96},{192,256},{224... | collective-permute-start | bytes 1572872 | tf_op jit(solution)/shard_map/ppermute | solution.py:35
  111.0 12.4 %collective-permute-start.21 = (bf16[2,2,128,512]{3,2,1,0:T(8,128)(2,1)S(1)}, bf16[2,2,128,512]{3,2,1,0:T(8,128)(2,1)S(1)}, u32[]{:S(2)}, u32[]{:S(2)}) collective-permute-start(bf16[2,2,128,512]{3,2,1,0:T(8,128)(2,1)S(1)} %pad_maximum_fusion.4), channel_id=1, source_target_pairs={{2,0},{3,1},{4,2},{5,3},{6,4},{7,5},{8,6},{9,7},{10,8},{11,9},{12,... | collective-permute-start | bytes 1572872 | tf_op jit(solution)/shard_map/ppermute | solution.py:51
  115.5 10.2 %collective-permute-start.20 = (bf16[2,2,128,512]{3,2,1,0:T(8,128)(2,1)S(1)}, bf16[2,2,128,512]{3,2,1,0:T(8,128)(2,1)S(1)}, u32[]{:S(2)}, u32[]{:S(2)}) collective-permute-start(bf16[2,2,128,512]{3,2,1,0:T(8,128)(2,1)S(1)} %add_convert_fusion.1), channel_id=1, source_target_pairs={{0,64},{32,480},{64,128},{96,32},{128,192},{160,96},{192,256},{224... | collective-permute-start | bytes 1572872 | tf_op jit(solution)/shard_map/ppermute | solution.py:35
  117.8 13.5 %collective-permute-start.16 = (bf16[2,2,128,512]{3,2,1,0:T(8,128)(2,1)S(1)}, bf16[2,2,128,512]{3,2,1,0:T(8,128)(2,1)S(1)}, u32[]{:S(2)}, u32[]{:S(2)}) collective-permute-start(bf16[2,2,128,512]{3,2,1,0:T(8,128)(2,1)S(1)} %add_convert_fusion.3), channel_id=1, source_target_pairs={{0,64},{32,480},{64,128},{96,32},{128,192},{160,96},{192,256},{224... | collective-permute-start | bytes 1572872 | tf_op jit(solution)/shard_map/ppermute | solution.py:35
  123.4 7.8 %copy-start = (bf16[2,2,128,512]{3,2,1,0:T(8,128)(2,1)}, bf16[2,2,128,512]{3,2,1,0:T(8,128)(2,1)S(1)}, u32[]{:S(2)}) copy-start(bf16[2,2,128,512]{3,2,1,0:T(8,128)(2,1)S(1)} %collective-permute-done.21.refs_1_) | copy-start | bytes 1572868
  125.8 13.1 %collective-permute-start.22 = (bf16[2,2,128,512]{3,2,1,0:T(8,128)(2,1)S(1)}, bf16[2,2,128,512]{3,2,1,0:T(8,128)(2,1)S(1)}, u32[]{:S(2)}, u32[]{:S(2)}) collective-permute-start(bf16[2,2,128,512]{3,2,1,0:T(8,128)(2,1)S(1)} %pad_maximum_fusion.5), channel_id=1, source_target_pairs={{1,0},{2,1},{3,2},{4,3},{5,4},{6,5},{7,6},{8,7},{9,8},{10,9},{11,1... | collective-permute-start | bytes 1572872 | tf_op jit(solution)/shard_map/ppermute | solution.py:51
  127.9 11.2 %collective-permute-start.23 = (bf16[2,2,128,512]{3,2,1,0:T(8,128)(2,1)S(1)}, bf16[2,2,128,512]{3,2,1,0:T(8,128)(2,1)S(1)}, u32[]{:S(2)}, u32[]{:S(2)}) collective-permute-start(bf16[2,2,128,512]{3,2,1,0:T(8,128)(2,1)S(1)} %add_convert_fusion), channel_id=1, source_target_pairs={{0,64},{32,480},{64,128},{96,32},{128,192},{160,96},{192,256},{224... | collective-permute-start | bytes 1572872 | tf_op jit(solution)/shard_map/ppermute | solution.py:35
  131.2 7.8 %slice-start = ((bf16[2,2,128,512]{3,2,1,0:T(8,128)(2,1)}), bf16[1,2,128,512]{3,2,1,0:T(8,128)(2,1)S(1)}, s32[]{:S(2)}) async-start(bf16[2,2,128,512]{3,2,1,0:T(8,128)(2,1)} %copy-done), calls=%async_computation | async-start | bytes 524288 | tf_op jit(solution)/shard_map/slice | solution.py:416
  131.3 19.2 %copy-start.1 = (bf16[2,2,128,512]{3,2,1,0:T(8,128)(2,1)S(1)}, bf16[2,2,128,512]{3,2,1,0:T(8,128)(2,1)}, u32[]{:S(2)}) copy-start(bf16[2,2,128,512]{3,2,1,0:T(8,128)(2,1)} %copy-done) | copy-start | bytes 1572868
  131.5 17.1 %collective-permute-start.17 = (bf16[2,2,128,512]{3,2,1,0:T(8,128)(2,1)S(1)}, bf16[2,2,128,512]{3,2,1,0:T(8,128)(2,1)S(1)}, u32[]{:S(2)}, u32[]{:S(2)}) collective-permute-start(bf16[2,2,128,512]{3,2,1,0:T(8,128)(2,1)S(1)} %add_convert_fusion.2), channel_id=1, source_target_pairs={{0,64},{32,480},{64,128},{96,32},{128,192},{160,96},{192,256},{224... | collective-permute-start | bytes 1572872 | tf_op jit(solution)/shard_map/ppermute | solution.py:35
  139.1 9.6 %collective-permute-start.24 = (bf16[2,2,128,512]{3,2,1,0:T(8,128)(2,1)S(1)}, bf16[2,2,128,512]{3,2,1,0:T(8,128)(2,1)S(1)}, u32[]{:S(2)}, u32[]{:S(2)}) collective-permute-start(bf16[2,2,128,512]{3,2,1,0:T(8,128)(2,1)S(1)} %collective-permute-done.23), channel_id=1, source_target_pairs={{0,32},{32,0},{64,96},{96,64},{128,160},{160,128},{192,224},{224,1... | collective-permute-start | bytes 1572872 | tf_op jit(solution)/shard_map/ppermute | solution.py:40
  146.7 3.8 %collective-permute-start.25 = (bf16[2,2,128,512]{3,2,1,0:T(8,128)(2,1)S(1)}, bf16[2,2,128,512]{3,2,1,0:T(8,128)(2,1)S(1)}, u32[]{:S(2)}, u32[]{:S(2)}) collective-permute-start(bf16[2,2,128,512]{3,2,1,0:T(8,128)(2,1)S(1)} %pad_maximum_fusion.6), channel_id=1, source_target_pairs={{0,32},{32,0},{64,96},{96,64},{128,160},{160,128},{192,224},{224,1... | collective-permute-start | bytes 1572872 | tf_op jit(solution)/shard_map/ppermute | solution.py:40

commit v9 on v8

--- a/solution.py
+++ b/solution.py
@@ -363,16 +363,16 @@
     wanted = jnp.stack(wanted).astype(i32)
     hits = jnp.stack([slot_in(mine, wanted), slot_in(theirs, wanted)])
     last = jnp.concatenate([given, hits[1, 7 * NB :]]).astype(i32)
-    tables = (given, pick_table, table, hits[:, : 2 * NB], hits[:, 2 * NB : 7 * NB], last)
-    sibling, tables = lax.optimization_barrier((sibling, tables))
+    tables = (pick_table, table, hits[:, : 2 * NB], hits[:, 2 * NB : 7 * NB], last)
+    sibling, given = lax.optimization_barrier((sibling, given))
     flow_b = [ring_step(sibling)]
-    given, pick_table, table, hits_first, hits_rest, last = tables
 
     flow_a.append(ring_step(flow_a[0]))
     keep, give = offer(given, keys, values)
     given_here = swap_cores(give)
     two = dom_step(jnp.stack([keep[1], given_here[1]]), 2)
-    flow_b[0], two = lax.optimization_barrier((flow_b[0], two))
+    flow_b[0], two, tables = lax.optimization_barrier((flow_b[0], two, tables))
+    pick_table, table, hits_first, hits_rest, last = tables
     flow_b.append(ring_step(flow_b[0]))
     flow_a.append(ring_step(flow_a[1]))
     flow_b.append(ring_step(flow_b[1]))

time: 154 us -> 153 us (level)
  local copies, waits for them, and re-layouts: 2.83 us -> 4.73 us
  transfers between devices with their start and end apart: 26 -> 26, of which waited for: 15 -> 14; matrix products, arithmetic and copies ran while one was open for 3% -> 5% of each run, Pallas kernels for 2% -> 2%
where the time goes in v9:
time: 153 us; the launch traced here: 152 us
  starting transfers between devices  92.4 us (60%)
  waiting for transfers between devices  31.4 us (21%)
  Pallas kernels  18.9 us (12%)
  local copies, waits for them, and re-layouts  4.73 us (3%)
  other arithmetic  3.3 us (2%)
    ppermute x14, starting transfers between devices, ring_step(): lax.ppermute(array, 'group', [(g, (g + (2 if g % 2 == 0 else -2)) % size)...  51.2 us
    ppermute x8, starting transfers between devices, swap_cores(): return lax.ppermute(array, 'group', [(g, g ^ 1) for g in range(size)])  24.3 us
    ppermute x4, starting transfers between devices, dom_step(): return lax.ppermute(array, ('group', 'dom'), pairs)  16.9 us
    ppermute x4, waiting for transfers between devices, dom_step(): return lax.ppermute(array, ('group', 'dom'), pairs)  12.3 us
    ppermute x14, waiting for transfers between devices, ring_step(): lax.ppermute(array, 'group', [(g, (g + (2 if g % 2 == 0 else -2)) % size)...  12.2 us
    pallas_call x1, Pallas kernels, attend(): pl.pallas_call(attend_kernel, out_shape=(jax.ShapeDtypeStruct((NB, BS, D)...  12.1 us
    ppermute x8, waiting for transfers between devices, swap_cores(): return lax.ppermute(array, 'group', [(g, g ^ 1) for g in range(size)])  6.92 us
  transfers between devices with their start and end apart: 26, of which 14 were waited for; matrix products, arithmetic and copies ran while one was open for 5% of the time, Pallas kernels for 2%

profile of v9, /device:TPU:57, one launch (start us, length us, event | category | flops | bytes accessed | tf_op | source)
XLA Modules:
  0.0 152.2 jit_solution(14605368686436578940)
XLA Ops:
  0.7 1.1 pad_maximum_fusion.refs_0_
  1.8 10.7 %collective-permute-start.4 = (bf16[2,256,512]{2,1,0:T(8,128)(2,1)S(1)}, bf16[2,256,512]{2,1,0:T(8,128)(2,1)S(1)}, u32[]{:S(2)}, u32[]{:S(2)}) collective-permute-start(bf16[2,256,512]{2,1,0:T(8,128)(2,1)S(1)} %pad_maximum_fusion.refs_0_), channel_id=1, source_target_pairs={{0,64},{32,480},{64,128},{96,32},{128,192},{160,96},{192,256},{224... | collective-permute-start | bytes 1572872 | tf_op jit(solution)/shard_map/ppermute | solution.py:35
  12.5 1.9 %collective-permute-start = (bf16[2,256,512]{2,1,0:T(8,128)(2,1)S(1)}, bf16[2,256,512]{2,1,0:T(8,128)(2,1)S(1)}, u32[]{:S(2)}, u32[]{:S(2)}) collective-permute-start(bf16[2,256,512]{2,1,0:T(8,128)(2,1)S(1)} %pad_maximum_fusion.refs_0_), channel_id=1, source_target_pairs={{0,32},{32,0},{64,96},{96,64},{128,160},{160,128},{192,224},{224,1... | collective-permute-start | bytes 1572872 | tf_op jit(solution)/shard_map/ppermute | solution.py:40
  14.5 0.8 copy.15
  15.4 0.2 select_reduce_fusion.3
  15.6 0.1 add.216
  15.8 0.8 copy.14
  16.6 0.1 stack.114
  16.6 0.1 select_reduce_fusion.2
  17.2 0.1 fusion.2
  17.4 0.1 reduce_max.18
  17.6 0.1 rev.3
  17.8 2.0 %shard_map.93 = (bf16[2,2,128,512]{3,2,1,0:T(8,128)(2,1)S(1)}, bf16[2,2,128,512]{3,2,1,0:T(8,128)(2,1)S(1)}) custom-call(s32[4]{0:T(128)S(1)} %broadcast_select_fusion.2.table, bf16[256,512]{1,0:T(8,128)(2,1)S(1)} %copy-done.3, bf16[256,512]{1,0:T(8,128)(2,1)S(1)} %copy-done.2), custom_call_target="tpu_custom_call" | custom-call | bytes 2097152 | tf_op jit(solution)/shard_map/pallas_call | solution.py:122
  19.7 2.4 %collective-permute-start.2 = (bf16[2,2,128,512]{3,2,1,0:T(8,128)(2,1)S(1)}, bf16[2,2,128,512]{3,2,1,0:T(8,128)(2,1)}, u32[]{:S(2)}, u32[]{:S(2)}) collective-permute-start(bf16[2,2,128,512]{3,2,1,0:T(8,128)(2,1)S(1)} %get-tuple-element.47), channel_id=1, source_target_pairs={{0,32},{32,0},{64,96},{96,64},{128,160},{160,128},{192,224},{224,1... | collective-permute-start | bytes 1572872 | tf_op jit(solution)/shard_map/ppermute | solution.py:40
  22.5 2.2 %collective-permute-start.1 = (bf16[2,256,512]{2,1,0:T(8,128)(2,1)S(1)}, bf16[2,256,512]{2,1,0:T(8,128)(2,1)S(1)}, u32[]{:S(2)}, u32[]{:S(2)}) collective-permute-start(bf16[2,256,512]{2,1,0:T(8,128)(2,1)S(1)} %collective-permute-done.refs_0_.refs_4_), channel_id=1, source_target_pairs={{0,64},{32,480},{64,128},{96,32},{128,192},{160,96},{192,256},{224... | collective-permute-start | bytes 1572872 | tf_op jit(solution)/shard_map/ppermute | solution.py:35
  24.7 3.6 %collective-permute-start.5 = (bf16[2,256,512]{2,1,0:T(8,128)(2,1)S(1)}, bf16[2,256,512]{2,1,0:T(8,128)(2,1)S(1)}, u32[]{:S(2)}, u32[]{:S(2)}) collective-permute-start(bf16[2,256,512]{2,1,0:T(8,128)(2,1)S(1)} %collective-permute-done.4.refs_1_.refs_5_), channel_id=1, source_target_pairs={{0,64},{32,480},{64,128},{96,32},{128,192},{160,96},{192,256},{224... | collective-permute-start | bytes 1572872 | tf_op jit(solution)/shard_map/ppermute | solution.py:35
  28.3 1.0 slice.73
  29.3 5.4 %collective-permute-start.3 = (bf16[2,2,128,512]{3,2,1,0:T(8,128)(2,1)S(1)}, bf16[2,2,128,512]{3,2,1,0:T(8,128)(2,1)S(1)}, u32[]{:S(2)}, u32[]{:S(2)}) collective-permute-start(bf16[2,2,128,512]{3,2,1,0:T(8,128)(2,1)S(1)} %pad_maximum_fusion.1), channel_id=1, source_target_pairs={{0,2},{1,3},{2,4},{3,5},{4,6},{5,7},{6,8},{7,9},{8,10},{9,11},{10,... | collective-permute-start | bytes 1572872 | tf_op jit(solution)/shard_map/ppermute | solution.py:51
  34.8 0.2 select_reduce_fusion
  35.0 3.3 %collective-permute-done.5.refs_2_.refs_6_ = bf16[2,256,512]{2,1,0:T(8,128)(2,1)S(1)} collective-permute-done((bf16[2,256,512]{2,1,0:T(8,128)(2,1)S(1)}, bf16[2,256,512]{2,1,0:T(8,128)(2,1)S(1)}, u32[]{:S(2)}, u32[]{:S(2)}) %collective-permute-start.5) | collective-permute-done | bytes 524320 | tf_op jit(solution)/shard_map/ppermute | solution.py:35
  38.3 3.4 %collective-permute-start.6 = (bf16[2,256,512]{2,1,0:T(8,128)(2,1)S(1)}, bf16[2,256,512]{2,1,0:T(8,128)(2,1)S(1)}, u32[]{:S(2)}, u32[]{:S(2)}) collective-permute-start(bf16[2,256,512]{2,1,0:T(8,128)(2,1)S(1)} %collective-permute-done.5.refs_2_.refs_6_), channel_id=1, source_target_pairs={{0,64},{32,480},{64,128},{96,32},{128,192},{160,96},{192,256},{224... | collective-permute-start | bytes 1572872 | tf_op jit(solution)/shard_map/ppermute | solution.py:35
  41.7 4.1 %collective-permute-done.3.refs_2_ = bf16[2,2,128,512]{3,2,1,0:T(8,128)(2,1)S(1)} collective-permute-done((bf16[2,2,128,512]{3,2,1,0:T(8,128)(2,1)S(1)}, bf16[2,2,128,512]{3,2,1,0:T(8,128)(2,1)S(1)}, u32[]{:S(2)}, u32[]{:S(2)}) %collective-permute-start.3) | collective-permute-done | bytes 524320 | tf_op jit(solution)/shard_map/ppermute | solution.py:51
  45.8 2.7 %collective-permute-start.10 = (bf16[2,256,512]{2,1,0:T(8,128)(2,1)S(1)}, bf16[2,256,512]{2,1,0:T(8,128)(2,1)S(1)}, u32[]{:S(2)}, u32[]{:S(2)}) collective-permute-start(bf16[2,256,512]{2,1,0:T(8,128)(2,1)S(1)} %collective-permute-done.1.refs_5_.refs_9_), channel_id=1, source_target_pairs={{0,64},{32,480},{64,128},{96,32},{128,192},{160,96},{192,256},{224... | collective-permute-start | bytes 1572872 | tf_op jit(solution)/shard_map/ppermute | solution.py:35
  48.6 1.0 slice.64
  49.6 3.2 %collective-permute-start.7 = (bf16[2,256,512]{2,1,0:T(8,128)(2,1)S(1)}, bf16[2,256,512]{2,1,0:T(8,128)(2,1)S(1)}, u32[]{:S(2)}, u32[]{:S(2)}) collective-permute-start(bf16[2,256,512]{2,1,0:T(8,128)(2,1)S(1)} %collective-permute-done.6.refs_3_.refs_7_), channel_id=1, source_target_pairs={{0,64},{32,480},{64,128},{96,32},{128,192},{160,96},{192,256},{224... | collective-permute-start | bytes 1572872 | tf_op jit(solution)/shard_map/ppermute | solution.py:35
  52.8 5.2 %collective-permute-start.8 = (bf16[2,2,128,512]{3,2,1,0:T(8,128)(2,1)S(1)}, bf16[2,2,128,512]{3,2,1,0:T(8,128)(2,1)S(1)}, u32[]{:S(2)}, u32[]{:S(2)}) collective-permute-start(bf16[2,2,128,512]{3,2,1,0:T(8,128)(2,1)S(1)} %pad_maximum_fusion.2), channel_id=1, source_target_pairs={{0,1},{1,2},{2,3},{3,4},{4,5},{5,6},{6,7},{7,8},{8,9},{9,10},{10,1... | collective-permute-start | bytes 1572872 | tf_op jit(solution)/shard_map/ppermute | solution.py:51
  58.0 1.9 %collective-permute-start.11 = (bf16[2,256,512]{2,1,0:T(8,128)(2,1)S(1)}, bf16[2,256,512]{2,1,0:T(8,128)(2,1)S(1)}, u32[]{:S(2)}, u32[]{:S(2)}) collective-permute-start(bf16[2,256,512]{2,1,0:T(8,128)(2,1)S(1)} %collective-permute-done.10.refs_6_.refs_10_), channel_id=1, source_target_pairs={{0,64},{32,480},{64,128},{96,32},{128,192},{160,96},{192,256},{224... | collective-permute-start | bytes 1572872 | tf_op jit(solution)/shard_map/ppermute | solution.py:35
  59.9 1.7 %collective-permute-done.7.refs_4_.refs_8_ = bf16[2,256,512]{2,1,0:T(8,128)(2,1)S(1)} collective-permute-done((bf16[2,256,512]{2,1,0:T(8,128)(2,1)S(1)}, bf16[2,256,512]{2,1,0:T(8,128)(2,1)S(1)}, u32[]{:S(2)}, u32[]{:S(2)}) %collective-permute-start.7) | collective-permute-done | bytes 524320 | tf_op jit(solution)/shard_map/ppermute | solution.py:35
  61.7 2.5 %collective-permute-done.8.refs_1_ = bf16[2,2,128,512]{3,2,1,0:T(8,128)(2,1)S(1)} collective-permute-done((bf16[2,2,128,512]{3,2,1,0:T(8,128)(2,1)S(1)}, bf16[2,2,128,512]{3,2,1,0:T(8,128)(2,1)S(1)}, u32[]{:S(2)}, u32[]{:S(2)}) %collective-permute-start.8) | collective-permute-done | bytes 524320 | tf_op jit(solution)/shard_map/ppermute | solution.py:51
  64.1 4.1 %collective-permute-done.11.refs_7_.refs_11_ = bf16[2,256,512]{2,1,0:T(8,128)(2,1)S(1)} collective-permute-done((bf16[2,256,512]{2,1,0:T(8,128)(2,1)S(1)}, bf16[2,256,512]{2,1,0:T(8,128)(2,1)S(1)}, u32[]{:S(2)}, u32[]{:S(2)}) %collective-permute-start.11) | collective-permute-done | bytes 524320 | tf_op jit(solution)/shard_map/ppermute | solution.py:35
  68.2 1.1 shard_map.94
  69.3 4.4 %collective-permute-start.12 = (bf16[6,2,128,512]{3,2,1,0:T(8,128)(2,1)S(1)}, bf16[6,2,128,512]{3,2,1,0:T(8,128)(2,1)S(1)}, u32[]{:S(2)}, u32[]{:S(2)}) collective-permute-start(bf16[6,2,128,512]{3,2,1,0:T(8,128)(2,1)S(1)} %shard_map.94), channel_id=1, source_target_pairs={{0,32},{32,0},{64,96},{96,64},{128,160},{160,128},{192,224},{224,1... | collective-permute-start | bytes 4718600 | tf_op jit(solution)/shard_map/ppermute | solution.py:40
  73.9 1.9 %collective-permute-start.9 = (bf16[2,2,128,512]{3,2,1,0:T(8,128)(2,1)S(1)}, bf16[2,2,128,512]{3,2,1,0:T(8,128)(2,1)S(1)}, u32[]{:S(2)}, u32[]{:S(2)}) collective-permute-start(bf16[2,2,128,512]{3,2,1,0:T(8,128)(2,1)S(1)} %pad_maximum_fusion.3), channel_id=1, source_target_pairs={{0,32},{32,0},{64,96},{96,64},{128,160},{160,128},{192,224},{224,1... | collective-permute-start | bytes 1572872 | tf_op jit(solution)/shard_map/ppermute | solution.py:40
  75.8 1.9 %collective-permute-done.9.refs_3_ = bf16[2,2,128,512]{3,2,1,0:T(8,128)(2,1)S(1)} collective-permute-done((bf16[2,2,128,512]{3,2,1,0:T(8,128)(2,1)S(1)}, bf16[2,2,128,512]{3,2,1,0:T(8,128)(2,1)S(1)}, u32[]{:S(2)}, u32[]{:S(2)}) %collective-permute-start.9) | collective-permute-done | bytes 524320 | tf_op jit(solution)/shard_map/ppermute | solution.py:40
  77.7 12.1 %shard_map.95 = (bf16[2,128,512]{2,1,0:T(8,128)(2,1)}, bf16[2,128,512]{2,1,0:T(8,128)(2,1)}, bf16[2,2,128,512]{3,2,1,0:T(8,128)(2,1)S(1)}, bf16[6,2,128,512]{3,2...) custom-call(s32[4,14]{1,0:T(4,128)S(1)} %pad_add_fusion.table, ...), custom_call_target="tpu_custom_call" | custom-call | flops 1409286144 | bytes 12582912 | tf_op jit(solution)/shard_map/pallas_call | solution.py:232
  89.8 2.1 %collective-permute-start.13 = (bf16[6,2,128,512]{3,2,1,0:T(8,128)(2,1)S(1)}, bf16[6,2,128,512]{3,2,1,0:T(8,128)(2,1)S(1)}, u32[]{:S(2)}, u32[]{:S(2)}) collective-permute-start(bf16[6,2,128,512]{3,2,1,0:T(8,128)(2,1)S(1)} %get-tuple-element.61.mine), channel_id=1, source_target_pairs={{0,32},{32,0},{64,96},{96,64},{128,160},{160,128},{192,224},{224,1... | collective-permute-start | bytes 4718600 | tf_op jit(solution)/shard_map/ppermute | solution.py:40
  91.9 3.2 %collective-permute-done.13.theirs = bf16[6,2,128,512]{3,2,1,0:T(8,128)(2,1)S(1)} collective-permute-done((bf16[6,2,128,512]{3,2,1,0:T(8,128)(2,1)S(1)}, bf16[6,2,128,512]{3,2,1,0:T(8,128)(2,1)S(1)}, u32[]{:S(2)}, u32[]{:S(2)}) %collective-permute-start.13) | collective-permute-done | bytes 1572896 | tf_op jit(solution)/shard_map/ppermute | solution.py:40
  95.1 0.9 shard_map.96
  96.0 3.3 %collective-permute-start.14 = (bf16[2,2,128,512]{3,2,1,0:T(8,128)(2,1)S(1)}, bf16[2,2,128,512]{3,2,1,0:T(8,128)(2,1)S(1)}, u32[]{:S(2)}, u32[]{:S(2)}) collective-permute-start(bf16[2,2,128,512]{3,2,1,0:T(8,128)(2,1)S(1)} %get-tuple-element.65), channel_id=1, source_target_pairs={{0,64},{32,480},{64,128},{96,32},{128,192},{160,96},{192,256},{224... | collective-permute-start | bytes 1572872 | tf_op jit(solution)/shard_map/ppermute | solution.py:35
  99.3 1.9 %collective-permute-start.18 = (bf16[2,2,128,512]{3,2,1,0:T(8,128)(2,1)S(1)}, bf16[2,2,128,512]{3,2,1,0:T(8,128)(2,1)S(1)}, u32[]{:S(2)}, u32[]{:S(2)}) collective-permute-start(bf16[2,2,128,512]{3,2,1,0:T(8,128)(2,1)S(1)} %get-tuple-element.71), channel_id=1, source_target_pairs={{0,32},{32,0},{64,96},{96,64},{128,160},{160,128},{192,224},{224,1... | collective-permute-start | bytes 1572872 | tf_op jit(solution)/shard_map/ppermute | solution.py:40
  101.2 3.6 %collective-permute-start.19 = (bf16[2,2,128,512]{3,2,1,0:T(8,128)(2,1)S(1)}, bf16[2,2,128,512]{3,2,1,0:T(8,128)(2,1)S(1)}, u32[]{:S(2)}, u32[]{:S(2)}) collective-permute-start(bf16[2,2,128,512]{3,2,1,0:T(8,128)(2,1)S(1)} %get-tuple-element.72), channel_id=1, source_target_pairs={{0,64},{32,480},{64,128},{96,32},{128,192},{160,96},{192,256},{224... | collective-permute-start | bytes 1572872 | tf_op jit(solution)/shard_map/ppermute | solution.py:35
  104.9 1.0 shard_map.97
  105.9 0.3 collective-permute-done.14
  106.2 0.1 add_convert_fusion.4
  106.3 4.2 %collective-permute-start.15 = (bf16[2,2,128,512]{3,2,1,0:T(8,128)(2,1)S(1)}, bf16[2,2,128,512]{3,2,1,0:T(8,128)(2,1)S(1)}, u32[]{:S(2)}, u32[]{:S(2)}) collective-permute-start(bf16[2,2,128,512]{3,2,1,0:T(8,128)(2,1)S(1)} %add_convert_fusion.4), channel_id=1, source_target_pairs={{0,64},{32,480},{64,128},{96,32},{128,192},{160,96},{192,256},{224... | collective-permute-start | bytes 1572872 | tf_op jit(solution)/shard_map/ppermute | solution.py:35
  110.7 4.4 %collective-permute-start.21 = (bf16[2,2,128,512]{3,2,1,0:T(8,128)(2,1)S(1)}, bf16[2,2,128,512]{3,2,1,0:T(8,128)(2,1)S(1)}, u32[]{:S(2)}, u32[]{:S(2)}) collective-permute-start(bf16[2,2,128,512]{3,2,1,0:T(8,128)(2,1)S(1)} %pad_maximum_fusion.4), channel_id=1, source_target_pairs={{2,0},{3,1},{4,2},{5,3},{6,4},{7,5},{8,6},{9,7},{10,8},{11,9},{12,... | collective-permute-start | bytes 1572872 | tf_op jit(solution)/shard_map/ppermute | solution.py:51
  115.1 0.1 add_convert_fusion.1
  115.2 1.9 %collective-permute-start.20 = (bf16[2,2,128,512]{3,2,1,0:T(8,128)(2,1)S(1)}, bf16[2,2,128,512]{3,2,1,0:T(8,128)(2,1)S(1)}, u32[]{:S(2)}, u32[]{:S(2)}) collective-permute-start(bf16[2,2,128,512]{3,2,1,0:T(8,128)(2,1)S(1)} %add_convert_fusion.1), channel_id=1, source_target_pairs={{0,64},{32,480},{64,128},{96,32},{128,192},{160,96},{192,256},{224... | collective-permute-start | bytes 1572872 | tf_op jit(solution)/shard_map/ppermute | solution.py:35
  117.2 0.3 collective-permute-done.15
  117.4 0.1 add_convert_fusion.3
  117.6 4.3 %collective-permute-start.16 = (bf16[2,2,128,512]{3,2,1,0:T(8,128)(2,1)S(1)}, bf16[2,2,128,512]{3,2,1,0:T(8,128)(2,1)S(1)}, u32[]{:S(2)}, u32[]{:S(2)}) collective-permute-start(bf16[2,2,128,512]{3,2,1,0:T(8,128)(2,1)S(1)} %add_convert_fusion.3), channel_id=1, source_target_pairs={{0,64},{32,480},{64,128},{96,32},{128,192},{160,96},{192,256},{224... | collective-permute-start | bytes 1572872 | tf_op jit(solution)/shard_map/ppermute | solution.py:35
  121.9 1.2 collective-permute-done.21.refs_1_
  123.1 2.4 %collective-permute-done.20 = bf16[2,2,128,512]{3,2,1,0:T(8,128)(2,1)S(1)} collective-permute-done((bf16[2,2,128,512]{3,2,1,0:T(8,128)(2,1)S(1)}, bf16[2,2,128,512]{3,2,1,0:T(8,128)(2,1)S(1)}, u32[]{:S(2)}, u32[]{:S(2)}) %collective-permute-start.20) | collective-permute-done | bytes 524320 | tf_op jit(solution)/shard_map/ppermute | solution.py:35
  125.6 1.9 %collective-permute-start.22 = (bf16[2,2,128,512]{3,2,1,0:T(8,128)(2,1)S(1)}, bf16[2,2,128,512]{3,2,1,0:T(8,128)(2,1)S(1)}, u32[]{:S(2)}, u32[]{:S(2)}) collective-permute-start(bf16[2,2,128,512]{3,2,1,0:T(8,128)(2,1)S(1)} %pad_maximum_fusion.5), channel_id=1, source_target_pairs={{1,0},{2,1},{3,2},{4,3},{5,4},{6,5},{7,6},{8,7},{9,8},{10,9},{11,1... | collective-permute-start | bytes 1572872 | tf_op jit(solution)/shard_map/ppermute | solution.py:51
  127.5 0.1 add_convert_fusion
  127.6 3.2 %collective-permute-start.23 = (bf16[2,2,128,512]{3,2,1,0:T(8,128)(2,1)S(1)}, bf16[2,2,128,512]{3,2,1,0:T(8,128)(2,1)S(1)}, u32[]{:S(2)}, u32[]{:S(2)}) collective-permute-start(bf16[2,2,128,512]{3,2,1,0:T(8,128)(2,1)S(1)} %add_convert_fusion), channel_id=1, source_target_pairs={{0,64},{32,480},{64,128},{96,32},{128,192},{160,96},{192,256},{224... | collective-permute-start | bytes 1572872 | tf_op jit(solution)/shard_map/ppermute | solution.py:35
  130.9 0.2 collective-permute-done.16
  131.1 0.1 add_convert_fusion.2
  131.2 3.0 %collective-permute-start.17 = (bf16[2,2,128,512]{3,2,1,0:T(8,128)(2,1)S(1)}, bf16[2,2,128,512]{3,2,1,0:T(8,128)(2,1)S(1)}, u32[]{:S(2)}, u32[]{:S(2)}) collective-permute-start(bf16[2,2,128,512]{3,2,1,0:T(8,128)(2,1)S(1)} %add_convert_fusion.2), channel_id=1, source_target_pairs={{0,64},{32,480},{64,128},{96,32},{128,192},{160,96},{192,256},{224... | collective-permute-start | bytes 1572872 | tf_op jit(solution)/shard_map/ppermute | solution.py:35
  134.2 4.5 %collective-permute-done.22.refs_0_ = bf16[2,2,128,512]{3,2,1,0:T(8,128)(2,1)S(1)} collective-permute-done((bf16[2,2,128,512]{3,2,1,0:T(8,128)(2,1)S(1)}, bf16[2,2,128,512]{3,2,1,0:T(8,128)(2,1)S(1)}, u32[]{:S(2)}, u32[]{:S(2)}) %collective-permute-start.22) | collective-permute-done | bytes 524320 | tf_op jit(solution)/shard_map/ppermute | solution.py:51
  138.8 7.6 %collective-permute-start.24 = (bf16[2,2,128,512]{3,2,1,0:T(8,128)(2,1)S(1)}, bf16[2,2,128,512]{3,2,1,0:T(8,128)(2,1)S(1)}, u32[]{:S(2)}, u32[]{:S(2)}) collective-permute-start(bf16[2,2,128,512]{3,2,1,0:T(8,128)(2,1)S(1)} %collective-permute-done.23), channel_id=1, source_target_pairs={{0,32},{32,0},{64,96},{96,64},{128,160},{160,128},{192,224},{224,1... | collective-permute-start | bytes 1572872 | tf_op jit(solution)/shard_map/ppermute | solution.py:40
  146.4 1.9 %collective-permute-start.25 = (bf16[2,2,128,512]{3,2,1,0:T(8,128)(2,1)S(1)}, bf16[2,2,128,512]{3,2,1,0:T(8,128)(2,1)S(1)}, u32[]{:S(2)}, u32[]{:S(2)}) collective-permute-start(bf16[2,2,128,512]{3,2,1,0:T(8,128)(2,1)S(1)} %pad_maximum_fusion.6), channel_id=1, source_target_pairs={{0,32},{32,0},{64,96},{96,64},{128,160},{160,128},{192,224},{224,1... | collective-permute-start | bytes 1572872 | tf_op jit(solution)/shard_map/ppermute | solution.py:40
  148.4 1.9 %collective-permute-done.25.refs_2_ = bf16[2,2,128,512]{3,2,1,0:T(8,128)(2,1)S(1)} collective-permute-done((bf16[2,2,128,512]{3,2,1,0:T(8,128)(2,1)S(1)}, bf16[2,2,128,512]{3,2,1,0:T(8,128)(2,1)S(1)}, u32[]{:S(2)}, u32[]{:S(2)}) %collective-permute-start.25) | collective-permute-done | bytes 524320 | tf_op jit(solution)/shard_map/ppermute | solution.py:40
  150.2 1.9 %shard_map.98 = (bf16[256,512]{1,0:T(8,128)(2,1)}, bf16[256,512]{1,0:T(8,128)(2,1)}) custom-call(s32[6]{0:T(128)S(1)} %pad_add_fusion.6.table, bf16[2,2,128,512]{3,2,1,0:T(8,128)(2,1)S(1)} %get-tuple-element.60.near, bf16[6,2,128,512]{3,2,1,0:T(8,128)(2,1)S(1)} %collective-permute-done.13.theirs, ...), custom_call_target="tpu_custom_call" | custom-call | flops 4194304 | bytes 6291456 | tf_op jit(solution)/shard_map/pallas_call | solution.py:306
  (66 shorter events, 1.8 us)
Async XLA Ops:
  0.6 17.1 %copy-start.3 = (bf16[256,512]{1,0:T(8,128)(2,1)S(1)}, bf16[256,512]{1,0:T(8,128)(2,1)}, u32[]{:S(2)}) copy-start(bf16[256,512]{1,0:T(8,128)(2,1)} %keys.1) | copy-start | bytes 786436
  0.6 17.1 %copy-start.2 = (bf16[256,512]{1,0:T(8,128)(2,1)S(1)}, bf16[256,512]{1,0:T(8,128)(2,1)}, u32[]{:S(2)}) copy-start(bf16[256,512]{1,0:T(8,128)(2,1)} %values.1) | copy-start | bytes 786436
  1.8 22.9 %collective-permute-start.4 = (bf16[2,256,512]{2,1,0:T(8,128)(2,1)S(1)}, bf16[2,256,512]{2,1,0:T(8,128)(2,1)S(1)}, u32[]{:S(2)}, u32[]{:S(2)}) collective-permute-start(bf16[2,256,512]{2,1,0:T(8,128)(2,1)S(1)} %pad_maximum_fusion.refs_0_), channel_id=1, source_target_pairs={{0,64},{32,480},{64,128},{96,32},{128,192},{160,96},{192,256},{224... | collective-permute-start | bytes 1572872 | tf_op jit(solution)/shard_map/ppermute | solution.py:35
  12.5 5.3 %collective-permute-start = (bf16[2,256,512]{2,1,0:T(8,128)(2,1)S(1)}, bf16[2,256,512]{2,1,0:T(8,128)(2,1)S(1)}, u32[]{:S(2)}, u32[]{:S(2)}) collective-permute-start(bf16[2,256,512]{2,1,0:T(8,128)(2,1)S(1)} %pad_maximum_fusion.refs_0_), channel_id=1, source_target_pairs={{0,32},{32,0},{64,96},{96,64},{128,160},{160,128},{192,224},{224,1... | collective-permute-start | bytes 1572872 | tf_op jit(solution)/shard_map/ppermute | solution.py:40
  19.7 8.5 %collective-permute-start.2 = (bf16[2,2,128,512]{3,2,1,0:T(8,128)(2,1)S(1)}, bf16[2,2,128,512]{3,2,1,0:T(8,128)(2,1)}, u32[]{:S(2)}, u32[]{:S(2)}) collective-permute-start(bf16[2,2,128,512]{3,2,1,0:T(8,128)(2,1)S(1)} %get-tuple-element.47), channel_id=1, source_target_pairs={{0,32},{32,0},{64,96},{96,64},{128,160},{160,128},{192,224},{224,1... | collective-permute-start | bytes 1572872 | tf_op jit(solution)/shard_map/ppermute | solution.py:40
  22.5 19.2 %collective-permute-start.1 = (bf16[2,256,512]{2,1,0:T(8,128)(2,1)S(1)}, bf16[2,256,512]{2,1,0:T(8,128)(2,1)S(1)}, u32[]{:S(2)}, u32[]{:S(2)}) collective-permute-start(bf16[2,256,512]{2,1,0:T(8,128)(2,1)S(1)} %collective-permute-done.refs_0_.refs_4_), channel_id=1, source_target_pairs={{0,64},{32,480},{64,128},{96,32},{128,192},{160,96},{192,256},{224... | collective-permute-start | bytes 1572872 | tf_op jit(solution)/shard_map/ppermute | solution.py:35
  24.7 13.6 %collective-permute-start.5 = (bf16[2,256,512]{2,1,0:T(8,128)(2,1)S(1)}, bf16[2,256,512]{2,1,0:T(8,128)(2,1)S(1)}, u32[]{:S(2)}, u32[]{:S(2)}) collective-permute-start(bf16[2,256,512]{2,1,0:T(8,128)(2,1)S(1)} %collective-permute-done.4.refs_1_.refs_5_), channel_id=1, source_target_pairs={{0,64},{32,480},{64,128},{96,32},{128,192},{160,96},{192,256},{224... | collective-permute-start | bytes 1572872 | tf_op jit(solution)/shard_map/ppermute | solution.py:35
  29.3 16.5 %collective-permute-start.3 = (bf16[2,2,128,512]{3,2,1,0:T(8,128)(2,1)S(1)}, bf16[2,2,128,512]{3,2,1,0:T(8,128)(2,1)S(1)}, u32[]{:S(2)}, u32[]{:S(2)}) collective-permute-start(bf16[2,2,128,512]{3,2,1,0:T(8,128)(2,1)S(1)} %pad_maximum_fusion.1), channel_id=1, source_target_pairs={{0,2},{1,3},{2,4},{3,5},{4,6},{5,7},{6,8},{7,9},{8,10},{9,11},{10,... | collective-permute-start | bytes 1572872 | tf_op jit(solution)/shard_map/ppermute | solution.py:51
  38.3 11.3 %collective-permute-start.6 = (bf16[2,256,512]{2,1,0:T(8,128)(2,1)S(1)}, bf16[2,256,512]{2,1,0:T(8,128)(2,1)S(1)}, u32[]{:S(2)}, u32[]{:S(2)}) collective-permute-start(bf16[2,256,512]{2,1,0:T(8,128)(2,1)S(1)} %collective-permute-done.5.refs_2_.refs_6_), channel_id=1, source_target_pairs={{0,64},{32,480},{64,128},{96,32},{128,192},{160,96},{192,256},{224... | collective-permute-start | bytes 1572872 | tf_op jit(solution)/shard_map/ppermute | solution.py:35
  45.8 12.2 %collective-permute-start.10 = (bf16[2,256,512]{2,1,0:T(8,128)(2,1)S(1)}, bf16[2,256,512]{2,1,0:T(8,128)(2,1)S(1)}, u32[]{:S(2)}, u32[]{:S(2)}) collective-permute-start(bf16[2,256,512]{2,1,0:T(8,128)(2,1)S(1)} %collective-permute-done.1.refs_5_.refs_9_), channel_id=1, source_target_pairs={{0,64},{32,480},{64,128},{96,32},{128,192},{160,96},{192,256},{224... | collective-permute-start | bytes 1572872 | tf_op jit(solution)/shard_map/ppermute | solution.py:35
  49.6 12.1 %collective-permute-start.7 = (bf16[2,256,512]{2,1,0:T(8,128)(2,1)S(1)}, bf16[2,256,512]{2,1,0:T(8,128)(2,1)S(1)}, u32[]{:S(2)}, u32[]{:S(2)}) collective-permute-start(bf16[2,256,512]{2,1,0:T(8,128)(2,1)S(1)} %collective-permute-done.6.refs_3_.refs_7_), channel_id=1, source_target_pairs={{0,64},{32,480},{64,128},{96,32},{128,192},{160,96},{192,256},{224... | collective-permute-start | bytes 1572872 | tf_op jit(solution)/shard_map/ppermute | solution.py:35
  52.8 11.3 %collective-permute-start.8 = (bf16[2,2,128,512]{3,2,1,0:T(8,128)(2,1)S(1)}, bf16[2,2,128,512]{3,2,1,0:T(8,128)(2,1)S(1)}, u32[]{:S(2)}, u32[]{:S(2)}) collective-permute-start(bf16[2,2,128,512]{3,2,1,0:T(8,128)(2,1)S(1)} %pad_maximum_fusion.2), channel_id=1, source_target_pairs={{0,1},{1,2},{2,3},{3,4},{4,5},{5,6},{6,7},{7,8},{8,9},{9,10},{10,1... | collective-permute-start | bytes 1572872 | tf_op jit(solution)/shard_map/ppermute | solution.py:51
  58.0 10.2 %collective-permute-start.11 = (bf16[2,256,512]{2,1,0:T(8,128)(2,1)S(1)}, bf16[2,256,512]{2,1,0:T(8,128)(2,1)S(1)}, u32[]{:S(2)}, u32[]{:S(2)}) collective-permute-start(bf16[2,256,512]{2,1,0:T(8,128)(2,1)S(1)} %collective-permute-done.10.refs_6_.refs_10_), channel_id=1, source_target_pairs={{0,64},{32,480},{64,128},{96,32},{128,192},{160,96},{192,256},{224... | collective-permute-start | bytes 1572872 | tf_op jit(solution)/shard_map/ppermute | solution.py:35
  69.3 8.4 %copy-start.4 = (bf16[256,512]{1,0:T(8,128)(2,1)S(1)}, bf16[256,512]{1,0:T(8,128)(2,1)}, u32[]{:S(2)}) copy-start(bf16[256,512]{1,0:T(8,128)(2,1)} %param.6) | copy-start | bytes 786436
  69.3 8.4 %copy-start.5 = (bf16[256,512]{1,0:T(8,128)(2,1)S(1)}, bf16[256,512]{1,0:T(8,128)(2,1)}, u32[]{:S(2)}) copy-start(bf16[256,512]{1,0:T(8,128)(2,1)} %param.9) | copy-start | bytes 786436
  69.3 8.3 %collective-permute-start.12 = (bf16[6,2,128,512]{3,2,1,0:T(8,128)(2,1)S(1)}, bf16[6,2,128,512]{3,2,1,0:T(8,128)(2,1)S(1)}, u32[]{:S(2)}, u32[]{:S(2)}) collective-permute-start(bf16[6,2,128,512]{3,2,1,0:T(8,128)(2,1)S(1)} %shard_map.94), channel_id=1, source_target_pairs={{0,32},{32,0},{64,96},{96,64},{128,160},{160,128},{192,224},{224,1... | collective-permute-start | bytes 4718600 | tf_op jit(solution)/shard_map/ppermute | solution.py:40
  73.9 3.8 %collective-permute-start.9 = (bf16[2,2,128,512]{3,2,1,0:T(8,128)(2,1)S(1)}, bf16[2,2,128,512]{3,2,1,0:T(8,128)(2,1)S(1)}, u32[]{:S(2)}, u32[]{:S(2)}) collective-permute-start(bf16[2,2,128,512]{3,2,1,0:T(8,128)(2,1)S(1)} %pad_maximum_fusion.3), channel_id=1, source_target_pairs={{0,32},{32,0},{64,96},{96,64},{128,160},{160,128},{192,224},{224,1... | collective-permute-start | bytes 1572872 | tf_op jit(solution)/shard_map/ppermute | solution.py:40
  89.8 5.3 %collective-permute-start.13 = (bf16[6,2,128,512]{3,2,1,0:T(8,128)(2,1)S(1)}, bf16[6,2,128,512]{3,2,1,0:T(8,128)(2,1)S(1)}, u32[]{:S(2)}, u32[]{:S(2)}) collective-permute-start(bf16[6,2,128,512]{3,2,1,0:T(8,128)(2,1)S(1)} %get-tuple-element.61.mine), channel_id=1, source_target_pairs={{0,32},{32,0},{64,96},{96,64},{128,160},{160,128},{192,224},{224,1... | collective-permute-start | bytes 4718600 | tf_op jit(solution)/shard_map/ppermute | solution.py:40
  96.0 10.2 %collective-permute-start.14 = (bf16[2,2,128,512]{3,2,1,0:T(8,128)(2,1)S(1)}, bf16[2,2,128,512]{3,2,1,0:T(8,128)(2,1)S(1)}, u32[]{:S(2)}, u32[]{:S(2)}) collective-permute-start(bf16[2,2,128,512]{3,2,1,0:T(8,128)(2,1)S(1)} %get-tuple-element.65), channel_id=1, source_target_pairs={{0,64},{32,480},{64,128},{96,32},{128,192},{160,96},{192,256},{224... | collective-permute-start | bytes 1572872 | tf_op jit(solution)/shard_map/ppermute | solution.py:35
  99.3 11.3 %collective-permute-start.18 = (bf16[2,2,128,512]{3,2,1,0:T(8,128)(2,1)S(1)}, bf16[2,2,128,512]{3,2,1,0:T(8,128)(2,1)S(1)}, u32[]{:S(2)}, u32[]{:S(2)}) collective-permute-start(bf16[2,2,128,512]{3,2,1,0:T(8,128)(2,1)S(1)} %get-tuple-element.71), channel_id=1, source_target_pairs={{0,32},{32,0},{64,96},{96,64},{128,160},{160,128},{192,224},{224,1... | collective-permute-start | bytes 1572872 | tf_op jit(solution)/shard_map/ppermute | solution.py:40
  101.2 13.9 %collective-permute-start.19 = (bf16[2,2,128,512]{3,2,1,0:T(8,128)(2,1)S(1)}, bf16[2,2,128,512]{3,2,1,0:T(8,128)(2,1)S(1)}, u32[]{:S(2)}, u32[]{:S(2)}) collective-permute-start(bf16[2,2,128,512]{3,2,1,0:T(8,128)(2,1)S(1)} %get-tuple-element.72), channel_id=1, source_target_pairs={{0,64},{32,480},{64,128},{96,32},{128,192},{160,96},{192,256},{224... | collective-permute-start | bytes 1572872 | tf_op jit(solution)/shard_map/ppermute | solution.py:35
  106.3 11.1 %collective-permute-start.15 = (bf16[2,2,128,512]{3,2,1,0:T(8,128)(2,1)S(1)}, bf16[2,2,128,512]{3,2,1,0:T(8,128)(2,1)S(1)}, u32[]{:S(2)}, u32[]{:S(2)}) collective-permute-start(bf16[2,2,128,512]{3,2,1,0:T(8,128)(2,1)S(1)} %add_convert_fusion.4), channel_id=1, source_target_pairs={{0,64},{32,480},{64,128},{96,32},{128,192},{160,96},{192,256},{224... | collective-permute-start | bytes 1572872 | tf_op jit(solution)/shard_map/ppermute | solution.py:35
  110.7 12.4 %collective-permute-start.21 = (bf16[2,2,128,512]{3,2,1,0:T(8,128)(2,1)S(1)}, bf16[2,2,128,512]{3,2,1,0:T(8,128)(2,1)S(1)}, u32[]{:S(2)}, u32[]{:S(2)}) collective-permute-start(bf16[2,2,128,512]{3,2,1,0:T(8,128)(2,1)S(1)} %pad_maximum_fusion.4), channel_id=1, source_target_pairs={{2,0},{3,1},{4,2},{5,3},{6,4},{7,5},{8,6},{9,7},{10,8},{11,9},{12,... | collective-permute-start | bytes 1572872 | tf_op jit(solution)/shard_map/ppermute | solution.py:51
  115.2 10.2 %collective-permute-start.20 = (bf16[2,2,128,512]{3,2,1,0:T(8,128)(2,1)S(1)}, bf16[2,2,128,512]{3,2,1,0:T(8,128)(2,1)S(1)}, u32[]{:S(2)}, u32[]{:S(2)}) collective-permute-start(bf16[2,2,128,512]{3,2,1,0:T(8,128)(2,1)S(1)} %add_convert_fusion.1), channel_id=1, source_target_pairs={{0,64},{32,480},{64,128},{96,32},{128,192},{160,96},{192,256},{224... | collective-permute-start | bytes 1572872 | tf_op jit(solution)/shard_map/ppermute | solution.py:35
  117.6 13.5 %collective-permute-start.16 = (bf16[2,2,128,512]{3,2,1,0:T(8,128)(2,1)S(1)}, bf16[2,2,128,512]{3,2,1,0:T(8,128)(2,1)S(1)}, u32[]{:S(2)}, u32[]{:S(2)}) collective-permute-start(bf16[2,2,128,512]{3,2,1,0:T(8,128)(2,1)S(1)} %add_convert_fusion.3), channel_id=1, source_target_pairs={{0,64},{32,480},{64,128},{96,32},{128,192},{160,96},{192,256},{224... | collective-permute-start | bytes 1572872 | tf_op jit(solution)/shard_map/ppermute | solution.py:35
  123.1 7.7 %copy-start = (bf16[2,2,128,512]{3,2,1,0:T(8,128)(2,1)}, bf16[2,2,128,512]{3,2,1,0:T(8,128)(2,1)S(1)}, u32[]{:S(2)}) copy-start(bf16[2,2,128,512]{3,2,1,0:T(8,128)(2,1)S(1)} %collective-permute-done.21.refs_1_) | copy-start | bytes 1572868
  125.6 13.1 %collective-permute-start.22 = (bf16[2,2,128,512]{3,2,1,0:T(8,128)(2,1)S(1)}, bf16[2,2,128,512]{3,2,1,0:T(8,128)(2,1)S(1)}, u32[]{:S(2)}, u32[]{:S(2)}) collective-permute-start(bf16[2,2,128,512]{3,2,1,0:T(8,128)(2,1)S(1)} %pad_maximum_fusion.5), channel_id=1, source_target_pairs={{1,0},{2,1},{3,2},{4,3},{5,4},{6,5},{7,6},{8,7},{9,8},{10,9},{11,1... | collective-permute-start | bytes 1572872 | tf_op jit(solution)/shard_map/ppermute | solution.py:51
  127.6 11.1 %collective-permute-start.23 = (bf16[2,2,128,512]{3,2,1,0:T(8,128)(2,1)S(1)}, bf16[2,2,128,512]{3,2,1,0:T(8,128)(2,1)S(1)}, u32[]{:S(2)}, u32[]{:S(2)}) collective-permute-start(bf16[2,2,128,512]{3,2,1,0:T(8,128)(2,1)S(1)} %add_convert_fusion), channel_id=1, source_target_pairs={{0,64},{32,480},{64,128},{96,32},{128,192},{160,96},{192,256},{224... | collective-permute-start | bytes 1572872 | tf_op jit(solution)/shard_map/ppermute | solution.py:35
  130.8 7.9 %slice-start = ((bf16[2,2,128,512]{3,2,1,0:T(8,128)(2,1)}), bf16[1,2,128,512]{3,2,1,0:T(8,128)(2,1)S(1)}, s32[]{:S(2)}) async-start(bf16[2,2,128,512]{3,2,1,0:T(8,128)(2,1)} %copy-done), calls=%async_computation | async-start | bytes 524288 | tf_op jit(solution)/shard_map/slice | solution.py:416
  131.1 19.1 %copy-start.1 = (bf16[2,2,128,512]{3,2,1,0:T(8,128)(2,1)S(1)}, bf16[2,2,128,512]{3,2,1,0:T(8,128)(2,1)}, u32[]{:S(2)}) copy-start(bf16[2,2,128,512]{3,2,1,0:T(8,128)(2,1)} %copy-done) | copy-start | bytes 1572868
  131.2 17.1 %collective-permute-start.17 = (bf16[2,2,128,512]{3,2,1,0:T(8,128)(2,1)S(1)}, bf16[2,2,128,512]{3,2,1,0:T(8,128)(2,1)S(1)}, u32[]{:S(2)}, u32[]{:S(2)}) collective-permute-start(bf16[2,2,128,512]{3,2,1,0:T(8,128)(2,1)S(1)} %add_convert_fusion.2), channel_id=1, source_target_pairs={{0,64},{32,480},{64,128},{96,32},{128,192},{160,96},{192,256},{224... | collective-permute-start | bytes 1572872 | tf_op jit(solution)/shard_map/ppermute | solution.py:35
  138.8 9.6 %collective-permute-start.24 = (bf16[2,2,128,512]{3,2,1,0:T(8,128)(2,1)S(1)}, bf16[2,2,128,512]{3,2,1,0:T(8,128)(2,1)S(1)}, u32[]{:S(2)}, u32[]{:S(2)}) collective-permute-start(bf16[2,2,128,512]{3,2,1,0:T(8,128)(2,1)S(1)} %collective-permute-done.23), channel_id=1, source_target_pairs={{0,32},{32,0},{64,96},{96,64},{128,160},{160,128},{192,224},{224,1... | collective-permute-start | bytes 1572872 | tf_op jit(solution)/shard_map/ppermute | solution.py:40
  146.4 3.8 %collective-permute-start.25 = (bf16[2,2,128,512]{3,2,1,0:T(8,128)(2,1)S(1)}, bf16[2,2,128,512]{3,2,1,0:T(8,128)(2,1)S(1)}, u32[]{:S(2)}, u32[]{:S(2)}) collective-permute-start(bf16[2,2,128,512]{3,2,1,0:T(8,128)(2,1)S(1)} %pad_maximum_fusion.6), channel_id=1, source_target_pairs={{0,32},{32,0},{64,96},{96,64},{128,160},{160,128},{192,224},{224,1... | collective-permute-start | bytes 1572872 | tf_op jit(solution)/shard_map/ppermute | solution.py:40
